TPU v7x, 32 devices: a whole 2x2x4 slice. The times are simulated.
32 devices in a mesh: groups: 2 (over x), orient: 8 (over z, y), tile: 2 (over core).
Axes of the slice: x: 2, y: 2, z: 4, core: 2. Of those that a mesh axis runs over, the one named last changes fastest.
Arguments:
- spectra: float32 [16, 2, 256, 256], P(('groups', 'orient'), None, 'tile'), parts along dimension 0, may hold values from -6 to 6
- templates: float32 [8, 2, 256, 256], P('orient', None, 'tile'), may hold values from -1600 to 1600, as said below
- weights: float32 [512, 256], P('groups'), parts along dimension 0, may hold values from 0.1 to 1
Outputs:
- peak: float32 [16, 256, 256], P(('groups', 'orient'), 'tile'), parts along dimension 0
- mean_map: float32 [16, 256, 256], P(('groups', 'orient'), 'tile'), parts along dimension 0
- mean_square: float32 [16, 256, 256], P(('groups', 'orient'), 'tile'), parts along dimension 0
There are 2 independent parts, one for each index of `groups`. A program takes and returns all parts, laid end to end along the dimension named above; an argument that names none is the same for every part. Nothing has to cross between parts.
Inputs may be any that keep to these rules, and one draw needn't show every extreme that they name: `templates`: finite real values.
All inputs are finite; a program needn't handle non-finite values.
Results may differ from a plain program's by a relative error of at most 0.00029.
Values sent between devices are 32-bit elements; how exact they have to be, the bound alone decides.
No kernel may reach another device: no remote copies, remote signals or barrier semaphores. Data moves between devices by JAX's collectives and lax.ppermute only.
A program may use at most 64 MiB of HBM per device.

v0:
```python
import math

import jax
import jax.numpy as jnp
from jax import lax
from jax.sharding import PartitionSpec as P


def shifted(x, axis, by):
    peers = lax.axis_size(axis)
    return lax.ppermute(x, axis, [(i, (i + by) % peers) for i in range(peers)])


def twiddle(rows, cols, side):
    phase = rows[:, None] * cols[None, :] % side
    angle = phase.astype(jnp.float32) * (2.0 * math.pi / side)
    return (jnp.cos(angle), jnp.sin(angle))


def shards(spectra, templates, weights):
    side = spectra.shape[3]
    half = spectra.shape[2]
    n_orient = lax.axis_size("orient")
    out_rows = lax.axis_index("tile") * half + lax.iota(jnp.int32, half)
    freq = lax.iota(jnp.int32, side)
    row_cos, row_sin = twiddle(out_rows, freq, side)
    col_cos, col_sin = twiddle(freq, freq, side)
    row_table = jnp.concatenate([row_cos, row_sin], 0)
    highest = lax.Precision.HIGHEST
    whole_templates = lax.all_gather(templates, "tile", axis=2, tiled=True)
    power = jnp.mean(whole_templates * whole_templates, axis=(1, 2, 3), keepdims=True)
    scaling = jnp.sqrt(power + 1e-06)

    def correlate(full, template):
        real_part = (full[:, 0] * template[0] + full[:, 1] * template[1]) * weights
        imag_part = (full[:, 1] * template[0] - full[:, 0] * template[1]) * weights
        stack_real = jnp.einsum("yk,nkx->nyx", row_table, real_part, precision=highest)
        stack_imag = jnp.einsum("yk,nkx->nyx", row_table, imag_part, precision=highest)
        along_real = stack_real[:, :half] - stack_imag[:, half:]
        along_imag = stack_imag[:, :half] + stack_real[:, half:]
        maps = jnp.einsum("nyk,kx->nyx", along_real, col_cos, precision=highest)
        maps = maps - jnp.einsum("nyk,kx->nyx", along_imag, col_sin, precision=highest)
        return maps / side

    def absorb(stats, full, pieces):

        def one_orientation(carry, template):
            maps = correlate(full, template)
            best, total, squares = carry
            return ((jnp.maximum(best, maps), total + maps, squares + maps * maps), None)

        result, _ = lax.scan(one_orientation, stats, pieces)
        return result

    stat_shape = (spectra.shape[0], half, side)
    initial = (
        jnp.full(stat_shape, -jnp.inf, jnp.float32),
        jnp.zeros(stat_shape, jnp.float32),
        jnp.zeros(stat_shape, jnp.float32),
    )
    normed = whole_templates / scaling

    def visit(step, carry):
        held, best, total, squares = carry
        full = lax.all_gather(held, "tile", axis=2, tiled=True)
        best, total, squares = absorb((best, total, squares), full, normed)
        return shifted((held, best, total, squares), "orient", 1)

    _, best, total, squares = lax.fori_loop(0, n_orient, visit, (spectra,) + initial)
    count = n_orient * templates.shape[0]
    return (best, total / count, squares / count)


def solution(mesh):
    in_specs = (
        P(("groups", "orient"), None, "tile", None),
        P("orient", None, "tile", None),
        P("groups", None),
    )
    out_specs = (
        P(("groups", "orient"), "tile", None),
        P(("groups", "orient"), "tile", None),
        P(("groups", "orient"), "tile", None),
    )
    return jax.shard_map(shards, mesh=mesh, in_specs=in_specs, out_specs=out_specs, check_vma=False)
```

profile of v0, /device:TPU:0, one launch (start us, length us, event | category | flops | bytes accessed | tf_op | source)
XLA Modules:
  0.0 173.7 jit_solution(17262018775637251267)
XLA Ops:
  1.3 0.9 copy-done.2
  2.2 2.2 %all_gather.6 = f32[1,2,256,256]{3,2,1,0:T(8,128)S(1)} all-gather(f32[1,2,128,256]{3,2,1,0:T(8,128)S(1)} %copy-done.2), channel_id=1, replica_groups=mesh['groups'=2,'orient'=8,'tile'=2] {'tile'}, dimensions={2}, use_global_device_ids=true | all-gather | bytes 786432 | tf_op jit(solution)/shard_map/all_gather | solution.py:30
  4.4 0.7 multiply_reduce_fusion
  6.0 0.8 copy-done.1
  6.9 165.4 %while.16 = (s32[]{:T(128)}, f32[1,2,128,256]{3,2,1,0:T(8,128)S(1)}, f32[1,128,256]{2,1,0:T(8,128)S(1)}, f32[1,128,256]{2,1,0:T(8,128)S(1)}, f32[1,128,256]{2,1,...) while((s32[]{:T(128)}, ...), condition=%wide.region_2.3_spmd.clone, body=%wide.region_1.2_spmd.clone.sunk | while | flops 606601216 | bytes 9175293 | solution.py:69
  6.9 2.9 %collective-permute-start = (f32[1,2,128,256]{3,2,1,0:T(8,128)S(1)}, f32[1,2,128,256]{3,2,1,0:T(8,128)S(1)}, u32[]{:S(2)}, u32[]{:S(2)}) collective-permute-start(f32[1,2,128,256]{3,2,1,0:T(8,128)S(1)} %copy.12), channel_id=1, source_target_pairs={{0,2},{2,4},{4,6},{6,8},{8,10},{10,12},{12,14},{14,0},{1,3},{3,5},... | collective-permute-start | bytes 786440 | tf_op jit(solution)/shard_map/while/body/eval_jaxpr/ppermute | solution.py:11
  9.9 2.2 %all_gather.9 = f32[1,2,256,256]{3,2,1,0:T(8,128)S(1)} all-gather(f32[1,2,128,256]{3,2,1,0:T(8,128)S(1)} %copy.12), channel_id=1, replica_groups=mesh['groups'=2,'orient'=8,'tile'=2] {'tile'}, dimensions={2}, use_global_device_ids=true | all-gather | bytes 786432 | tf_op jit(solution)/shard_map/while/body/eval_jaxpr/all_gather | solution.py:65
  13.3 1.3 fusion.63
  14.6 1.3 bitcast_add_fusion.3
  16.0 1.6 collective-permute-start.1
  17.5 1.5 collective-permute-start.2
  19.1 1.5 collective-permute-start.3
  20.6 4.5 %collective-permute-done.1 = f32[1,128,256]{2,1,0:T(8,128)S(1)} collective-permute-done((f32[1,128,256]{2,1,0:T(8,128)S(1)}, f32[1,128,256]{2,1,0:T(8,128)S(1)}, u32[]{:S(2)}, u32[]{:S(2)}) %collective-permute-start.1) | collective-permute-done | bytes 131104 | tf_op jit(solution)/shard_map/while/body/eval_jaxpr/ppermute | solution.py:11
  25.0 2.8 %collective-permute-done.2 = f32[1,128,256]{2,1,0:T(8,128)S(1)} collective-permute-done((f32[1,128,256]{2,1,0:T(8,128)S(1)}, f32[1,128,256]{2,1,0:T(8,128)S(1)}, u32[]{:S(2)}, u32[]{:S(2)}) %collective-permute-start.2) | collective-permute-done | bytes 131104 | tf_op jit(solution)/shard_map/while/body/eval_jaxpr/ppermute | solution.py:11
  27.9 2.0 %collective-permute-done.3 = f32[1,128,256]{2,1,0:T(8,128)S(1)} collective-permute-done((f32[1,128,256]{2,1,0:T(8,128)S(1)}, f32[1,128,256]{2,1,0:T(8,128)S(1)}, u32[]{:S(2)}, u32[]{:S(2)}) %collective-permute-start.3) | collective-permute-done | bytes 131104 | tf_op jit(solution)/shard_map/while/body/eval_jaxpr/ppermute | solution.py:11
  30.0 2.2 %all_gather.9 = f32[1,2,256,256]{3,2,1,0:T(8,128)S(1)} all-gather(f32[1,2,128,256]{3,2,1,0:T(8,128)S(1)} %copy.12), channel_id=1, replica_groups=mesh['groups'=2,'orient'=8,'tile'=2] {'tile'}, dimensions={2}, use_global_device_ids=true | all-gather | bytes 786432 | tf_op jit(solution)/shard_map/while/body/eval_jaxpr/all_gather | solution.py:65
  33.4 1.3 fusion.63
  34.7 1.3 bitcast_add_fusion.3
  36.1 1.3 collective-permute-start.1
  37.9 2.4 %collective-permute-start.3 = (f32[1,128,256]{2,1,0:T(8,128)S(1)}, f32[1,128,256]{2,1,0:T(8,128)S(1)}, u32[]{:S(2)}, u32[]{:S(2)}) collective-permute-start(f32[1,128,256]{2,1,0:T(8,128)S(1)} %get-tuple-element.186), channel_id=1, source_target_pairs={{0,2},{2,4},{4,6},{6,8},{8,10},{10,12},{12,14},{14,0},{1,3},{3,5},... | collective-permute-start | bytes 393224 | tf_op jit(solution)/shard_map/while/body/eval_jaxpr/ppermute | solution.py:11
  40.4 4.7 %collective-permute-done.1 = f32[1,128,256]{2,1,0:T(8,128)S(1)} collective-permute-done((f32[1,128,256]{2,1,0:T(8,128)S(1)}, f32[1,128,256]{2,1,0:T(8,128)S(1)}, u32[]{:S(2)}, u32[]{:S(2)}) %collective-permute-start.1) | collective-permute-done | bytes 131104 | tf_op jit(solution)/shard_map/while/body/eval_jaxpr/ppermute | solution.py:11
  45.1 2.8 %collective-permute-done.2 = f32[1,128,256]{2,1,0:T(8,128)S(1)} collective-permute-done((f32[1,128,256]{2,1,0:T(8,128)S(1)}, f32[1,128,256]{2,1,0:T(8,128)S(1)}, u32[]{:S(2)}, u32[]{:S(2)}) %collective-permute-start.2) | collective-permute-done | bytes 131104 | tf_op jit(solution)/shard_map/while/body/eval_jaxpr/ppermute | solution.py:11
  47.9 2.3 %collective-permute-done.3 = f32[1,128,256]{2,1,0:T(8,128)S(1)} collective-permute-done((f32[1,128,256]{2,1,0:T(8,128)S(1)}, f32[1,128,256]{2,1,0:T(8,128)S(1)}, u32[]{:S(2)}, u32[]{:S(2)}) %collective-permute-start.3) | collective-permute-done | bytes 131104 | tf_op jit(solution)/shard_map/while/body/eval_jaxpr/ppermute | solution.py:11
  50.3 2.2 %all_gather.9 = f32[1,2,256,256]{3,2,1,0:T(8,128)S(1)} all-gather(f32[1,2,128,256]{3,2,1,0:T(8,128)S(1)} %copy.12), channel_id=1, replica_groups=mesh['groups'=2,'orient'=8,'tile'=2] {'tile'}, dimensions={2}, use_global_device_ids=true | all-gather | bytes 786432 | tf_op jit(solution)/shard_map/while/body/eval_jaxpr/all_gather | solution.py:65
  53.8 1.3 fusion.63
  55.1 1.3 bitcast_add_fusion.3
  56.5 1.3 collective-permute-start.2
  57.7 1.5 collective-permute-start.3
  59.3 6.2 %collective-permute-done.1 = f32[1,128,256]{2,1,0:T(8,128)S(1)} collective-permute-done((f32[1,128,256]{2,1,0:T(8,128)S(1)}, f32[1,128,256]{2,1,0:T(8,128)S(1)}, u32[]{:S(2)}, u32[]{:S(2)}) %collective-permute-start.1) | collective-permute-done | bytes 131104 | tf_op jit(solution)/shard_map/while/body/eval_jaxpr/ppermute | solution.py:11
  65.5 2.8 %collective-permute-done.2 = f32[1,128,256]{2,1,0:T(8,128)S(1)} collective-permute-done((f32[1,128,256]{2,1,0:T(8,128)S(1)}, f32[1,128,256]{2,1,0:T(8,128)S(1)}, u32[]{:S(2)}, u32[]{:S(2)}) %collective-permute-start.2) | collective-permute-done | bytes 131104 | tf_op jit(solution)/shard_map/while/body/eval_jaxpr/ppermute | solution.py:11
  68.3 2.3 %collective-permute-done.3 = f32[1,128,256]{2,1,0:T(8,128)S(1)} collective-permute-done((f32[1,128,256]{2,1,0:T(8,128)S(1)}, f32[1,128,256]{2,1,0:T(8,128)S(1)}, u32[]{:S(2)}, u32[]{:S(2)}) %collective-permute-start.3) | collective-permute-done | bytes 131104 | tf_op jit(solution)/shard_map/while/body/eval_jaxpr/ppermute | solution.py:11
  70.7 2.2 %all_gather.9 = f32[1,2,256,256]{3,2,1,0:T(8,128)S(1)} all-gather(f32[1,2,128,256]{3,2,1,0:T(8,128)S(1)} %copy.12), channel_id=1, replica_groups=mesh['groups'=2,'orient'=8,'tile'=2] {'tile'}, dimensions={2}, use_global_device_ids=true | all-gather | bytes 786432 | tf_op jit(solution)/shard_map/while/body/eval_jaxpr/all_gather | solution.py:65
  74.1 1.3 fusion.63
  75.4 1.3 bitcast_add_fusion.3
  76.9 2.1 %collective-permute-start.3 = (f32[1,128,256]{2,1,0:T(8,128)S(1)}, f32[1,128,256]{2,1,0:T(8,128)S(1)}, u32[]{:S(2)}, u32[]{:S(2)}) collective-permute-start(f32[1,128,256]{2,1,0:T(8,128)S(1)} %get-tuple-element.186), channel_id=1, source_target_pairs={{0,2},{2,4},{4,6},{6,8},{8,10},{10,12},{12,14},{14,0},{1,3},{3,5},... | collective-permute-start | bytes 393224 | tf_op jit(solution)/shard_map/while/body/eval_jaxpr/ppermute | solution.py:11
  79.0 6.8 %collective-permute-done.1 = f32[1,128,256]{2,1,0:T(8,128)S(1)} collective-permute-done((f32[1,128,256]{2,1,0:T(8,128)S(1)}, f32[1,128,256]{2,1,0:T(8,128)S(1)}, u32[]{:S(2)}, u32[]{:S(2)}) %collective-permute-start.1) | collective-permute-done | bytes 131104 | tf_op jit(solution)/shard_map/while/body/eval_jaxpr/ppermute | solution.py:11
  85.8 2.8 %collective-permute-done.2 = f32[1,128,256]{2,1,0:T(8,128)S(1)} collective-permute-done((f32[1,128,256]{2,1,0:T(8,128)S(1)}, f32[1,128,256]{2,1,0:T(8,128)S(1)}, u32[]{:S(2)}, u32[]{:S(2)}) %collective-permute-start.2) | collective-permute-done | bytes 131104 | tf_op jit(solution)/shard_map/while/body/eval_jaxpr/ppermute | solution.py:11
  88.6 2.3 %collective-permute-done.3 = f32[1,128,256]{2,1,0:T(8,128)S(1)} collective-permute-done((f32[1,128,256]{2,1,0:T(8,128)S(1)}, f32[1,128,256]{2,1,0:T(8,128)S(1)}, u32[]{:S(2)}, u32[]{:S(2)}) %collective-permute-start.3) | collective-permute-done | bytes 131104 | tf_op jit(solution)/shard_map/while/body/eval_jaxpr/ppermute | solution.py:11
  91.0 2.2 %all_gather.9 = f32[1,2,256,256]{3,2,1,0:T(8,128)S(1)} all-gather(f32[1,2,128,256]{3,2,1,0:T(8,128)S(1)} %copy.12), channel_id=1, replica_groups=mesh['groups'=2,'orient'=8,'tile'=2] {'tile'}, dimensions={2}, use_global_device_ids=true | all-gather | bytes 786432 | tf_op jit(solution)/shard_map/while/body/eval_jaxpr/all_gather | solution.py:65
  94.5 1.3 fusion.63
  95.8 1.3 bitcast_add_fusion.3
  97.7 8.5 %collective-permute-done.1 = f32[1,128,256]{2,1,0:T(8,128)S(1)} collective-permute-done((f32[1,128,256]{2,1,0:T(8,128)S(1)}, f32[1,128,256]{2,1,0:T(8,128)S(1)}, u32[]{:S(2)}, u32[]{:S(2)}) %collective-permute-start.1) | collective-permute-done | bytes 131104 | tf_op jit(solution)/shard_map/while/body/eval_jaxpr/ppermute | solution.py:11
  106.2 2.8 %collective-permute-done.2 = f32[1,128,256]{2,1,0:T(8,128)S(1)} collective-permute-done((f32[1,128,256]{2,1,0:T(8,128)S(1)}, f32[1,128,256]{2,1,0:T(8,128)S(1)}, u32[]{:S(2)}, u32[]{:S(2)}) %collective-permute-start.2) | collective-permute-done | bytes 131104 | tf_op jit(solution)/shard_map/while/body/eval_jaxpr/ppermute | solution.py:11
  109.0 2.3 %collective-permute-done.3 = f32[1,128,256]{2,1,0:T(8,128)S(1)} collective-permute-done((f32[1,128,256]{2,1,0:T(8,128)S(1)}, f32[1,128,256]{2,1,0:T(8,128)S(1)}, u32[]{:S(2)}, u32[]{:S(2)}) %collective-permute-start.3) | collective-permute-done | bytes 131104 | tf_op jit(solution)/shard_map/while/body/eval_jaxpr/ppermute | solution.py:11
  111.4 2.2 %all_gather.9 = f32[1,2,256,256]{3,2,1,0:T(8,128)S(1)} all-gather(f32[1,2,128,256]{3,2,1,0:T(8,128)S(1)} %copy.12), channel_id=1, replica_groups=mesh['groups'=2,'orient'=8,'tile'=2] {'tile'}, dimensions={2}, use_global_device_ids=true | all-gather | bytes 786432 | tf_op jit(solution)/shard_map/while/body/eval_jaxpr/all_gather | solution.py:65
  114.8 1.3 fusion.63
  116.1 1.3 bitcast_add_fusion.3
  118.2 8.4 %collective-permute-done.1 = f32[1,128,256]{2,1,0:T(8,128)S(1)} collective-permute-done((f32[1,128,256]{2,1,0:T(8,128)S(1)}, f32[1,128,256]{2,1,0:T(8,128)S(1)}, u32[]{:S(2)}, u32[]{:S(2)}) %collective-permute-start.1) | collective-permute-done | bytes 131104 | tf_op jit(solution)/shard_map/while/body/eval_jaxpr/ppermute | solution.py:11
  126.5 2.8 %collective-permute-done.2 = f32[1,128,256]{2,1,0:T(8,128)S(1)} collective-permute-done((f32[1,128,256]{2,1,0:T(8,128)S(1)}, f32[1,128,256]{2,1,0:T(8,128)S(1)}, u32[]{:S(2)}, u32[]{:S(2)}) %collective-permute-start.2) | collective-permute-done | bytes 131104 | tf_op jit(solution)/shard_map/while/body/eval_jaxpr/ppermute | solution.py:11
  129.3 2.3 %collective-permute-done.3 = f32[1,128,256]{2,1,0:T(8,128)S(1)} collective-permute-done((f32[1,128,256]{2,1,0:T(8,128)S(1)}, f32[1,128,256]{2,1,0:T(8,128)S(1)}, u32[]{:S(2)}, u32[]{:S(2)}) %collective-permute-start.3) | collective-permute-done | bytes 131104 | tf_op jit(solution)/shard_map/while/body/eval_jaxpr/ppermute | solution.py:11
  131.7 2.2 %all_gather.9 = f32[1,2,256,256]{3,2,1,0:T(8,128)S(1)} all-gather(f32[1,2,128,256]{3,2,1,0:T(8,128)S(1)} %copy.12), channel_id=1, replica_groups=mesh['groups'=2,'orient'=8,'tile'=2] {'tile'}, dimensions={2}, use_global_device_ids=true | all-gather | bytes 786432 | tf_op jit(solution)/shard_map/while/body/eval_jaxpr/all_gather | solution.py:65
  135.2 1.3 fusion.63
  136.5 1.3 bitcast_add_fusion.3
  138.5 8.4 %collective-permute-done.1 = f32[1,128,256]{2,1,0:T(8,128)S(1)} collective-permute-done((f32[1,128,256]{2,1,0:T(8,128)S(1)}, f32[1,128,256]{2,1,0:T(8,128)S(1)}, u32[]{:S(2)}, u32[]{:S(2)}) %collective-permute-start.1) | collective-permute-done | bytes 131104 | tf_op jit(solution)/shard_map/while/body/eval_jaxpr/ppermute | solution.py:11
  146.9 2.8 %collective-permute-done.2 = f32[1,128,256]{2,1,0:T(8,128)S(1)} collective-permute-done((f32[1,128,256]{2,1,0:T(8,128)S(1)}, f32[1,128,256]{2,1,0:T(8,128)S(1)}, u32[]{:S(2)}, u32[]{:S(2)}) %collective-permute-start.2) | collective-permute-done | bytes 131104 | tf_op jit(solution)/shard_map/while/body/eval_jaxpr/ppermute | solution.py:11
  149.7 2.3 %collective-permute-done.3 = f32[1,128,256]{2,1,0:T(8,128)S(1)} collective-permute-done((f32[1,128,256]{2,1,0:T(8,128)S(1)}, f32[1,128,256]{2,1,0:T(8,128)S(1)}, u32[]{:S(2)}, u32[]{:S(2)}) %collective-permute-start.3) | collective-permute-done | bytes 131104 | tf_op jit(solution)/shard_map/while/body/eval_jaxpr/ppermute | solution.py:11
  152.1 2.2 %all_gather.9 = f32[1,2,256,256]{3,2,1,0:T(8,128)S(1)} all-gather(f32[1,2,128,256]{3,2,1,0:T(8,128)S(1)} %copy.12), channel_id=1, replica_groups=mesh['groups'=2,'orient'=8,'tile'=2] {'tile'}, dimensions={2}, use_global_device_ids=true | all-gather | bytes 786432 | tf_op jit(solution)/shard_map/while/body/eval_jaxpr/all_gather | solution.py:65
  155.5 1.3 fusion.63
  156.8 1.3 bitcast_add_fusion.3
  158.9 8.4 %collective-permute-done.1 = f32[1,128,256]{2,1,0:T(8,128)S(1)} collective-permute-done((f32[1,128,256]{2,1,0:T(8,128)S(1)}, f32[1,128,256]{2,1,0:T(8,128)S(1)}, u32[]{:S(2)}, u32[]{:S(2)}) %collective-permute-start.1) | collective-permute-done | bytes 131104 | tf_op jit(solution)/shard_map/while/body/eval_jaxpr/ppermute | solution.py:11
  167.2 2.8 %collective-permute-done.2 = f32[1,128,256]{2,1,0:T(8,128)S(1)} collective-permute-done((f32[1,128,256]{2,1,0:T(8,128)S(1)}, f32[1,128,256]{2,1,0:T(8,128)S(1)}, u32[]{:S(2)}, u32[]{:S(2)}) %collective-permute-start.2) | collective-permute-done | bytes 131104 | tf_op jit(solution)/shard_map/while/body/eval_jaxpr/ppermute | solution.py:11
  170.0 2.3 %collective-permute-done.3 = f32[1,128,256]{2,1,0:T(8,128)S(1)} collective-permute-done((f32[1,128,256]{2,1,0:T(8,128)S(1)}, f32[1,128,256]{2,1,0:T(8,128)S(1)}, u32[]{:S(2)}, u32[]{:S(2)}) %collective-permute-start.3) | collective-permute-done | bytes 131104 | tf_op jit(solution)/shard_map/while/body/eval_jaxpr/ppermute | solution.py:11
  172.3 0.7 broadcast_multiply_fusion
  173.1 0.7 copy.26
  (66 shorter events, 14.9 us)
Async XLA Ops:
  1.2 1.0 copy-start.2
  5.9 1.0 copy-start.1
  5.9 1.0 copy-start
  6.9 22.9 %collective-permute-start = (f32[1,2,128,256]{3,2,1,0:T(8,128)S(1)}, f32[1,2,128,256]{3,2,1,0:T(8,128)S(1)}, u32[]{:S(2)}, u32[]{:S(2)}) collective-permute-start(f32[1,2,128,256]{3,2,1,0:T(8,128)S(1)} %copy.12), channel_id=1, source_target_pairs={{0,2},{2,4},{4,6},{6,8},{8,10},{10,12},{12,14},{14,0},{1,3},{3,5},... | collective-permute-start | bytes 786440 | tf_op jit(solution)/shard_map/while/body/eval_jaxpr/ppermute | solution.py:11
  16.0 9.1 %collective-permute-start.1 = (f32[1,128,256]{2,1,0:T(8,128)S(1)}, f32[1,128,256]{2,1,0:T(8,128)S(1)}, u32[]{:S(2)}, u32[]{:S(2)}) collective-permute-start(f32[1,128,256]{2,1,0:T(8,128)S(1)} %get-tuple-element.184), channel_id=1, source_target_pairs={{0,2},{2,4},{4,6},{6,8},{8,10},{10,12},{12,14},{14,0},{1,3},{3,5},... | collective-permute-start | bytes 393224 | tf_op jit(solution)/shard_map/while/body/eval_jaxpr/ppermute | solution.py:11
  17.5 10.3 %collective-permute-start.2 = (f32[1,128,256]{2,1,0:T(8,128)S(1)}, f32[1,128,256]{2,1,0:T(8,128)S(1)}, u32[]{:S(2)}, u32[]{:S(2)}) collective-permute-start(f32[1,128,256]{2,1,0:T(8,128)S(1)} %get-tuple-element.185), channel_id=1, source_target_pairs={{0,2},{2,4},{4,6},{6,8},{8,10},{10,12},{12,14},{14,0},{1,3},{3,5},... | collective-permute-start | bytes 393224 | tf_op jit(solution)/shard_map/while/body/eval_jaxpr/ppermute | solution.py:11
  19.1 10.8 %collective-permute-start.3 = (f32[1,128,256]{2,1,0:T(8,128)S(1)}, f32[1,128,256]{2,1,0:T(8,128)S(1)}, u32[]{:S(2)}, u32[]{:S(2)}) collective-permute-start(f32[1,128,256]{2,1,0:T(8,128)S(1)} %get-tuple-element.186), channel_id=1, source_target_pairs={{0,2},{2,4},{4,6},{6,8},{8,10},{10,12},{12,14},{14,0},{1,3},{3,5},... | collective-permute-start | bytes 393224 | tf_op jit(solution)/shard_map/while/body/eval_jaxpr/ppermute | solution.py:11
  29.9 20.3 %collective-permute-start = (f32[1,2,128,256]{3,2,1,0:T(8,128)S(1)}, f32[1,2,128,256]{3,2,1,0:T(8,128)S(1)}, u32[]{:S(2)}, u32[]{:S(2)}) collective-permute-start(f32[1,2,128,256]{3,2,1,0:T(8,128)S(1)} %copy.12), channel_id=1, source_target_pairs={{0,2},{2,4},{4,6},{6,8},{8,10},{10,12},{12,14},{14,0},{1,3},{3,5},... | collective-permute-start | bytes 786440 | tf_op jit(solution)/shard_map/while/body/eval_jaxpr/ppermute | solution.py:11
  36.1 9.1 %collective-permute-start.1 = (f32[1,128,256]{2,1,0:T(8,128)S(1)}, f32[1,128,256]{2,1,0:T(8,128)S(1)}, u32[]{:S(2)}, u32[]{:S(2)}) collective-permute-start(f32[1,128,256]{2,1,0:T(8,128)S(1)} %get-tuple-element.184), channel_id=1, source_target_pairs={{0,2},{2,4},{4,6},{6,8},{8,10},{10,12},{12,14},{14,0},{1,3},{3,5},... | collective-permute-start | bytes 393224 | tf_op jit(solution)/shard_map/while/body/eval_jaxpr/ppermute | solution.py:11
  37.3 10.6 %collective-permute-start.2 = (f32[1,128,256]{2,1,0:T(8,128)S(1)}, f32[1,128,256]{2,1,0:T(8,128)S(1)}, u32[]{:S(2)}, u32[]{:S(2)}) collective-permute-start(f32[1,128,256]{2,1,0:T(8,128)S(1)} %get-tuple-element.185), channel_id=1, source_target_pairs={{0,2},{2,4},{4,6},{6,8},{8,10},{10,12},{12,14},{14,0},{1,3},{3,5},... | collective-permute-start | bytes 393224 | tf_op jit(solution)/shard_map/while/body/eval_jaxpr/ppermute | solution.py:11
  37.9 12.3 %collective-permute-start.3 = (f32[1,128,256]{2,1,0:T(8,128)S(1)}, f32[1,128,256]{2,1,0:T(8,128)S(1)}, u32[]{:S(2)}, u32[]{:S(2)}) collective-permute-start(f32[1,128,256]{2,1,0:T(8,128)S(1)} %get-tuple-element.186), channel_id=1, source_target_pairs={{0,2},{2,4},{4,6},{6,8},{8,10},{10,12},{12,14},{14,0},{1,3},{3,5},... | collective-permute-start | bytes 393224 | tf_op jit(solution)/shard_map/while/body/eval_jaxpr/ppermute | solution.py:11
  50.2 20.3 %collective-permute-start = (f32[1,2,128,256]{3,2,1,0:T(8,128)S(1)}, f32[1,2,128,256]{3,2,1,0:T(8,128)S(1)}, u32[]{:S(2)}, u32[]{:S(2)}) collective-permute-start(f32[1,2,128,256]{3,2,1,0:T(8,128)S(1)} %copy.12), channel_id=1, source_target_pairs={{0,2},{2,4},{4,6},{6,8},{8,10},{10,12},{12,14},{14,0},{1,3},{3,5},... | collective-permute-start | bytes 786440 | tf_op jit(solution)/shard_map/while/body/eval_jaxpr/ppermute | solution.py:11
  56.4 9.1 %collective-permute-start.1 = (f32[1,128,256]{2,1,0:T(8,128)S(1)}, f32[1,128,256]{2,1,0:T(8,128)S(1)}, u32[]{:S(2)}, u32[]{:S(2)}) collective-permute-start(f32[1,128,256]{2,1,0:T(8,128)S(1)} %get-tuple-element.184), channel_id=1, source_target_pairs={{0,2},{2,4},{4,6},{6,8},{8,10},{10,12},{12,14},{14,0},{1,3},{3,5},... | collective-permute-start | bytes 393224 | tf_op jit(solution)/shard_map/while/body/eval_jaxpr/ppermute | solution.py:11
  56.5 11.8 %collective-permute-start.2 = (f32[1,128,256]{2,1,0:T(8,128)S(1)}, f32[1,128,256]{2,1,0:T(8,128)S(1)}, u32[]{:S(2)}, u32[]{:S(2)}) collective-permute-start(f32[1,128,256]{2,1,0:T(8,128)S(1)} %get-tuple-element.185), channel_id=1, source_target_pairs={{0,2},{2,4},{4,6},{6,8},{8,10},{10,12},{12,14},{14,0},{1,3},{3,5},... | collective-permute-start | bytes 393224 | tf_op jit(solution)/shard_map/while/body/eval_jaxpr/ppermute | solution.py:11
  57.7 12.8 %collective-permute-start.3 = (f32[1,128,256]{2,1,0:T(8,128)S(1)}, f32[1,128,256]{2,1,0:T(8,128)S(1)}, u32[]{:S(2)}, u32[]{:S(2)}) collective-permute-start(f32[1,128,256]{2,1,0:T(8,128)S(1)} %get-tuple-element.186), channel_id=1, source_target_pairs={{0,2},{2,4},{4,6},{6,8},{8,10},{10,12},{12,14},{14,0},{1,3},{3,5},... | collective-permute-start | bytes 393224 | tf_op jit(solution)/shard_map/while/body/eval_jaxpr/ppermute | solution.py:11
  70.6 20.3 %collective-permute-start = (f32[1,2,128,256]{3,2,1,0:T(8,128)S(1)}, f32[1,2,128,256]{3,2,1,0:T(8,128)S(1)}, u32[]{:S(2)}, u32[]{:S(2)}) collective-permute-start(f32[1,2,128,256]{3,2,1,0:T(8,128)S(1)} %copy.12), channel_id=1, source_target_pairs={{0,2},{2,4},{4,6},{6,8},{8,10},{10,12},{12,14},{14,0},{1,3},{3,5},... | collective-permute-start | bytes 786440 | tf_op jit(solution)/shard_map/while/body/eval_jaxpr/ppermute | solution.py:11
  76.8 9.1 %collective-permute-start.1 = (f32[1,128,256]{2,1,0:T(8,128)S(1)}, f32[1,128,256]{2,1,0:T(8,128)S(1)}, u32[]{:S(2)}, u32[]{:S(2)}) collective-permute-start(f32[1,128,256]{2,1,0:T(8,128)S(1)} %get-tuple-element.184), channel_id=1, source_target_pairs={{0,2},{2,4},{4,6},{6,8},{8,10},{10,12},{12,14},{14,0},{1,3},{3,5},... | collective-permute-start | bytes 393224 | tf_op jit(solution)/shard_map/while/body/eval_jaxpr/ppermute | solution.py:11
  76.8 11.8 %collective-permute-start.2 = (f32[1,128,256]{2,1,0:T(8,128)S(1)}, f32[1,128,256]{2,1,0:T(8,128)S(1)}, u32[]{:S(2)}, u32[]{:S(2)}) collective-permute-start(f32[1,128,256]{2,1,0:T(8,128)S(1)} %get-tuple-element.185), channel_id=1, source_target_pairs={{0,2},{2,4},{4,6},{6,8},{8,10},{10,12},{12,14},{14,0},{1,3},{3,5},... | collective-permute-start | bytes 393224 | tf_op jit(solution)/shard_map/while/body/eval_jaxpr/ppermute | solution.py:11
  76.9 14.0 %collective-permute-start.3 = (f32[1,128,256]{2,1,0:T(8,128)S(1)}, f32[1,128,256]{2,1,0:T(8,128)S(1)}, u32[]{:S(2)}, u32[]{:S(2)}) collective-permute-start(f32[1,128,256]{2,1,0:T(8,128)S(1)} %get-tuple-element.186), channel_id=1, source_target_pairs={{0,2},{2,4},{4,6},{6,8},{8,10},{10,12},{12,14},{14,0},{1,3},{3,5},... | collective-permute-start | bytes 393224 | tf_op jit(solution)/shard_map/while/body/eval_jaxpr/ppermute | solution.py:11
  91.0 20.3 %collective-permute-start = (f32[1,2,128,256]{3,2,1,0:T(8,128)S(1)}, f32[1,2,128,256]{3,2,1,0:T(8,128)S(1)}, u32[]{:S(2)}, u32[]{:S(2)}) collective-permute-start(f32[1,2,128,256]{3,2,1,0:T(8,128)S(1)} %copy.12), channel_id=1, source_target_pairs={{0,2},{2,4},{4,6},{6,8},{8,10},{10,12},{12,14},{14,0},{1,3},{3,5},... | collective-permute-start | bytes 786440 | tf_op jit(solution)/shard_map/while/body/eval_jaxpr/ppermute | solution.py:11
  97.1 9.1 %collective-permute-start.1 = (f32[1,128,256]{2,1,0:T(8,128)S(1)}, f32[1,128,256]{2,1,0:T(8,128)S(1)}, u32[]{:S(2)}, u32[]{:S(2)}) collective-permute-start(f32[1,128,256]{2,1,0:T(8,128)S(1)} %get-tuple-element.184), channel_id=1, source_target_pairs={{0,2},{2,4},{4,6},{6,8},{8,10},{10,12},{12,14},{14,0},{1,3},{3,5},... | collective-permute-start | bytes 393224 | tf_op jit(solution)/shard_map/while/body/eval_jaxpr/ppermute | solution.py:11
  97.2 11.8 %collective-permute-start.2 = (f32[1,128,256]{2,1,0:T(8,128)S(1)}, f32[1,128,256]{2,1,0:T(8,128)S(1)}, u32[]{:S(2)}, u32[]{:S(2)}) collective-permute-start(f32[1,128,256]{2,1,0:T(8,128)S(1)} %get-tuple-element.185), channel_id=1, source_target_pairs={{0,2},{2,4},{4,6},{6,8},{8,10},{10,12},{12,14},{14,0},{1,3},{3,5},... | collective-permute-start | bytes 393224 | tf_op jit(solution)/shard_map/while/body/eval_jaxpr/ppermute | solution.py:11
  97.2 14.0 %collective-permute-start.3 = (f32[1,128,256]{2,1,0:T(8,128)S(1)}, f32[1,128,256]{2,1,0:T(8,128)S(1)}, u32[]{:S(2)}, u32[]{:S(2)}) collective-permute-start(f32[1,128,256]{2,1,0:T(8,128)S(1)} %get-tuple-element.186), channel_id=1, source_target_pairs={{0,2},{2,4},{4,6},{6,8},{8,10},{10,12},{12,14},{14,0},{1,3},{3,5},... | collective-permute-start | bytes 393224 | tf_op jit(solution)/shard_map/while/body/eval_jaxpr/ppermute | solution.py:11
  111.3 20.3 %collective-permute-start = (f32[1,2,128,256]{3,2,1,0:T(8,128)S(1)}, f32[1,2,128,256]{3,2,1,0:T(8,128)S(1)}, u32[]{:S(2)}, u32[]{:S(2)}) collective-permute-start(f32[1,2,128,256]{3,2,1,0:T(8,128)S(1)} %copy.12), channel_id=1, source_target_pairs={{0,2},{2,4},{4,6},{6,8},{8,10},{10,12},{12,14},{14,0},{1,3},{3,5},... | collective-permute-start | bytes 786440 | tf_op jit(solution)/shard_map/while/body/eval_jaxpr/ppermute | solution.py:11
  117.5 9.1 %collective-permute-start.1 = (f32[1,128,256]{2,1,0:T(8,128)S(1)}, f32[1,128,256]{2,1,0:T(8,128)S(1)}, u32[]{:S(2)}, u32[]{:S(2)}) collective-permute-start(f32[1,128,256]{2,1,0:T(8,128)S(1)} %get-tuple-element.184), channel_id=1, source_target_pairs={{0,2},{2,4},{4,6},{6,8},{8,10},{10,12},{12,14},{14,0},{1,3},{3,5},... | collective-permute-start | bytes 393224 | tf_op jit(solution)/shard_map/while/body/eval_jaxpr/ppermute | solution.py:11
  117.5 11.8 %collective-permute-start.2 = (f32[1,128,256]{2,1,0:T(8,128)S(1)}, f32[1,128,256]{2,1,0:T(8,128)S(1)}, u32[]{:S(2)}, u32[]{:S(2)}) collective-permute-start(f32[1,128,256]{2,1,0:T(8,128)S(1)} %get-tuple-element.185), channel_id=1, source_target_pairs={{0,2},{2,4},{4,6},{6,8},{8,10},{10,12},{12,14},{14,0},{1,3},{3,5},... | collective-permute-start | bytes 393224 | tf_op jit(solution)/shard_map/while/body/eval_jaxpr/ppermute | solution.py:11
  117.6 14.0 %collective-permute-start.3 = (f32[1,128,256]{2,1,0:T(8,128)S(1)}, f32[1,128,256]{2,1,0:T(8,128)S(1)}, u32[]{:S(2)}, u32[]{:S(2)}) collective-permute-start(f32[1,128,256]{2,1,0:T(8,128)S(1)} %get-tuple-element.186), channel_id=1, source_target_pairs={{0,2},{2,4},{4,6},{6,8},{8,10},{10,12},{12,14},{14,0},{1,3},{3,5},... | collective-permute-start | bytes 393224 | tf_op jit(solution)/shard_map/while/body/eval_jaxpr/ppermute | solution.py:11
  131.7 20.3 %collective-permute-start = (f32[1,2,128,256]{3,2,1,0:T(8,128)S(1)}, f32[1,2,128,256]{3,2,1,0:T(8,128)S(1)}, u32[]{:S(2)}, u32[]{:S(2)}) collective-permute-start(f32[1,2,128,256]{3,2,1,0:T(8,128)S(1)} %copy.12), channel_id=1, source_target_pairs={{0,2},{2,4},{4,6},{6,8},{8,10},{10,12},{12,14},{14,0},{1,3},{3,5},... | collective-permute-start | bytes 786440 | tf_op jit(solution)/shard_map/while/body/eval_jaxpr/ppermute | solution.py:11
  137.8 9.1 %collective-permute-start.1 = (f32[1,128,256]{2,1,0:T(8,128)S(1)}, f32[1,128,256]{2,1,0:T(8,128)S(1)}, u32[]{:S(2)}, u32[]{:S(2)}) collective-permute-start(f32[1,128,256]{2,1,0:T(8,128)S(1)} %get-tuple-element.184), channel_id=1, source_target_pairs={{0,2},{2,4},{4,6},{6,8},{8,10},{10,12},{12,14},{14,0},{1,3},{3,5},... | collective-permute-start | bytes 393224 | tf_op jit(solution)/shard_map/while/body/eval_jaxpr/ppermute | solution.py:11
  137.9 11.8 %collective-permute-start.2 = (f32[1,128,256]{2,1,0:T(8,128)S(1)}, f32[1,128,256]{2,1,0:T(8,128)S(1)}, u32[]{:S(2)}, u32[]{:S(2)}) collective-permute-start(f32[1,128,256]{2,1,0:T(8,128)S(1)} %get-tuple-element.185), channel_id=1, source_target_pairs={{0,2},{2,4},{4,6},{6,8},{8,10},{10,12},{12,14},{14,0},{1,3},{3,5},... | collective-permute-start | bytes 393224 | tf_op jit(solution)/shard_map/while/body/eval_jaxpr/ppermute | solution.py:11
  138.0 14.0 %collective-permute-start.3 = (f32[1,128,256]{2,1,0:T(8,128)S(1)}, f32[1,128,256]{2,1,0:T(8,128)S(1)}, u32[]{:S(2)}, u32[]{:S(2)}) collective-permute-start(f32[1,128,256]{2,1,0:T(8,128)S(1)} %get-tuple-element.186), channel_id=1, source_target_pairs={{0,2},{2,4},{4,6},{6,8},{8,10},{10,12},{12,14},{14,0},{1,3},{3,5},... | collective-permute-start | bytes 393224 | tf_op jit(solution)/shard_map/while/body/eval_jaxpr/ppermute | solution.py:11
  152.0 20.3 %collective-permute-start = (f32[1,2,128,256]{3,2,1,0:T(8,128)S(1)}, f32[1,2,128,256]{3,2,1,0:T(8,128)S(1)}, u32[]{:S(2)}, u32[]{:S(2)}) collective-permute-start(f32[1,2,128,256]{3,2,1,0:T(8,128)S(1)} %copy.12), channel_id=1, source_target_pairs={{0,2},{2,4},{4,6},{6,8},{8,10},{10,12},{12,14},{14,0},{1,3},{3,5},... | collective-permute-start | bytes 786440 | tf_op jit(solution)/shard_map/while/body/eval_jaxpr/ppermute | solution.py:11
  158.2 9.1 %collective-permute-start.1 = (f32[1,128,256]{2,1,0:T(8,128)S(1)}, f32[1,128,256]{2,1,0:T(8,128)S(1)}, u32[]{:S(2)}, u32[]{:S(2)}) collective-permute-start(f32[1,128,256]{2,1,0:T(8,128)S(1)} %get-tuple-element.184), channel_id=1, source_target_pairs={{0,2},{2,4},{4,6},{6,8},{8,10},{10,12},{12,14},{14,0},{1,3},{3,5},... | collective-permute-start | bytes 393224 | tf_op jit(solution)/shard_map/while/body/eval_jaxpr/ppermute | solution.py:11
  158.2 11.8 %collective-permute-start.2 = (f32[1,128,256]{2,1,0:T(8,128)S(1)}, f32[1,128,256]{2,1,0:T(8,128)S(1)}, u32[]{:S(2)}, u32[]{:S(2)}) collective-permute-start(f32[1,128,256]{2,1,0:T(8,128)S(1)} %get-tuple-element.185), channel_id=1, source_target_pairs={{0,2},{2,4},{4,6},{6,8},{8,10},{10,12},{12,14},{14,0},{1,3},{3,5},... | collective-permute-start | bytes 393224 | tf_op jit(solution)/shard_map/while/body/eval_jaxpr/ppermute | solution.py:11
  158.3 14.0 %collective-permute-start.3 = (f32[1,128,256]{2,1,0:T(8,128)S(1)}, f32[1,128,256]{2,1,0:T(8,128)S(1)}, u32[]{:S(2)}, u32[]{:S(2)}) collective-permute-start(f32[1,128,256]{2,1,0:T(8,128)S(1)} %get-tuple-element.186), channel_id=1, source_target_pairs={{0,2},{2,4},{4,6},{6,8},{8,10},{10,12},{12,14},{14,0},{1,3},{3,5},... | collective-permute-start | bytes 393224 | tf_op jit(solution)/shard_map/while/body/eval_jaxpr/ppermute | solution.py:11
where the time goes:
time: 174 us
  waiting for transfers between devices  96.4 us (55%)
  matrix products  31 us (18%)
  starting transfers between devices  20 us (11%)
  blocking collectives  19.7 us (11%)
  local copies, waits for them, and re-layouts  2.67 us (2%)
  other arithmetic  2.11 us (1%)
    ppermute x32, waiting for transfers between devices, shifted(): return lax.ppermute(x, axis, [(i, (i + by) % peers) for i in range(peers)])  96.4 us
    ppermute x32, starting transfers between devices, shifted(): return lax.ppermute(x, axis, [(i, (i + by) % peers) for i in range(peers)])  20 us
    all_gather x8, blocking collectives, visit(): full = lax.all_gather(held, 'tile', axis=2, tiled=True)  17.4 us
    dot_general x8, matrix products, correlate(): jnp.einsum('nyk,kx->nyx', along_imag, col_sin, precision=highest)  10.5 us
    dot_general x8, matrix products, correlate(): maps = jnp.einsum('nyk,kx->nyx', along_real, col_cos, precision=highest)  10.4 us
    dot_general x8, matrix products, correlate(): jnp.einsum('yk,nkx->nyx', row_table, real_part, precision=highest)  5.05 us
    dot_general x8, matrix products, correlate(): jnp.einsum('yk,nkx->nyx', row_table, imag_part, precision=highest)  5.05 us
  transfers between devices with their start and end apart: 32, of which 24 were waited for; matrix products, arithmetic and copies ran while one was open for 18% of the time, Pallas kernels for 0%

commit v1 on v0

v1 whole, which is shorter than its diff:
```python
import functools
import math

import jax
import jax.numpy as jnp
import numpy as np
from jax import lax
from jax.experimental import pallas as pl
from jax.experimental.pallas import tpu as pltpu
from jax.sharding import PartitionSpec as P


def split_table(table):
    table = table.astype(np.float32)
    high = table.astype(jnp.bfloat16)
    low = (table - high.astype(np.float32)).astype(jnp.bfloat16)
    return np.stack([high, low])


def column_table(side):
    mid = side // 2
    k = np.arange(side)[:, None]
    x = np.arange(mid)[None, :]
    angle = 2.0 * math.pi * (k * x % side) / side
    right = np.sin(angle)
    right[:, 0] = np.cos(math.pi * k[:, 0])
    return split_table(np.concatenate([np.cos(angle), right], 1))


def row_table(side, half):
    y = np.arange(side)[:, None]
    k = np.arange(half)[None, :]
    angle = 2.0 * math.pi * (k * y % side) / side
    return split_table(np.concatenate([np.cos(angle), -np.sin(angle)], 1))


def unfold_table(mid):
    table = np.zeros((mid, mid), np.float32)
    k = np.arange(mid)
    table[(mid - k) % mid, k] = 1.0
    return table


def parts(x):
    high = x.astype(jnp.bfloat16)
    low = (x - high.astype(jnp.float32)).astype(jnp.bfloat16)
    return high, low


def dot(a, b):
    return jnp.dot(a, b, preferred_element_type=jnp.float32)


def correlate_kernel(s_ref, w_ref, q_ref, col_ref, row_ref, keep_ref, send_ref, sw_ref, rt_ref):
    half, side = s_ref.shape[1], s_ref.shape[2]
    mid = side // 2
    here = lax.axis_index("tile")

    @pl.when(pl.program_id(0) == 0)
    def _():
        w = w_ref[pl.ds(pl.multiple_of(here * half, half), half), :]
        sw_ref[0] = s_ref[0] * w
        sw_ref[1] = s_ref[1] * w
        odd = lax.broadcasted_iota(jnp.int32, (half, side), 0) % 2
        sign = (1 - 2 * odd * here).astype(jnp.float32)
        for n in range(2):
            mine = row_ref[n, pl.ds(pl.multiple_of(here * half, half), half), :].astype(jnp.float32)
            other = row_ref[n, pl.ds(pl.multiple_of((1 - here) * half, half), half), :].astype(jnp.float32)
            rt_ref[n, :half] = (mine * sign).astype(jnp.bfloat16)
            rt_ref[n, half:] = (other * sign).astype(jnp.bfloat16)

    sr, si = sw_ref[0], sw_ref[1]
    qr, qi = q_ref[0, 0], q_ref[0, 1]
    squares = jnp.sum((qr * qr + qi * qi).reshape(half // 8, 8, side), axis=0)
    power = jnp.broadcast_to(jnp.sum(squares), (8, side))
    z = jnp.concatenate([sr * qr + si * qi, si * qr - sr * qi], 0)
    zh, zl = parts(z)
    ch, cl = col_ref[0], col_ref[1]
    m = dot(zh, ch) + (dot(zl, ch) + dot(zh, cl))
    mcr, mci = m[:half, :mid], m[half:, :mid]
    msr, msi = m[:half, mid:], m[half:, mid:]
    first = lax.broadcasted_iota(jnp.int32, (half, mid), 1) == 0
    real = jnp.concatenate([mcr - jnp.where(first, 0.0, msi), jnp.where(first, msr, mcr + msi)], 1)
    imag = jnp.concatenate([mci + jnp.where(first, 0.0, msr), jnp.where(first, msi, mci - msr)], 1)
    ah, al = parts(jnp.concatenate([real, imag], 0))
    rh, rl = rt_ref[0], rt_ref[1]
    p = dot(rh, ah) + (dot(rh, al) + dot(rl, ah))
    keep_ref[0, :half] = p[:half]
    keep_ref[0, half:] = power
    send_ref[0, :half] = p[half:]
    send_ref[0, half:] = power


def stats_kernel(count, entries, keep_ref, recv_ref, fold_ref, peak_ref, mean_ref, square_ref, flip_ref):
    side = keep_ref.shape[2]
    half = keep_ref.shape[1] - 8
    mid = side // 2
    for block in range(half // 8):
        rows = pl.ds(block * 8, 8)
        best = total = squares = None
        for o in range(count):
            power = (keep_ref[o, half:] + recv_ref[o, half:]) * (1.0 / entries)
            scale = lax.rsqrt(power + 1e-6) * (1.0 / side)
            c = (keep_ref[o, rows] + recv_ref[o, rows]) * scale
            if o == 0:
                best, total, squares = c, c, c * c
            else:
                best, total, squares = jnp.maximum(best, c), total + c, squares + c * c
        total = total * (1.0 / count)
        squares = squares * (1.0 / count)
        for n, (ref, value) in enumerate(((peak_ref, best), (mean_ref, total), (square_ref, squares))):
            ref[0, rows, :mid] = value[:, :mid]
            flip_ref[pl.ds(n * half + block * 8, 8)] = value[:, mid:]
    right = jnp.dot(flip_ref[...], fold_ref[...], precision=lax.Precision.HIGHEST, preferred_element_type=jnp.float32)
    for n, ref in enumerate((peak_ref, mean_ref, square_ref)):
        ref[0, :, mid:] = right[n * half:(n + 1) * half]


def shards(spectra, templates, weights):
    half, side = spectra.shape[2:]
    gathered = lax.all_gather(templates[0], "orient", axis=0)
    count = gathered.shape[0]
    whole = lambda *shape: pl.BlockSpec(shape, lambda i: (0,) * len(shape))
    one = lambda *shape: pl.BlockSpec((1,) + shape, lambda i: (i,) + (0,) * len(shape))
    keep, send = pl.pallas_call(
        correlate_kernel,
        grid=(count,),
        in_specs=[whole(2, half, side), whole(side, side), one(2, half, side), whole(2, side, side), whole(2, side, side)],
        out_specs=[one(half + 8, side)] * 2,
        out_shape=[jax.ShapeDtypeStruct((count, half + 8, side), jnp.float32)] * 2,
        scratch_shapes=[pltpu.VMEM((2, half, side), jnp.float32), pltpu.VMEM((2, side, side), jnp.bfloat16)],
        compiler_params=pltpu.CompilerParams(vmem_limit_bytes=24 << 20),
        name="correlate",
    )(spectra[0], weights, gathered, jnp.asarray(column_table(side)), jnp.asarray(row_table(side, half)))
    recv = lax.ppermute(send, "tile", [(0, 1), (1, 0)])
    vmem = pl.BlockSpec(memory_space=pltpu.VMEM)
    out = jax.ShapeDtypeStruct((1, half, side), jnp.float32)
    return tuple(pl.pallas_call(
        functools.partial(stats_kernel, count, 2 * side * side),
        in_specs=[vmem] * 3,
        out_specs=[vmem] * 3,
        out_shape=[out] * 3,
        scratch_shapes=[pltpu.VMEM((3 * half, side // 2), jnp.float32)],
        compiler_params=pltpu.CompilerParams(vmem_limit_bytes=24 << 20),
        name="statistics",
    )(keep, recv, jnp.asarray(unfold_table(side // 2))))


def solution(mesh):
    in_specs = (
        P(("groups", "orient"), None, "tile", None),
        P("orient", None, "tile", None),
        P("groups", None),
    )
    out_specs = (P(("groups", "orient"), "tile", None),) * 3
    return jax.shard_map(shards, mesh=mesh, in_specs=in_specs, out_specs=out_specs, check_vma=False)
```

time: 174 us -> 84.4 us (0.49)
  waiting for transfers between devices: 96.4 us -> 57.7 us
  matrix products: 31 us -> 0 us
  starting transfers between devices: 20 us -> 0.11 us
  blocking collectives: 19.7 us -> 0 us
  between operations: 1.41 us -> 14 us
  Pallas kernels: 0 us -> 6.88 us
  local copies, waits for them, and re-layouts: 2.67 us -> 5.39 us
  other arithmetic: 2.11 us -> 0 us
    ppermute x32 -> x1, waiting for transfers between devices: 96.4 us -> 2.74 us  [shards(): recv = lax.ppermute(send, 'tile', [(0, 1), (1, 0)])]
    all_gather x0 -> x1, waiting for transfers between devices: none -> 54.2 us  [shards(): gathered = lax.all_gather(templates[0], 'orient', axis=0)]
    dot_general x32 -> x0, matrix products: 31 us -> none  [the longest x8 10.5 us: correlate(): jnp.einsum('nyk,kx->nyx', along_imag, col_sin, precision=highest)]
    ppermute x32 -> x1, starting transfers between devices: 20 us -> 0.07 us  [shards(): recv = lax.ppermute(send, 'tile', [(0, 1), (1, 0)])]
    all_gather x9 -> x0, blocking collectives: 19.7 us -> none  [the longest x8 17.4 us: visit(): full = lax.all_gather(held, 'tile', axis=2, tiled=True)]
    pallas_call x0 -> x2, Pallas kernels: none -> 6.88 us  [the longest x1 5.71 us: shards(): pl.pallas_call(correlate_kernel, grid=(count,), in_specs=[whole(2, half,...]
    unnamed x7 -> x12, local copies, waits for them, and re-layouts: 2.5 us -> 5.39 us
  transfers between devices with their start and end apart: 32 -> 2, of which waited for: 24 -> 2; matrix products, arithmetic and copies ran while one was open for 18% -> 0% of each run, Pallas kernels for 0% -> 0%
where the time goes in v1:
time: 84.4 us; the launch traced here: 84.1 us
  waiting for transfers between devices  57.7 us (68%)
  between operations  14 us (17%)
  Pallas kernels  6.88 us (8%)
  local copies, waits for them, and re-layouts  5.39 us (6%)
    all_gather x1, waiting for transfers between devices, shards(): gathered = lax.all_gather(templates[0], 'orient', axis=0)  54.2 us
    pallas_call x1, Pallas kernels, shards(): pl.pallas_call(correlate_kernel, grid=(count,), in_specs=[whole(2, half,...  5.71 us
    unnamed x12, local copies, waits for them, and re-layouts  5.39 us
    ppermute x1, waiting for transfers between devices, shards(): recv = lax.ppermute(send, 'tile', [(0, 1), (1, 0)])  2.74 us
  transfers between devices with their start and end apart: 2, of which 2 were waited for; matrix products, arithmetic and copies ran while one was open for 0% of the time, Pallas kernels for 0%

profile of v1, /device:TPU:0, one launch (start us, length us, event | category | flops | bytes accessed | tf_op | source)
XLA Modules:
  0.0 84.1 jit_solution(14147149252980834860)
XLA Ops:
  7.2 0.0 all-gather.2.cloned.1.call-start
  7.2 0.7 all-gather.2.cloned.1.call-update
  7.9 54.2 %all-gather.2.cloned.1.call-done.q_ref = f32[8,2,128,256]{3,2,1,0:T(8,128)} async-done(((f32[1,2,128,256]{3,2,1,0:T(8,128)}), f32[8,2,128,256]{3,2,1,0:T(8,128)}) %all-gather.2.cloned.1.call-update) | async-done | bytes 2097168 | tf_op jit(solution)/shard_map/all_gather | solution.py:121
  62.1 0.0 copy-start
  62.1 1.6 %copy-done = f32[8,2,128,256]{3,2,1,0:T(8,128)S(1)} copy-done((f32[8,2,128,256]{3,2,1,0:T(8,128)S(1)}, f32[8,2,128,256]{3,2,1,0:T(8,128)}, u32[]{:S(2)}) %copy-start) | copy-done | bytes 2097176
  63.7 0.0 copy-start.1
  63.7 0.9 %copy-done.1 = f32[1,2,128,256]{3,2,1,0:T(8,128)S(1)} copy-done((f32[1,2,128,256]{3,2,1,0:T(8,128)S(1)}, f32[1,2,128,256]{3,2,1,0:T(8,128)}, u32[]{:S(2)}) %copy-start.1) | copy-done | bytes 262168
  64.7 0.0 copy-start.2
  64.7 0.9 %copy-done.2 = f32[256,256]{1,0:T(8,128)S(1)} copy-done((f32[256,256]{1,0:T(8,128)S(1)}, f32[256,256]{1,0:T(8,128)}, u32[]{:S(2)}) %copy-start.2) | copy-done | bytes 262168
  65.6 0.0 copy-start.3
  65.6 0.9 %copy-done.3 = bf16[2,256,256]{2,1,0:T(8,128)(2,1)S(1)} copy-done((bf16[2,256,256]{2,1,0:T(8,128)(2,1)S(1)}, bf16[2,256,256]{2,1,0:T(8,128)(2,1)}, u32[]{:S(2)}) %copy-start.3) | copy-done | bytes 262168
  66.6 0.0 copy-start.4
  66.6 0.9 %copy-done.4 = bf16[2,256,256]{2,1,0:T(8,128)(2,1)S(1)} copy-done((bf16[2,256,256]{2,1,0:T(8,128)(2,1)S(1)}, bf16[2,256,256]{2,1,0:T(8,128)(2,1)}, u32[]{:S(2)}) %copy-start.4) | copy-done | bytes 262168
  67.5 0.0 copy-start.5
  67.5 5.7 %correlate.1 = (f32[8,136,256]{2,1,0:T(8,128)S(1)}, f32[8,136,256]{2,1,0:T(8,128)S(1)}) custom-call(f32[2,128,256]{2,1,0:T(8,128)S(1)} %bitcast.1, f32[256,256]{1,0:T(8,128)S(1)} %copy-done.2, f32[8,2,128,256]{3,2,1,0:T(8,128)S(1)} %copy-done, bf16[2,256,256]{2,1,0:T(8,128)(2,1)S(1)} %copy-done.4, bf16[2,256,256]{2,1,0:T(8,128)(2,1)S(1)} %copy-done.3), custom_call_target="tpu_custom_call" | custom-call | tf_op jit(solution)/shard_map/correlate/pallas_call | solution.py:125
  73.3 0.1 collective-permute-start
  73.3 2.7 %collective-permute-done.recv_ref = f32[8,136,256]{2,1,0:T(8,128)S(1)} collective-permute-done((f32[8,136,256]{2,1,0:T(8,128)S(1)}, f32[8,136,256]{2,1,0:T(8,128)S(1)}, u32[]{:S(2)}, u32[]{:S(2)}) %collective-permute-start) | collective-permute-done | bytes 1114144 | tf_op jit(solution)/shard_map/ppermute | solution.py:135
  76.1 0.0 copy-done.5
  76.1 1.2 %statistics.1 = (f32[1,128,256]{2,1,0:T(8,128)}, f32[1,128,256]{2,1,0:T(8,128)}, f32[1,128,256]{2,1,0:T(8,128)}) custom-call(f32[8,136,256]{2,1,0:T(8,128)S(1)} %get-tuple-element.5.keep_ref, f32[8,136,256]{2,1,0:T(8,128)S(1)} %collective-permute-done.recv_ref, f32[128,128]{1,0:T(8,128)S(1)} %copy-done.5), custom_call_target="tpu_custom_call" | custom-call | tf_op jit(solution)/shard_map/statistics/pallas_call | solution.py:138
Async XLA Ops:
  7.2 55.0 %all-gather.2.cloned.1.call-start = ((), (), s32[]{:S(2)}) async-start(), calls=%async_computation | async-start | bytes 2359296 | tf_op jit(solution)/shard_map/all_gather | solution.py:121
  62.1 1.6 %copy-start = (f32[8,2,128,256]{3,2,1,0:T(8,128)S(1)}, f32[8,2,128,256]{3,2,1,0:T(8,128)}, u32[]{:S(2)}) copy-start(f32[8,2,128,256]{3,2,1,0:T(8,128)} %all-gather.2.cloned.1.call-done.q_ref) | copy-start | bytes 6291460
  63.7 0.9 %copy-start.1 = (f32[1,2,128,256]{3,2,1,0:T(8,128)S(1)}, f32[1,2,128,256]{3,2,1,0:T(8,128)}, u32[]{:S(2)}) copy-start(f32[1,2,128,256]{3,2,1,0:T(8,128)} %param.6) | copy-start | bytes 786436
  64.7 0.9 %copy-start.2 = (f32[256,256]{1,0:T(8,128)S(1)}, f32[256,256]{1,0:T(8,128)}, u32[]{:S(2)}) copy-start(f32[256,256]{1,0:T(8,128)} %w_ref.1) | copy-start | bytes 786436
  65.6 0.9 %copy-start.3 = (bf16[2,256,256]{2,1,0:T(8,128)(2,1)S(1)}, bf16[2,256,256]{2,1,0:T(8,128)(2,1)}, u32[]{:S(2)}) copy-start(bf16[2,256,256]{2,1,0:T(8,128)(2,1)} %constant.7.clone.row_ref) | copy-start | bytes 786436
  66.6 0.9 %copy-start.4 = (bf16[2,256,256]{2,1,0:T(8,128)(2,1)S(1)}, bf16[2,256,256]{2,1,0:T(8,128)(2,1)}, u32[]{:S(2)}) copy-start(bf16[2,256,256]{2,1,0:T(8,128)(2,1)} %constant.6.clone.col_ref) | copy-start | bytes 786436
  67.5 8.5 %copy-start.5 = (f32[128,128]{1,0:T(8,128)S(1)}, f32[128,128]{1,0:T(8,128)}, u32[]{:S(2)}) copy-start(f32[128,128]{1,0:T(8,128)} %constant.8.clone.fold_ref) | copy-start | bytes 196612
  73.3 2.8 %collective-permute-start = (f32[8,136,256]{2,1,0:T(8,128)S(1)}, f32[8,136,256]{2,1,0:T(8,128)S(1)}, u32[]{:S(2)}, u32[]{:S(2)}) collective-permute-start(f32[8,136,256]{2,1,0:T(8,128)S(1)} %get-tuple-element.6), channel_id=1, source_target_pairs={{0,1},{1,0},{2,3},{3,2},{4,5},{5,4},{6,7},{7,6},{8,9},{9,8},{10,11... | collective-permute-start | bytes 3342344 | tf_op jit(solution)/shard_map/ppermute | solution.py:135
Sparse Core Ops, SparseCore 0:
  10.1 51.9 all-gather.1

commit v2 on v1

v2 whole, which is shorter than its diff:
```python
import functools
import math

import jax
import jax.numpy as jnp
import numpy as np
from jax import lax
from jax.experimental import pallas as pl
from jax.experimental.pallas import tpu as pltpu
from jax.sharding import PartitionSpec as P


def split_table(table):
    table = table.astype(np.float32)
    high = table.astype(jnp.bfloat16)
    low = (table - high.astype(np.float32)).astype(jnp.bfloat16)
    return np.stack([high, low])


def column_table(side):
    mid = side // 2
    k = np.arange(side)[:, None]
    x = np.arange(mid)[None, :]
    angle = 2.0 * math.pi * (k * x % side) / side
    right = np.sin(angle)
    right[:, 0] = np.cos(math.pi * k[:, 0])
    return split_table(np.concatenate([np.cos(angle), right], 1))


def row_table(side, half):
    y = np.arange(side)[:, None]
    k = np.arange(half)[None, :]
    angle = 2.0 * math.pi * (k * y % side) / side
    return split_table(np.concatenate([np.cos(angle), -np.sin(angle)], 1))


def unfold_table(mid):
    table = np.zeros((mid, mid), np.float32)
    k = np.arange(mid)
    table[(mid - k) % mid, k] = 1.0
    return table


def parts(x):
    high = x.astype(jnp.bfloat16)
    low = (x - high.astype(jnp.float32)).astype(jnp.bfloat16)
    return high, low


def dot(a, b):
    return jnp.dot(a, b, preferred_element_type=jnp.float32)


def prepare(s_ref, w_ref, row_ref, coef_ref, rt_ref):
    half, side = s_ref.shape[1], s_ref.shape[2]
    here = lax.axis_index("tile")
    swap = lax.axis_index("groups") % 2
    mine = pl.ds(pl.multiple_of(here * half, half), half)
    other = pl.ds(pl.multiple_of((1 - here) * half, half), half)
    w = w_ref[mine, :]
    u, v = s_ref[swap] * w, s_ref[1 - swap] * w
    turn = (1 - 2 * swap).astype(jnp.float32)
    coef_ref[0], coef_ref[1], coef_ref[2], coef_ref[3] = u, v, u * turn, v * turn
    odd = lax.broadcasted_iota(jnp.int32, (half, side), 0) % 2
    sign = (1 - 2 * odd * here).astype(jnp.float32)
    for n in range(2):
        rt_ref[n, :half] = (row_ref[n, mine, :].astype(jnp.float32) * sign).astype(jnp.bfloat16)
        rt_ref[n, half:] = (row_ref[n, other, :].astype(jnp.float32) * sign).astype(jnp.bfloat16)


def correlate(a, b, coef_ref, col_ref, rt_ref, keep_ref, send_ref, n):
    half, side = a.shape
    mid = side // 2
    squares = jnp.sum((a * a + b * b).reshape(half // 8, 8, side), axis=0)
    power = jnp.broadcast_to(jnp.sum(squares), (8, side))
    z = jnp.concatenate([coef_ref[0] * a + coef_ref[1] * b, coef_ref[3] * a - coef_ref[2] * b], 0)
    zh, zl = parts(z)
    ch, cl = col_ref[0], col_ref[1]
    m = dot(zh, ch) + (dot(zl, ch) + dot(zh, cl))
    mcr, mci = m[:half, :mid], m[half:, :mid]
    msr, msi = m[:half, mid:], m[half:, mid:]
    first = lax.broadcasted_iota(jnp.int32, (half, mid), 1) == 0
    real = jnp.concatenate([mcr - jnp.where(first, 0.0, msi), jnp.where(first, msr, mcr + msi)], 1)
    imag = jnp.concatenate([mci + jnp.where(first, 0.0, msr), jnp.where(first, msi, mci - msr)], 1)
    ah, al = parts(jnp.concatenate([real, imag], 0))
    rh, rl = rt_ref[0], rt_ref[1]
    p = dot(rh, ah) + (dot(rh, al) + dot(rl, ah))
    keep_ref[n, :half] = p[:half]
    keep_ref[n, half:] = power
    send_ref[n, :half] = p[half:]
    send_ref[n, half:] = power


def first_kernel(s_ref, w_ref, row_ref, col_ref, t_ref, coef_ref, rt_ref, keep_ref, send_ref):
    prepare(s_ref, w_ref, row_ref, coef_ref, rt_ref)
    swap = lax.axis_index("groups") % 2
    correlate(t_ref[swap], t_ref[1 - swap], coef_ref, col_ref, rt_ref, keep_ref, send_ref, 0)


def more_kernel(wholes, coef_ref, rt_ref, col_ref, *refs):
    inputs, (keep_ref, send_ref) = refs[:-2], refs[-2:]
    swap = lax.axis_index("groups") % 2
    n = 0
    for ref in inputs[:wholes]:
        for i in range(ref.shape[0] // 2):
            correlate(ref[2 * i + swap], ref[2 * i + 1 - swap], coef_ref, col_ref, rt_ref, keep_ref, send_ref, n)
            n += 1
    for a_ref, b_ref in zip(inputs[wholes::2], inputs[wholes + 1::2]):
        correlate(a_ref[...], b_ref[...], coef_ref, col_ref, rt_ref, keep_ref, send_ref, n)
        n += 1


def stats_kernel(calls, entries, *refs):
    keeps, recvs = refs[:calls], refs[calls:2 * calls]
    fold_ref, peak_ref, mean_ref, square_ref, flip_ref = refs[2 * calls:]
    side = keeps[0].shape[2]
    half = keeps[0].shape[1] - 8
    mid = side // 2
    pairs = [(keep, recv, n) for keep, recv in zip(keeps, recvs) for n in range(keep.shape[0])]
    count = len(pairs)
    for block in range(half // 8):
        rows = pl.ds(block * 8, 8)
        best = total = squares = None
        for keep, recv, n in pairs:
            power = (keep[n, half:] + recv[n, half:]) * (1.0 / entries)
            scale = lax.rsqrt(power + 1e-6) * (1.0 / side)
            c = (keep[n, rows] + recv[n, rows]) * scale
            if best is None:
                best, total, squares = c, c, c * c
            else:
                best, total, squares = jnp.maximum(best, c), total + c, squares + c * c
        total = total * (1.0 / count)
        squares = squares * (1.0 / count)
        for n, (ref, value) in enumerate(((peak_ref, best), (mean_ref, total), (square_ref, squares))):
            ref[0, rows, :mid] = value[:, :mid]
            flip_ref[pl.ds(n * half + block * 8, 8)] = value[:, mid:]
    right = jnp.dot(flip_ref[...], fold_ref[...], precision=lax.Precision.HIGHEST, preferred_element_type=jnp.float32)
    for n, ref in enumerate((peak_ref, mean_ref, square_ref)):
        ref[0, :, mid:] = right[n * half:(n + 1) * half]


def flipped(x, axis, bits):
    return lax.ppermute(x, axis, [(i, i ^ bits) for i in range(lax.axis_size(axis))])


def fetch(template):
    orients = lax.axis_size("orient")
    if lax.axis_size("groups") != 2 or orients != 8:
        rest = [flipped(template, "orient", k) for k in range(1, orients)]
        return [(rest[i:i + 2], []) for i in range(0, len(rest), 2)]
    part = lax.dynamic_index_in_dim(template, lax.axis_index("groups"), 0, keepdims=False)
    beside = flipped(template, "orient", 1)
    far = [flipped(part, "orient", 2 * k) for k in (1, 2, 3)]
    sets = []
    for k, mine in enumerate(far):
        partner = flipped(mine, "groups", 1)
        column = flipped(mine, "orient", 1)
        corner = flipped(column, "groups", 1) if k < 2 else flipped(partner, "orient", 1)
        sets.append(([beside] if k == 0 else [], [mine, partner, column, corner]))
    return sets


def shards(spectra, templates, weights):
    half, side = spectra.shape[2:]
    vmem = pl.BlockSpec(memory_space=pltpu.VMEM)
    params = pltpu.CompilerParams(vmem_limit_bytes=24 << 20)
    shape = lambda *dims, dtype=jnp.float32: jax.ShapeDtypeStruct(dims, dtype)
    columns = jnp.asarray(column_table(side))
    rows = jnp.asarray(row_table(side, half))
    coef, table, keep, send = pl.pallas_call(
        first_kernel,
        in_specs=[vmem] * 5,
        out_specs=[vmem] * 4,
        out_shape=[shape(4, half, side), shape(2, side, side, dtype=jnp.bfloat16)] + [shape(1, half + 8, side)] * 2,
        compiler_params=params,
        name="first",
    )(spectra[0], weights, rows, columns, templates[0])
    keeps, recvs = [keep], [flipped(send, "tile", 1)]
    for wholes, pieces in fetch(templates[0]):
        count = len(wholes) + len(pieces) // 2
        keep, send = pl.pallas_call(
            functools.partial(more_kernel, len(wholes)),
            in_specs=[vmem] * (3 + len(wholes) + len(pieces)),
            out_specs=[vmem] * 2,
            out_shape=[shape(count, half + 8, side)] * 2,
            compiler_params=params,
            name="more",
        )(coef, table, columns, *wholes, *pieces)
        keeps.append(keep)
        recvs.append(flipped(send, "tile", 1))
    return tuple(pl.pallas_call(
        functools.partial(stats_kernel, len(keeps), 2 * side * side),
        in_specs=[vmem] * (2 * len(keeps) + 1),
        out_specs=[vmem] * 3,
        out_shape=[shape(1, half, side)] * 3,
        scratch_shapes=[pltpu.VMEM((3 * half, side // 2), jnp.float32)],
        compiler_params=params,
        name="statistics",
    )(*keeps, *recvs, jnp.asarray(unfold_table(side // 2))))


def solution(mesh):
    in_specs = (
        P(("groups", "orient"), None, "tile", None),
        P("orient", None, "tile", None),
        P("groups", None),
    )
    out_specs = (P(("groups", "orient"), "tile", None),) * 3
    return jax.shard_map(shards, mesh=mesh, in_specs=in_specs, out_specs=out_specs, check_vma=False)
```

time: 84.4 us -> 44.1 us (0.52)
  waiting for transfers between devices: 57.7 us -> 13.7 us
  starting transfers between devices: 0.11 us -> 19.7 us
  between operations: 14 us -> 0.73 us
  Pallas kernels: 6.88 us -> 4.84 us
    all_gather x1 -> x0, waiting for transfers between devices: 54.2 us -> none  [shards(): gathered = lax.all_gather(templates[0], 'orient', axis=0)]
    ppermute x1 -> x17, starting transfers between devices: 0.07 us -> 19.7 us  [flipped(): lax.ppermute(x, axis, [(i, i ^ bits) for i in range(lax.axis_size(axis))])]
    ppermute x1 -> x17, waiting for transfers between devices: 2.74 us -> 13.7 us  [flipped(): lax.ppermute(x, axis, [(i, i ^ bits) for i in range(lax.axis_size(axis))])]
    pallas_call x2 -> x5, Pallas kernels: 6.88 us -> 4.84 us  [the longest x3 2.93 us: shards(): pl.pallas_call(functools.partial(more_kernel, len(wholes)), in_specs=[vme...]
    unnamed x12, local copies, waits for them, and re-layouts: 5.39 us -> 3.81 us
    squeeze x0 -> x1, local copies, waits for them, and re-layouts: none -> 0.96 us  [fetch(): lax.dynamic_index_in_dim(template, lax.axis_index('groups'), 0, keepdims=...]
  transfers between devices with their start and end apart: 2 -> 17, of which waited for: 2 -> 8; matrix products, arithmetic and copies ran while one was open for 0% -> 0% of each run, Pallas kernels for 0% -> 8%
where the time goes in v2:
time: 44.1 us; the launch traced here: 43.8 us
  starting transfers between devices  19.7 us (45%)
  waiting for transfers between devices  13.7 us (31%)
  Pallas kernels  4.84 us (11%)
  local copies, waits for them, and re-layouts  4.77 us (11%)
  between operations  0.73 us (2%)
    ppermute x17, starting transfers between devices, flipped(): lax.ppermute(x, axis, [(i, i ^ bits) for i in range(lax.axis_size(axis))])  19.7 us
    ppermute x17, waiting for transfers between devices, flipped(): lax.ppermute(x, axis, [(i, i ^ bits) for i in range(lax.axis_size(axis))])  13.7 us
    unnamed x12, local copies, waits for them, and re-layouts  3.81 us
    pallas_call x3, Pallas kernels, shards(): pl.pallas_call(functools.partial(more_kernel, len(wholes)), in_specs=[vme...  2.93 us
    pallas_call x1, Pallas kernels, shards(): pl.pallas_call(functools.partial(stats_kernel, len(keeps), 2 * side * sid...  1.21 us
    squeeze x1, local copies, waits for them, and re-layouts, fetch(): lax.dynamic_index_in_dim(template, lax.axis_index('groups'), 0, keepdims=...  0.96 us
  transfers between devices with their start and end apart: 17, of which 8 were waited for; matrix products, arithmetic and copies ran while one was open for 0% of the time, Pallas kernels for 8%

profile of v2, /device:TPU:0, one launch (start us, length us, event | category | flops | bytes accessed | tf_op | source)
XLA Modules:
  0.0 43.8 jit_solution(17248158352306419031)
XLA Ops:
  0.6 0.0 copy-start
  0.6 1.0 %dynamic-slice_bitcast_fusion = f32[128,256]{1,0:T(8,128)S(1)} fusion(f32[1,2,128,256]{3,2,1,0:T(8,128)} %param.7, s32[]{:T(128)S(6)} %select_n.4), kind=kLoop, calls=%fused_computation | loop fusion | bytes 262148 | tf_op jit(solution)/shard_map/jit(dynamic_index_in_dim)/squeeze | solution.py:151
  1.6 3.1 %collective-permute-start.1 = (f32[128,256]{1,0:T(8,128)S(1)}, f32[128,256]{1,0:T(8,128)S(1)}, u32[]{:S(2)}, u32[]{:S(2)}) collective-permute-start(f32[128,256]{1,0:T(8,128)S(1)} %dynamic-slice_bitcast_fusion), channel_id=1, source_target_pairs={{0,4},{2,6},{4,0},{6,2},{8,12},{10,14},{12,8},{14,10},{1,5},{3,7},... | collective-permute-start | bytes 393224 | tf_op jit(solution)/shard_map/ppermute | solution.py:143
  4.7 1.5 %collective-permute-start = (f32[2,128,256]{2,1,0:T(8,128)}, f32[2,128,256]{2,1,0:T(8,128)S(1)}, u32[]{:S(2)}, u32[]{:S(2)}) collective-permute-start(f32[2,128,256]{2,1,0:T(8,128)} %bitcast.4), channel_id=1, source_target_pairs={{0,2},{2,0},{4,6},{6,4},{8,10},{10,8},{12,14},{14,12},{1,3},{3,1},... | collective-permute-start | bytes 786440 | tf_op jit(solution)/shard_map/ppermute | solution.py:143
  6.2 2.0 %collective-permute-done.1.refs_1_ = f32[128,256]{1,0:T(8,128)S(1)} collective-permute-done((f32[128,256]{1,0:T(8,128)S(1)}, f32[128,256]{1,0:T(8,128)S(1)}, u32[]{:S(2)}, u32[]{:S(2)}) %collective-permute-start.1) | collective-permute-done | bytes 131104 | tf_op jit(solution)/shard_map/ppermute | solution.py:143
  8.2 1.7 %collective-permute-start.3 = (f32[128,256]{1,0:T(8,128)S(1)}, f32[128,256]{1,0:T(8,128)S(1)}, u32[]{:S(2)}, u32[]{:S(2)}) collective-permute-start(f32[128,256]{1,0:T(8,128)S(1)} %collective-permute-done.1.refs_1_), channel_id=1, source_target_pairs={{0,2},{2,0},{4,6},{6,4},{8,10},{10,8},{12,14},{14,12},{1,3},{3,1},... | collective-permute-start | bytes 393224 | tf_op jit(solution)/shard_map/ppermute | solution.py:143
  9.9 3.6 %collective-permute-start.9 = (f32[128,256]{1,0:T(8,128)S(1)}, f32[128,256]{1,0:T(8,128)S(1)}, u32[]{:S(2)}, u32[]{:S(2)}) collective-permute-start(f32[128,256]{1,0:T(8,128)S(1)} %dynamic-slice_bitcast_fusion), channel_id=1, source_target_pairs={{0,12},{2,14},{4,8},{6,10},{8,4},{10,6},{12,0},{14,2},{1,13},{3,15... | collective-permute-start | bytes 393224 | tf_op jit(solution)/shard_map/ppermute | solution.py:143
  13.5 0.0 collective-permute-start.5
  13.5 1.5 %collective-permute-start.2 = (f32[128,256]{1,0:T(8,128)S(1)}, f32[128,256]{1,0:T(8,128)S(1)}, u32[]{:S(2)}, u32[]{:S(2)}) collective-permute-start(f32[128,256]{1,0:T(8,128)S(1)} %collective-permute-done.1.refs_1_), channel_id=1, source_target_pairs={{0,16},{16,0},{1,17},{17,1},{2,18},{18,2},{3,19},{19,3},{4,20},{20... | collective-permute-start | bytes 393224 | tf_op jit(solution)/shard_map/ppermute | solution.py:143
  15.0 0.5 %collective-permute-done.3.refs_3_ = f32[128,256]{1,0:T(8,128)S(1)} collective-permute-done((f32[128,256]{1,0:T(8,128)S(1)}, f32[128,256]{1,0:T(8,128)S(1)}, u32[]{:S(2)}, u32[]{:S(2)}) %collective-permute-start.3) | collective-permute-done | bytes 131104 | tf_op jit(solution)/shard_map/ppermute | solution.py:143
  15.5 1.5 %collective-permute-start.4 = (f32[128,256]{1,0:T(8,128)S(1)}, f32[128,256]{1,0:T(8,128)S(1)}, u32[]{:S(2)}, u32[]{:S(2)}) collective-permute-start(f32[128,256]{1,0:T(8,128)S(1)} %collective-permute-done.3.refs_3_), channel_id=1, source_target_pairs={{0,16},{16,0},{1,17},{17,1},{2,18},{18,2},{3,19},{19,3},{4,20},{20... | collective-permute-start | bytes 393224 | tf_op jit(solution)/shard_map/ppermute | solution.py:143
  17.0 0.4 collective-permute-done.9.refs_0_
  17.3 1.5 %collective-permute-start.10 = (f32[128,256]{1,0:T(8,128)S(1)}, f32[128,256]{1,0:T(8,128)S(1)}, u32[]{:S(2)}, u32[]{:S(2)}) collective-permute-start(f32[128,256]{1,0:T(8,128)S(1)} %collective-permute-done.9.refs_0_), channel_id=1, source_target_pairs={{0,16},{16,0},{1,17},{17,1},{2,18},{18,2},{3,19},{19,3},{4,20},{20... | collective-permute-start | bytes 393224 | tf_op jit(solution)/shard_map/ppermute | solution.py:143
  18.8 4.6 %collective-permute-done.5.refs_0_ = f32[128,256]{1,0:T(8,128)S(1)} collective-permute-done((f32[128,256]{1,0:T(8,128)S(1)}, f32[128,256]{1,0:T(8,128)S(1)}, u32[]{:S(2)}, u32[]{:S(2)}) %collective-permute-start.5) | collective-permute-done | bytes 131104 | tf_op jit(solution)/shard_map/ppermute | solution.py:143
  23.4 0.5 %collective-permute-start.7 = (f32[128,256]{1,0:T(8,128)S(1)}, f32[128,256]{1,0:T(8,128)S(1)}, u32[]{:S(2)}, u32[]{:S(2)}) collective-permute-start(f32[128,256]{1,0:T(8,128)S(1)} %collective-permute-done.5.refs_0_), channel_id=1, source_target_pairs={{0,2},{2,0},{4,6},{6,4},{8,10},{10,8},{12,14},{14,12},{1,3},{3,1},... | collective-permute-start | bytes 393224 | tf_op jit(solution)/shard_map/ppermute | solution.py:143
  23.9 0.0 copy-done
  23.9 0.0 copy-start.1
  23.9 0.9 %copy-done.1 = f32[1,2,128,256]{3,2,1,0:T(8,128)S(1)} copy-done((f32[1,2,128,256]{3,2,1,0:T(8,128)S(1)}, f32[1,2,128,256]{3,2,1,0:T(8,128)}, u32[]{:S(2)}) %copy-start.1) | copy-done | bytes 262168
  24.9 0.0 copy-start.2
  24.9 0.9 %copy-done.2 = f32[1,2,128,256]{3,2,1,0:T(8,128)S(1)} copy-done((f32[1,2,128,256]{3,2,1,0:T(8,128)S(1)}, f32[1,2,128,256]{3,2,1,0:T(8,128)}, u32[]{:S(2)}) %copy-start.2) | copy-done | bytes 262168
  25.8 0.0 copy-start.3
  25.8 0.9 %copy-done.3 = f32[256,256]{1,0:T(8,128)S(1)} copy-done((f32[256,256]{1,0:T(8,128)S(1)}, f32[256,256]{1,0:T(8,128)}, u32[]{:S(2)}) %copy-start.3) | copy-done | bytes 262168
  26.8 0.0 copy-start.4
  26.8 0.9 %copy-done.4 = bf16[2,256,256]{2,1,0:T(8,128)(2,1)S(1)} copy-done((bf16[2,256,256]{2,1,0:T(8,128)(2,1)S(1)}, bf16[2,256,256]{2,1,0:T(8,128)(2,1)}, u32[]{:S(2)}) %copy-start.4) | copy-done | bytes 262168
  27.7 0.7 %first.1 = (f32[4,128,256]{2,1,0:T(8,128)S(1)}, bf16[2,256,256]{2,1,0:T(8,128)(2,1)S(1)}, f32[1,136,256]{2,1,0:T(8,128)S(1)}, f32[1,136,256]{2,1,0:T(8,128)S(1)}) custom-call(f32[2,128,256]{2,1,0:T(8,128)S(1)} %bitcast.6, f32[256,256]{1,0:T(8,128)S(1)} %copy-done.3, bf16[2,256,256]{2,1,0:T(8,128)(2,1)S(1)} %copy-done.4, bf16[2,256,256]{2,1,0:T(8,128)(2,1)S(1)} %copy-done, ...), custom_call_target="tpu_custom_call" | custom-call | tf_op jit(solution)/shard_map/first/pallas_call | solution.py:170
  28.4 0.0 collective-permute-done.2.refs_2_
  28.4 0.0 collective-permute-done.refs_0_
  28.4 0.0 collective-permute-done.4.refs_4_
  28.4 1.1 %more.3 = (f32[3,136,256]{2,1,0:T(8,128)S(1)}, f32[3,136,256]{2,1,0:T(8,128)S(1)}) custom-call(f32[4,128,256]{2,1,0:T(8,128)S(1)} %get-tuple-element.14.coef_ref, bf16[2,256,256]{2,1,0:T(8,128)(2,1)S(1)} %get-tuple-element.15.rt_ref, bf16[2,256,256]{2,1,0:T(8,128)(2,1)S(1)} %copy-done, f32[2,128,256]{2,1,0:T(8,128)S(1)} %collective-permute-done.refs_0_, ...), custom_call_target="tpu_custom_call" | custom-call | tf_op jit(solution)/shard_map/more/pallas_call | solution.py:181
  29.6 0.1 collective-permute-start.14
  29.6 1.6 %collective-permute-start.11 = (f32[128,256]{1,0:T(8,128)S(1)}, f32[128,256]{1,0:T(8,128)S(1)}, u32[]{:S(2)}, u32[]{:S(2)}) collective-permute-start(f32[128,256]{1,0:T(8,128)S(1)} %collective-permute-done.9.refs_0_), channel_id=1, source_target_pairs={{0,2},{2,0},{4,6},{6,4},{8,10},{10,8},{12,14},{14,12},{1,3},{3,1},... | collective-permute-start | bytes 393224 | tf_op jit(solution)/shard_map/ppermute | solution.py:143
  31.2 0.0 collective-permute-done.10.refs_1_
  31.2 0.5 %collective-permute-start.12 = (f32[128,256]{1,0:T(8,128)S(1)}, f32[128,256]{1,0:T(8,128)S(1)}, u32[]{:S(2)}, u32[]{:S(2)}) collective-permute-start(f32[128,256]{1,0:T(8,128)S(1)} %collective-permute-done.10.refs_1_), channel_id=1, source_target_pairs={{0,2},{2,0},{4,6},{6,4},{8,10},{10,8},{12,14},{14,12},{1,3},{3,1},... | collective-permute-start | bytes 393224 | tf_op jit(solution)/shard_map/ppermute | solution.py:143
  31.7 1.5 %collective-permute-start.6 = (f32[128,256]{1,0:T(8,128)S(1)}, f32[128,256]{1,0:T(8,128)S(1)}, u32[]{:S(2)}, u32[]{:S(2)}) collective-permute-start(f32[128,256]{1,0:T(8,128)S(1)} %collective-permute-done.5.refs_0_), channel_id=1, source_target_pairs={{0,16},{16,0},{1,17},{17,1},{2,18},{18,2},{3,19},{19,3},{4,20},{20... | collective-permute-start | bytes 393224 | tf_op jit(solution)/shard_map/ppermute | solution.py:143
  33.2 0.0 collective-permute-done.7.refs_2_
  33.2 0.5 %collective-permute-start.8 = (f32[128,256]{1,0:T(8,128)S(1)}, f32[128,256]{1,0:T(8,128)S(1)}, u32[]{:S(2)}, u32[]{:S(2)}) collective-permute-start(f32[128,256]{1,0:T(8,128)S(1)} %collective-permute-done.7.refs_2_), channel_id=1, source_target_pairs={{0,16},{16,0},{1,17},{17,1},{2,18},{18,2},{3,19},{19,3},{4,20},{20... | collective-permute-start | bytes 393224 | tf_op jit(solution)/shard_map/ppermute | solution.py:143
  33.8 2.2 %collective-permute-done.11.refs_2_ = f32[128,256]{1,0:T(8,128)S(1)} collective-permute-done((f32[128,256]{1,0:T(8,128)S(1)}, f32[128,256]{1,0:T(8,128)S(1)}, u32[]{:S(2)}, u32[]{:S(2)}) %collective-permute-start.11) | collective-permute-done | bytes 131104 | tf_op jit(solution)/shard_map/ppermute | solution.py:143
  36.0 2.4 %collective-permute-done.12.refs_3_ = f32[128,256]{1,0:T(8,128)S(1)} collective-permute-done((f32[128,256]{1,0:T(8,128)S(1)}, f32[128,256]{1,0:T(8,128)S(1)}, u32[]{:S(2)}, u32[]{:S(2)}) %collective-permute-start.12) | collective-permute-done | bytes 131104 | tf_op jit(solution)/shard_map/ppermute | solution.py:143
  38.4 0.9 %more.5 = (f32[2,136,256]{2,1,0:T(8,128)S(1)}, f32[2,136,256]{2,1,0:T(8,128)S(1)}) custom-call(f32[4,128,256]{2,1,0:T(8,128)S(1)} %get-tuple-element.14.coef_ref, bf16[2,256,256]{2,1,0:T(8,128)(2,1)S(1)} %get-tuple-element.15.rt_ref, bf16[2,256,256]{2,1,0:T(8,128)(2,1)S(1)} %copy-done, f32[128,256]{1,0:T(8,128)S(1)} %collective-permute-done.9.refs_0_, ...), custom_call_target="tpu_custom_call" | custom-call | tf_op jit(solution)/shard_map/more/pallas_call | solution.py:181
  39.3 0.0 copy-start.5
  39.3 0.1 collective-permute-start.16
  39.4 0.0 collective-permute-done.6.refs_1_
  39.4 0.5 %collective-permute-done.8.refs_3_ = f32[128,256]{1,0:T(8,128)S(1)} collective-permute-done((f32[128,256]{1,0:T(8,128)S(1)}, f32[128,256]{1,0:T(8,128)S(1)}, u32[]{:S(2)}, u32[]{:S(2)}) %collective-permute-start.8) | collective-permute-done | bytes 131104 | tf_op jit(solution)/shard_map/ppermute | solution.py:143
  39.8 0.9 %more.4 = (f32[2,136,256]{2,1,0:T(8,128)S(1)}, f32[2,136,256]{2,1,0:T(8,128)S(1)}) custom-call(f32[4,128,256]{2,1,0:T(8,128)S(1)} %get-tuple-element.14.coef_ref, bf16[2,256,256]{2,1,0:T(8,128)(2,1)S(1)} %get-tuple-element.15.rt_ref, bf16[2,256,256]{2,1,0:T(8,128)(2,1)S(1)} %copy-done, f32[128,256]{1,0:T(8,128)S(1)} %collective-permute-done.5.refs_0_, ...), custom_call_target="tpu_custom_call" | custom-call | tf_op jit(solution)/shard_map/more/pallas_call | solution.py:181
  40.7 0.1 collective-permute-start.15
  40.8 0.5 %collective-permute-start.13 = (f32[1,136,256]{2,1,0:T(8,128)S(1)}, f32[1,136,256]{2,1,0:T(8,128)S(1)}, u32[]{:S(2)}, u32[]{:S(2)}) collective-permute-start(f32[1,136,256]{2,1,0:T(8,128)S(1)} %get-tuple-element.19), channel_id=1, source_target_pairs={{0,1},{1,0},{2,3},{3,2},{4,5},{5,4},{6,7},{7,6},{8,9},{9,8},{10,11... | collective-permute-start | bytes 417800 | tf_op jit(solution)/shard_map/ppermute | solution.py:143
  41.3 1.2 %collective-permute-done.13.refs_4_ = f32[1,136,256]{2,1,0:T(8,128)S(1)} collective-permute-done((f32[1,136,256]{2,1,0:T(8,128)S(1)}, f32[1,136,256]{2,1,0:T(8,128)S(1)}, u32[]{:S(2)}, u32[]{:S(2)}) %collective-permute-start.13) | collective-permute-done | bytes 139296 | tf_op jit(solution)/shard_map/ppermute | solution.py:143
  42.6 0.0 collective-permute-done.16.refs_7_
  42.6 0.0 collective-permute-done.15.refs_6_
  42.6 0.0 collective-permute-done.14.refs_5_
  42.6 0.0 copy-done.5
  42.6 1.2 %statistics.1 = (f32[1,128,256]{2,1,0:T(8,128)}, f32[1,128,256]{2,1,0:T(8,128)}, f32[1,128,256]{2,1,0:T(8,128)}) custom-call(f32[1,136,256]{2,1,0:T(8,128)S(1)} %get-tuple-element.13.refs_0_, f32[3,136,256]{2,1,0:T(8,128)S(1)} %get-tuple-element.16.refs_1_, f32[2,136,256]{2,1,0:T(8,128)S(1)} %get-tuple-element.17.refs_2_, ...), custom_call_target="tpu_custom_call" | custom-call | tf_op jit(solution)/shard_map/statistics/pallas_call | solution.py:191
Async XLA Ops:
  0.6 23.3 %copy-start = (bf16[2,256,256]{2,1,0:T(8,128)(2,1)S(1)}, bf16[2,256,256]{2,1,0:T(8,128)(2,1)}, u32[]{:S(2)}) copy-start(bf16[2,256,256]{2,1,0:T(8,128)(2,1)} %constant.19.clone.col_ref) | copy-start | bytes 786436
  1.6 6.6 %collective-permute-start.1 = (f32[128,256]{1,0:T(8,128)S(1)}, f32[128,256]{1,0:T(8,128)S(1)}, u32[]{:S(2)}, u32[]{:S(2)}) collective-permute-start(f32[128,256]{1,0:T(8,128)S(1)} %dynamic-slice_bitcast_fusion), channel_id=1, source_target_pairs={{0,4},{2,6},{4,0},{6,2},{8,12},{10,14},{12,8},{14,10},{1,5},{3,7},... | collective-permute-start | bytes 393224 | tf_op jit(solution)/shard_map/ppermute | solution.py:143
  4.7 23.7 %collective-permute-start = (f32[2,128,256]{2,1,0:T(8,128)}, f32[2,128,256]{2,1,0:T(8,128)S(1)}, u32[]{:S(2)}, u32[]{:S(2)}) collective-permute-start(f32[2,128,256]{2,1,0:T(8,128)} %bitcast.4), channel_id=1, source_target_pairs={{0,2},{2,0},{4,6},{6,4},{8,10},{10,8},{12,14},{14,12},{1,3},{3,1},... | collective-permute-start | bytes 786440 | tf_op jit(solution)/shard_map/ppermute | solution.py:143
  8.2 7.3 %collective-permute-start.3 = (f32[128,256]{1,0:T(8,128)S(1)}, f32[128,256]{1,0:T(8,128)S(1)}, u32[]{:S(2)}, u32[]{:S(2)}) collective-permute-start(f32[128,256]{1,0:T(8,128)S(1)} %collective-permute-done.1.refs_1_), channel_id=1, source_target_pairs={{0,2},{2,0},{4,6},{6,4},{8,10},{10,8},{12,14},{14,12},{1,3},{3,1},... | collective-permute-start | bytes 393224 | tf_op jit(solution)/shard_map/ppermute | solution.py:143
  9.9 7.5 %collective-permute-start.9 = (f32[128,256]{1,0:T(8,128)S(1)}, f32[128,256]{1,0:T(8,128)S(1)}, u32[]{:S(2)}, u32[]{:S(2)}) collective-permute-start(f32[128,256]{1,0:T(8,128)S(1)} %dynamic-slice_bitcast_fusion), channel_id=1, source_target_pairs={{0,12},{2,14},{4,8},{6,10},{8,4},{10,6},{12,0},{14,2},{1,13},{3,15... | collective-permute-start | bytes 393224 | tf_op jit(solution)/shard_map/ppermute | solution.py:143
  13.5 9.9 %collective-permute-start.5 = (f32[128,256]{1,0:T(8,128)S(1)}, f32[128,256]{1,0:T(8,128)S(1)}, u32[]{:S(2)}, u32[]{:S(2)}) collective-permute-start(f32[128,256]{1,0:T(8,128)S(1)} %dynamic-slice_bitcast_fusion), channel_id=1, source_target_pairs={{0,8},{2,10},{4,12},{6,14},{8,0},{10,2},{12,4},{14,6},{1,9},{3,11}... | collective-permute-start | bytes 393224 | tf_op jit(solution)/shard_map/ppermute | solution.py:143
  13.5 14.9 %collective-permute-start.2 = (f32[128,256]{1,0:T(8,128)S(1)}, f32[128,256]{1,0:T(8,128)S(1)}, u32[]{:S(2)}, u32[]{:S(2)}) collective-permute-start(f32[128,256]{1,0:T(8,128)S(1)} %collective-permute-done.1.refs_1_), channel_id=1, source_target_pairs={{0,16},{16,0},{1,17},{17,1},{2,18},{18,2},{3,19},{19,3},{4,20},{20... | collective-permute-start | bytes 393224 | tf_op jit(solution)/shard_map/ppermute | solution.py:143
  15.5 13.0 %collective-permute-start.4 = (f32[128,256]{1,0:T(8,128)S(1)}, f32[128,256]{1,0:T(8,128)S(1)}, u32[]{:S(2)}, u32[]{:S(2)}) collective-permute-start(f32[128,256]{1,0:T(8,128)S(1)} %collective-permute-done.3.refs_3_), channel_id=1, source_target_pairs={{0,16},{16,0},{1,17},{17,1},{2,18},{18,2},{3,19},{19,3},{4,20},{20... | collective-permute-start | bytes 393224 | tf_op jit(solution)/shard_map/ppermute | solution.py:143
  17.3 13.9 %collective-permute-start.10 = (f32[128,256]{1,0:T(8,128)S(1)}, f32[128,256]{1,0:T(8,128)S(1)}, u32[]{:S(2)}, u32[]{:S(2)}) collective-permute-start(f32[128,256]{1,0:T(8,128)S(1)} %collective-permute-done.9.refs_0_), channel_id=1, source_target_pairs={{0,16},{16,0},{1,17},{17,1},{2,18},{18,2},{3,19},{19,3},{4,20},{20... | collective-permute-start | bytes 393224 | tf_op jit(solution)/shard_map/ppermute | solution.py:143
  23.4 9.8 %collective-permute-start.7 = (f32[128,256]{1,0:T(8,128)S(1)}, f32[128,256]{1,0:T(8,128)S(1)}, u32[]{:S(2)}, u32[]{:S(2)}) collective-permute-start(f32[128,256]{1,0:T(8,128)S(1)} %collective-permute-done.5.refs_0_), channel_id=1, source_target_pairs={{0,2},{2,0},{4,6},{6,4},{8,10},{10,8},{12,14},{14,12},{1,3},{3,1},... | collective-permute-start | bytes 393224 | tf_op jit(solution)/shard_map/ppermute | solution.py:143
  23.9 1.0 %copy-start.1 = (f32[1,2,128,256]{3,2,1,0:T(8,128)S(1)}, f32[1,2,128,256]{3,2,1,0:T(8,128)}, u32[]{:S(2)}) copy-start(f32[1,2,128,256]{3,2,1,0:T(8,128)} %param.7) | copy-start | bytes 786436
  24.9 0.9 %copy-start.2 = (f32[1,2,128,256]{3,2,1,0:T(8,128)S(1)}, f32[1,2,128,256]{3,2,1,0:T(8,128)}, u32[]{:S(2)}) copy-start(f32[1,2,128,256]{3,2,1,0:T(8,128)} %param.6) | copy-start | bytes 786436
  25.8 0.9 %copy-start.3 = (f32[256,256]{1,0:T(8,128)S(1)}, f32[256,256]{1,0:T(8,128)}, u32[]{:S(2)}) copy-start(f32[256,256]{1,0:T(8,128)} %w_ref.1) | copy-start | bytes 786436
  26.8 0.9 %copy-start.4 = (bf16[2,256,256]{2,1,0:T(8,128)(2,1)S(1)}, bf16[2,256,256]{2,1,0:T(8,128)(2,1)}, u32[]{:S(2)}) copy-start(bf16[2,256,256]{2,1,0:T(8,128)(2,1)} %constant.20.clone.row_ref) | copy-start | bytes 786436
  29.6 13.0 %collective-permute-start.14 = (f32[3,136,256]{2,1,0:T(8,128)S(1)}, f32[3,136,256]{2,1,0:T(8,128)S(1)}, u32[]{:S(2)}, u32[]{:S(2)}) collective-permute-start(f32[3,136,256]{2,1,0:T(8,128)S(1)} %get-tuple-element.20), channel_id=1, source_target_pairs={{0,1},{1,0},{2,3},{3,2},{4,5},{5,4},{6,7},{7,6},{8,9},{9,8},{10,11... | collective-permute-start | bytes 1253384 | tf_op jit(solution)/shard_map/ppermute | solution.py:143
  29.6 6.4 %collective-permute-start.11 = (f32[128,256]{1,0:T(8,128)S(1)}, f32[128,256]{1,0:T(8,128)S(1)}, u32[]{:S(2)}, u32[]{:S(2)}) collective-permute-start(f32[128,256]{1,0:T(8,128)S(1)} %collective-permute-done.9.refs_0_), channel_id=1, source_target_pairs={{0,2},{2,0},{4,6},{6,4},{8,10},{10,8},{12,14},{14,12},{1,3},{3,1},... | collective-permute-start | bytes 393224 | tf_op jit(solution)/shard_map/ppermute | solution.py:143
  31.2 7.1 %collective-permute-start.12 = (f32[128,256]{1,0:T(8,128)S(1)}, f32[128,256]{1,0:T(8,128)S(1)}, u32[]{:S(2)}, u32[]{:S(2)}) collective-permute-start(f32[128,256]{1,0:T(8,128)S(1)} %collective-permute-done.10.refs_1_), channel_id=1, source_target_pairs={{0,2},{2,0},{4,6},{6,4},{8,10},{10,8},{12,14},{14,12},{1,3},{3,1},... | collective-permute-start | bytes 393224 | tf_op jit(solution)/shard_map/ppermute | solution.py:143
  31.7 7.6 %collective-permute-start.6 = (f32[128,256]{1,0:T(8,128)S(1)}, f32[128,256]{1,0:T(8,128)S(1)}, u32[]{:S(2)}, u32[]{:S(2)}) collective-permute-start(f32[128,256]{1,0:T(8,128)S(1)} %collective-permute-done.5.refs_0_), channel_id=1, source_target_pairs={{0,16},{16,0},{1,17},{17,1},{2,18},{18,2},{3,19},{19,3},{4,20},{20... | collective-permute-start | bytes 393224 | tf_op jit(solution)/shard_map/ppermute | solution.py:143
  33.2 6.6 %collective-permute-start.8 = (f32[128,256]{1,0:T(8,128)S(1)}, f32[128,256]{1,0:T(8,128)S(1)}, u32[]{:S(2)}, u32[]{:S(2)}) collective-permute-start(f32[128,256]{1,0:T(8,128)S(1)} %collective-permute-done.7.refs_2_), channel_id=1, source_target_pairs={{0,16},{16,0},{1,17},{17,1},{2,18},{18,2},{3,19},{19,3},{4,20},{20... | collective-permute-start | bytes 393224 | tf_op jit(solution)/shard_map/ppermute | solution.py:143
  39.3 3.3 %copy-start.5 = (f32[128,128]{1,0:T(8,128)S(1)}, f32[128,128]{1,0:T(8,128)}, u32[]{:S(2)}) copy-start(f32[128,128]{1,0:T(8,128)} %constant.21.clone.refs_8_) | copy-start | bytes 196612
  39.3 3.3 %collective-permute-start.16 = (f32[2,136,256]{2,1,0:T(8,128)S(1)}, f32[2,136,256]{2,1,0:T(8,128)S(1)}, u32[]{:S(2)}, u32[]{:S(2)}) collective-permute-start(f32[2,136,256]{2,1,0:T(8,128)S(1)} %get-tuple-element.22), channel_id=1, source_target_pairs={{0,1},{1,0},{2,3},{3,2},{4,5},{5,4},{6,7},{7,6},{8,9},{9,8},{10,11... | collective-permute-start | bytes 835592 | tf_op jit(solution)/shard_map/ppermute | solution.py:143
  40.7 1.8 %collective-permute-start.15 = (f32[2,136,256]{2,1,0:T(8,128)S(1)}, f32[2,136,256]{2,1,0:T(8,128)S(1)}, u32[]{:S(2)}, u32[]{:S(2)}) collective-permute-start(f32[2,136,256]{2,1,0:T(8,128)S(1)} %get-tuple-element.21), channel_id=1, source_target_pairs={{0,1},{1,0},{2,3},{3,2},{4,5},{5,4},{6,7},{7,6},{8,9},{9,8},{10,11... | collective-permute-start | bytes 835592 | tf_op jit(solution)/shard_map/ppermute | solution.py:143
  40.8 1.7 %collective-permute-start.13 = (f32[1,136,256]{2,1,0:T(8,128)S(1)}, f32[1,136,256]{2,1,0:T(8,128)S(1)}, u32[]{:S(2)}, u32[]{:S(2)}) collective-permute-start(f32[1,136,256]{2,1,0:T(8,128)S(1)} %get-tuple-element.19), channel_id=1, source_target_pairs={{0,1},{1,0},{2,3},{3,2},{4,5},{5,4},{6,7},{7,6},{8,9},{9,8},{10,11... | collective-permute-start | bytes 417800 | tf_op jit(solution)/shard_map/ppermute | solution.py:143

commit v3 on v2

--- a/solution.py
+++ b/solution.py
@@ -97,17 +97,15 @@
     correlate(t_ref[swap], t_ref[1 - swap], coef_ref, col_ref, rt_ref, keep_ref, send_ref, 0)
 
 
-def more_kernel(wholes, coef_ref, rt_ref, col_ref, *refs):
+def more_kernel(wholes, places, coef_ref, rt_ref, col_ref, *refs):
     inputs, (keep_ref, send_ref) = refs[:-2], refs[-2:]
+    whole_refs, part_refs = inputs[:wholes], inputs[wholes:]
     swap = lax.axis_index("groups") % 2
-    n = 0
-    for ref in inputs[:wholes]:
-        for i in range(ref.shape[0] // 2):
-            correlate(ref[2 * i + swap], ref[2 * i + 1 - swap], coef_ref, col_ref, rt_ref, keep_ref, send_ref, n)
-            n += 1
-    for a_ref, b_ref in zip(inputs[wholes::2], inputs[wholes + 1::2]):
-        correlate(a_ref[...], b_ref[...], coef_ref, col_ref, rt_ref, keep_ref, send_ref, n)
-        n += 1
+    for n, ref in enumerate(whole_refs):
+        correlate(ref[swap], ref[1 - swap], coef_ref, col_ref, rt_ref, keep_ref, send_ref, n)
+    for i in range(0, len(places), 2):
+        a, b = (part_refs[array][index] for array, index in places[i:i + 2])
+        correlate(a, b, coef_ref, col_ref, rt_ref, keep_ref, send_ref, wholes + i // 2)
 
 
 def stats_kernel(calls, entries, *refs):
@@ -143,51 +141,79 @@
     return lax.ppermute(x, axis, [(i, i ^ bits) for i in range(lax.axis_size(axis))])
 
 
-def fetch(template):
-    orients = lax.axis_size("orient")
-    if lax.axis_size("groups") != 2 or orients != 8:
-        rest = [flipped(template, "orient", k) for k in range(1, orients)]
-        return [(rest[i:i + 2], []) for i in range(0, len(rest), 2)]
-    part = lax.dynamic_index_in_dim(template, lax.axis_index("groups"), 0, keepdims=False)
-    beside = flipped(template, "orient", 1)
-    far = [flipped(part, "orient", 2 * k) for k in (1, 2, 3)]
-    sets = []
-    for k, mine in enumerate(far):
-        partner = flipped(mine, "groups", 1)
-        column = flipped(mine, "orient", 1)
-        corner = flipped(column, "groups", 1) if k < 2 else flipped(partner, "orient", 1)
-        sets.append(([beside] if k == 0 else [], [mine, partner, column, corner]))
-    return sets
-
-
 def shards(spectra, templates, weights):
     half, side = spectra.shape[2:]
+    orients = lax.axis_size("orient")
     vmem = pl.BlockSpec(memory_space=pltpu.VMEM)
     params = pltpu.CompilerParams(vmem_limit_bytes=24 << 20)
     shape = lambda *dims, dtype=jnp.float32: jax.ShapeDtypeStruct(dims, dtype)
     columns = jnp.asarray(column_table(side))
     rows = jnp.asarray(row_table(side, half))
-    coef, table, keep, send = pl.pallas_call(
-        first_kernel,
-        in_specs=[vmem] * 5,
-        out_specs=[vmem] * 4,
-        out_shape=[shape(4, half, side), shape(2, side, side, dtype=jnp.bfloat16)] + [shape(1, half + 8, side)] * 2,
-        compiler_params=params,
-        name="first",
-    )(spectra[0], weights, rows, columns, templates[0])
-    keeps, recvs = [keep], [flipped(send, "tile", 1)]
-    for wholes, pieces in fetch(templates[0]):
+    template = templates[0]
+
+    def first(template):
+        return pl.pallas_call(
+            first_kernel,
+            in_specs=[vmem] * 5,
+            out_specs=[vmem] * 4,
+            out_shape=[shape(4, half, side), shape(2, side, side, dtype=jnp.bfloat16)] + [shape(1, half + 8, side)] * 2,
+            compiler_params=params,
+            name="first",
+        )(spectra[0], weights, rows, columns, template)
+
+    def more(coef, table, wholes, *pieces):
         count = len(wholes) + len(pieces) // 2
-        keep, send = pl.pallas_call(
-            functools.partial(more_kernel, len(wholes)),
-            in_specs=[vmem] * (3 + len(wholes) + len(pieces)),
+        arrays = []
+        for array, _ in pieces:
+            if not any(array is other for other in arrays):
+                arrays.append(array)
+        places = tuple(([array is other for other in arrays].index(True), index) for array, index in pieces)
+        return pl.pallas_call(
+            functools.partial(more_kernel, len(wholes), places),
+            in_specs=[vmem] * (3 + len(wholes) + len(arrays)),
             out_specs=[vmem] * 2,
             out_shape=[shape(count, half + 8, side)] * 2,
             compiler_params=params,
             name="more",
-        )(coef, table, columns, *wholes, *pieces)
+        )(coef, table, columns, *wholes, *arrays)
+
+    keeps, recvs = [], []
+
+    def swap(keep, send):
         keeps.append(keep)
         recvs.append(flipped(send, "tile", 1))
+
+    if lax.axis_size("groups") == 2 and orients == 8:
+        part = lax.dynamic_index_in_dim(template, lax.axis_index("groups"), 0)
+        near = [flipped(part, "orient", 2 * k) for k in (1, 2)]
+        beside = flipped(template, "orient", 1)
+        coef, table, keep, send = first(template)
+        near1, near2, late_part, send, beside = lax.optimization_barrier((*near, part, send, beside))
+        both = jnp.concatenate([near1, near2], 0)
+        far = flipped(late_part, "orient", 6)
+        both_x = flipped(both, "groups", 1)
+        both_y = flipped(both, "orient", 1)
+        swap(keep, send)
+        keep, send = more(coef, table, [beside])
+        far, both_x, both_y, send = lax.optimization_barrier((far, both_x, both_y, send))
+        last_x = flipped(jnp.concatenate([far, both_y[:1]], 0), "groups", 1)
+        last_y = flipped(jnp.concatenate([far, both_x[1:]], 0), "orient", 1)
+        swap(keep, send)
+        keep, send = more(coef, table, [], (both, 0), (both_x, 0), (both, 1), (both_x, 1))
+        last_x, last_y, send = lax.optimization_barrier((last_x, last_y, send))
+        cut = half // 2
+        corner_x = flipped(last_y[:1, :cut], "groups", 1)
+        corner_y = flipped(last_x[:1, cut:], "orient", 1)
+        swap(keep, send)
+        swap(*more(coef, table, [], (both_y, 0), (last_x, 1), (both_y, 1), (last_y, 1), (far, 0), (last_x, 0)))
+        corner = jnp.concatenate([corner_x, corner_y], 1)
+        swap(*more(coef, table, [], (last_y, 0), (corner, 0)))
+    else:
+        coef, table, keep, send = first(template)
+        swap(keep, send)
+        rest = [flipped(template, "orient", k) for k in range(1, orients)]
+        for i in range(0, len(rest), 2):
+            swap(*more(coef, table, rest[i:i + 2]))
     return tuple(pl.pallas_call(
         functools.partial(stats_kernel, len(keeps), 2 * side * side),
         in_specs=[vmem] * (2 * len(keeps) + 1),

time: 44.1 us -> 41.3 us (0.937)
  starting transfers between devices: 19.7 us -> 17.6 us
  waiting for transfers between devices: 13.7 us -> 12.5 us
  Pallas kernels: 4.84 us -> 5.3 us
    ppermute x17 -> x15, starting transfers between devices: 19.7 us -> 17.6 us  [flipped(): lax.ppermute(x, axis, [(i, i ^ bits) for i in range(lax.axis_size(axis))])]
    ppermute x17 -> x15, waiting for transfers between devices: 13.7 us -> 12.5 us  [flipped(): lax.ppermute(x, axis, [(i, i ^ bits) for i in range(lax.axis_size(axis))])]
    squeeze x1 -> x0, local copies, waits for them, and re-layouts: 0.96 us -> none  [fetch(): lax.dynamic_index_in_dim(template, lax.axis_index('groups'), 0, keepdims=...]
    dynamic_slice x0 -> x1, local copies, waits for them, and re-layouts: none -> 0.95 us  [shards(): part = lax.dynamic_index_in_dim(template, lax.axis_index('groups'), 0)]
    pallas_call x4 -> x5, Pallas kernels: 3.63 us -> 4.1 us  [the longest x4 3.4 us: more(): pl.pallas_call(functools.partial(more_kernel, len(wholes), places), in_sp...]
    unnamed x12 -> x13, local copies, waits for them, and re-layouts: 3.81 us -> 3.82 us
  transfers between devices with their start and end apart: 17 -> 15, of which waited for: 8 -> 7; matrix products, arithmetic and copies ran while one was open for 0% -> 2% of each run, Pallas kernels for 8% -> 7%
where the time goes in v3:
time: 41.3 us; the launch traced here: 41 us
  starting transfers between devices  17.6 us (43%)
  waiting for transfers between devices  12.5 us (30%)
  Pallas kernels  5.3 us (13%)
  local copies, waits for them, and re-layouts  4.81 us (12%)
  between operations  0.76 us (2%)
    ppermute x15, starting transfers between devices, flipped(): lax.ppermute(x, axis, [(i, i ^ bits) for i in range(lax.axis_size(axis))])  17.6 us
    ppermute x15, waiting for transfers between devices, flipped(): lax.ppermute(x, axis, [(i, i ^ bits) for i in range(lax.axis_size(axis))])  12.5 us
    unnamed x13, local copies, waits for them, and re-layouts  3.82 us
    pallas_call x4, Pallas kernels, more(): pl.pallas_call(functools.partial(more_kernel, len(wholes), places), in_sp...  3.4 us
    pallas_call x1, Pallas kernels, shards(): pl.pallas_call(functools.partial(stats_kernel, len(keeps), 2 * side * sid...  1.19 us
    dynamic_slice x1, local copies, waits for them, and re-layouts, shards(): part = lax.dynamic_index_in_dim(template, lax.axis_index('groups'), 0)  0.95 us
  transfers between devices with their start and end apart: 15, of which 7 were waited for; matrix products, arithmetic and copies ran while one was open for 2% of the time, Pallas kernels for 7%

profile of v3, /device:TPU:0, one launch (start us, length us, event | category | flops | bytes accessed | tf_op | source)
XLA Modules:
  0.0 41.0 jit_solution(1975040649044942074)
XLA Ops:
  0.6 0.0 copy-start
  0.6 3.0 %collective-permute-start.2 = (f32[2,128,256]{2,1,0:T(8,128)}, f32[2,128,256]{2,1,0:T(8,128)S(1)}, u32[]{:S(2)}, u32[]{:S(2)}) collective-permute-start(f32[2,128,256]{2,1,0:T(8,128)} %bitcast.4), channel_id=1, source_target_pairs={{0,2},{2,0},{4,6},{6,4},{8,10},{10,8},{12,14},{14,12},{1,3},{3,1},... | collective-permute-start | bytes 786440 | tf_op jit(solution)/shard_map/ppermute | solution.py:141
  3.7 0.9 %dynamic-slice_bitcast_fusion = f32[1,128,256]{2,1,0:T(8,128)S(1)} fusion(f32[1,2,128,256]{3,2,1,0:T(8,128)} %param.7, s32[]{:T(128)S(6)} %select_n.4), kind=kLoop, calls=%fused_computation.3 | loop fusion | bytes 262148 | tf_op jit(solution)/shard_map/jit(dynamic_index_in_dim)/dynamic_slice | solution.py:187
  4.6 1.6 %collective-permute-start = (f32[1,128,256]{2,1,0:T(8,128)S(1)}, f32[1,128,256]{2,1,0:T(8,128)S(1)}, u32[]{:S(2)}, u32[]{:S(2)}) collective-permute-start(f32[1,128,256]{2,1,0:T(8,128)S(1)} %dynamic-slice_bitcast_fusion), channel_id=1, source_target_pairs={{0,4},{2,6},{4,0},{6,2},{8,12},{10,14},{12,8},{14,10},{1,5},{3,7},... | collective-permute-start | bytes 393224 | tf_op jit(solution)/shard_map/ppermute | solution.py:141
  6.3 2.6 %collective-permute-start.1 = (f32[1,128,256]{2,1,0:T(8,128)S(1)}, f32[1,128,256]{2,1,0:T(8,128)S(1)}, u32[]{:S(2)}, u32[]{:S(2)}) collective-permute-start(f32[1,128,256]{2,1,0:T(8,128)S(1)} %dynamic-slice_bitcast_fusion), channel_id=1, source_target_pairs={{0,8},{2,10},{4,12},{6,14},{8,0},{10,2},{12,4},{14,6},{1,9},{3,11}... | collective-permute-start | bytes 393224 | tf_op jit(solution)/shard_map/ppermute | solution.py:141
  8.9 0.0 copy-done
  8.9 0.0 copy-start.1
  8.9 0.9 %copy-done.1 = f32[1,2,128,256]{3,2,1,0:T(8,128)S(1)} copy-done((f32[1,2,128,256]{3,2,1,0:T(8,128)S(1)}, f32[1,2,128,256]{3,2,1,0:T(8,128)}, u32[]{:S(2)}) %copy-start.1) | copy-done | bytes 262168
  9.8 0.0 copy-start.2
  9.8 0.9 %copy-done.2 = f32[1,2,128,256]{3,2,1,0:T(8,128)S(1)} copy-done((f32[1,2,128,256]{3,2,1,0:T(8,128)S(1)}, f32[1,2,128,256]{3,2,1,0:T(8,128)}, u32[]{:S(2)}) %copy-start.2) | copy-done | bytes 262168
  10.8 0.0 copy-start.3
  10.8 0.9 %copy-done.3 = f32[256,256]{1,0:T(8,128)S(1)} copy-done((f32[256,256]{1,0:T(8,128)S(1)}, f32[256,256]{1,0:T(8,128)}, u32[]{:S(2)}) %copy-start.3) | copy-done | bytes 262168
  11.7 0.0 copy-start.4
  11.7 0.9 %copy-done.4 = bf16[2,256,256]{2,1,0:T(8,128)(2,1)S(1)} copy-done((bf16[2,256,256]{2,1,0:T(8,128)(2,1)S(1)}, bf16[2,256,256]{2,1,0:T(8,128)(2,1)}, u32[]{:S(2)}) %copy-start.4) | copy-done | bytes 262168
  12.7 0.7 %first.1 = (f32[4,128,256]{2,1,0:T(8,128)S(1)}, bf16[2,256,256]{2,1,0:T(8,128)(2,1)S(1)}, f32[1,136,256]{2,1,0:T(8,128)S(1)}, f32[1,136,256]{2,1,0:T(8,128)S(1)}) custom-call(f32[2,128,256]{2,1,0:T(8,128)S(1)} %bitcast.6, f32[256,256]{1,0:T(8,128)S(1)} %copy-done.3, bf16[2,256,256]{2,1,0:T(8,128)(2,1)S(1)} %copy-done.4, bf16[2,256,256]{2,1,0:T(8,128)(2,1)S(1)} %copy-done, ...), custom_call_target="tpu_custom_call" | custom-call | tf_op jit(solution)/shard_map/first/pallas_call | solution.py:155
  13.4 0.0 collective-permute-done
  13.4 1.3 %collective-permute-done.1 = f32[1,128,256]{2,1,0:T(8,128)S(1)} collective-permute-done((f32[1,128,256]{2,1,0:T(8,128)S(1)}, f32[1,128,256]{2,1,0:T(8,128)S(1)}, u32[]{:S(2)}, u32[]{:S(2)}) %collective-permute-start.1) | collective-permute-done | bytes 131104 | tf_op jit(solution)/shard_map/ppermute | solution.py:141
  14.7 0.0 collective-permute-done.2.refs_0_
  14.7 1.6 %collective-permute-start.4 = (f32[2,128,256]{2,1,0:T(8,128)S(1)}, f32[2,128,256]{2,1,0:T(8,128)S(1)}, u32[]{:S(2)}, u32[]{:S(2)}) collective-permute-start(f32[2,128,256]{2,1,0:T(8,128)S(1)} %constant_dynamic-update-slice_fusion.refs_0_), channel_id=1, source_target_pairs={{0,16},{16,0},{1,17},{17,1},{2,18},{18,2},{3,19},{19,3},{4,20},{20... | collective-permute-start | bytes 786440 | tf_op jit(solution)/shard_map/ppermute | solution.py:141
  16.3 0.5 %collective-permute-start.5 = (f32[2,128,256]{2,1,0:T(8,128)S(1)}, f32[2,128,256]{2,1,0:T(8,128)S(1)}, u32[]{:S(2)}, u32[]{:S(2)}) collective-permute-start(f32[2,128,256]{2,1,0:T(8,128)S(1)} %constant_dynamic-update-slice_fusion.refs_0_), channel_id=1, source_target_pairs={{0,2},{2,0},{4,6},{6,4},{8,10},{10,8},{12,14},{14,12},{1,3},{3,1},... | collective-permute-start | bytes 786440 | tf_op jit(solution)/shard_map/ppermute | solution.py:141
  16.8 2.5 %collective-permute-start.3 = (f32[1,128,256]{2,1,0:T(8,128)S(1)}, f32[1,128,256]{2,1,0:T(8,128)S(1)}, u32[]{:S(2)}, u32[]{:S(2)}) collective-permute-start(f32[1,128,256]{2,1,0:T(8,128)S(1)} %dynamic-slice_bitcast_fusion), channel_id=1, source_target_pairs={{0,12},{2,14},{4,8},{6,10},{8,4},{10,6},{12,0},{14,2},{1,13},{3,15... | collective-permute-start | bytes 393224 | tf_op jit(solution)/shard_map/ppermute | solution.py:141
  19.3 0.7 %more.4 = (f32[1,136,256]{2,1,0:T(8,128)S(1)}, f32[1,136,256]{2,1,0:T(8,128)S(1)}) custom-call(f32[4,128,256]{2,1,0:T(8,128)S(1)} %get-tuple-element.28.coef_ref, bf16[2,256,256]{2,1,0:T(8,128)(2,1)S(1)} %get-tuple-element.29.rt_ref, bf16[2,256,256]{2,1,0:T(8,128)(2,1)S(1)} %copy-done, f32[2,128,256]{2,1,0:T(8,128)S(1)} %collective-permute-done.2.refs_0_), custom_call_target="tpu_custom_call" | custom-call | tf_op jit(solution)/shard_map/more/pallas_call | solution.py:171
  20.0 3.6 %collective-permute-done.3.refs_3_ = f32[1,128,256]{2,1,0:T(8,128)S(1)} collective-permute-done((f32[1,128,256]{2,1,0:T(8,128)S(1)}, f32[1,128,256]{2,1,0:T(8,128)S(1)}, u32[]{:S(2)}, u32[]{:S(2)}) %collective-permute-start.3) | collective-permute-done | bytes 131104 | tf_op jit(solution)/shard_map/ppermute | solution.py:141
  23.6 0.0 collective-permute-done.4.refs_1_
  23.6 0.0 collective-permute-done.5.refs_0_
  23.6 0.6 %collective-permute-start.6 = (f32[2,128,256]{2,1,0:T(8,128)S(1)}, f32[2,128,256]{2,1,0:T(8,128)S(1)}, u32[]{:S(2)}, u32[]{:S(2)}) collective-permute-start(f32[2,128,256]{2,1,0:T(8,128)S(1)} %get-tuple-element.52), channel_id=1, source_target_pairs={{0,16},{16,0},{1,17},{17,1},{2,18},{18,2},{3,19},{19,3},{4,20},{20... | collective-permute-start | bytes 786440 | tf_op jit(solution)/shard_map/ppermute | solution.py:141
  24.3 1.5 %collective-permute-start.7 = (f32[2,128,256]{2,1,0:T(8,128)S(1)}, f32[2,128,256]{2,1,0:T(8,128)S(1)}, u32[]{:S(2)}, u32[]{:S(2)}) collective-permute-start(f32[2,128,256]{2,1,0:T(8,128)S(1)} %get-tuple-element.51), channel_id=1, source_target_pairs={{0,2},{2,0},{4,6},{6,4},{8,10},{10,8},{12,14},{14,12},{1,3},{3,1},... | collective-permute-start | bytes 786440 | tf_op jit(solution)/shard_map/ppermute | solution.py:141
  25.8 0.9 %more.5 = (f32[2,136,256]{2,1,0:T(8,128)S(1)}, f32[2,136,256]{2,1,0:T(8,128)S(1)}) custom-call(f32[4,128,256]{2,1,0:T(8,128)S(1)} %get-tuple-element.28.coef_ref, bf16[2,256,256]{2,1,0:T(8,128)(2,1)S(1)} %get-tuple-element.29.rt_ref, bf16[2,256,256]{2,1,0:T(8,128)(2,1)S(1)} %copy-done, f32[2,128,256]{2,1,0:T(8,128)S(1)} %constant_dynamic-update-slice_fusion.refs_0_, ...), custom_call_target="tpu_custom_call" | custom-call | tf_op jit(solution)/shard_map/more/pallas_call | solution.py:171
  26.7 3.4 %collective-permute-done.6.refs_1_ = f32[2,128,256]{2,1,0:T(8,128)S(1)} collective-permute-done((f32[2,128,256]{2,1,0:T(8,128)S(1)}, f32[2,128,256]{2,1,0:T(8,128)S(1)}, u32[]{:S(2)}, u32[]{:S(2)}) %collective-permute-start.6) | collective-permute-done | bytes 262176 | tf_op jit(solution)/shard_map/ppermute | solution.py:141
  30.1 0.5 %collective-permute-done.7.refs_2_.refs_0_ = f32[2,128,256]{2,1,0:T(8,128)S(1)} collective-permute-done((f32[2,128,256]{2,1,0:T(8,128)S(1)}, f32[2,128,256]{2,1,0:T(8,128)S(1)}, u32[]{:S(2)}, u32[]{:S(2)}) %collective-permute-start.7) | collective-permute-done | bytes 262176 | tf_op jit(solution)/shard_map/ppermute | solution.py:141
  30.6 1.1 %more.6 = (f32[3,136,256]{2,1,0:T(8,128)S(1)}, f32[3,136,256]{2,1,0:T(8,128)S(1)}) custom-call(f32[4,128,256]{2,1,0:T(8,128)S(1)} %get-tuple-element.28.coef_ref, bf16[2,256,256]{2,1,0:T(8,128)(2,1)S(1)} %get-tuple-element.29.rt_ref, bf16[2,256,256]{2,1,0:T(8,128)(2,1)S(1)} %copy-done, f32[2,128,256]{2,1,0:T(8,128)S(1)} %collective-permute-done.5.refs_0_, ...), custom_call_target="tpu_custom_call" | custom-call | tf_op jit(solution)/shard_map/more/pallas_call | solution.py:171
  31.7 0.1 collective-permute-start.13
  31.8 1.6 %collective-permute-start.9 = (f32[1,64,256]{2,1,0:T(8,128)S(1)}, f32[1,64,256]{2,1,0:T(8,128)S(1)}, u32[]{:S(2)}, u32[]{:S(2)}) collective-permute-start(f32[1,64,256]{2,1,0:T(8,128)S(1)} %slice.15), channel_id=1, source_target_pairs={{0,2},{2,0},{4,6},{6,4},{8,10},{10,8},{12,14},{14,12},{1,3},{3,1},... | collective-permute-start | bytes 196616 | tf_op jit(solution)/shard_map/ppermute | solution.py:141
  33.4 1.5 %collective-permute-start.8 = (f32[1,64,256]{2,1,0:T(8,128)S(1)}, f32[1,64,256]{2,1,0:T(8,128)S(1)}, u32[]{:S(2)}, u32[]{:S(2)}) collective-permute-start(f32[1,64,256]{2,1,0:T(8,128)S(1)} %slice.14), channel_id=1, source_target_pairs={{0,16},{16,0},{1,17},{17,1},{2,18},{18,2},{3,19},{19,3},{4,20},{20... | collective-permute-start | bytes 196616 | tf_op jit(solution)/shard_map/ppermute | solution.py:141
  34.9 0.0 collective-permute-start.12
  34.9 0.5 %collective-permute-start.10 = (f32[1,136,256]{2,1,0:T(8,128)S(1)}, f32[1,136,256]{2,1,0:T(8,128)S(1)}, u32[]{:S(2)}, u32[]{:S(2)}) collective-permute-start(f32[1,136,256]{2,1,0:T(8,128)S(1)} %get-tuple-element.46), channel_id=1, source_target_pairs={{0,1},{1,0},{2,3},{3,2},{4,5},{5,4},{6,7},{7,6},{8,9},{9,8},{10,11... | collective-permute-start | bytes 417800 | tf_op jit(solution)/shard_map/ppermute | solution.py:141
  35.4 0.9 %collective-permute-done.9 = f32[1,64,256]{2,1,0:T(8,128)S(1)} collective-permute-done((f32[1,64,256]{2,1,0:T(8,128)S(1)}, f32[1,64,256]{2,1,0:T(8,128)S(1)}, u32[]{:S(2)}, u32[]{:S(2)}) %collective-permute-start.9) | collective-permute-done | bytes 65568 | tf_op jit(solution)/shard_map/ppermute | solution.py:141
  36.3 0.0 collective-permute-start.11
  36.3 1.4 %collective-permute-done.8 = f32[1,64,256]{2,1,0:T(8,128)S(1)} collective-permute-done((f32[1,64,256]{2,1,0:T(8,128)S(1)}, f32[1,64,256]{2,1,0:T(8,128)S(1)}, u32[]{:S(2)}, u32[]{:S(2)}) %collective-permute-start.8) | collective-permute-done | bytes 65568 | tf_op jit(solution)/shard_map/ppermute | solution.py:141
  37.7 0.0 copy-start.5
  37.7 0.7 %more.7 = (f32[1,136,256]{2,1,0:T(8,128)S(1)}, f32[1,136,256]{2,1,0:T(8,128)S(1)}) custom-call(f32[4,128,256]{2,1,0:T(8,128)S(1)} %get-tuple-element.28.coef_ref, bf16[2,256,256]{2,1,0:T(8,128)(2,1)S(1)} %get-tuple-element.29.rt_ref, bf16[2,256,256]{2,1,0:T(8,128)(2,1)S(1)} %copy-done, f32[2,128,256]{2,1,0:T(8,128)S(1)} %collective-permute-done.7.refs_2_.refs_0_, ...), custom_call_target="tpu_custom_call" | custom-call | tf_op jit(solution)/shard_map/more/pallas_call | solution.py:171
  38.4 0.1 collective-permute-start.14
  38.5 0.0 collective-permute-done.10.refs_5_
  38.5 0.0 collective-permute-done.11.refs_6_
  38.5 1.3 %collective-permute-done.14.refs_9_ = f32[1,136,256]{2,1,0:T(8,128)S(1)} collective-permute-done((f32[1,136,256]{2,1,0:T(8,128)S(1)}, f32[1,136,256]{2,1,0:T(8,128)S(1)}, u32[]{:S(2)}, u32[]{:S(2)}) %collective-permute-start.14) | collective-permute-done | bytes 139296 | tf_op jit(solution)/shard_map/ppermute | solution.py:141
  39.8 0.0 collective-permute-done.12.refs_7_
  39.8 0.0 collective-permute-done.13.refs_8_
  39.8 0.0 copy-done.5
  39.8 1.2 %statistics.1 = (f32[1,128,256]{2,1,0:T(8,128)}, f32[1,128,256]{2,1,0:T(8,128)}, f32[1,128,256]{2,1,0:T(8,128)}) custom-call(f32[1,136,256]{2,1,0:T(8,128)S(1)} %get-tuple-element.27.refs_0_, f32[1,136,256]{2,1,0:T(8,128)S(1)} %get-tuple-element.32.refs_1_, f32[2,136,256]{2,1,0:T(8,128)S(1)} %get-tuple-element.38.refs_2_, ...), custom_call_target="tpu_custom_call" | custom-call | tf_op jit(solution)/shard_map/statistics/pallas_call | solution.py:217
  (8 shorter events, 0.1 us)
Async XLA Ops:
  0.6 8.2 %copy-start = (bf16[2,256,256]{2,1,0:T(8,128)(2,1)S(1)}, bf16[2,256,256]{2,1,0:T(8,128)(2,1)}, u32[]{:S(2)}) copy-start(bf16[2,256,256]{2,1,0:T(8,128)(2,1)} %constant.19.clone.col_ref) | copy-start | bytes 786436
  0.6 14.1 %collective-permute-start.2 = (f32[2,128,256]{2,1,0:T(8,128)}, f32[2,128,256]{2,1,0:T(8,128)S(1)}, u32[]{:S(2)}, u32[]{:S(2)}) collective-permute-start(f32[2,128,256]{2,1,0:T(8,128)} %bitcast.4), channel_id=1, source_target_pairs={{0,2},{2,0},{4,6},{6,4},{8,10},{10,8},{12,14},{14,12},{1,3},{3,1},... | collective-permute-start | bytes 786440 | tf_op jit(solution)/shard_map/ppermute | solution.py:141
  4.6 8.7 %collective-permute-start = (f32[1,128,256]{2,1,0:T(8,128)S(1)}, f32[1,128,256]{2,1,0:T(8,128)S(1)}, u32[]{:S(2)}, u32[]{:S(2)}) collective-permute-start(f32[1,128,256]{2,1,0:T(8,128)S(1)} %dynamic-slice_bitcast_fusion), channel_id=1, source_target_pairs={{0,4},{2,6},{4,0},{6,2},{8,12},{10,14},{12,8},{14,10},{1,5},{3,7},... | collective-permute-start | bytes 393224 | tf_op jit(solution)/shard_map/ppermute | solution.py:141
  6.3 8.4 %collective-permute-start.1 = (f32[1,128,256]{2,1,0:T(8,128)S(1)}, f32[1,128,256]{2,1,0:T(8,128)S(1)}, u32[]{:S(2)}, u32[]{:S(2)}) collective-permute-start(f32[1,128,256]{2,1,0:T(8,128)S(1)} %dynamic-slice_bitcast_fusion), channel_id=1, source_target_pairs={{0,8},{2,10},{4,12},{6,14},{8,0},{10,2},{12,4},{14,6},{1,9},{3,11}... | collective-permute-start | bytes 393224 | tf_op jit(solution)/shard_map/ppermute | solution.py:141
  8.9 1.0 %copy-start.1 = (f32[1,2,128,256]{3,2,1,0:T(8,128)S(1)}, f32[1,2,128,256]{3,2,1,0:T(8,128)}, u32[]{:S(2)}) copy-start(f32[1,2,128,256]{3,2,1,0:T(8,128)} %param.7) | copy-start | bytes 786436
  9.8 0.9 %copy-start.2 = (f32[1,2,128,256]{3,2,1,0:T(8,128)S(1)}, f32[1,2,128,256]{3,2,1,0:T(8,128)}, u32[]{:S(2)}) copy-start(f32[1,2,128,256]{3,2,1,0:T(8,128)} %param.6) | copy-start | bytes 786436
  10.8 0.9 %copy-start.3 = (f32[256,256]{1,0:T(8,128)S(1)}, f32[256,256]{1,0:T(8,128)}, u32[]{:S(2)}) copy-start(f32[256,256]{1,0:T(8,128)} %w_ref.1) | copy-start | bytes 786436
  11.7 0.9 %copy-start.4 = (bf16[2,256,256]{2,1,0:T(8,128)(2,1)S(1)}, bf16[2,256,256]{2,1,0:T(8,128)(2,1)}, u32[]{:S(2)}) copy-start(bf16[2,256,256]{2,1,0:T(8,128)(2,1)} %constant.20.clone.row_ref) | copy-start | bytes 786436
  14.7 8.8 %collective-permute-start.4 = (f32[2,128,256]{2,1,0:T(8,128)S(1)}, f32[2,128,256]{2,1,0:T(8,128)S(1)}, u32[]{:S(2)}, u32[]{:S(2)}) collective-permute-start(f32[2,128,256]{2,1,0:T(8,128)S(1)} %constant_dynamic-update-slice_fusion.refs_0_), channel_id=1, source_target_pairs={{0,16},{16,0},{1,17},{17,1},{2,18},{18,2},{3,19},{19,3},{4,20},{20... | collective-permute-start | bytes 786440 | tf_op jit(solution)/shard_map/ppermute | solution.py:141
  16.3 7.3 %collective-permute-start.5 = (f32[2,128,256]{2,1,0:T(8,128)S(1)}, f32[2,128,256]{2,1,0:T(8,128)S(1)}, u32[]{:S(2)}, u32[]{:S(2)}) collective-permute-start(f32[2,128,256]{2,1,0:T(8,128)S(1)} %constant_dynamic-update-slice_fusion.refs_0_), channel_id=1, source_target_pairs={{0,2},{2,0},{4,6},{6,4},{8,10},{10,8},{12,14},{14,12},{1,3},{3,1},... | collective-permute-start | bytes 786440 | tf_op jit(solution)/shard_map/ppermute | solution.py:141
  16.8 6.8 %collective-permute-start.3 = (f32[1,128,256]{2,1,0:T(8,128)S(1)}, f32[1,128,256]{2,1,0:T(8,128)S(1)}, u32[]{:S(2)}, u32[]{:S(2)}) collective-permute-start(f32[1,128,256]{2,1,0:T(8,128)S(1)} %dynamic-slice_bitcast_fusion), channel_id=1, source_target_pairs={{0,12},{2,14},{4,8},{6,10},{8,4},{10,6},{12,0},{14,2},{1,13},{3,15... | collective-permute-start | bytes 393224 | tf_op jit(solution)/shard_map/ppermute | solution.py:141
  23.6 6.4 %collective-permute-start.6 = (f32[2,128,256]{2,1,0:T(8,128)S(1)}, f32[2,128,256]{2,1,0:T(8,128)S(1)}, u32[]{:S(2)}, u32[]{:S(2)}) collective-permute-start(f32[2,128,256]{2,1,0:T(8,128)S(1)} %get-tuple-element.52), channel_id=1, source_target_pairs={{0,16},{16,0},{1,17},{17,1},{2,18},{18,2},{3,19},{19,3},{4,20},{20... | collective-permute-start | bytes 786440 | tf_op jit(solution)/shard_map/ppermute | solution.py:141
  24.3 6.4 %collective-permute-start.7 = (f32[2,128,256]{2,1,0:T(8,128)S(1)}, f32[2,128,256]{2,1,0:T(8,128)S(1)}, u32[]{:S(2)}, u32[]{:S(2)}) collective-permute-start(f32[2,128,256]{2,1,0:T(8,128)S(1)} %get-tuple-element.51), channel_id=1, source_target_pairs={{0,2},{2,0},{4,6},{6,4},{8,10},{10,8},{12,14},{14,12},{1,3},{3,1},... | collective-permute-start | bytes 786440 | tf_op jit(solution)/shard_map/ppermute | solution.py:141
  31.7 8.1 %collective-permute-start.13 = (f32[3,136,256]{2,1,0:T(8,128)S(1)}, f32[3,136,256]{2,1,0:T(8,128)S(1)}, u32[]{:S(2)}, u32[]{:S(2)}) collective-permute-start(f32[3,136,256]{2,1,0:T(8,128)S(1)} %get-tuple-element.49), channel_id=1, source_target_pairs={{0,1},{1,0},{2,3},{3,2},{4,5},{5,4},{6,7},{7,6},{8,9},{9,8},{10,11... | collective-permute-start | bytes 1253384 | tf_op jit(solution)/shard_map/ppermute | solution.py:141
  31.8 4.5 %collective-permute-start.9 = (f32[1,64,256]{2,1,0:T(8,128)S(1)}, f32[1,64,256]{2,1,0:T(8,128)S(1)}, u32[]{:S(2)}, u32[]{:S(2)}) collective-permute-start(f32[1,64,256]{2,1,0:T(8,128)S(1)} %slice.15), channel_id=1, source_target_pairs={{0,2},{2,0},{4,6},{6,4},{8,10},{10,8},{12,14},{14,12},{1,3},{3,1},... | collective-permute-start | bytes 196616 | tf_op jit(solution)/shard_map/ppermute | solution.py:141
  33.4 4.3 %collective-permute-start.8 = (f32[1,64,256]{2,1,0:T(8,128)S(1)}, f32[1,64,256]{2,1,0:T(8,128)S(1)}, u32[]{:S(2)}, u32[]{:S(2)}) collective-permute-start(f32[1,64,256]{2,1,0:T(8,128)S(1)} %slice.14), channel_id=1, source_target_pairs={{0,16},{16,0},{1,17},{17,1},{2,18},{18,2},{3,19},{19,3},{4,20},{20... | collective-permute-start | bytes 196616 | tf_op jit(solution)/shard_map/ppermute | solution.py:141
  34.9 4.9 %collective-permute-start.12 = (f32[2,136,256]{2,1,0:T(8,128)S(1)}, f32[2,136,256]{2,1,0:T(8,128)S(1)}, u32[]{:S(2)}, u32[]{:S(2)}) collective-permute-start(f32[2,136,256]{2,1,0:T(8,128)S(1)} %get-tuple-element.48), channel_id=1, source_target_pairs={{0,1},{1,0},{2,3},{3,2},{4,5},{5,4},{6,7},{7,6},{8,9},{9,8},{10,11... | collective-permute-start | bytes 835592 | tf_op jit(solution)/shard_map/ppermute | solution.py:141
  34.9 3.6 %collective-permute-start.10 = (f32[1,136,256]{2,1,0:T(8,128)S(1)}, f32[1,136,256]{2,1,0:T(8,128)S(1)}, u32[]{:S(2)}, u32[]{:S(2)}) collective-permute-start(f32[1,136,256]{2,1,0:T(8,128)S(1)} %get-tuple-element.46), channel_id=1, source_target_pairs={{0,1},{1,0},{2,3},{3,2},{4,5},{5,4},{6,7},{7,6},{8,9},{9,8},{10,11... | collective-permute-start | bytes 417800 | tf_op jit(solution)/shard_map/ppermute | solution.py:141
  36.3 2.2 %collective-permute-start.11 = (f32[1,136,256]{2,1,0:T(8,128)S(1)}, f32[1,136,256]{2,1,0:T(8,128)S(1)}, u32[]{:S(2)}, u32[]{:S(2)}) collective-permute-start(f32[1,136,256]{2,1,0:T(8,128)S(1)} %get-tuple-element.47), channel_id=1, source_target_pairs={{0,1},{1,0},{2,3},{3,2},{4,5},{5,4},{6,7},{7,6},{8,9},{9,8},{10,11... | collective-permute-start | bytes 417800 | tf_op jit(solution)/shard_map/ppermute | solution.py:141
  37.7 2.1 %copy-start.5 = (f32[128,128]{1,0:T(8,128)S(1)}, f32[128,128]{1,0:T(8,128)}, u32[]{:S(2)}) copy-start(f32[128,128]{1,0:T(8,128)} %constant.21.clone.refs_10_) | copy-start | bytes 196612
  38.4 1.4 %collective-permute-start.14 = (f32[1,136,256]{2,1,0:T(8,128)S(1)}, f32[1,136,256]{2,1,0:T(8,128)S(1)}, u32[]{:S(2)}, u32[]{:S(2)}) collective-permute-start(f32[1,136,256]{2,1,0:T(8,128)S(1)} %get-tuple-element.50), channel_id=1, source_target_pairs={{0,1},{1,0},{2,3},{3,2},{4,5},{5,4},{6,7},{7,6},{8,9},{9,8},{10,11... | collective-permute-start | bytes 417800 | tf_op jit(solution)/shard_map/ppermute | solution.py:141

commit v4 on v2

v4 whole, which is shorter than its diff:
```python
import functools
import math

import jax
import jax.numpy as jnp
import numpy as np
from jax import lax
from jax.experimental import pallas as pl
from jax.experimental.pallas import tpu as pltpu
from jax.sharding import PartitionSpec as P


def column_table(side):
    mid = side // 2
    k = np.arange(side)[:, None]
    x = np.arange(mid)[None, :]
    angle = 2.0 * math.pi * (k * x % side) / side
    right = np.sin(angle)
    right[:, 0] = np.cos(math.pi * k[:, 0])
    return np.concatenate([np.cos(angle), right], 1).astype(np.float32)


def row_table(side, half):
    y = np.arange(side)[:, None]
    k = np.arange(half)[None, :]
    angle = 2.0 * math.pi * (k * y % side) / side
    return np.concatenate([np.cos(angle), -np.sin(angle)], 1).astype(np.float32)


def unfold_table(mid):
    table = np.zeros((mid, mid), np.float32)
    k = np.arange(mid)
    table[(mid - k) % mid, k] = 1.0
    return table


def parts(x):
    high = x.astype(jnp.bfloat16)
    low = (x - high.astype(jnp.float32)).astype(jnp.bfloat16)
    return high, low


def dot(a, b):
    return jnp.dot(a, b, preferred_element_type=jnp.float32)


def prepare_kernel(s_hbm, w_hbm, row_hbm, col_hbm, coef_ref, rt_ref, ct_ref, s_ref, w_ref, row_ref, col_ref, sems):
    half, side = w_ref.shape
    here = lax.axis_index("tile")
    swap = lax.axis_index("groups") % 2
    mine = pl.ds(pl.multiple_of(here * half, half), half)
    other = pl.ds(pl.multiple_of((1 - here) * half, half), half)
    moves = (
        (s_hbm, s_ref),
        (w_hbm.at[mine], w_ref),
        (row_hbm.at[mine], row_ref.at[pl.ds(0, half)]),
        (row_hbm.at[other], row_ref.at[pl.ds(half, half)]),
        (col_hbm, col_ref),
    )
    copies = [pltpu.make_async_copy(source, target, sems.at[n]) for n, (source, target) in enumerate(moves)]
    for copy in copies:
        copy.start()
    for copy in copies:
        copy.wait()
    w = w_ref[...]
    u, v = s_ref[swap] * w, s_ref[1 - swap] * w
    turn = (1 - 2 * swap).astype(jnp.float32)
    coef_ref[0], coef_ref[1], coef_ref[2], coef_ref[3] = u, v, u * turn, v * turn
    ct_ref[0], ct_ref[1] = parts(col_ref[...])
    odd = lax.broadcasted_iota(jnp.int32, (side, side), 0) % 2
    rt_ref[0], rt_ref[1] = parts(row_ref[...] * (1 - 2 * odd * here).astype(jnp.float32))


def correlate(a, b, coef_ref, col_ref, rt_ref, keep_ref, send_ref, n):
    half, side = a.shape
    mid = side // 2
    squares = jnp.sum((a * a + b * b).reshape(half // 8, 8, side), axis=0)
    power = jnp.broadcast_to(jnp.sum(squares), (8, side))
    z = jnp.concatenate([coef_ref[0] * a + coef_ref[1] * b, coef_ref[3] * a - coef_ref[2] * b], 0)
    zh, zl = parts(z)
    ch, cl = col_ref[0], col_ref[1]
    m = dot(zh, ch) + (dot(zl, ch) + dot(zh, cl))
    mcr, mci = m[:half, :mid], m[half:, :mid]
    msr, msi = m[:half, mid:], m[half:, mid:]
    first = lax.broadcasted_iota(jnp.int32, (half, mid), 1) == 0
    real = jnp.concatenate([mcr - jnp.where(first, 0.0, msi), jnp.where(first, msr, mcr + msi)], 1)
    imag = jnp.concatenate([mci + jnp.where(first, 0.0, msr), jnp.where(first, msi, mci - msr)], 1)
    ah, al = parts(jnp.concatenate([real, imag], 0))
    rh, rl = rt_ref[0], rt_ref[1]
    p = dot(rh, ah) + (dot(rh, al) + dot(rl, ah))
    keep_ref[n, :half] = p[:half]
    keep_ref[n, half:] = power
    send_ref[n, :half] = p[half:]
    send_ref[n, half:] = power


def maps_kernel(wholes, places, coef_ref, rt_ref, col_ref, *refs):
    inputs, (keep_ref, send_ref) = refs[:-2], refs[-2:]
    whole_refs, part_refs = inputs[:wholes], inputs[wholes:]
    swap = lax.axis_index("groups") % 2
    for n, ref in enumerate(whole_refs):
        correlate(ref[swap], ref[1 - swap], coef_ref, col_ref, rt_ref, keep_ref, send_ref, n)
    for n, pair in enumerate(places):
        a, b = (jnp.concatenate([part_refs[array][start:stop] for array, start, stop in piece], 0) for piece in pair)
        correlate(a, b, coef_ref, col_ref, rt_ref, keep_ref, send_ref, wholes + n)


def stats_kernel(calls, entries, *refs):
    keeps, recvs = refs[:calls], refs[calls:2 * calls]
    fold_ref, peak_ref, mean_ref, square_ref, flip_ref = refs[2 * calls:]
    side = keeps[0].shape[2]
    half = keeps[0].shape[1] - 8
    mid = side // 2
    pairs = [(keep, recv, n) for keep, recv in zip(keeps, recvs) for n in range(keep.shape[0])]
    count = len(pairs)
    for block in range(half // 8):
        rows = pl.ds(block * 8, 8)
        best = total = squares = None
        for keep, recv, n in pairs:
            power = (keep[n, half:] + recv[n, half:]) * (1.0 / entries)
            scale = lax.rsqrt(power + 1e-6) * (1.0 / side)
            c = (keep[n, rows] + recv[n, rows]) * scale
            if best is None:
                best, total, squares = c, c, c * c
            else:
                best, total, squares = jnp.maximum(best, c), total + c, squares + c * c
        total = total * (1.0 / count)
        squares = squares * (1.0 / count)
        for n, (ref, value) in enumerate(((peak_ref, best), (mean_ref, total), (square_ref, squares))):
            ref[0, rows, :mid] = value[:, :mid]
            flip_ref[pl.ds(n * half + block * 8, 8)] = value[:, mid:]
    right = jnp.dot(flip_ref[...], fold_ref[...], precision=lax.Precision.HIGHEST, preferred_element_type=jnp.float32)
    for n, ref in enumerate((peak_ref, mean_ref, square_ref)):
        ref[0, :, mid:] = right[n * half:(n + 1) * half]


def flipped(x, axis, bits):
    return lax.ppermute(x, axis, [(i, i ^ bits) for i in range(lax.axis_size(axis))])


def shards(spectra, templates, weights):
    half, side = spectra.shape[2:]
    orients = lax.axis_size("orient")
    vmem = pl.BlockSpec(memory_space=pltpu.VMEM)
    hbm = pl.BlockSpec(memory_space=pltpu.HBM)
    params = pltpu.CompilerParams(vmem_limit_bytes=24 << 20)
    shape = lambda *dims, dtype=jnp.float32: jax.ShapeDtypeStruct(dims, dtype)
    scratch = lambda *dims: pltpu.VMEM(dims, jnp.float32)
    template = templates[0]

    coef, table, columns = pl.pallas_call(
        prepare_kernel,
        in_specs=[hbm] * 4,
        out_specs=[vmem] * 3,
        out_shape=[shape(4, half, side)] + [shape(2, side, side, dtype=jnp.bfloat16)] * 2,
        scratch_shapes=[
            scratch(2, half, side), scratch(half, side), scratch(side, side), scratch(side, side), pltpu.SemaphoreType.DMA((5,)),
        ],
        compiler_params=params,
        name="prepare",
    )(spectra[0], weights, jnp.asarray(row_table(side, half)), jnp.asarray(column_table(side)))

    def maps(wholes, arrays=(), places=()):
        return pl.pallas_call(
            functools.partial(maps_kernel, len(wholes), places),
            in_specs=[vmem] * (3 + len(wholes) + len(arrays)),
            out_specs=[vmem] * 2,
            out_shape=[shape(len(wholes) + len(places), half + 8, side)] * 2,
            compiler_params=params,
            name="maps",
        )(coef, table, columns, *wholes, *arrays)

    if lax.axis_size("groups") == 2 and orients == 8:
        plane = lax.axis_index("groups")
        cut = half // 2
        part = lax.dynamic_index_in_dim(template, plane, 0, keepdims=False)
        near1, near2 = (flipped(part, "orient", 2 * k) for k in (1, 2))
        beside = flipped(template, "orient", 1)
        near1, near2, beside, part, coef = lax.optimization_barrier((near1, near2, beside, part, coef))
        near = jnp.concatenate([near1, near2], 0)
        far = flipped(part, "orient", 6)
        near_x = flipped(near, "groups", 1)
        near_y = flipped(near, "orient", 1)
        rest = lax.dynamic_index_in_dim(template, 1 - plane, 0, keepdims=False)
        far, near_x, near_y, rest = lax.optimization_barrier((far, near_x, near_y, rest))
        last_x = flipped(jnp.concatenate([far, near_y[:half + cut]], 0), "groups", 1)
        last_y = flipped(jnp.concatenate([far, near_x[half + cut:]], 0), "orient", 1)
        corner = flipped(rest, "orient", 7)
        early = maps(
            [template, beside],
            [near, near_x],
            (
                (((0, 0, half),), ((1, 0, half),)),
                (((0, half, side),), ((1, half, side),)),
            ),
        )
        early_recv = flipped(early[1], "tile", 1)
        last_x, last_y, corner, early_recv = lax.optimization_barrier((last_x, last_y, corner, early_recv))
        late = maps(
            [],
            [near_y, last_x, last_y, far, corner],
            (
                (((0, 0, half),), ((1, half, side),)),
                (((0, half, side),), ((1, side, side + cut), (2, half, half + cut))),
                (((3, 0, half),), ((1, 0, half),)),
                (((2, 0, half),), ((4, 0, half),)),
            ),
        )
        keeps, recvs = [early[0], late[0]], [early_recv, flipped(late[1], "tile", 1)]
    else:
        rest = [template] + [flipped(template, "orient", k) for k in range(1, orients)]
        calls = [maps(rest[i:i + 4]) for i in range(0, len(rest), 4)]
        keeps = [keep for keep, _ in calls]
        recvs = [flipped(send, "tile", 1) for _, send in calls]
    return tuple(pl.pallas_call(
        functools.partial(stats_kernel, len(keeps), 2 * side * side),
        in_specs=[vmem] * (2 * len(keeps) + 1),
        out_specs=[vmem] * 3,
        out_shape=[shape(1, half, side)] * 3,
        scratch_shapes=[scratch(3 * half, side // 2)],
        compiler_params=params,
        name="statistics",
    )(*keeps, *recvs, jnp.asarray(unfold_table(side // 2))))


def solution(mesh):
    in_specs = (
        P(("groups", "orient"), None, "tile", None),
        P("orient", None, "tile", None),
        P("groups", None),
    )
    out_specs = (P(("groups", "orient"), "tile", None),) * 3
    return jax.shard_map(shards, mesh=mesh, in_specs=in_specs, out_specs=out_specs, check_vma=False)
```

time: 44.1 us -> 39.3 us (0.89)
  local copies, waits for them, and re-layouts: 4.77 us -> 3 us
  waiting for transfers between devices: 13.7 us -> 12.3 us
  starting transfers between devices: 19.7 us -> 18.5 us
    unnamed x12 -> x13, local copies, waits for them, and re-layouts: 3.81 us -> 1.93 us
    ppermute x17 -> x11, waiting for transfers between devices: 13.7 us -> 12.3 us  [flipped(): lax.ppermute(x, axis, [(i, i ^ bits) for i in range(lax.axis_size(axis))])]
    ppermute x17 -> x11, starting transfers between devices: 19.7 us -> 18.5 us  [flipped(): lax.ppermute(x, axis, [(i, i ^ bits) for i in range(lax.axis_size(axis))])]
    pallas_call x4 -> x3, Pallas kernels: 3.63 us -> 3.37 us  [the longest x2 2.64 us: maps(): pl.pallas_call(functools.partial(maps_kernel, len(wholes), places), in_sp...]
  transfers between devices with their start and end apart: 17 -> 11, of which waited for: 8 -> 6; matrix products, arithmetic and copies ran while one was open for 0% -> 3% of each run, Pallas kernels for 8% -> 2%
where the time goes in v4:
time: 39.3 us; the launch traced here: 39.1 us
  starting transfers between devices  18.5 us (47%)
  waiting for transfers between devices  12.3 us (31%)
  Pallas kernels  4.54 us (12%)
  local copies, waits for them, and re-layouts  3 us (8%)
  between operations  0.72 us (2%)
    ppermute x11, starting transfers between devices, flipped(): lax.ppermute(x, axis, [(i, i ^ bits) for i in range(lax.axis_size(axis))])  18.5 us
    ppermute x11, waiting for transfers between devices, flipped(): lax.ppermute(x, axis, [(i, i ^ bits) for i in range(lax.axis_size(axis))])  12.3 us
    pallas_call x2, Pallas kernels, maps(): pl.pallas_call(functools.partial(maps_kernel, len(wholes), places), in_sp...  2.64 us
    unnamed x13, local copies, waits for them, and re-layouts  1.93 us
    pallas_call x1, Pallas kernels, shards(): pl.pallas_call(functools.partial(stats_kernel, len(keeps), 2 * side * sid...  1.17 us
    squeeze x1, local copies, waits for them, and re-layouts, shards(): rest = lax.dynamic_index_in_dim(template, 1 - plane, 0, keepdims=False)  1.04 us
  transfers between devices with their start and end apart: 11, of which 6 were waited for; matrix products, arithmetic and copies ran while one was open for 3% of the time, Pallas kernels for 2%

profile of v4, /device:TPU:0, one launch (start us, length us, event | category | flops | bytes accessed | tf_op | source)
XLA Modules:
  0.0 39.1 jit_solution(10640288065891691585)
XLA Ops:
  0.6 3.0 %collective-permute-start.2 = (f32[2,128,256]{2,1,0:T(8,128)}, f32[2,128,256]{2,1,0:T(8,128)S(1)}, u32[]{:S(2)}, u32[]{:S(2)}) collective-permute-start(f32[2,128,256]{2,1,0:T(8,128)} %bitcast.6), channel_id=1, source_target_pairs={{0,2},{2,0},{4,6},{6,4},{8,10},{10,8},{12,14},{14,12},{1,3},{3,1},... | collective-permute-start | bytes 786440 | tf_op jit(solution)/shard_map/ppermute | solution.py:138
  3.7 0.0 copy-start.1
  3.7 0.0 copy-start.2
  3.7 1.0 %dynamic-slice_bitcast_fusion = (f32[128,256]{1,0:T(8,128)S(1)}, f32[128,256]{1,0:T(8,128)S(1)}) fusion(f32[1,2,128,256]{3,2,1,0:T(8,128)} %param.7, s32[]{:T(128)S(6)} %select_n.8, s32[]{:T(128)S(6)} %select_n.7), kind=kLoop, calls=%fused_computation.2 | loop fusion | bytes 524296 | tf_op jit(solution)/shard_map/jit(dynamic_index_in_dim)/squeeze | solution.py:184
  4.7 2.7 %collective-permute-start.1 = (f32[128,256]{1,0:T(8,128)S(1)}, f32[128,256]{1,0:T(8,128)S(1)}, u32[]{:S(2)}, u32[]{:S(2)}) collective-permute-start(f32[128,256]{1,0:T(8,128)S(1)} %get-tuple-element.30), channel_id=1, source_target_pairs={{0,8},{2,10},{4,12},{6,14},{8,0},{10,2},{12,4},{14,6},{1,9},{3,11}... | collective-permute-start | bytes 393224 | tf_op jit(solution)/shard_map/ppermute | solution.py:138
  7.4 1.6 %collective-permute-start = (f32[128,256]{1,0:T(8,128)S(1)}, f32[128,256]{1,0:T(8,128)S(1)}, u32[]{:S(2)}, u32[]{:S(2)}) collective-permute-start(f32[128,256]{1,0:T(8,128)S(1)} %get-tuple-element.30), channel_id=1, source_target_pairs={{0,4},{2,6},{4,0},{6,2},{8,12},{10,14},{12,8},{14,10},{1,5},{3,7},... | collective-permute-start | bytes 393224 | tf_op jit(solution)/shard_map/ppermute | solution.py:138
  8.9 0.0 copy-done.1
  8.9 0.0 copy-done.2
  8.9 0.0 copy-start.3
  9.0 0.9 %copy-done.3 = f32[256,256]{1,0:T(8,128)S(1)} copy-done((f32[256,256]{1,0:T(8,128)S(1)}, f32[256,256]{1,0:T(8,128)}, u32[]{:S(2)}) %copy-start.3) | copy-done | bytes 262168
  9.9 0.0 copy-start.4
  9.9 0.9 %copy-done.4 = f32[256,256]{1,0:T(8,128)S(1)} copy-done((f32[256,256]{1,0:T(8,128)S(1)}, f32[256,256]{1,0:T(8,128)}, u32[]{:S(2)}) %copy-start.4) | copy-done | bytes 262168
  10.9 0.7 %prepare.1 = (f32[4,128,256]{2,1,0:T(8,128)S(1)}, bf16[2,256,256]{2,1,0:T(8,128)(2,1)S(1)}, bf16[2,256,256]{2,1,0:T(8,128)(2,1)S(1)}) custom-call(f32[2,128,256]{2,1,0:T(8,128)S(1)} %bitcast.8, f32[256,256]{1,0:T(8,128)S(1)} %copy-done.2, f32[256,256]{1,0:T(8,128)S(1)} %copy-done.4, f32[256,256]{1,0:T(8,128)S(1)} %copy-done.3), custom_call_target="tpu_custom_call" | custom-call | tf_op jit(solution)/shard_map/prepare/pallas_call | solution.py:151
  11.6 2.0 %collective-permute-done.1 = f32[128,256]{1,0:T(8,128)S(1)} collective-permute-done((f32[128,256]{1,0:T(8,128)S(1)}, f32[128,256]{1,0:T(8,128)S(1)}, u32[]{:S(2)}, u32[]{:S(2)}) %collective-permute-start.1) | collective-permute-done | bytes 131104 | tf_op jit(solution)/shard_map/ppermute | solution.py:138
  13.5 0.2 collective-permute-done
  13.8 0.0 collective-permute-done.2.refs_1_
  13.8 0.0 copy-start
  13.8 0.5 %collective-permute-start.5 = (f32[256,256]{1,0:T(8,128)S(1)}, f32[256,256]{1,0:T(8,128)S(1)}, u32[]{:S(2)}, u32[]{:S(2)}) collective-permute-start(f32[256,256]{1,0:T(8,128)S(1)} %constant_dynamic-update-slice_fusion.refs_2_), channel_id=1, source_target_pairs={{0,2},{2,0},{4,6},{6,4},{8,10},{10,8},{12,14},{14,12},{1,3},{3,1},... | collective-permute-start | bytes 786440 | tf_op jit(solution)/shard_map/ppermute | solution.py:138
  14.3 1.5 %collective-permute-start.4 = (f32[256,256]{1,0:T(8,128)S(1)}, f32[256,256]{1,0:T(8,128)S(1)}, u32[]{:S(2)}, u32[]{:S(2)}) collective-permute-start(f32[256,256]{1,0:T(8,128)S(1)} %constant_dynamic-update-slice_fusion.refs_2_), channel_id=1, source_target_pairs={{0,16},{16,0},{1,17},{17,1},{2,18},{18,2},{3,19},{19,3},{4,20},{20... | collective-permute-start | bytes 786440 | tf_op jit(solution)/shard_map/ppermute | solution.py:138
  15.9 3.2 %collective-permute-start.3 = (f32[128,256]{1,0:T(8,128)S(1)}, f32[128,256]{1,0:T(8,128)S(1)}, u32[]{:S(2)}, u32[]{:S(2)}) collective-permute-start(f32[128,256]{1,0:T(8,128)S(1)} %get-tuple-element.30), channel_id=1, source_target_pairs={{0,12},{2,14},{4,8},{6,10},{8,4},{10,6},{12,0},{14,2},{1,13},{3,15... | collective-permute-start | bytes 393224 | tf_op jit(solution)/shard_map/ppermute | solution.py:138
  19.0 3.6 %collective-permute-done.3.refs_3_ = f32[128,256]{1,0:T(8,128)S(1)} collective-permute-done((f32[128,256]{1,0:T(8,128)S(1)}, f32[128,256]{1,0:T(8,128)S(1)}, u32[]{:S(2)}, u32[]{:S(2)}) %collective-permute-start.3) | collective-permute-done | bytes 131104 | tf_op jit(solution)/shard_map/ppermute | solution.py:138
  22.7 0.0 collective-permute-done.5.refs_0_
  22.7 0.0 collective-permute-done.4.refs_3_
  22.7 0.0 copy-done
  22.7 1.3 %maps.2 = (f32[4,136,256]{2,1,0:T(8,128)S(1)}, f32[4,136,256]{2,1,0:T(8,128)S(1)}) custom-call(f32[4,128,256]{2,1,0:T(8,128)S(1)} %get-tuple-element.24.coef_ref, bf16[2,256,256]{2,1,0:T(8,128)(2,1)S(1)} %get-tuple-element.25.rt_ref, bf16[2,256,256]{2,1,0:T(8,128)(2,1)S(1)} %get-tuple-element.26.col_ref, f32[2,128,256]{2,1,0:T(8,128)S(1)} %bitcast.7, ...), custom_call_target="tpu_custom_call" | custom-call | tf_op jit(solution)/shard_map/maps/pallas_call | solution.py:164
  24.0 0.1 collective-permute-start.9
  24.2 0.6 %collective-permute-start.6 = (f32[320,256]{1,0:T(8,128)S(1)}, f32[320,256]{1,0:T(8,128)S(1)}, u32[]{:S(2)}, u32[]{:S(2)}) collective-permute-start(f32[320,256]{1,0:T(8,128)S(1)} %pad_maximum_fusion), channel_id=1, source_target_pairs={{0,16},{16,0},{1,17},{17,1},{2,18},{18,2},{3,19},{19,3},{4,20},{20... | collective-permute-start | bytes 983048 | tf_op jit(solution)/shard_map/ppermute | solution.py:138
  24.7 0.0 copy-start.5
  24.7 1.6 %collective-permute-start.7 = (f32[192,256]{1,0:T(8,128)S(1)}, f32[192,256]{1,0:T(8,128)S(1)}, u32[]{:S(2)}, u32[]{:S(2)}) collective-permute-start(f32[192,256]{1,0:T(8,128)S(1)} %pad_maximum_fusion.1), channel_id=1, source_target_pairs={{0,2},{2,0},{4,6},{6,4},{8,10},{10,8},{12,14},{14,12},{1,3},{3,1},... | collective-permute-start | bytes 589832 | tf_op jit(solution)/shard_map/ppermute | solution.py:138
  26.4 3.7 %collective-permute-start.8 = (f32[128,256]{1,0:T(8,128)S(1)}, f32[128,256]{1,0:T(8,128)S(1)}, u32[]{:S(2)}, u32[]{:S(2)}) collective-permute-start(f32[128,256]{1,0:T(8,128)S(1)} %get-tuple-element.35), channel_id=1, source_target_pairs={{0,14},{2,12},{4,10},{6,8},{8,6},{10,4},{12,2},{14,0},{1,15},{3,13... | collective-permute-start | bytes 393224 | tf_op jit(solution)/shard_map/ppermute | solution.py:138
  30.1 4.5 %collective-permute-done.8.refs_4_ = f32[128,256]{1,0:T(8,128)S(1)} collective-permute-done((f32[128,256]{1,0:T(8,128)S(1)}, f32[128,256]{1,0:T(8,128)S(1)}, u32[]{:S(2)}, u32[]{:S(2)}) %collective-permute-start.8) | collective-permute-done | bytes 131104 | tf_op jit(solution)/shard_map/ppermute | solution.py:138
  34.6 0.1 collective-permute-done.7.refs_2_
  34.6 0.0 collective-permute-done.6.refs_1_
  34.6 0.0 collective-permute-done.9.refs_2_
  34.6 1.3 %maps.3 = (f32[4,136,256]{2,1,0:T(8,128)S(1)}, f32[4,136,256]{2,1,0:T(8,128)S(1)}) custom-call(f32[4,128,256]{2,1,0:T(8,128)S(1)} %get-tuple-element.24.coef_ref, bf16[2,256,256]{2,1,0:T(8,128)(2,1)S(1)} %get-tuple-element.25.rt_ref, bf16[2,256,256]{2,1,0:T(8,128)(2,1)S(1)} %get-tuple-element.26.col_ref, f32[256,256]{1,0:T(8,128)S(1)} %collective-permute-done.5.refs_0_, ...), custom_call_target="tpu_custom_call" | custom-call | tf_op jit(solution)/shard_map/maps/pallas_call | solution.py:164
  36.0 0.1 collective-permute-start.10
  36.0 1.9 %collective-permute-done.10.refs_3_ = f32[4,136,256]{2,1,0:T(8,128)S(1)} collective-permute-done((f32[4,136,256]{2,1,0:T(8,128)S(1)}, f32[4,136,256]{2,1,0:T(8,128)S(1)}, u32[]{:S(2)}, u32[]{:S(2)}) %collective-permute-start.10) | collective-permute-done | bytes 557088 | tf_op jit(solution)/shard_map/ppermute | solution.py:138
  38.0 0.0 copy-done.5
  38.0 1.2 %statistics.1 = (f32[1,128,256]{2,1,0:T(8,128)}, f32[1,128,256]{2,1,0:T(8,128)}, f32[1,128,256]{2,1,0:T(8,128)}) custom-call(f32[4,136,256]{2,1,0:T(8,128)S(1)} %get-tuple-element.32.refs_0_, f32[4,136,256]{2,1,0:T(8,128)S(1)} %get-tuple-element.40.refs_1_, f32[4,136,256]{2,1,0:T(8,128)S(1)} %collective-permute-done.9.refs_2_, ...), custom_call_target="tpu_custom_call" | custom-call | tf_op jit(solution)/shard_map/statistics/pallas_call | solution.py:215
  (6 shorter events, 0.1 us)
Async XLA Ops:
  0.6 13.1 %collective-permute-start.2 = (f32[2,128,256]{2,1,0:T(8,128)}, f32[2,128,256]{2,1,0:T(8,128)S(1)}, u32[]{:S(2)}, u32[]{:S(2)}) collective-permute-start(f32[2,128,256]{2,1,0:T(8,128)} %bitcast.6), channel_id=1, source_target_pairs={{0,2},{2,0},{4,6},{6,4},{8,10},{10,8},{12,14},{14,12},{1,3},{3,1},... | collective-permute-start | bytes 786440 | tf_op jit(solution)/shard_map/ppermute | solution.py:138
  3.7 5.3 %copy-start.1 = (f32[1,2,128,256]{3,2,1,0:T(8,128)S(1)}, f32[1,2,128,256]{3,2,1,0:T(8,128)}, u32[]{:S(2)}) copy-start(f32[1,2,128,256]{3,2,1,0:T(8,128)} %param.6) | copy-start | bytes 786436
  3.7 5.3 %copy-start.2 = (f32[256,256]{1,0:T(8,128)S(1)}, f32[256,256]{1,0:T(8,128)}, u32[]{:S(2)}) copy-start(f32[256,256]{1,0:T(8,128)} %w_hbm.1) | copy-start | bytes 786436
  4.7 8.8 %collective-permute-start.1 = (f32[128,256]{1,0:T(8,128)S(1)}, f32[128,256]{1,0:T(8,128)S(1)}, u32[]{:S(2)}, u32[]{:S(2)}) collective-permute-start(f32[128,256]{1,0:T(8,128)S(1)} %get-tuple-element.30), channel_id=1, source_target_pairs={{0,8},{2,10},{4,12},{6,14},{8,0},{10,2},{12,4},{14,6},{1,9},{3,11}... | collective-permute-start | bytes 393224 | tf_op jit(solution)/shard_map/ppermute | solution.py:138
  7.4 6.4 %collective-permute-start = (f32[128,256]{1,0:T(8,128)S(1)}, f32[128,256]{1,0:T(8,128)S(1)}, u32[]{:S(2)}, u32[]{:S(2)}) collective-permute-start(f32[128,256]{1,0:T(8,128)S(1)} %get-tuple-element.30), channel_id=1, source_target_pairs={{0,4},{2,6},{4,0},{6,2},{8,12},{10,14},{12,8},{14,10},{1,5},{3,7},... | collective-permute-start | bytes 393224 | tf_op jit(solution)/shard_map/ppermute | solution.py:138
  8.9 1.0 %copy-start.3 = (f32[256,256]{1,0:T(8,128)S(1)}, f32[256,256]{1,0:T(8,128)}, u32[]{:S(2)}) copy-start(f32[256,256]{1,0:T(8,128)} %constant.27.clone.col_hbm) | copy-start | bytes 786436
  9.9 0.9 %copy-start.4 = (f32[256,256]{1,0:T(8,128)S(1)}, f32[256,256]{1,0:T(8,128)}, u32[]{:S(2)}) copy-start(f32[256,256]{1,0:T(8,128)} %constant.26.clone.row_hbm) | copy-start | bytes 786436
  13.8 8.9 %copy-start = (f32[1,2,128,256]{3,2,1,0:T(8,128)S(1)}, f32[1,2,128,256]{3,2,1,0:T(8,128)}, u32[]{:S(2)}) copy-start(f32[1,2,128,256]{3,2,1,0:T(8,128)} %param.7) | copy-start | bytes 786436
  13.8 8.9 %collective-permute-start.5 = (f32[256,256]{1,0:T(8,128)S(1)}, f32[256,256]{1,0:T(8,128)S(1)}, u32[]{:S(2)}, u32[]{:S(2)}) collective-permute-start(f32[256,256]{1,0:T(8,128)S(1)} %constant_dynamic-update-slice_fusion.refs_2_), channel_id=1, source_target_pairs={{0,2},{2,0},{4,6},{6,4},{8,10},{10,8},{12,14},{14,12},{1,3},{3,1},... | collective-permute-start | bytes 786440 | tf_op jit(solution)/shard_map/ppermute | solution.py:138
  14.3 8.4 %collective-permute-start.4 = (f32[256,256]{1,0:T(8,128)S(1)}, f32[256,256]{1,0:T(8,128)S(1)}, u32[]{:S(2)}, u32[]{:S(2)}) collective-permute-start(f32[256,256]{1,0:T(8,128)S(1)} %constant_dynamic-update-slice_fusion.refs_2_), channel_id=1, source_target_pairs={{0,16},{16,0},{1,17},{17,1},{2,18},{18,2},{3,19},{19,3},{4,20},{20... | collective-permute-start | bytes 786440 | tf_op jit(solution)/shard_map/ppermute | solution.py:138
  15.9 6.8 %collective-permute-start.3 = (f32[128,256]{1,0:T(8,128)S(1)}, f32[128,256]{1,0:T(8,128)S(1)}, u32[]{:S(2)}, u32[]{:S(2)}) collective-permute-start(f32[128,256]{1,0:T(8,128)S(1)} %get-tuple-element.30), channel_id=1, source_target_pairs={{0,12},{2,14},{4,8},{6,10},{8,4},{10,6},{12,0},{14,2},{1,13},{3,15... | collective-permute-start | bytes 393224 | tf_op jit(solution)/shard_map/ppermute | solution.py:138
  24.0 10.6 %collective-permute-start.9 = (f32[4,136,256]{2,1,0:T(8,128)S(1)}, f32[4,136,256]{2,1,0:T(8,128)S(1)}, u32[]{:S(2)}, u32[]{:S(2)}) collective-permute-start(f32[4,136,256]{2,1,0:T(8,128)S(1)} %get-tuple-element.36), channel_id=1, source_target_pairs={{0,1},{1,0},{2,3},{3,2},{4,5},{5,4},{6,7},{7,6},{8,9},{9,8},{10,11... | collective-permute-start | bytes 1671176 | tf_op jit(solution)/shard_map/ppermute | solution.py:138
  24.2 10.5 %collective-permute-start.6 = (f32[320,256]{1,0:T(8,128)S(1)}, f32[320,256]{1,0:T(8,128)S(1)}, u32[]{:S(2)}, u32[]{:S(2)}) collective-permute-start(f32[320,256]{1,0:T(8,128)S(1)} %pad_maximum_fusion), channel_id=1, source_target_pairs={{0,16},{16,0},{1,17},{17,1},{2,18},{18,2},{3,19},{19,3},{4,20},{20... | collective-permute-start | bytes 983048 | tf_op jit(solution)/shard_map/ppermute | solution.py:138
  24.7 13.3 %copy-start.5 = (f32[128,128]{1,0:T(8,128)S(1)}, f32[128,128]{1,0:T(8,128)}, u32[]{:S(2)}) copy-start(f32[128,128]{1,0:T(8,128)} %constant.28.clone.refs_4_) | copy-start | bytes 196612
  24.7 9.9 %collective-permute-start.7 = (f32[192,256]{1,0:T(8,128)S(1)}, f32[192,256]{1,0:T(8,128)S(1)}, u32[]{:S(2)}, u32[]{:S(2)}) collective-permute-start(f32[192,256]{1,0:T(8,128)S(1)} %pad_maximum_fusion.1), channel_id=1, source_target_pairs={{0,2},{2,0},{4,6},{6,4},{8,10},{10,8},{12,14},{14,12},{1,3},{3,1},... | collective-permute-start | bytes 589832 | tf_op jit(solution)/shard_map/ppermute | solution.py:138
  26.4 8.2 %collective-permute-start.8 = (f32[128,256]{1,0:T(8,128)S(1)}, f32[128,256]{1,0:T(8,128)S(1)}, u32[]{:S(2)}, u32[]{:S(2)}) collective-permute-start(f32[128,256]{1,0:T(8,128)S(1)} %get-tuple-element.35), channel_id=1, source_target_pairs={{0,14},{2,12},{4,10},{6,8},{8,6},{10,4},{12,2},{14,0},{1,15},{3,13... | collective-permute-start | bytes 393224 | tf_op jit(solution)/shard_map/ppermute | solution.py:138
  36.0 2.0 %collective-permute-start.10 = (f32[4,136,256]{2,1,0:T(8,128)S(1)}, f32[4,136,256]{2,1,0:T(8,128)S(1)}, u32[]{:S(2)}, u32[]{:S(2)}) collective-permute-start(f32[4,136,256]{2,1,0:T(8,128)S(1)} %get-tuple-element.42), channel_id=1, source_target_pairs={{0,1},{1,0},{2,3},{3,2},{4,5},{5,4},{6,7},{7,6},{8,9},{9,8},{10,11... | collective-permute-start | bytes 1671176 | tf_op jit(solution)/shard_map/ppermute | solution.py:138

commit v5 on v4

--- a/solution.py
+++ b/solution.py
@@ -75,7 +75,7 @@
     half, side = a.shape
     mid = side // 2
     squares = jnp.sum((a * a + b * b).reshape(half // 8, 8, side), axis=0)
-    power = jnp.broadcast_to(jnp.sum(squares), (8, side))
+    power = jnp.broadcast_to(jnp.sum(squares), (keep_ref.shape[1] - half, side))
     z = jnp.concatenate([coef_ref[0] * a + coef_ref[1] * b, coef_ref[3] * a - coef_ref[2] * b], 0)
     zh, zl = parts(z)
     ch, cl = col_ref[0], col_ref[1]
@@ -108,8 +108,7 @@
 def stats_kernel(calls, entries, *refs):
     keeps, recvs = refs[:calls], refs[calls:2 * calls]
     fold_ref, peak_ref, mean_ref, square_ref, flip_ref = refs[2 * calls:]
-    side = keeps[0].shape[2]
-    half = keeps[0].shape[1] - 8
+    half, side = peak_ref.shape[1:]
     mid = side // 2
     pairs = [(keep, recv, n) for keep, recv in zip(keeps, recvs) for n in range(keep.shape[0])]
     count = len(pairs)
@@ -117,7 +116,7 @@
         rows = pl.ds(block * 8, 8)
         best = total = squares = None
         for keep, recv, n in pairs:
-            power = (keep[n, half:] + recv[n, half:]) * (1.0 / entries)
+            power = (keep[n, half:half + 8] + recv[n, half:half + 8]) * (1.0 / entries)
             scale = lax.rsqrt(power + 1e-6) * (1.0 / side)
             c = (keep[n, rows] + recv[n, rows]) * scale
             if best is None:
@@ -160,32 +159,30 @@
         name="prepare",
     )(spectra[0], weights, jnp.asarray(row_table(side, half)), jnp.asarray(column_table(side)))
 
-    def maps(wholes, arrays=(), places=()):
+    def maps(wholes, arrays=(), places=(), extra=8):
         return pl.pallas_call(
             functools.partial(maps_kernel, len(wholes), places),
             in_specs=[vmem] * (3 + len(wholes) + len(arrays)),
             out_specs=[vmem] * 2,
-            out_shape=[shape(len(wholes) + len(places), half + 8, side)] * 2,
+            out_shape=[shape(len(wholes) + len(places), half + extra, side)] * 2,
             compiler_params=params,
             name="maps",
         )(coef, table, columns, *wholes, *arrays)
 
     if lax.axis_size("groups") == 2 and orients == 8:
-        plane = lax.axis_index("groups")
         cut = half // 2
-        part = lax.dynamic_index_in_dim(template, plane, 0, keepdims=False)
+        part = lax.dynamic_index_in_dim(template, lax.axis_index("groups"), 0, keepdims=False)
         near1, near2 = (flipped(part, "orient", 2 * k) for k in (1, 2))
-        beside = flipped(template, "orient", 1)
-        near1, near2, beside, part, coef = lax.optimization_barrier((near1, near2, beside, part, coef))
+        beside = flipped(lax.optimization_barrier((template, part))[0], "orient", 1)
+        near1, near2, beside, coef = lax.optimization_barrier((near1, near2, beside, coef))
         near = jnp.concatenate([near1, near2], 0)
-        far = flipped(part, "orient", 6)
+        far = flipped(near2, "orient", 2)
         near_x = flipped(near, "groups", 1)
         near_y = flipped(near, "orient", 1)
-        rest = lax.dynamic_index_in_dim(template, 1 - plane, 0, keepdims=False)
-        far, near_x, near_y, rest = lax.optimization_barrier((far, near_x, near_y, rest))
+        far, near_x, near_y = lax.optimization_barrier((far, near_x, near_y))
         last_x = flipped(jnp.concatenate([far, near_y[:half + cut]], 0), "groups", 1)
         last_y = flipped(jnp.concatenate([far, near_x[half + cut:]], 0), "orient", 1)
-        corner = flipped(rest, "orient", 7)
+        corner = flipped(near_x[half:], "orient", 3)
         early = maps(
             [template, beside],
             [near, near_x],
@@ -193,9 +190,9 @@
                 (((0, 0, half),), ((1, 0, half),)),
                 (((0, half, side),), ((1, half, side),)),
             ),
+            16,
         )
-        early_recv = flipped(early[1], "tile", 1)
-        last_x, last_y, corner, early_recv = lax.optimization_barrier((last_x, last_y, corner, early_recv))
+        last_x, last_y, corner, early = lax.optimization_barrier((last_x, last_y, corner, early))
         late = maps(
             [],
             [near_y, last_x, last_y, far, corner],
@@ -206,12 +203,12 @@
                 (((2, 0, half),), ((4, 0, half),)),
             ),
         )
-        keeps, recvs = [early[0], late[0]], [early_recv, flipped(late[1], "tile", 1)]
+        calls = [early, late]
     else:
         rest = [template] + [flipped(template, "orient", k) for k in range(1, orients)]
         calls = [maps(rest[i:i + 4]) for i in range(0, len(rest), 4)]
-        keeps = [keep for keep, _ in calls]
-        recvs = [flipped(send, "tile", 1) for _, send in calls]
+    keeps = [keep for keep, _ in calls]
+    recvs = [flipped(send, "tile", 1) for _, send in calls]
     return tuple(pl.pallas_call(
         functools.partial(stats_kernel, len(keeps), 2 * side * side),
         in_specs=[vmem] * (2 * len(keeps) + 1),

time: 39.3 us -> 35.8 us (0.911)
  the two profiles are of different devices: /device:TPU:0 before, /device:TPU:25 now
where the time goes in v5:
time: 35.8 us; the launch traced here: 35.5 us
  waiting for transfers between devices  15.9 us (44%)
  starting transfers between devices  9.45 us (26%)
  local copies, waits for them, and re-layouts  4.85 us (14%)
  Pallas kernels  4.55 us (13%)
  between operations  0.72 us (2%)
    ppermute x11, waiting for transfers between devices, flipped(): lax.ppermute(x, axis, [(i, i ^ bits) for i in range(lax.axis_size(axis))])  15.9 us
    ppermute x11, starting transfers between devices, flipped(): lax.ppermute(x, axis, [(i, i ^ bits) for i in range(lax.axis_size(axis))])  9.45 us
    unnamed x13, local copies, waits for them, and re-layouts  3.84 us
    pallas_call x2, Pallas kernels, maps(): pl.pallas_call(functools.partial(maps_kernel, len(wholes), places), in_sp...  2.64 us
    pallas_call x1, Pallas kernels, shards(): pl.pallas_call(functools.partial(stats_kernel, len(keeps), 2 * side * sid...  1.18 us
    squeeze x1, local copies, waits for them, and re-layouts, shards(): lax.dynamic_index_in_dim(template, lax.axis_index('groups'), 0, keepdims=...  0.97 us
    pallas_call x1, Pallas kernels, shards(): pl.pallas_call(prepare_kernel, in_specs=[hbm] * 4, out_specs=[vmem] * 3,...  0.73 us
  transfers between devices with their start and end apart: 11, of which 6 were waited for; matrix products, arithmetic and copies ran while one was open for 0% of the time, Pallas kernels for 9%

profile of v5, /device:TPU:25, one launch (start us, length us, event | category | flops | bytes accessed | tf_op | source)
XLA Modules:
  0.0 35.5 jit_solution(10132180603746347178)
XLA Ops:
  0.6 0.0 copy-start
  0.6 1.0 %dynamic-slice_bitcast_fusion = f32[128,256]{1,0:T(8,128)S(1)} fusion(f32[1,2,128,256]{3,2,1,0:T(8,128)} %param.7, s32[]{:T(128)S(6)} %select_n.4), kind=kLoop, calls=%fused_computation.2 | loop fusion | bytes 262148 | tf_op jit(solution)/shard_map/jit(dynamic_index_in_dim)/squeeze | solution.py:174
  1.6 0.0 copy-done
  1.6 1.3 %collective-permute-start.2 = (f32[2,128,256]{2,1,0:T(8,128)S(1)}, f32[2,128,256]{2,1,0:T(8,128)S(1)}, u32[]{:S(2)}, u32[]{:S(2)}) collective-permute-start(f32[2,128,256]{2,1,0:T(8,128)S(1)} %bitcast.4), channel_id=1, source_target_pairs={{0,2},{2,0},{4,6},{6,4},{8,10},{10,8},{12,14},{14,12},{1,3},{3,1},... | collective-permute-start | bytes 786440 | tf_op jit(solution)/shard_map/ppermute | solution.py:137
  2.9 0.1 collective-permute-start.1
  3.0 0.2 collective-permute-start
  3.2 0.0 copy-start.1
  3.2 0.9 %copy-done.1 = f32[1,2,128,256]{3,2,1,0:T(8,128)S(1)} copy-done((f32[1,2,128,256]{3,2,1,0:T(8,128)S(1)}, f32[1,2,128,256]{3,2,1,0:T(8,128)}, u32[]{:S(2)}) %copy-start.1) | copy-done | bytes 262168
  4.1 0.0 copy-start.2
  4.1 0.9 %copy-done.2 = f32[256,256]{1,0:T(8,128)S(1)} copy-done((f32[256,256]{1,0:T(8,128)S(1)}, f32[256,256]{1,0:T(8,128)}, u32[]{:S(2)}) %copy-start.2) | copy-done | bytes 262168
  5.1 0.0 copy-start.3
  5.1 0.9 %copy-done.3 = f32[256,256]{1,0:T(8,128)S(1)} copy-done((f32[256,256]{1,0:T(8,128)S(1)}, f32[256,256]{1,0:T(8,128)}, u32[]{:S(2)}) %copy-start.3) | copy-done | bytes 262168
  6.0 0.0 copy-start.4
  6.0 0.9 %copy-done.4 = f32[256,256]{1,0:T(8,128)S(1)} copy-done((f32[256,256]{1,0:T(8,128)S(1)}, f32[256,256]{1,0:T(8,128)}, u32[]{:S(2)}) %copy-start.4) | copy-done | bytes 262168
  7.0 0.7 %prepare.1 = (f32[4,128,256]{2,1,0:T(8,128)S(1)}, bf16[2,256,256]{2,1,0:T(8,128)(2,1)S(1)}, bf16[2,256,256]{2,1,0:T(8,128)(2,1)S(1)}) custom-call(f32[2,128,256]{2,1,0:T(8,128)S(1)} %bitcast.6, f32[256,256]{1,0:T(8,128)S(1)} %copy-done.2, f32[256,256]{1,0:T(8,128)S(1)} %copy-done.4, f32[256,256]{1,0:T(8,128)S(1)} %copy-done.3), custom_call_target="tpu_custom_call" | custom-call | tf_op jit(solution)/shard_map/prepare/pallas_call | solution.py:150
  7.7 4.2 %collective-permute-done.1 = f32[128,256]{1,0:T(8,128)S(1)} collective-permute-done((f32[128,256]{1,0:T(8,128)S(1)}, f32[128,256]{1,0:T(8,128)S(1)}, u32[]{:S(2)}, u32[]{:S(2)}) %collective-permute-start.1) | collective-permute-done | bytes 131104 | tf_op jit(solution)/shard_map/ppermute | solution.py:137
  11.9 0.0 collective-permute-done
  12.0 0.0 collective-permute-done.2.refs_1_
  12.0 0.3 collective-permute-start.5
  12.3 1.2 %collective-permute-start.4 = (f32[256,256]{1,0:T(8,128)S(1)}, f32[256,256]{1,0:T(8,128)S(1)}, u32[]{:S(2)}, u32[]{:S(2)}) collective-permute-start(f32[256,256]{1,0:T(8,128)S(1)} %constant_dynamic-update-slice_fusion.refs_2_), channel_id=1, source_target_pairs={{0,16},{16,0},{1,17},{17,1},{2,18},{18,2},{3,19},{19,3},{4,20},{20... | collective-permute-start | bytes 786440 | tf_op jit(solution)/shard_map/ppermute | solution.py:137
  13.5 0.0 collective-permute-start.3
  13.5 4.1 %collective-permute-done.3.refs_3_ = f32[128,256]{1,0:T(8,128)S(1)} collective-permute-done((f32[128,256]{1,0:T(8,128)S(1)}, f32[128,256]{1,0:T(8,128)S(1)}, u32[]{:S(2)}, u32[]{:S(2)}) %collective-permute-start.3) | collective-permute-done | bytes 131104 | tf_op jit(solution)/shard_map/ppermute | solution.py:137
  17.6 1.8 %collective-permute-done.5.refs_0_ = f32[256,256]{1,0:T(8,128)S(1)} collective-permute-done((f32[256,256]{1,0:T(8,128)S(1)}, f32[256,256]{1,0:T(8,128)S(1)}, u32[]{:S(2)}, u32[]{:S(2)}) %collective-permute-start.5) | collective-permute-done | bytes 262176 | tf_op jit(solution)/shard_map/ppermute | solution.py:137
  19.4 0.0 collective-permute-done.4.refs_3_
  19.5 1.3 %collective-permute-start.6 = (f32[320,256]{1,0:T(8,128)S(1)}, f32[320,256]{1,0:T(8,128)S(1)}, u32[]{:S(2)}, u32[]{:S(2)}) collective-permute-start(f32[320,256]{1,0:T(8,128)S(1)} %pad_maximum_fusion), channel_id=1, source_target_pairs={{0,16},{16,0},{1,17},{17,1},{2,18},{18,2},{3,19},{19,3},{4,20},{20... | collective-permute-start | bytes 983048 | tf_op jit(solution)/shard_map/ppermute | solution.py:137
  20.8 1.2 %collective-permute-start.7 = (f32[192,256]{1,0:T(8,128)S(1)}, f32[192,256]{1,0:T(8,128)S(1)}, u32[]{:S(2)}, u32[]{:S(2)}) collective-permute-start(f32[192,256]{1,0:T(8,128)S(1)} %pad_maximum_fusion.1), channel_id=1, source_target_pairs={{0,2},{2,0},{4,6},{6,4},{8,10},{10,8},{12,14},{14,12},{1,3},{3,1},... | collective-permute-start | bytes 589832 | tf_op jit(solution)/shard_map/ppermute | solution.py:137
  22.0 0.1 collective-permute-start.8
  22.1 1.3 %maps.2 = (f32[4,144,256]{2,1,0:T(8,128)S(1)}, f32[4,144,256]{2,1,0:T(8,128)S(1)}) custom-call(f32[4,128,256]{2,1,0:T(8,128)S(1)} %get-tuple-element.30.coef_ref, bf16[2,256,256]{2,1,0:T(8,128)(2,1)S(1)} %get-tuple-element.31.rt_ref, bf16[2,256,256]{2,1,0:T(8,128)(2,1)S(1)} %get-tuple-element.32.col_ref, f32[2,128,256]{2,1,0:T(8,128)S(1)} %bitcast.5, ...), custom_call_target="tpu_custom_call" | custom-call | tf_op jit(solution)/shard_map/maps/pallas_call | solution.py:163
  23.4 3.5 %collective-permute-done.8.refs_4_ = f32[128,256]{1,0:T(8,128)S(1)} collective-permute-done((f32[128,256]{1,0:T(8,128)S(1)}, f32[128,256]{1,0:T(8,128)S(1)}, u32[]{:S(2)}, u32[]{:S(2)}) %collective-permute-start.8) | collective-permute-done | bytes 131104 | tf_op jit(solution)/shard_map/ppermute | solution.py:137
  26.9 0.0 collective-permute-done.7.refs_2_
  26.9 0.3 collective-permute-done.6.refs_1_
  27.2 0.0 copy-start.5
  27.2 3.8 %collective-permute-start.9 = (f32[4,144,256]{2,1,0:T(8,128)S(1)}, f32[4,144,256]{2,1,0:T(8,128)S(1)}, u32[]{:S(2)}, u32[]{:S(2)}) collective-permute-start(f32[4,144,256]{2,1,0:T(8,128)S(1)} %get-tuple-element.41), channel_id=1, source_target_pairs={{0,1},{1,0},{2,3},{3,2},{4,5},{5,4},{6,7},{7,6},{8,9},{9,8},{10,11... | collective-permute-start | bytes 1769480 | tf_op jit(solution)/shard_map/ppermute | solution.py:137
  31.0 1.3 %maps.3 = (f32[4,136,256]{2,1,0:T(8,128)S(1)}, f32[4,136,256]{2,1,0:T(8,128)S(1)}) custom-call(f32[4,128,256]{2,1,0:T(8,128)S(1)} %get-tuple-element.30.coef_ref, bf16[2,256,256]{2,1,0:T(8,128)(2,1)S(1)} %get-tuple-element.31.rt_ref, bf16[2,256,256]{2,1,0:T(8,128)(2,1)S(1)} %get-tuple-element.32.col_ref, f32[256,256]{1,0:T(8,128)S(1)} %collective-permute-done.5.refs_0_, ...), custom_call_target="tpu_custom_call" | custom-call | tf_op jit(solution)/shard_map/maps/pallas_call | solution.py:163
  32.3 0.1 collective-permute-start.10
  32.4 1.9 %collective-permute-done.10.refs_3_ = f32[4,136,256]{2,1,0:T(8,128)S(1)} collective-permute-done((f32[4,136,256]{2,1,0:T(8,128)S(1)}, f32[4,136,256]{2,1,0:T(8,128)S(1)}, u32[]{:S(2)}, u32[]{:S(2)}) %collective-permute-start.10) | collective-permute-done | bytes 557088 | tf_op jit(solution)/shard_map/ppermute | solution.py:137
  34.3 0.0 collective-permute-done.9.refs_2_
  34.3 0.0 copy-done.5
  34.3 1.2 %statistics.1 = (f32[1,128,256]{2,1,0:T(8,128)}, f32[1,128,256]{2,1,0:T(8,128)}, f32[1,128,256]{2,1,0:T(8,128)}) custom-call(f32[4,144,256]{2,1,0:T(8,128)S(1)} %get-tuple-element.36.refs_0_, f32[4,136,256]{2,1,0:T(8,128)S(1)} %get-tuple-element.40.refs_1_, f32[4,144,256]{2,1,0:T(8,128)S(1)} %collective-permute-done.9.refs_2_, ...), custom_call_target="tpu_custom_call" | custom-call | tf_op jit(solution)/shard_map/statistics/pallas_call | solution.py:212
  (7 shorter events, 0.1 us)
Async XLA Ops:
  0.6 1.0 %copy-start = (f32[1,2,128,256]{3,2,1,0:T(8,128)S(1)}, f32[1,2,128,256]{3,2,1,0:T(8,128)}, u32[]{:S(2)}) copy-start(f32[1,2,128,256]{3,2,1,0:T(8,128)} %param.7) | copy-start | bytes 786436
  1.6 10.3 %collective-permute-start.2 = (f32[2,128,256]{2,1,0:T(8,128)S(1)}, f32[2,128,256]{2,1,0:T(8,128)S(1)}, u32[]{:S(2)}, u32[]{:S(2)}) collective-permute-start(f32[2,128,256]{2,1,0:T(8,128)S(1)} %bitcast.4), channel_id=1, source_target_pairs={{0,2},{2,0},{4,6},{6,4},{8,10},{10,8},{12,14},{14,12},{1,3},{3,1},... | collective-permute-start | bytes 786440 | tf_op jit(solution)/shard_map/ppermute | solution.py:137
  2.9 9.0 %collective-permute-start.1 = (f32[128,256]{1,0:T(8,128)S(1)}, f32[128,256]{1,0:T(8,128)S(1)}, u32[]{:S(2)}, u32[]{:S(2)}) collective-permute-start(f32[128,256]{1,0:T(8,128)S(1)} %dynamic-slice_bitcast_fusion), channel_id=1, source_target_pairs={{0,8},{2,10},{4,12},{6,14},{8,0},{10,2},{12,4},{14,6},{1,9},{3,11}... | collective-permute-start | bytes 393224 | tf_op jit(solution)/shard_map/ppermute | solution.py:137
  3.0 9.0 %collective-permute-start = (f32[128,256]{1,0:T(8,128)S(1)}, f32[128,256]{1,0:T(8,128)S(1)}, u32[]{:S(2)}, u32[]{:S(2)}) collective-permute-start(f32[128,256]{1,0:T(8,128)S(1)} %dynamic-slice_bitcast_fusion), channel_id=1, source_target_pairs={{0,4},{2,6},{4,0},{6,2},{8,12},{10,14},{12,8},{14,10},{1,5},{3,7},... | collective-permute-start | bytes 393224 | tf_op jit(solution)/shard_map/ppermute | solution.py:137
  3.2 0.9 %copy-start.1 = (f32[1,2,128,256]{3,2,1,0:T(8,128)S(1)}, f32[1,2,128,256]{3,2,1,0:T(8,128)}, u32[]{:S(2)}) copy-start(f32[1,2,128,256]{3,2,1,0:T(8,128)} %param.6) | copy-start | bytes 786436
  4.1 0.9 %copy-start.2 = (f32[256,256]{1,0:T(8,128)S(1)}, f32[256,256]{1,0:T(8,128)}, u32[]{:S(2)}) copy-start(f32[256,256]{1,0:T(8,128)} %w_hbm.1) | copy-start | bytes 786436
  5.1 0.9 %copy-start.3 = (f32[256,256]{1,0:T(8,128)S(1)}, f32[256,256]{1,0:T(8,128)}, u32[]{:S(2)}) copy-start(f32[256,256]{1,0:T(8,128)} %constant.20.clone.col_hbm) | copy-start | bytes 786436
  6.0 0.9 %copy-start.4 = (f32[256,256]{1,0:T(8,128)S(1)}, f32[256,256]{1,0:T(8,128)}, u32[]{:S(2)}) copy-start(f32[256,256]{1,0:T(8,128)} %constant.19.clone.row_hbm) | copy-start | bytes 786436
  12.0 7.4 %collective-permute-start.5 = (f32[256,256]{1,0:T(8,128)S(1)}, f32[256,256]{1,0:T(8,128)S(1)}, u32[]{:S(2)}, u32[]{:S(2)}) collective-permute-start(f32[256,256]{1,0:T(8,128)S(1)} %constant_dynamic-update-slice_fusion.refs_2_), channel_id=1, source_target_pairs={{0,2},{2,0},{4,6},{6,4},{8,10},{10,8},{12,14},{14,12},{1,3},{3,1},... | collective-permute-start | bytes 786440 | tf_op jit(solution)/shard_map/ppermute | solution.py:137
  12.3 7.2 %collective-permute-start.4 = (f32[256,256]{1,0:T(8,128)S(1)}, f32[256,256]{1,0:T(8,128)S(1)}, u32[]{:S(2)}, u32[]{:S(2)}) collective-permute-start(f32[256,256]{1,0:T(8,128)S(1)} %constant_dynamic-update-slice_fusion.refs_2_), channel_id=1, source_target_pairs={{0,16},{16,0},{1,17},{17,1},{2,18},{18,2},{3,19},{19,3},{4,20},{20... | collective-permute-start | bytes 786440 | tf_op jit(solution)/shard_map/ppermute | solution.py:137
  13.5 4.1 %collective-permute-start.3 = (f32[128,256]{1,0:T(8,128)S(1)}, f32[128,256]{1,0:T(8,128)S(1)}, u32[]{:S(2)}, u32[]{:S(2)}) collective-permute-start(f32[128,256]{1,0:T(8,128)S(1)} %collective-permute-done.1), channel_id=1, source_target_pairs={{0,4},{2,6},{4,0},{6,2},{8,12},{10,14},{12,8},{14,10},{1,5},{3,7},... | collective-permute-start | bytes 393224 | tf_op jit(solution)/shard_map/ppermute | solution.py:137
  19.5 7.7 %collective-permute-start.6 = (f32[320,256]{1,0:T(8,128)S(1)}, f32[320,256]{1,0:T(8,128)S(1)}, u32[]{:S(2)}, u32[]{:S(2)}) collective-permute-start(f32[320,256]{1,0:T(8,128)S(1)} %pad_maximum_fusion), channel_id=1, source_target_pairs={{0,16},{16,0},{1,17},{17,1},{2,18},{18,2},{3,19},{19,3},{4,20},{20... | collective-permute-start | bytes 983048 | tf_op jit(solution)/shard_map/ppermute | solution.py:137
  20.8 6.1 %collective-permute-start.7 = (f32[192,256]{1,0:T(8,128)S(1)}, f32[192,256]{1,0:T(8,128)S(1)}, u32[]{:S(2)}, u32[]{:S(2)}) collective-permute-start(f32[192,256]{1,0:T(8,128)S(1)} %pad_maximum_fusion.1), channel_id=1, source_target_pairs={{0,2},{2,0},{4,6},{6,4},{8,10},{10,8},{12,14},{14,12},{1,3},{3,1},... | collective-permute-start | bytes 589832 | tf_op jit(solution)/shard_map/ppermute | solution.py:137
  22.0 4.9 %collective-permute-start.8 = (f32[128,256]{1,0:T(8,128)S(1)}, f32[128,256]{1,0:T(8,128)S(1)}, u32[]{:S(2)}, u32[]{:S(2)}) collective-permute-start(f32[128,256]{1,0:T(8,128)S(1)} %slice.11), channel_id=1, source_target_pairs={{0,6},{2,4},{4,2},{6,0},{8,14},{10,12},{12,10},{14,8},{1,7},{3,5},... | collective-permute-start | bytes 393224 | tf_op jit(solution)/shard_map/ppermute | solution.py:137
  27.2 7.1 %copy-start.5 = (f32[128,128]{1,0:T(8,128)S(1)}, f32[128,128]{1,0:T(8,128)}, u32[]{:S(2)}) copy-start(f32[128,128]{1,0:T(8,128)} %constant.21.clone.refs_4_) | copy-start | bytes 196612
  27.2 7.1 %collective-permute-start.9 = (f32[4,144,256]{2,1,0:T(8,128)S(1)}, f32[4,144,256]{2,1,0:T(8,128)S(1)}, u32[]{:S(2)}, u32[]{:S(2)}) collective-permute-start(f32[4,144,256]{2,1,0:T(8,128)S(1)} %get-tuple-element.41), channel_id=1, source_target_pairs={{0,1},{1,0},{2,3},{3,2},{4,5},{5,4},{6,7},{7,6},{8,9},{9,8},{10,11... | collective-permute-start | bytes 1769480 | tf_op jit(solution)/shard_map/ppermute | solution.py:137
  32.3 2.0 %collective-permute-start.10 = (f32[4,136,256]{2,1,0:T(8,128)S(1)}, f32[4,136,256]{2,1,0:T(8,128)S(1)}, u32[]{:S(2)}, u32[]{:S(2)}) collective-permute-start(f32[4,136,256]{2,1,0:T(8,128)S(1)} %get-tuple-element.42), channel_id=1, source_target_pairs={{0,1},{1,0},{2,3},{3,2},{4,5},{5,4},{6,7},{7,6},{8,9},{9,8},{10,11... | collective-permute-start | bytes 1671176 | tf_op jit(solution)/shard_map/ppermute | solution.py:137

commit v6 on v5

--- a/solution.py
+++ b/solution.py
@@ -100,9 +100,15 @@
     swap = lax.axis_index("groups") % 2
     for n, ref in enumerate(whole_refs):
         correlate(ref[swap], ref[1 - swap], coef_ref, col_ref, rt_ref, keep_ref, send_ref, n)
-    for n, pair in enumerate(places):
-        a, b = (jnp.concatenate([part_refs[array][start:stop] for array, start, stop in piece], 0) for piece in pair)
-        correlate(a, b, coef_ref, col_ref, rt_ref, keep_ref, send_ref, wholes + n)
+    half = coef_ref.shape[1]
+    first_core = lax.axis_index("tile") == 0
+
+    def read(even, odd, row):
+        here = part_refs[even][row:row + half]
+        return here if even == odd else jnp.where(first_core, here, part_refs[odd][row:row + half])
+
+    for n, (a, b) in enumerate(places):
+        correlate(read(*a), read(*b), coef_ref, col_ref, rt_ref, keep_ref, send_ref, wholes + n)
 
 
 def stats_kernel(calls, entries, *refs):
@@ -137,6 +143,17 @@
     return lax.ppermute(x, axis, [(i, i ^ bits) for i in range(lax.axis_size(axis))])
 
 
+def crossed(x, even, odd):
+    groups, orients, cores = (lax.axis_size(axis) for axis in ("groups", "orient", "tile"))
+    pairs = []
+    for g in range(groups):
+        for o in range(orients):
+            for c in range(cores):
+                group_bits, orient_bits = odd if c else even
+                pairs.append(((g * orients + o) * cores + c, ((g ^ group_bits) * orients + (o ^ orient_bits)) * cores + c))
+    return lax.ppermute(x, ("groups", "orient", "tile"), pairs)
+
+
 def shards(spectra, templates, weights):
     half, side = spectra.shape[2:]
     orients = lax.axis_size("orient")
@@ -170,37 +187,38 @@
         )(coef, table, columns, *wholes, *arrays)
 
     if lax.axis_size("groups") == 2 and orients == 8:
-        cut = half // 2
+        core = lax.axis_index("tile")
         part = lax.dynamic_index_in_dim(template, lax.axis_index("groups"), 0, keepdims=False)
         near1, near2 = (flipped(part, "orient", 2 * k) for k in (1, 2))
         beside = flipped(lax.optimization_barrier((template, part))[0], "orient", 1)
-        near1, near2, beside, coef = lax.optimization_barrier((near1, near2, beside, coef))
+        near1, near2, beside = lax.optimization_barrier((near1, near2, beside))
         near = jnp.concatenate([near1, near2], 0)
         far = flipped(near2, "orient", 2)
-        near_x = flipped(near, "groups", 1)
-        near_y = flipped(near, "orient", 1)
-        far, near_x, near_y = lax.optimization_barrier((far, near_x, near_y))
-        last_x = flipped(jnp.concatenate([far, near_y[:half + cut]], 0), "groups", 1)
-        last_y = flipped(jnp.concatenate([far, near_x[half + cut:]], 0), "orient", 1)
-        corner = flipped(near_x[half:], "orient", 3)
+        near_b = crossed(near, (0, 1), (1, 0))
+        near_a = crossed(near, (1, 0), (0, 1))
+        far, near_a, near_b, coef = lax.optimization_barrier((far, near_a, near_b, coef))
+        rows = lambda x, n: lax.dynamic_slice_in_dim(x, n * half, half)
+        corner = crossed(near_a[half:], (0, 3), (1, 2))
+        last_b = crossed(jnp.concatenate([far, rows(near_a, 1 - core)], 0), (0, 1), (1, 0))
+        last_a = crossed(jnp.concatenate([far, rows(near_b, core)], 0), (1, 0), (0, 1))
         early = maps(
             [template, beside],
-            [near, near_x],
+            [near, near_a, near_b],
             (
-                (((0, 0, half),), ((1, 0, half),)),
-                (((0, half, side),), ((1, half, side),)),
+                ((0, 0, 0), (1, 2, 0)),
+                ((0, 0, half), (1, 2, half)),
             ),
             16,
         )
-        last_x, last_y, corner, early = lax.optimization_barrier((last_x, last_y, corner, early))
+        last_a, last_b, corner, early = lax.optimization_barrier((last_a, last_b, corner, early))
         late = maps(
             [],
-            [near_y, last_x, last_y, far, corner],
+            [near_a, near_b, last_a, last_b, far, corner],
             (
-                (((0, 0, half),), ((1, half, side),)),
-                (((0, half, side),), ((1, side, side + cut), (2, half, half + cut))),
-                (((3, 0, half),), ((1, 0, half),)),
-                (((2, 0, half),), ((4, 0, half),)),
+                ((1, 0, 0), (2, 3, half)),
+                ((1, 0, half), (3, 2, half)),
+                ((4, 4, 0), (2, 3, 0)),
+                ((3, 2, 0), (5, 5, 0)),
             ),
         )
         calls = [early, late]

time: 35.8 us -> 36.4 us (1.017)
  the two profiles are of different devices: /device:TPU:25 before, /device:TPU:27 now
where the time goes in v6:
time: 36.4 us; the launch traced here: 36.2 us
  waiting for transfers between devices  23.5 us (65%)
  Pallas kernels  4.55 us (12%)
  starting transfers between devices  4.36 us (12%)
  local copies, waits for them, and re-layouts  2.96 us (8%)
  between operations  0.73 us (2%)
    ppermute x6, waiting for transfers between devices, flipped(): lax.ppermute(x, axis, [(i, i ^ bits) for i in range(lax.axis_size(axis))])  12.2 us
    ppermute x5, waiting for transfers between devices, crossed(): return lax.ppermute(x, ('groups', 'orient', 'tile'), pairs)  11.3 us
    pallas_call x2, Pallas kernels, maps(): pl.pallas_call(functools.partial(maps_kernel, len(wholes), places), in_sp...  2.64 us
    ppermute x5, starting transfers between devices, crossed(): return lax.ppermute(x, ('groups', 'orient', 'tile'), pairs)  2.19 us
    ppermute x6, starting transfers between devices, flipped(): lax.ppermute(x, axis, [(i, i ^ bits) for i in range(lax.axis_size(axis))])  2.18 us
    unnamed x13, local copies, waits for them, and re-layouts  1.94 us
    pallas_call x1, Pallas kernels, shards(): pl.pallas_call(functools.partial(stats_kernel, len(keeps), 2 * side * sid...  1.18 us
    squeeze x1, local copies, waits for them, and re-layouts, shards(): lax.dynamic_index_in_dim(template, lax.axis_index('groups'), 0, keepdims=...  0.97 us
  transfers between devices with their start and end apart: 11, of which 8 were waited for; matrix products, arithmetic and copies ran while one was open for 0% of the time, Pallas kernels for 9%

profile of v6, /device:TPU:27, one launch (start us, length us, event | category | flops | bytes accessed | tf_op | source)
XLA Modules:
  0.0 36.2 jit_solution(77076670837846912)
XLA Ops:
  0.6 0.0 copy-start
  0.6 1.0 %dynamic-slice_bitcast_fusion = f32[128,256]{1,0:T(8,128)S(1)} fusion(f32[1,2,128,256]{3,2,1,0:T(8,128)} %param.7, s32[]{:T(128)S(6)} %select_n.10), kind=kLoop, calls=%fused_computation.2 | loop fusion | bytes 262148 | tf_op jit(solution)/shard_map/jit(dynamic_index_in_dim)/squeeze | solution.py:191
  1.6 0.0 copy-done
  1.6 0.0 copy-start.1
  1.6 0.0 copy-start.2
  1.7 1.3 %collective-permute-start.2 = (f32[2,128,256]{2,1,0:T(8,128)S(1)}, f32[2,128,256]{2,1,0:T(8,128)S(1)}, u32[]{:S(2)}, u32[]{:S(2)}) collective-permute-start(f32[2,128,256]{2,1,0:T(8,128)S(1)} %bitcast.4), channel_id=1, source_target_pairs={{0,2},{2,0},{4,6},{6,4},{8,10},{10,8},{12,14},{14,12},{1,3},{3,1},... | collective-permute-start | bytes 786440 | tf_op jit(solution)/shard_map/ppermute | solution.py:143
  3.0 0.1 collective-permute-start.1
  3.0 0.2 collective-permute-start
  3.2 8.8 %collective-permute-done.1 = f32[128,256]{1,0:T(8,128)S(1)} collective-permute-done((f32[128,256]{1,0:T(8,128)S(1)}, f32[128,256]{1,0:T(8,128)S(1)}, u32[]{:S(2)}, u32[]{:S(2)}) %collective-permute-start.1) | collective-permute-done | bytes 131104 | tf_op jit(solution)/shard_map/ppermute | solution.py:143
  12.0 0.0 collective-permute-done
  12.0 0.0 collective-permute-done.2.refs_1_
  12.0 0.3 collective-permute-start.5
  12.3 0.2 collective-permute-start.4
  12.6 0.0 collective-permute-start.3
  12.6 0.0 copy-done.1
  12.6 0.0 copy-done.2
  12.6 0.0 copy-start.3
  12.6 0.9 %copy-done.3 = f32[256,256]{1,0:T(8,128)S(1)} copy-done((f32[256,256]{1,0:T(8,128)S(1)}, f32[256,256]{1,0:T(8,128)}, u32[]{:S(2)}) %copy-start.3) | copy-done | bytes 262168
  13.5 0.0 copy-start.4
  13.5 0.9 %copy-done.4 = f32[256,256]{1,0:T(8,128)S(1)} copy-done((f32[256,256]{1,0:T(8,128)S(1)}, f32[256,256]{1,0:T(8,128)}, u32[]{:S(2)}) %copy-start.4) | copy-done | bytes 262168
  14.5 0.7 %prepare.1 = (f32[4,128,256]{2,1,0:T(8,128)S(1)}, bf16[2,256,256]{2,1,0:T(8,128)(2,1)S(1)}, bf16[2,256,256]{2,1,0:T(8,128)(2,1)S(1)}) custom-call(f32[2,128,256]{2,1,0:T(8,128)S(1)} %bitcast.6, f32[256,256]{1,0:T(8,128)S(1)} %copy-done.2, f32[256,256]{1,0:T(8,128)S(1)} %copy-done.4, f32[256,256]{1,0:T(8,128)S(1)} %copy-done.3), custom_call_target="tpu_custom_call" | custom-call | tf_op jit(solution)/shard_map/prepare/pallas_call | solution.py:167
  15.2 1.5 %collective-permute-done.3.refs_4_ = f32[128,256]{1,0:T(8,128)S(1)} collective-permute-done((f32[128,256]{1,0:T(8,128)S(1)}, f32[128,256]{1,0:T(8,128)S(1)}, u32[]{:S(2)}, u32[]{:S(2)}) %collective-permute-start.3) | collective-permute-done | bytes 131104 | tf_op jit(solution)/shard_map/ppermute | solution.py:143
  16.7 2.2 %collective-permute-done.5.refs_4_.refs_1_ = f32[256,256]{1,0:T(8,128)S(1)} collective-permute-done((f32[256,256]{1,0:T(8,128)S(1)}, f32[256,256]{1,0:T(8,128)S(1)}, u32[]{:S(2)}, u32[]{:S(2)}) %collective-permute-start.5) | collective-permute-done | bytes 262176 | tf_op jit(solution)/shard_map/ppermute | solution.py:154
  18.9 1.1 %collective-permute-done.4.refs_3_.refs_0_ = f32[256,256]{1,0:T(8,128)S(1)} collective-permute-done((f32[256,256]{1,0:T(8,128)S(1)}, f32[256,256]{1,0:T(8,128)S(1)}, u32[]{:S(2)}, u32[]{:S(2)}) %collective-permute-start.4) | collective-permute-done | bytes 262176 | tf_op jit(solution)/shard_map/ppermute | solution.py:154
  20.1 1.4 %collective-permute-start.7 = (f32[256,256]{1,0:T(8,128)S(1)}, f32[256,256]{1,0:T(8,128)S(1)}, u32[]{:S(2)}, u32[]{:S(2)}) collective-permute-start(f32[256,256]{1,0:T(8,128)S(1)} %get-tuple-element.45), channel_id=1, source_target_pairs={{0,2},{1,17},{2,0},{3,19},{4,6},{5,21},{6,4},{7,23},{8,10},{9,25},... | collective-permute-start | bytes 786440 | tf_op jit(solution)/shard_map/ppermute | solution.py:154
  21.5 0.2 collective-permute-start.6
  21.7 0.0 collective-permute-start.8
  21.7 1.3 %maps.2 = (f32[4,144,256]{2,1,0:T(8,128)S(1)}, f32[4,144,256]{2,1,0:T(8,128)S(1)}) custom-call(f32[4,128,256]{2,1,0:T(8,128)S(1)} %get-tuple-element.30.coef_ref, bf16[2,256,256]{2,1,0:T(8,128)(2,1)S(1)} %get-tuple-element.31.rt_ref, bf16[2,256,256]{2,1,0:T(8,128)(2,1)S(1)} %get-tuple-element.32.col_ref, f32[2,128,256]{2,1,0:T(8,128)S(1)} %bitcast.5, ...), custom_call_target="tpu_custom_call" | custom-call | tf_op jit(solution)/shard_map/maps/pallas_call | solution.py:180
  23.1 3.7 %collective-permute-done.8.refs_5_ = f32[128,256]{1,0:T(8,128)S(1)} collective-permute-done((f32[128,256]{1,0:T(8,128)S(1)}, f32[128,256]{1,0:T(8,128)S(1)}, u32[]{:S(2)}, u32[]{:S(2)}) %collective-permute-start.8) | collective-permute-done | bytes 131104 | tf_op jit(solution)/shard_map/ppermute | solution.py:154
  26.8 1.0 %collective-permute-done.7.refs_3_ = f32[256,256]{1,0:T(8,128)S(1)} collective-permute-done((f32[256,256]{1,0:T(8,128)S(1)}, f32[256,256]{1,0:T(8,128)S(1)}, u32[]{:S(2)}, u32[]{:S(2)}) %collective-permute-start.7) | collective-permute-done | bytes 262176 | tf_op jit(solution)/shard_map/ppermute | solution.py:154
  27.8 3.3 %collective-permute-done.6.refs_2_ = f32[256,256]{1,0:T(8,128)S(1)} collective-permute-done((f32[256,256]{1,0:T(8,128)S(1)}, f32[256,256]{1,0:T(8,128)S(1)}, u32[]{:S(2)}, u32[]{:S(2)}) %collective-permute-start.6) | collective-permute-done | bytes 262176 | tf_op jit(solution)/shard_map/ppermute | solution.py:154
  31.1 0.0 copy-start.5
  31.1 0.6 %collective-permute-start.9 = (f32[4,144,256]{2,1,0:T(8,128)S(1)}, f32[4,144,256]{2,1,0:T(8,128)S(1)}, u32[]{:S(2)}, u32[]{:S(2)}) collective-permute-start(f32[4,144,256]{2,1,0:T(8,128)S(1)} %get-tuple-element.41), channel_id=1, source_target_pairs={{0,1},{1,0},{2,3},{3,2},{4,5},{5,4},{6,7},{7,6},{8,9},{9,8},{10,11... | collective-permute-start | bytes 1769480 | tf_op jit(solution)/shard_map/ppermute | solution.py:143
  31.6 1.3 %maps.3 = (f32[4,136,256]{2,1,0:T(8,128)S(1)}, f32[4,136,256]{2,1,0:T(8,128)S(1)}) custom-call(f32[4,128,256]{2,1,0:T(8,128)S(1)} %get-tuple-element.30.coef_ref, bf16[2,256,256]{2,1,0:T(8,128)(2,1)S(1)} %get-tuple-element.31.rt_ref, bf16[2,256,256]{2,1,0:T(8,128)(2,1)S(1)} %get-tuple-element.32.col_ref, ...), custom_call_target="tpu_custom_call" | custom-call | tf_op jit(solution)/shard_map/maps/pallas_call | solution.py:180
  33.0 0.1 collective-permute-start.10
  33.0 1.9 %collective-permute-done.10.refs_3_ = f32[4,136,256]{2,1,0:T(8,128)S(1)} collective-permute-done((f32[4,136,256]{2,1,0:T(8,128)S(1)}, f32[4,136,256]{2,1,0:T(8,128)S(1)}, u32[]{:S(2)}, u32[]{:S(2)}) %collective-permute-start.10) | collective-permute-done | bytes 557088 | tf_op jit(solution)/shard_map/ppermute | solution.py:143
  35.0 0.0 collective-permute-done.9.refs_2_
  35.0 0.0 copy-done.5
  35.0 1.2 %statistics.1 = (f32[1,128,256]{2,1,0:T(8,128)}, f32[1,128,256]{2,1,0:T(8,128)}, f32[1,128,256]{2,1,0:T(8,128)}) custom-call(f32[4,144,256]{2,1,0:T(8,128)S(1)} %get-tuple-element.36.refs_0_, f32[4,136,256]{2,1,0:T(8,128)S(1)} %get-tuple-element.40.refs_1_, f32[4,144,256]{2,1,0:T(8,128)S(1)} %collective-permute-done.9.refs_2_, ...), custom_call_target="tpu_custom_call" | custom-call | tf_op jit(solution)/shard_map/statistics/pallas_call | solution.py:230
  (5 shorter events, 0.1 us)
Async XLA Ops:
  0.6 1.0 %copy-start = (f32[1,2,128,256]{3,2,1,0:T(8,128)S(1)}, f32[1,2,128,256]{3,2,1,0:T(8,128)}, u32[]{:S(2)}) copy-start(f32[1,2,128,256]{3,2,1,0:T(8,128)} %param.7) | copy-start | bytes 786436
  1.6 10.9 %copy-start.1 = (f32[1,2,128,256]{3,2,1,0:T(8,128)S(1)}, f32[1,2,128,256]{3,2,1,0:T(8,128)}, u32[]{:S(2)}) copy-start(f32[1,2,128,256]{3,2,1,0:T(8,128)} %param.6) | copy-start | bytes 786436
  1.6 10.9 %copy-start.2 = (f32[256,256]{1,0:T(8,128)S(1)}, f32[256,256]{1,0:T(8,128)}, u32[]{:S(2)}) copy-start(f32[256,256]{1,0:T(8,128)} %w_hbm.1) | copy-start | bytes 786436
  1.7 10.3 %collective-permute-start.2 = (f32[2,128,256]{2,1,0:T(8,128)S(1)}, f32[2,128,256]{2,1,0:T(8,128)S(1)}, u32[]{:S(2)}, u32[]{:S(2)}) collective-permute-start(f32[2,128,256]{2,1,0:T(8,128)S(1)} %bitcast.4), channel_id=1, source_target_pairs={{0,2},{2,0},{4,6},{6,4},{8,10},{10,8},{12,14},{14,12},{1,3},{3,1},... | collective-permute-start | bytes 786440 | tf_op jit(solution)/shard_map/ppermute | solution.py:143
  3.0 9.0 %collective-permute-start.1 = (f32[128,256]{1,0:T(8,128)S(1)}, f32[128,256]{1,0:T(8,128)S(1)}, u32[]{:S(2)}, u32[]{:S(2)}) collective-permute-start(f32[128,256]{1,0:T(8,128)S(1)} %dynamic-slice_bitcast_fusion), channel_id=1, source_target_pairs={{0,8},{2,10},{4,12},{6,14},{8,0},{10,2},{12,4},{14,6},{1,9},{3,11}... | collective-permute-start | bytes 393224 | tf_op jit(solution)/shard_map/ppermute | solution.py:143
  3.0 9.0 %collective-permute-start = (f32[128,256]{1,0:T(8,128)S(1)}, f32[128,256]{1,0:T(8,128)S(1)}, u32[]{:S(2)}, u32[]{:S(2)}) collective-permute-start(f32[128,256]{1,0:T(8,128)S(1)} %dynamic-slice_bitcast_fusion), channel_id=1, source_target_pairs={{0,4},{2,6},{4,0},{6,2},{8,12},{10,14},{12,8},{14,10},{1,5},{3,7},... | collective-permute-start | bytes 393224 | tf_op jit(solution)/shard_map/ppermute | solution.py:143
  12.0 6.9 %collective-permute-start.5 = (f32[256,256]{1,0:T(8,128)S(1)}, f32[256,256]{1,0:T(8,128)S(1)}, u32[]{:S(2)}, u32[]{:S(2)}) collective-permute-start(f32[256,256]{1,0:T(8,128)S(1)} %constant_dynamic-update-slice_fusion.refs_2_), channel_id=1, source_target_pairs={{0,2},{1,17},{2,0},{3,19},{4,6},{5,21},{6,4},{7,23},{8,10},{9,25},... | collective-permute-start | bytes 786440 | tf_op jit(solution)/shard_map/ppermute | solution.py:154
  12.3 7.7 %collective-permute-start.4 = (f32[256,256]{1,0:T(8,128)S(1)}, f32[256,256]{1,0:T(8,128)S(1)}, u32[]{:S(2)}, u32[]{:S(2)}) collective-permute-start(f32[256,256]{1,0:T(8,128)S(1)} %constant_dynamic-update-slice_fusion.refs_2_), channel_id=1, source_target_pairs={{0,16},{1,3},{2,18},{3,1},{4,20},{5,7},{6,22},{7,5},{8,24},{9,11},... | collective-permute-start | bytes 786440 | tf_op jit(solution)/shard_map/ppermute | solution.py:154
  12.6 4.1 %collective-permute-start.3 = (f32[128,256]{1,0:T(8,128)S(1)}, f32[128,256]{1,0:T(8,128)S(1)}, u32[]{:S(2)}, u32[]{:S(2)}) collective-permute-start(f32[128,256]{1,0:T(8,128)S(1)} %collective-permute-done.1), channel_id=1, source_target_pairs={{0,4},{2,6},{4,0},{6,2},{8,12},{10,14},{12,8},{14,10},{1,5},{3,7},... | collective-permute-start | bytes 393224 | tf_op jit(solution)/shard_map/ppermute | solution.py:143
  12.6 1.0 %copy-start.3 = (f32[256,256]{1,0:T(8,128)S(1)}, f32[256,256]{1,0:T(8,128)}, u32[]{:S(2)}) copy-start(f32[256,256]{1,0:T(8,128)} %constant.29.clone.col_hbm) | copy-start | bytes 786436
  13.5 0.9 %copy-start.4 = (f32[256,256]{1,0:T(8,128)S(1)}, f32[256,256]{1,0:T(8,128)}, u32[]{:S(2)}) copy-start(f32[256,256]{1,0:T(8,128)} %constant.28.clone.row_hbm) | copy-start | bytes 786436
  20.1 7.7 %collective-permute-start.7 = (f32[256,256]{1,0:T(8,128)S(1)}, f32[256,256]{1,0:T(8,128)S(1)}, u32[]{:S(2)}, u32[]{:S(2)}) collective-permute-start(f32[256,256]{1,0:T(8,128)S(1)} %get-tuple-element.45), channel_id=1, source_target_pairs={{0,2},{1,17},{2,0},{3,19},{4,6},{5,21},{6,4},{7,23},{8,10},{9,25},... | collective-permute-start | bytes 786440 | tf_op jit(solution)/shard_map/ppermute | solution.py:154
  21.5 9.6 %collective-permute-start.6 = (f32[256,256]{1,0:T(8,128)S(1)}, f32[256,256]{1,0:T(8,128)S(1)}, u32[]{:S(2)}, u32[]{:S(2)}) collective-permute-start(f32[256,256]{1,0:T(8,128)S(1)} %get-tuple-element.46), channel_id=1, source_target_pairs={{0,16},{1,3},{2,18},{3,1},{4,20},{5,7},{6,22},{7,5},{8,24},{9,11},... | collective-permute-start | bytes 786440 | tf_op jit(solution)/shard_map/ppermute | solution.py:154
  21.7 5.1 %collective-permute-start.8 = (f32[128,256]{1,0:T(8,128)S(1)}, f32[128,256]{1,0:T(8,128)S(1)}, u32[]{:S(2)}, u32[]{:S(2)}) collective-permute-start(f32[128,256]{1,0:T(8,128)S(1)} %get-tuple-element.43), channel_id=1, source_target_pairs={{0,6},{1,21},{2,4},{3,23},{4,2},{5,17},{6,0},{7,19},{8,14},{9,29},... | collective-permute-start | bytes 393224 | tf_op jit(solution)/shard_map/ppermute | solution.py:154
  31.1 3.9 %copy-start.5 = (f32[128,128]{1,0:T(8,128)S(1)}, f32[128,128]{1,0:T(8,128)}, u32[]{:S(2)}) copy-start(f32[128,128]{1,0:T(8,128)} %constant.30.clone.refs_4_) | copy-start | bytes 196612
  31.1 3.9 %collective-permute-start.9 = (f32[4,144,256]{2,1,0:T(8,128)S(1)}, f32[4,144,256]{2,1,0:T(8,128)S(1)}, u32[]{:S(2)}, u32[]{:S(2)}) collective-permute-start(f32[4,144,256]{2,1,0:T(8,128)S(1)} %get-tuple-element.41), channel_id=1, source_target_pairs={{0,1},{1,0},{2,3},{3,2},{4,5},{5,4},{6,7},{7,6},{8,9},{9,8},{10,11... | collective-permute-start | bytes 1769480 | tf_op jit(solution)/shard_map/ppermute | solution.py:143
  33.0 2.0 %collective-permute-start.10 = (f32[4,136,256]{2,1,0:T(8,128)S(1)}, f32[4,136,256]{2,1,0:T(8,128)S(1)}, u32[]{:S(2)}, u32[]{:S(2)}) collective-permute-start(f32[4,136,256]{2,1,0:T(8,128)S(1)} %get-tuple-element.42), channel_id=1, source_target_pairs={{0,1},{1,0},{2,3},{3,2},{4,5},{5,4},{6,7},{7,6},{8,9},{9,8},{10,11... | collective-permute-start | bytes 1671176 | tf_op jit(solution)/shard_map/ppermute | solution.py:143

commit v7 on v5

--- a/solution.py
+++ b/solution.py
@@ -44,7 +44,7 @@
     return jnp.dot(a, b, preferred_element_type=jnp.float32)
 
 
-def prepare_kernel(s_hbm, w_hbm, row_hbm, col_hbm, coef_ref, rt_ref, ct_ref, s_ref, w_ref, row_ref, col_ref, sems):
+def prepare_kernel(s_hbm, w_hbm, table_hbm, coef_ref, rt_ref, ct_ref, s_ref, w_ref, row_ref, col_ref, sems):
     half, side = w_ref.shape
     here = lax.axis_index("tile")
     swap = lax.axis_index("groups") % 2
@@ -53,9 +53,9 @@
     moves = (
         (s_hbm, s_ref),
         (w_hbm.at[mine], w_ref),
-        (row_hbm.at[mine], row_ref.at[pl.ds(0, half)]),
-        (row_hbm.at[other], row_ref.at[pl.ds(half, half)]),
-        (col_hbm, col_ref),
+        (table_hbm.at[0, mine], row_ref.at[pl.ds(0, half)]),
+        (table_hbm.at[0, other], row_ref.at[pl.ds(half, half)]),
+        (table_hbm.at[1], col_ref),
     )
     copies = [pltpu.make_async_copy(source, target, sems.at[n]) for n, (source, target) in enumerate(moves)]
     for copy in copies:
@@ -100,8 +100,9 @@
     swap = lax.axis_index("groups") % 2
     for n, ref in enumerate(whole_refs):
         correlate(ref[swap], ref[1 - swap], coef_ref, col_ref, rt_ref, keep_ref, send_ref, n)
+    half = coef_ref.shape[1]
     for n, pair in enumerate(places):
-        a, b = (jnp.concatenate([part_refs[array][start:stop] for array, start, stop in piece], 0) for piece in pair)
+        a, b = (part_refs[array][row:row + half] for array, row in pair)
         correlate(a, b, coef_ref, col_ref, rt_ref, keep_ref, send_ref, wholes + n)
 
 
@@ -149,7 +150,7 @@
 
     coef, table, columns = pl.pallas_call(
         prepare_kernel,
-        in_specs=[hbm] * 4,
+        in_specs=[hbm] * 3,
         out_specs=[vmem] * 3,
         out_shape=[shape(4, half, side)] + [shape(2, side, side, dtype=jnp.bfloat16)] * 2,
         scratch_shapes=[
@@ -157,7 +158,7 @@
         ],
         compiler_params=params,
         name="prepare",
-    )(spectra[0], weights, jnp.asarray(row_table(side, half)), jnp.asarray(column_table(side)))
+    )(spectra[0], weights, jnp.asarray(np.stack([row_table(side, half), column_table(side)])))
 
     def maps(wholes, arrays=(), places=(), extra=8):
         return pl.pallas_call(
@@ -170,37 +171,30 @@
         )(coef, table, columns, *wholes, *arrays)
 
     if lax.axis_size("groups") == 2 and orients == 8:
-        cut = half // 2
-        part = lax.dynamic_index_in_dim(template, lax.axis_index("groups"), 0, keepdims=False)
+        plane = lax.axis_index("groups")
+        pick = lambda whole, n: lax.dynamic_index_in_dim(whole, n, 0, keepdims=False)
+        part = pick(template, plane)
         near1, near2 = (flipped(part, "orient", 2 * k) for k in (1, 2))
         beside = flipped(lax.optimization_barrier((template, part))[0], "orient", 1)
-        near1, near2, beside, coef = lax.optimization_barrier((near1, near2, beside, coef))
+        near1, near2, beside = lax.optimization_barrier((near1, near2, beside))
         near = jnp.concatenate([near1, near2], 0)
-        far = flipped(near2, "orient", 2)
+        far = flipped(jnp.concatenate([near2, pick(beside, 1 - plane)], 0), "orient", 2)
         near_x = flipped(near, "groups", 1)
         near_y = flipped(near, "orient", 1)
-        far, near_x, near_y = lax.optimization_barrier((far, near_x, near_y))
-        last_x = flipped(jnp.concatenate([far, near_y[:half + cut]], 0), "groups", 1)
-        last_y = flipped(jnp.concatenate([far, near_x[half + cut:]], 0), "orient", 1)
+        far, near_x, near_y, coef = lax.optimization_barrier((far, near_x, near_y, coef))
+        last_x = flipped(jnp.concatenate([far[:half], near_y[half:]], 0), "groups", 1)
         corner = flipped(near_x[half:], "orient", 3)
-        early = maps(
-            [template, beside],
-            [near, near_x],
-            (
-                (((0, 0, half),), ((1, 0, half),)),
-                (((0, half, side),), ((1, half, side),)),
-            ),
-            16,
-        )
+        last_y = flipped(far[:half], "orient", 1)
+        early = maps([template, beside], [near, near_x], (((0, 0), (1, 0)), ((0, half), (1, half))), 16)
         last_x, last_y, corner, early = lax.optimization_barrier((last_x, last_y, corner, early))
         late = maps(
             [],
             [near_y, last_x, last_y, far, corner],
             (
-                (((0, 0, half),), ((1, half, side),)),
-                (((0, half, side),), ((1, side, side + cut), (2, half, half + cut))),
-                (((3, 0, half),), ((1, 0, half),)),
-                (((2, 0, half),), ((4, 0, half),)),
+                ((0, 0), (3, half)),
+                ((0, half), (1, half)),
+                ((3, 0), (1, 0)),
+                ((2, 0), (4, 0)),
             ),
         )
         calls = [early, late]

time: 35.8 us -> 35.4 us (0.989)
  the two profiles are of different devices: /device:TPU:25 before, /device:TPU:0 now
where the time goes in v7:
time: 35.4 us; the launch traced here: 35.2 us
  starting transfers between devices  15 us (42%)
  waiting for transfers between devices  13.8 us (39%)
  Pallas kernels  4.56 us (13%)
  local copies, waits for them, and re-layouts  1.08 us (3%)
  between operations  0.74 us (2%)
    ppermute x11, starting transfers between devices, flipped(): lax.ppermute(x, axis, [(i, i ^ bits) for i in range(lax.axis_size(axis))])  15 us
    ppermute x11, waiting for transfers between devices, flipped(): lax.ppermute(x, axis, [(i, i ^ bits) for i in range(lax.axis_size(axis))])  13.8 us
    pallas_call x2, Pallas kernels, maps(): pl.pallas_call(functools.partial(maps_kernel, len(wholes), places), in_sp...  2.64 us
    pallas_call x1, Pallas kernels, shards(): pl.pallas_call(functools.partial(stats_kernel, len(keeps), 2 * side * sid...  1.18 us
    squeeze x2, local copies, waits for them, and re-layouts, shards(): lax.dynamic_index_in_dim(whole, n, 0, keepdims=False)  0.98 us
    pallas_call x1, Pallas kernels, shards(): pl.pallas_call(prepare_kernel, in_specs=[hbm] * 3, out_specs=[vmem] * 3,...  0.75 us
  transfers between devices with their start and end apart: 11, of which 8 were waited for; matrix products, arithmetic and copies ran while one was open for 0% of the time, Pallas kernels for 10%

profile of v7, /device:TPU:0, one launch (start us, length us, event | category | flops | bytes accessed | tf_op | source)
XLA Modules:
  0.0 35.2 jit_solution(17446548572876912899)
XLA Ops:
  0.6 0.0 copy-start
  0.6 1.0 %dynamic-slice_bitcast_fusion.1 = f32[128,256]{1,0:T(8,128)S(1)} fusion(f32[1,2,128,256]{3,2,1,0:T(8,128)} %param.6, s32[]{:T(128)S(6)} %select_n.7), kind=kLoop, calls=%fused_computation.3 | loop fusion | bytes 262148 | tf_op jit(solution)/shard_map/jit(dynamic_index_in_dim)/squeeze | solution.py:175
  1.6 0.0 copy-done
  1.6 3.0 %collective-permute-start.2 = (f32[2,128,256]{2,1,0:T(8,128)S(1)}, f32[2,128,256]{2,1,0:T(8,128)S(1)}, u32[]{:S(2)}, u32[]{:S(2)}) collective-permute-start(f32[2,128,256]{2,1,0:T(8,128)S(1)} %bitcast.6), channel_id=1, source_target_pairs={{0,2},{2,0},{4,6},{6,4},{8,10},{10,8},{12,14},{14,12},{1,3},{3,1},... | collective-permute-start | bytes 786440 | tf_op jit(solution)/shard_map/ppermute | solution.py:138
  4.7 2.6 %collective-permute-start.1 = (f32[128,256]{1,0:T(8,128)S(1)}, f32[128,256]{1,0:T(8,128)S(1)}, u32[]{:S(2)}, u32[]{:S(2)}) collective-permute-start(f32[128,256]{1,0:T(8,128)S(1)} %dynamic-slice_bitcast_fusion.1), channel_id=1, source_target_pairs={{0,8},{2,10},{4,12},{6,14},{8,0},{10,2},{12,4},{14,6},{1,9},{3,11}... | collective-permute-start | bytes 393224 | tf_op jit(solution)/shard_map/ppermute | solution.py:138
  7.3 1.6 %collective-permute-start = (f32[128,256]{1,0:T(8,128)S(1)}, f32[128,256]{1,0:T(8,128)S(1)}, u32[]{:S(2)}, u32[]{:S(2)}) collective-permute-start(f32[128,256]{1,0:T(8,128)S(1)} %dynamic-slice_bitcast_fusion.1), channel_id=1, source_target_pairs={{0,4},{2,6},{4,0},{6,2},{8,12},{10,14},{12,8},{14,10},{1,5},{3,7},... | collective-permute-start | bytes 393224 | tf_op jit(solution)/shard_map/ppermute | solution.py:138
  8.8 4.6 %collective-permute-done.1 = f32[128,256]{1,0:T(8,128)S(1)} collective-permute-done((f32[128,256]{1,0:T(8,128)S(1)}, f32[128,256]{1,0:T(8,128)S(1)}, u32[]{:S(2)}, u32[]{:S(2)}) %collective-permute-start.1) | collective-permute-done | bytes 131104 | tf_op jit(solution)/shard_map/ppermute | solution.py:138
  13.4 0.2 collective-permute-done
  13.6 0.0 collective-permute-done.2.refs_1_
  13.7 0.0 copy-start.1
  13.7 0.5 %collective-permute-start.5 = (f32[256,256]{1,0:T(8,128)S(1)}, f32[256,256]{1,0:T(8,128)S(1)}, u32[]{:S(2)}, u32[]{:S(2)}) collective-permute-start(f32[256,256]{1,0:T(8,128)S(1)} %constant_dynamic-update-slice_fusion.refs_2_), channel_id=1, source_target_pairs={{0,2},{2,0},{4,6},{6,4},{8,10},{10,8},{12,14},{14,12},{1,3},{3,1},... | collective-permute-start | bytes 786440 | tf_op jit(solution)/shard_map/ppermute | solution.py:138
  14.2 1.5 %collective-permute-start.4 = (f32[256,256]{1,0:T(8,128)S(1)}, f32[256,256]{1,0:T(8,128)S(1)}, u32[]{:S(2)}, u32[]{:S(2)}) collective-permute-start(f32[256,256]{1,0:T(8,128)S(1)} %constant_dynamic-update-slice_fusion.refs_2_), channel_id=1, source_target_pairs={{0,16},{16,0},{1,17},{17,1},{2,18},{18,2},{3,19},{19,3},{4,20},{20... | collective-permute-start | bytes 786440 | tf_op jit(solution)/shard_map/ppermute | solution.py:138
  15.8 0.0 copy-start.2
  15.8 0.0 copy-start.3
  15.8 1.4 %collective-permute-start.3 = (f32[256,256]{1,0:T(8,128)S(1)}, f32[256,256]{1,0:T(8,128)S(1)}, u32[]{:S(2)}, u32[]{:S(2)}) collective-permute-start(f32[256,256]{1,0:T(8,128)S(1)} %pad_maximum_fusion), channel_id=1, source_target_pairs={{0,4},{2,6},{4,0},{6,2},{8,12},{10,14},{12,8},{14,10},{1,5},{3,7},... | collective-permute-start | bytes 786440 | tf_op jit(solution)/shard_map/ppermute | solution.py:138
  17.3 0.0 copy-done.1
  17.3 0.0 copy-done.2
  17.3 0.0 copy-done.3
  17.3 0.7 %prepare.1 = (f32[4,128,256]{2,1,0:T(8,128)S(1)}, bf16[2,256,256]{2,1,0:T(8,128)(2,1)S(1)}, bf16[2,256,256]{2,1,0:T(8,128)(2,1)S(1)}) custom-call(f32[2,128,256]{2,1,0:T(8,128)S(1)} %bitcast.8, f32[256,256]{1,0:T(8,128)S(1)} %copy-done.3, f32[2,256,256]{2,1,0:T(8,128)S(1)} %copy-done.1), custom_call_target="tpu_custom_call" | custom-call | tf_op jit(solution)/shard_map/prepare/pallas_call | solution.py:151
  18.0 2.1 %collective-permute-done.5.refs_0_ = f32[256,256]{1,0:T(8,128)S(1)} collective-permute-done((f32[256,256]{1,0:T(8,128)S(1)}, f32[256,256]{1,0:T(8,128)S(1)}, u32[]{:S(2)}, u32[]{:S(2)}) %collective-permute-start.5) | collective-permute-done | bytes 262176 | tf_op jit(solution)/shard_map/ppermute | solution.py:138
  20.1 0.5 %collective-permute-done.4.refs_3_ = f32[256,256]{1,0:T(8,128)S(1)} collective-permute-done((f32[256,256]{1,0:T(8,128)S(1)}, f32[256,256]{1,0:T(8,128)S(1)}, u32[]{:S(2)}, u32[]{:S(2)}) %collective-permute-start.4) | collective-permute-done | bytes 262176 | tf_op jit(solution)/shard_map/ppermute | solution.py:138
  20.6 1.7 %collective-permute-done.3.refs_3_ = f32[256,256]{1,0:T(8,128)S(1)} collective-permute-done((f32[256,256]{1,0:T(8,128)S(1)}, f32[256,256]{1,0:T(8,128)S(1)}, u32[]{:S(2)}, u32[]{:S(2)}) %collective-permute-start.3) | collective-permute-done | bytes 262176 | tf_op jit(solution)/shard_map/ppermute | solution.py:138
  22.3 0.5 %collective-permute-start.6 = (f32[256,256]{1,0:T(8,128)S(1)}, f32[256,256]{1,0:T(8,128)S(1)}, u32[]{:S(2)}, u32[]{:S(2)}) collective-permute-start(f32[256,256]{1,0:T(8,128)S(1)} %pad_maximum_fusion.1), channel_id=1, source_target_pairs={{0,16},{16,0},{1,17},{17,1},{2,18},{18,2},{3,19},{19,3},{4,20},{20... | collective-permute-start | bytes 786440 | tf_op jit(solution)/shard_map/ppermute | solution.py:138
  22.9 2.7 %collective-permute-start.8 = (f32[128,256]{1,0:T(8,128)S(1)}, f32[128,256]{1,0:T(8,128)S(1)}, u32[]{:S(2)}, u32[]{:S(2)}) collective-permute-start(f32[128,256]{1,0:T(8,128)S(1)} %slice.12), channel_id=1, source_target_pairs={{0,6},{2,4},{4,2},{6,0},{8,14},{10,12},{12,10},{14,8},{1,7},{3,5},... | collective-permute-start | bytes 393224 | tf_op jit(solution)/shard_map/ppermute | solution.py:138
  25.6 0.5 %collective-permute-start.7 = (f32[128,256]{1,0:T(8,128)S(1)}, f32[128,256]{1,0:T(8,128)S(1)}, u32[]{:S(2)}, u32[]{:S(2)}) collective-permute-start(f32[128,256]{1,0:T(8,128)S(1)} %slice.10), channel_id=1, source_target_pairs={{0,2},{2,0},{4,6},{6,4},{8,10},{10,8},{12,14},{14,12},{1,3},{3,1},... | collective-permute-start | bytes 393224 | tf_op jit(solution)/shard_map/ppermute | solution.py:138
  26.1 1.3 %maps.2 = (f32[4,144,256]{2,1,0:T(8,128)S(1)}, f32[4,144,256]{2,1,0:T(8,128)S(1)}) custom-call(f32[4,128,256]{2,1,0:T(8,128)S(1)} %get-tuple-element.31.coef_ref, bf16[2,256,256]{2,1,0:T(8,128)(2,1)S(1)} %get-tuple-element.32.rt_ref, bf16[2,256,256]{2,1,0:T(8,128)(2,1)S(1)} %get-tuple-element.33.col_ref, f32[2,128,256]{2,1,0:T(8,128)S(1)} %bitcast.7, ...), custom_call_target="tpu_custom_call" | custom-call | tf_op jit(solution)/shard_map/maps/pallas_call | solution.py:164
  27.4 1.4 %collective-permute-done.8.refs_4_ = f32[128,256]{1,0:T(8,128)S(1)} collective-permute-done((f32[128,256]{1,0:T(8,128)S(1)}, f32[128,256]{1,0:T(8,128)S(1)}, u32[]{:S(2)}, u32[]{:S(2)}) %collective-permute-start.8) | collective-permute-done | bytes 131104 | tf_op jit(solution)/shard_map/ppermute | solution.py:138
  28.8 1.8 %collective-permute-done.7.refs_2_ = f32[128,256]{1,0:T(8,128)S(1)} collective-permute-done((f32[128,256]{1,0:T(8,128)S(1)}, f32[128,256]{1,0:T(8,128)S(1)}, u32[]{:S(2)}, u32[]{:S(2)}) %collective-permute-start.7) | collective-permute-done | bytes 131104 | tf_op jit(solution)/shard_map/ppermute | solution.py:138
  30.6 0.0 collective-permute-done.6.refs_1_
  30.6 0.0 copy-start.4
  30.6 0.0 collective-permute-start.9
  30.6 1.3 %maps.3 = (f32[4,136,256]{2,1,0:T(8,128)S(1)}, f32[4,136,256]{2,1,0:T(8,128)S(1)}) custom-call(f32[4,128,256]{2,1,0:T(8,128)S(1)} %get-tuple-element.31.coef_ref, bf16[2,256,256]{2,1,0:T(8,128)(2,1)S(1)} %get-tuple-element.32.rt_ref, bf16[2,256,256]{2,1,0:T(8,128)(2,1)S(1)} %get-tuple-element.33.col_ref, f32[256,256]{1,0:T(8,128)S(1)} %collective-permute-done.5.refs_0_, ...), custom_call_target="tpu_custom_call" | custom-call | tf_op jit(solution)/shard_map/maps/pallas_call | solution.py:164
  31.9 0.6 %collective-permute-start.10 = (f32[4,136,256]{2,1,0:T(8,128)S(1)}, f32[4,136,256]{2,1,0:T(8,128)S(1)}, u32[]{:S(2)}, u32[]{:S(2)}) collective-permute-start(f32[4,136,256]{2,1,0:T(8,128)S(1)} %get-tuple-element.42), channel_id=1, source_target_pairs={{0,1},{1,0},{2,3},{3,2},{4,5},{5,4},{6,7},{7,6},{8,9},{9,8},{10,11... | collective-permute-start | bytes 1671176 | tf_op jit(solution)/shard_map/ppermute | solution.py:138
  32.5 1.6 %collective-permute-done.10.refs_3_ = f32[4,136,256]{2,1,0:T(8,128)S(1)} collective-permute-done((f32[4,136,256]{2,1,0:T(8,128)S(1)}, f32[4,136,256]{2,1,0:T(8,128)S(1)}, u32[]{:S(2)}, u32[]{:S(2)}) %collective-permute-start.10) | collective-permute-done | bytes 557088 | tf_op jit(solution)/shard_map/ppermute | solution.py:138
  34.1 0.0 collective-permute-done.9.refs_2_
  34.1 0.0 copy-done.4
  34.1 1.2 %statistics.1 = (f32[1,128,256]{2,1,0:T(8,128)}, f32[1,128,256]{2,1,0:T(8,128)}, f32[1,128,256]{2,1,0:T(8,128)}) custom-call(f32[4,144,256]{2,1,0:T(8,128)S(1)} %get-tuple-element.36.refs_0_, f32[4,136,256]{2,1,0:T(8,128)S(1)} %get-tuple-element.40.refs_1_, f32[4,144,256]{2,1,0:T(8,128)S(1)} %collective-permute-done.9.refs_2_, ...), custom_call_target="tpu_custom_call" | custom-call | tf_op jit(solution)/shard_map/statistics/pallas_call | solution.py:206
  (8 shorter events, 0.1 us)
Async XLA Ops:
  0.6 1.0 %copy-start = (f32[1,2,128,256]{3,2,1,0:T(8,128)S(1)}, f32[1,2,128,256]{3,2,1,0:T(8,128)}, u32[]{:S(2)}) copy-start(f32[1,2,128,256]{3,2,1,0:T(8,128)} %param.6) | copy-start | bytes 786436
  1.6 12.0 %collective-permute-start.2 = (f32[2,128,256]{2,1,0:T(8,128)S(1)}, f32[2,128,256]{2,1,0:T(8,128)S(1)}, u32[]{:S(2)}, u32[]{:S(2)}) collective-permute-start(f32[2,128,256]{2,1,0:T(8,128)S(1)} %bitcast.6), channel_id=1, source_target_pairs={{0,2},{2,0},{4,6},{6,4},{8,10},{10,8},{12,14},{14,12},{1,3},{3,1},... | collective-permute-start | bytes 786440 | tf_op jit(solution)/shard_map/ppermute | solution.py:138
  4.7 8.8 %collective-permute-start.1 = (f32[128,256]{1,0:T(8,128)S(1)}, f32[128,256]{1,0:T(8,128)S(1)}, u32[]{:S(2)}, u32[]{:S(2)}) collective-permute-start(f32[128,256]{1,0:T(8,128)S(1)} %dynamic-slice_bitcast_fusion.1), channel_id=1, source_target_pairs={{0,8},{2,10},{4,12},{6,14},{8,0},{10,2},{12,4},{14,6},{1,9},{3,11}... | collective-permute-start | bytes 393224 | tf_op jit(solution)/shard_map/ppermute | solution.py:138
  7.3 6.4 %collective-permute-start = (f32[128,256]{1,0:T(8,128)S(1)}, f32[128,256]{1,0:T(8,128)S(1)}, u32[]{:S(2)}, u32[]{:S(2)}) collective-permute-start(f32[128,256]{1,0:T(8,128)S(1)} %dynamic-slice_bitcast_fusion.1), channel_id=1, source_target_pairs={{0,4},{2,6},{4,0},{6,2},{8,12},{10,14},{12,8},{14,10},{1,5},{3,7},... | collective-permute-start | bytes 393224 | tf_op jit(solution)/shard_map/ppermute | solution.py:138
  13.7 3.6 %copy-start.1 = (f32[2,256,256]{2,1,0:T(8,128)S(1)}, f32[2,256,256]{2,1,0:T(8,128)}, u32[]{:S(2)}) copy-start(f32[2,256,256]{2,1,0:T(8,128)} %constant.23.clone.table_hbm) | copy-start | bytes 1572868
  13.7 6.4 %collective-permute-start.5 = (f32[256,256]{1,0:T(8,128)S(1)}, f32[256,256]{1,0:T(8,128)S(1)}, u32[]{:S(2)}, u32[]{:S(2)}) collective-permute-start(f32[256,256]{1,0:T(8,128)S(1)} %constant_dynamic-update-slice_fusion.refs_2_), channel_id=1, source_target_pairs={{0,2},{2,0},{4,6},{6,4},{8,10},{10,8},{12,14},{14,12},{1,3},{3,1},... | collective-permute-start | bytes 786440 | tf_op jit(solution)/shard_map/ppermute | solution.py:138
  14.2 6.4 %collective-permute-start.4 = (f32[256,256]{1,0:T(8,128)S(1)}, f32[256,256]{1,0:T(8,128)S(1)}, u32[]{:S(2)}, u32[]{:S(2)}) collective-permute-start(f32[256,256]{1,0:T(8,128)S(1)} %constant_dynamic-update-slice_fusion.refs_2_), channel_id=1, source_target_pairs={{0,16},{16,0},{1,17},{17,1},{2,18},{18,2},{3,19},{19,3},{4,20},{20... | collective-permute-start | bytes 786440 | tf_op jit(solution)/shard_map/ppermute | solution.py:138
  15.8 1.5 %copy-start.2 = (f32[1,2,128,256]{3,2,1,0:T(8,128)S(1)}, f32[1,2,128,256]{3,2,1,0:T(8,128)}, u32[]{:S(2)}) copy-start(f32[1,2,128,256]{3,2,1,0:T(8,128)} %param.5) | copy-start | bytes 786436
  15.8 1.5 %copy-start.3 = (f32[256,256]{1,0:T(8,128)S(1)}, f32[256,256]{1,0:T(8,128)}, u32[]{:S(2)}) copy-start(f32[256,256]{1,0:T(8,128)} %w_hbm.1) | copy-start | bytes 786436
  15.8 6.4 %collective-permute-start.3 = (f32[256,256]{1,0:T(8,128)S(1)}, f32[256,256]{1,0:T(8,128)S(1)}, u32[]{:S(2)}, u32[]{:S(2)}) collective-permute-start(f32[256,256]{1,0:T(8,128)S(1)} %pad_maximum_fusion), channel_id=1, source_target_pairs={{0,4},{2,6},{4,0},{6,2},{8,12},{10,14},{12,8},{14,10},{1,5},{3,7},... | collective-permute-start | bytes 786440 | tf_op jit(solution)/shard_map/ppermute | solution.py:138
  22.3 8.3 %collective-permute-start.6 = (f32[256,256]{1,0:T(8,128)S(1)}, f32[256,256]{1,0:T(8,128)S(1)}, u32[]{:S(2)}, u32[]{:S(2)}) collective-permute-start(f32[256,256]{1,0:T(8,128)S(1)} %pad_maximum_fusion.1), channel_id=1, source_target_pairs={{0,16},{16,0},{1,17},{17,1},{2,18},{18,2},{3,19},{19,3},{4,20},{20... | collective-permute-start | bytes 786440 | tf_op jit(solution)/shard_map/ppermute | solution.py:138
  22.9 5.9 %collective-permute-start.8 = (f32[128,256]{1,0:T(8,128)S(1)}, f32[128,256]{1,0:T(8,128)S(1)}, u32[]{:S(2)}, u32[]{:S(2)}) collective-permute-start(f32[128,256]{1,0:T(8,128)S(1)} %slice.12), channel_id=1, source_target_pairs={{0,6},{2,4},{4,2},{6,0},{8,14},{10,12},{12,10},{14,8},{1,7},{3,5},... | collective-permute-start | bytes 393224 | tf_op jit(solution)/shard_map/ppermute | solution.py:138
  25.6 5.0 %collective-permute-start.7 = (f32[128,256]{1,0:T(8,128)S(1)}, f32[128,256]{1,0:T(8,128)S(1)}, u32[]{:S(2)}, u32[]{:S(2)}) collective-permute-start(f32[128,256]{1,0:T(8,128)S(1)} %slice.10), channel_id=1, source_target_pairs={{0,2},{2,0},{4,6},{6,4},{8,10},{10,8},{12,14},{14,12},{1,3},{3,1},... | collective-permute-start | bytes 393224 | tf_op jit(solution)/shard_map/ppermute | solution.py:138
  30.6 3.5 %copy-start.4 = (f32[128,128]{1,0:T(8,128)S(1)}, f32[128,128]{1,0:T(8,128)}, u32[]{:S(2)}) copy-start(f32[128,128]{1,0:T(8,128)} %constant.24.clone.refs_4_) | copy-start | bytes 196612
  30.6 3.5 %collective-permute-start.9 = (f32[4,144,256]{2,1,0:T(8,128)S(1)}, f32[4,144,256]{2,1,0:T(8,128)S(1)}, u32[]{:S(2)}, u32[]{:S(2)}) collective-permute-start(f32[4,144,256]{2,1,0:T(8,128)S(1)} %get-tuple-element.41), channel_id=1, source_target_pairs={{0,1},{1,0},{2,3},{3,2},{4,5},{5,4},{6,7},{7,6},{8,9},{9,8},{10,11... | collective-permute-start | bytes 1769480 | tf_op jit(solution)/shard_map/ppermute | solution.py:138
  31.9 2.2 %collective-permute-start.10 = (f32[4,136,256]{2,1,0:T(8,128)S(1)}, f32[4,136,256]{2,1,0:T(8,128)S(1)}, u32[]{:S(2)}, u32[]{:S(2)}) collective-permute-start(f32[4,136,256]{2,1,0:T(8,128)S(1)} %get-tuple-element.42), channel_id=1, source_target_pairs={{0,1},{1,0},{2,3},{3,2},{4,5},{5,4},{6,7},{7,6},{8,9},{9,8},{10,11... | collective-permute-start | bytes 1671176 | tf_op jit(solution)/shard_map/ppermute | solution.py:138

commit v8 on v7

--- a/solution.py
+++ b/solution.py
@@ -100,9 +100,8 @@
     swap = lax.axis_index("groups") % 2
     for n, ref in enumerate(whole_refs):
         correlate(ref[swap], ref[1 - swap], coef_ref, col_ref, rt_ref, keep_ref, send_ref, n)
-    half = coef_ref.shape[1]
     for n, pair in enumerate(places):
-        a, b = (part_refs[array][row:row + half] for array, row in pair)
+        a, b = (jnp.concatenate([part_refs[array][start:stop] for array, start, stop in pieces], 0) for pieces in pair)
         correlate(a, b, coef_ref, col_ref, rt_ref, keep_ref, send_ref, wholes + n)
 
 
@@ -172,29 +171,40 @@
 
     if lax.axis_size("groups") == 2 and orients == 8:
         plane = lax.axis_index("groups")
-        pick = lambda whole, n: lax.dynamic_index_in_dim(whole, n, 0, keepdims=False)
-        part = pick(template, plane)
+        most = half - 8
+        part, rest = (lax.dynamic_index_in_dim(template, n, 0, keepdims=False) for n in (plane, 1 - plane))
         near1, near2 = (flipped(part, "orient", 2 * k) for k in (1, 2))
-        beside = flipped(lax.optimization_barrier((template, part))[0], "orient", 1)
-        near1, near2, beside = lax.optimization_barrier((near1, near2, beside))
+        beside = flipped(rest[:most], "orient", 1)
+        beside, near1, near2 = lax.optimization_barrier((beside, near1, near2))
         near = jnp.concatenate([near1, near2], 0)
-        far = flipped(jnp.concatenate([near2, pick(beside, 1 - plane)], 0), "orient", 2)
+        near_y = flipped(jnp.concatenate([near1, near2, part, rest[most:]], 0), "orient", 1)
         near_x = flipped(near, "groups", 1)
-        near_y = flipped(near, "orient", 1)
+        far = flipped(jnp.concatenate([near2, beside], 0), "orient", 2)
         far, near_x, near_y, coef = lax.optimization_barrier((far, near_x, near_y, coef))
-        last_x = flipped(jnp.concatenate([far[:half], near_y[half:]], 0), "groups", 1)
+        last_x = flipped(jnp.concatenate([far[:half], near_y[half:side - 8], near_y[most:half]], 0), "groups", 1)
+        last_y = flipped(jnp.concatenate([far[:half], near_x[side - 8:]], 0), "orient", 1)
         corner = flipped(near_x[half:], "orient", 3)
-        last_y = flipped(far[:half], "orient", 1)
-        early = maps([template, beside], [near, near_x], (((0, 0), (1, 0)), ((0, half), (1, half))), 16)
+        block = lambda array, start=0, rows=half: ((array, start, start + rows),)
+        early = maps(
+            [],
+            [part, rest, near_y, beside, near, near_x],
+            (
+                (block(0), block(1)),
+                (block(2, side), block(3, 0, most) + block(2, side + half, 8)),
+                (block(4), block(5)),
+                (block(4, half), block(5, half)),
+            ),
+            16,
+        )
         last_x, last_y, corner, early = lax.optimization_barrier((last_x, last_y, corner, early))
         late = maps(
             [],
             [near_y, last_x, last_y, far, corner],
             (
-                ((0, 0), (3, half)),
-                ((0, half), (1, half)),
-                ((3, 0), (1, 0)),
-                ((2, 0), (4, 0)),
+                (block(0), block(3, half, most) + block(1, side - 8, 8)),
+                (block(0, half), block(1, half, most) + block(2, half, 8)),
+                (block(3), block(1)),
+                (block(2), block(4)),
             ),
         )
         calls = [early, late]

time: 35.4 us -> 37 us (1.045)
  the two profiles are of different devices: /device:TPU:0 before, /device:TPU:25 now
where the time goes in v8:
time: 37 us; the launch traced here: 36.9 us
  waiting for transfers between devices  19.7 us (53%)
  starting transfers between devices  10.3 us (28%)
  Pallas kernels  4.8 us (13%)
  local copies, waits for them, and re-layouts  1.12 us (3%)
  between operations  0.78 us (2%)
    ppermute x11, waiting for transfers between devices, flipped(): lax.ppermute(x, axis, [(i, i ^ bits) for i in range(lax.axis_size(axis))])  19.7 us
    ppermute x11, starting transfers between devices, flipped(): lax.ppermute(x, axis, [(i, i ^ bits) for i in range(lax.axis_size(axis))])  10.3 us
    pallas_call x2, Pallas kernels, maps(): pl.pallas_call(functools.partial(maps_kernel, len(wholes), places), in_sp...  2.84 us
    pallas_call x1, Pallas kernels, shards(): pl.pallas_call(functools.partial(stats_kernel, len(keeps), 2 * side * sid...  1.21 us
    squeeze x1, local copies, waits for them, and re-layouts, shards(): lax.dynamic_index_in_dim(template, n, 0, keepdims=False)  1.03 us
    pallas_call x1, Pallas kernels, shards(): pl.pallas_call(prepare_kernel, in_specs=[hbm] * 3, out_specs=[vmem] * 3,...  0.75 us
  transfers between devices with their start and end apart: 11, of which 6 were waited for; matrix products, arithmetic and copies ran while one was open for 0% of the time, Pallas kernels for 10%

profile of v8, /device:TPU:25, one launch (start us, length us, event | category | flops | bytes accessed | tf_op | source)
XLA Modules:
  0.0 36.9 jit_solution(9327271267944961460)
XLA Ops:
  0.6 0.0 copy-start.4
  0.6 1.0 %dynamic-slice_bitcast_fusion.1 = (f32[128,256]{1,0:T(8,128)S(1)}, f32[128,256]{1,0:T(8,128)S(1)}) fusion(f32[1,2,128,256]{3,2,1,0:T(8,128)} %param.6, s32[]{:T(128)S(6)} %select_n.7, s32[]{:T(128)S(6)} %select_n.8), kind=kLoop, calls=%fused_computation.5 | loop fusion | bytes 524296 | tf_op jit(solution)/shard_map/jit(dynamic_index_in_dim)/squeeze | solution.py:175
  1.7 0.1 collective-permute-start.2
  1.8 0.2 collective-permute-start.1
  2.0 0.0 copy-done.4
  2.0 1.3 %collective-permute-start = (f32[120,256]{1,0:T(8,128)S(1)}, f32[120,256]{1,0:T(8,128)S(1)}, u32[]{:S(2)}, u32[]{:S(2)}) collective-permute-start(f32[120,256]{1,0:T(8,128)S(1)} %dynamic-slice_bitcast_fusion.2), channel_id=1, source_target_pairs={{0,2},{2,0},{4,6},{6,4},{8,10},{10,8},{12,14},{14,12},{1,3},{3,1},... | collective-permute-start | bytes 368648 | tf_op jit(solution)/shard_map/ppermute | solution.py:137
  3.3 2.8 %collective-permute-done.refs_3_ = f32[120,256]{1,0:T(8,128)S(1)} collective-permute-done((f32[120,256]{1,0:T(8,128)S(1)}, f32[120,256]{1,0:T(8,128)S(1)}, u32[]{:S(2)}, u32[]{:S(2)}) %collective-permute-start) | collective-permute-done | bytes 122912 | tf_op jit(solution)/shard_map/ppermute | solution.py:137
  6.1 4.7 %collective-permute-done.2 = f32[128,256]{1,0:T(8,128)S(1)} collective-permute-done((f32[128,256]{1,0:T(8,128)S(1)}, f32[128,256]{1,0:T(8,128)S(1)}, u32[]{:S(2)}, u32[]{:S(2)}) %collective-permute-start.2) | collective-permute-done | bytes 131104 | tf_op jit(solution)/shard_map/ppermute | solution.py:137
  10.8 0.0 collective-permute-done.1
  10.8 0.0 copy-start.1
  10.8 0.0 copy-start.2
  10.8 0.0 copy-start
  10.9 1.3 %collective-permute-start.5 = (f32[392,256]{1,0:T(8,128)S(1)}, f32[392,256]{1,0:T(8,128)S(1)}, u32[]{:S(2)}, u32[]{:S(2)}) collective-permute-start(f32[392,256]{1,0:T(8,128)S(1)} %pad_maximum_fusion), channel_id=1, source_target_pairs={{0,2},{2,0},{4,6},{6,4},{8,10},{10,8},{12,14},{14,12},{1,3},{3,1},... | collective-permute-start | bytes 1204232 | tf_op jit(solution)/shard_map/ppermute | solution.py:137
  12.2 1.3 %collective-permute-start.4 = (f32[256,256]{1,0:T(8,128)S(1)}, f32[256,256]{1,0:T(8,128)S(1)}, u32[]{:S(2)}, u32[]{:S(2)}) collective-permute-start(f32[256,256]{1,0:T(8,128)S(1)} %constant_dynamic-update-slice_fusion.refs_4_), channel_id=1, source_target_pairs={{0,16},{16,0},{1,17},{17,1},{2,18},{18,2},{3,19},{19,3},{4,20},{20... | collective-permute-start | bytes 786440 | tf_op jit(solution)/shard_map/ppermute | solution.py:137
  13.5 0.1 collective-permute-start.3
  13.5 0.0 copy-done.1
  13.6 0.0 copy-done.2
  13.6 0.0 copy-done
  13.6 0.8 %prepare.1 = (f32[4,128,256]{2,1,0:T(8,128)S(1)}, bf16[2,256,256]{2,1,0:T(8,128)(2,1)S(1)}, bf16[2,256,256]{2,1,0:T(8,128)(2,1)S(1)}) custom-call(f32[2,128,256]{2,1,0:T(8,128)S(1)} %bitcast.9, f32[256,256]{1,0:T(8,128)S(1)} %copy-done.2, f32[2,256,256]{2,1,0:T(8,128)S(1)} %copy-done), custom_call_target="tpu_custom_call" | custom-call | tf_op jit(solution)/shard_map/prepare/pallas_call | solution.py:150
  14.3 5.8 %collective-permute-done.3.refs_3_ = f32[248,256]{1,0:T(8,128)S(1)} collective-permute-done((f32[248,256]{1,0:T(8,128)S(1)}, f32[248,256]{1,0:T(8,128)S(1)}, u32[]{:S(2)}, u32[]{:S(2)}) %collective-permute-start.3) | collective-permute-done | bytes 253984 | tf_op jit(solution)/shard_map/ppermute | solution.py:137
  20.1 0.0 collective-permute-done.4.refs_5_
  20.1 1.2 %collective-permute-done.5.refs_2_.refs_0_ = f32[392,256]{1,0:T(8,128)S(1)} collective-permute-done((f32[392,256]{1,0:T(8,128)S(1)}, f32[392,256]{1,0:T(8,128)S(1)}, u32[]{:S(2)}, u32[]{:S(2)}) %collective-permute-start.5) | collective-permute-done | bytes 401440 | tf_op jit(solution)/shard_map/ppermute | solution.py:137
  21.3 1.3 %collective-permute-start.6 = (f32[256,256]{1,0:T(8,128)S(1)}, f32[256,256]{1,0:T(8,128)S(1)}, u32[]{:S(2)}, u32[]{:S(2)}) collective-permute-start(f32[256,256]{1,0:T(8,128)S(1)} %pad_maximum_fusion.1), channel_id=1, source_target_pairs={{0,16},{16,0},{1,17},{17,1},{2,18},{18,2},{3,19},{19,3},{4,20},{20... | collective-permute-start | bytes 786440 | tf_op jit(solution)/shard_map/ppermute | solution.py:137
  22.6 1.3 %collective-permute-start.7 = (f32[136,256]{1,0:T(8,128)S(1)}, f32[136,256]{1,0:T(8,128)S(1)}, u32[]{:S(2)}, u32[]{:S(2)}) collective-permute-start(f32[136,256]{1,0:T(8,128)S(1)} %pad_maximum_fusion.3), channel_id=1, source_target_pairs={{0,2},{2,0},{4,6},{6,4},{8,10},{10,8},{12,14},{14,12},{1,3},{3,1},... | collective-permute-start | bytes 417800 | tf_op jit(solution)/shard_map/ppermute | solution.py:137
  24.0 0.1 collective-permute-start.8
  24.0 1.4 %maps.2 = (f32[4,144,256]{2,1,0:T(8,128)S(1)}, f32[4,144,256]{2,1,0:T(8,128)S(1)}) custom-call(f32[4,128,256]{2,1,0:T(8,128)S(1)} %get-tuple-element.29.coef_ref, bf16[2,256,256]{2,1,0:T(8,128)(2,1)S(1)} %get-tuple-element.30.rt_ref, bf16[2,256,256]{2,1,0:T(8,128)(2,1)S(1)} %get-tuple-element.31.col_ref, f32[128,256]{1,0:T(8,128)S(1)} %get-tuple-element.42.refs_0_, ...), custom_call_target="tpu_custom_call" | custom-call | tf_op jit(solution)/shard_map/maps/pallas_call | solution.py:163
  25.5 3.4 %collective-permute-done.8.refs_4_ = f32[128,256]{1,0:T(8,128)S(1)} collective-permute-done((f32[128,256]{1,0:T(8,128)S(1)}, f32[128,256]{1,0:T(8,128)S(1)}, u32[]{:S(2)}, u32[]{:S(2)}) %collective-permute-start.8) | collective-permute-done | bytes 131104 | tf_op jit(solution)/shard_map/ppermute | solution.py:137
  28.8 0.0 collective-permute-done.7.refs_2_
  28.8 0.0 collective-permute-done.6.refs_1_
  28.9 0.0 copy-start.3
  28.9 3.3 %collective-permute-start.9 = (f32[4,144,256]{2,1,0:T(8,128)S(1)}, f32[4,144,256]{2,1,0:T(8,128)S(1)}, u32[]{:S(2)}, u32[]{:S(2)}) collective-permute-start(f32[4,144,256]{2,1,0:T(8,128)S(1)} %get-tuple-element.39), channel_id=1, source_target_pairs={{0,1},{1,0},{2,3},{3,2},{4,5},{5,4},{6,7},{7,6},{8,9},{9,8},{10,11... | collective-permute-start | bytes 1769480 | tf_op jit(solution)/shard_map/ppermute | solution.py:137
  32.2 1.4 %maps.3 = (f32[4,136,256]{2,1,0:T(8,128)S(1)}, f32[4,136,256]{2,1,0:T(8,128)S(1)}) custom-call(f32[4,128,256]{2,1,0:T(8,128)S(1)} %get-tuple-element.29.coef_ref, bf16[2,256,256]{2,1,0:T(8,128)(2,1)S(1)} %get-tuple-element.30.rt_ref, bf16[2,256,256]{2,1,0:T(8,128)(2,1)S(1)} %get-tuple-element.31.col_ref, ...), custom_call_target="tpu_custom_call" | custom-call | tf_op jit(solution)/shard_map/maps/pallas_call | solution.py:163
  33.6 0.1 collective-permute-start.10
  33.7 1.9 %collective-permute-done.10.refs_3_ = f32[4,136,256]{2,1,0:T(8,128)S(1)} collective-permute-done((f32[4,136,256]{2,1,0:T(8,128)S(1)}, f32[4,136,256]{2,1,0:T(8,128)S(1)}, u32[]{:S(2)}, u32[]{:S(2)}) %collective-permute-start.10) | collective-permute-done | bytes 557088 | tf_op jit(solution)/shard_map/ppermute | solution.py:137
  35.6 0.0 collective-permute-done.9.refs_2_
  35.6 0.0 copy-done.3
  35.6 1.2 %statistics.1 = (f32[1,128,256]{2,1,0:T(8,128)}, f32[1,128,256]{2,1,0:T(8,128)}, f32[1,128,256]{2,1,0:T(8,128)}) custom-call(f32[4,144,256]{2,1,0:T(8,128)S(1)} %get-tuple-element.34.refs_0_, f32[4,136,256]{2,1,0:T(8,128)S(1)} %get-tuple-element.38.refs_1_, f32[4,144,256]{2,1,0:T(8,128)S(1)} %collective-permute-done.9.refs_2_, ...), custom_call_target="tpu_custom_call" | custom-call | tf_op jit(solution)/shard_map/statistics/pallas_call | solution.py:216
  (13 shorter events, 0.1 us)
Async XLA Ops:
  0.6 1.4 %copy-start.4 = (f32[1,2,128,256]{3,2,1,0:T(8,128)S(1)}, f32[1,2,128,256]{3,2,1,0:T(8,128)}, u32[]{:S(2)}) copy-start(f32[1,2,128,256]{3,2,1,0:T(8,128)} %param.6) | copy-start | bytes 786436
  1.7 9.1 %collective-permute-start.2 = (f32[128,256]{1,0:T(8,128)S(1)}, f32[128,256]{1,0:T(8,128)S(1)}, u32[]{:S(2)}, u32[]{:S(2)}) collective-permute-start(f32[128,256]{1,0:T(8,128)S(1)} %get-tuple-element.42.refs_0_), channel_id=1, source_target_pairs={{0,8},{2,10},{4,12},{6,14},{8,0},{10,2},{12,4},{14,6},{1,9},{3,11}... | collective-permute-start | bytes 393224 | tf_op jit(solution)/shard_map/ppermute | solution.py:137
  1.8 9.0 %collective-permute-start.1 = (f32[128,256]{1,0:T(8,128)S(1)}, f32[128,256]{1,0:T(8,128)S(1)}, u32[]{:S(2)}, u32[]{:S(2)}) collective-permute-start(f32[128,256]{1,0:T(8,128)S(1)} %get-tuple-element.42.refs_0_), channel_id=1, source_target_pairs={{0,4},{2,6},{4,0},{6,2},{8,12},{10,14},{12,8},{14,10},{1,5},{3,7},... | collective-permute-start | bytes 393224 | tf_op jit(solution)/shard_map/ppermute | solution.py:137
  2.0 4.1 %collective-permute-start = (f32[120,256]{1,0:T(8,128)S(1)}, f32[120,256]{1,0:T(8,128)S(1)}, u32[]{:S(2)}, u32[]{:S(2)}) collective-permute-start(f32[120,256]{1,0:T(8,128)S(1)} %dynamic-slice_bitcast_fusion.2), channel_id=1, source_target_pairs={{0,2},{2,0},{4,6},{6,4},{8,10},{10,8},{12,14},{14,12},{1,3},{3,1},... | collective-permute-start | bytes 368648 | tf_op jit(solution)/shard_map/ppermute | solution.py:137
  10.8 2.8 %copy-start.1 = (f32[1,2,128,256]{3,2,1,0:T(8,128)S(1)}, f32[1,2,128,256]{3,2,1,0:T(8,128)}, u32[]{:S(2)}) copy-start(f32[1,2,128,256]{3,2,1,0:T(8,128)} %param.5) | copy-start | bytes 786436
  10.8 2.8 %copy-start.2 = (f32[256,256]{1,0:T(8,128)S(1)}, f32[256,256]{1,0:T(8,128)}, u32[]{:S(2)}) copy-start(f32[256,256]{1,0:T(8,128)} %w_hbm.1) | copy-start | bytes 786436
  10.8 2.7 %copy-start = (f32[2,256,256]{2,1,0:T(8,128)S(1)}, f32[2,256,256]{2,1,0:T(8,128)}, u32[]{:S(2)}) copy-start(f32[2,256,256]{2,1,0:T(8,128)} %constant.24.clone.table_hbm) | copy-start | bytes 1572868
  10.9 10.4 %collective-permute-start.5 = (f32[392,256]{1,0:T(8,128)S(1)}, f32[392,256]{1,0:T(8,128)S(1)}, u32[]{:S(2)}, u32[]{:S(2)}) collective-permute-start(f32[392,256]{1,0:T(8,128)S(1)} %pad_maximum_fusion), channel_id=1, source_target_pairs={{0,2},{2,0},{4,6},{6,4},{8,10},{10,8},{12,14},{14,12},{1,3},{3,1},... | collective-permute-start | bytes 1204232 | tf_op jit(solution)/shard_map/ppermute | solution.py:137
  12.2 7.9 %collective-permute-start.4 = (f32[256,256]{1,0:T(8,128)S(1)}, f32[256,256]{1,0:T(8,128)S(1)}, u32[]{:S(2)}, u32[]{:S(2)}) collective-permute-start(f32[256,256]{1,0:T(8,128)S(1)} %constant_dynamic-update-slice_fusion.refs_4_), channel_id=1, source_target_pairs={{0,16},{16,0},{1,17},{17,1},{2,18},{18,2},{3,19},{19,3},{4,20},{20... | collective-permute-start | bytes 786440 | tf_op jit(solution)/shard_map/ppermute | solution.py:137
  13.5 6.6 %collective-permute-start.3 = (f32[248,256]{1,0:T(8,128)S(1)}, f32[248,256]{1,0:T(8,128)S(1)}, u32[]{:S(2)}, u32[]{:S(2)}) collective-permute-start(f32[248,256]{1,0:T(8,128)S(1)} %pad_maximum_fusion.2), channel_id=1, source_target_pairs={{0,4},{2,6},{4,0},{6,2},{8,12},{10,14},{12,8},{14,10},{1,5},{3,7},... | collective-permute-start | bytes 761864 | tf_op jit(solution)/shard_map/ppermute | solution.py:137
  21.3 7.5 %collective-permute-start.6 = (f32[256,256]{1,0:T(8,128)S(1)}, f32[256,256]{1,0:T(8,128)S(1)}, u32[]{:S(2)}, u32[]{:S(2)}) collective-permute-start(f32[256,256]{1,0:T(8,128)S(1)} %pad_maximum_fusion.1), channel_id=1, source_target_pairs={{0,16},{16,0},{1,17},{17,1},{2,18},{18,2},{3,19},{19,3},{4,20},{20... | collective-permute-start | bytes 786440 | tf_op jit(solution)/shard_map/ppermute | solution.py:137
  22.6 6.2 %collective-permute-start.7 = (f32[136,256]{1,0:T(8,128)S(1)}, f32[136,256]{1,0:T(8,128)S(1)}, u32[]{:S(2)}, u32[]{:S(2)}) collective-permute-start(f32[136,256]{1,0:T(8,128)S(1)} %pad_maximum_fusion.3), channel_id=1, source_target_pairs={{0,2},{2,0},{4,6},{6,4},{8,10},{10,8},{12,14},{14,12},{1,3},{3,1},... | collective-permute-start | bytes 417800 | tf_op jit(solution)/shard_map/ppermute | solution.py:137
  24.0 4.9 %collective-permute-start.8 = (f32[128,256]{1,0:T(8,128)S(1)}, f32[128,256]{1,0:T(8,128)S(1)}, u32[]{:S(2)}, u32[]{:S(2)}) collective-permute-start(f32[128,256]{1,0:T(8,128)S(1)} %slice.36), channel_id=1, source_target_pairs={{0,6},{2,4},{4,2},{6,0},{8,14},{10,12},{12,10},{14,8},{1,7},{3,5},... | collective-permute-start | bytes 393224 | tf_op jit(solution)/shard_map/ppermute | solution.py:137
  28.9 6.8 %copy-start.3 = (f32[128,128]{1,0:T(8,128)S(1)}, f32[128,128]{1,0:T(8,128)}, u32[]{:S(2)}) copy-start(f32[128,128]{1,0:T(8,128)} %constant.25.clone.refs_4_) | copy-start | bytes 196612
  28.9 6.8 %collective-permute-start.9 = (f32[4,144,256]{2,1,0:T(8,128)S(1)}, f32[4,144,256]{2,1,0:T(8,128)S(1)}, u32[]{:S(2)}, u32[]{:S(2)}) collective-permute-start(f32[4,144,256]{2,1,0:T(8,128)S(1)} %get-tuple-element.39), channel_id=1, source_target_pairs={{0,1},{1,0},{2,3},{3,2},{4,5},{5,4},{6,7},{7,6},{8,9},{9,8},{10,11... | collective-permute-start | bytes 1769480 | tf_op jit(solution)/shard_map/ppermute | solution.py:137
  33.6 2.0 %collective-permute-start.10 = (f32[4,136,256]{2,1,0:T(8,128)S(1)}, f32[4,136,256]{2,1,0:T(8,128)S(1)}, u32[]{:S(2)}, u32[]{:S(2)}) collective-permute-start(f32[4,136,256]{2,1,0:T(8,128)S(1)} %get-tuple-element.40), channel_id=1, source_target_pairs={{0,1},{1,0},{2,3},{3,2},{4,5},{5,4},{6,7},{7,6},{8,9},{9,8},{10,11... | collective-permute-start | bytes 1671176 | tf_op jit(solution)/shard_map/ppermute | solution.py:137

commit v9 on v7

--- a/solution.py
+++ b/solution.py
@@ -100,9 +100,8 @@
     swap = lax.axis_index("groups") % 2
     for n, ref in enumerate(whole_refs):
         correlate(ref[swap], ref[1 - swap], coef_ref, col_ref, rt_ref, keep_ref, send_ref, n)
-    half = coef_ref.shape[1]
     for n, pair in enumerate(places):
-        a, b = (part_refs[array][row:row + half] for array, row in pair)
+        a, b = (jnp.concatenate([part_refs[array][start:stop] for array, start, stop in pieces], 0) for pieces in pair)
         correlate(a, b, coef_ref, col_ref, rt_ref, keep_ref, send_ref, wholes + n)
 
 
@@ -172,29 +171,31 @@
 
     if lax.axis_size("groups") == 2 and orients == 8:
         plane = lax.axis_index("groups")
+        cut, most = half // 2, half - 8
         pick = lambda whole, n: lax.dynamic_index_in_dim(whole, n, 0, keepdims=False)
         part = pick(template, plane)
         near1, near2 = (flipped(part, "orient", 2 * k) for k in (1, 2))
         beside = flipped(lax.optimization_barrier((template, part))[0], "orient", 1)
         near1, near2, beside = lax.optimization_barrier((near1, near2, beside))
         near = jnp.concatenate([near1, near2], 0)
-        far = flipped(jnp.concatenate([near2, pick(beside, 1 - plane)], 0), "orient", 2)
+        far = flipped(jnp.concatenate([near2, pick(beside, 1 - plane)[:cut]], 0), "orient", 2)
         near_x = flipped(near, "groups", 1)
         near_y = flipped(near, "orient", 1)
         far, near_x, near_y, coef = lax.optimization_barrier((far, near_x, near_y, coef))
-        last_x = flipped(jnp.concatenate([far[:half], near_y[half:]], 0), "groups", 1)
+        last_x = flipped(jnp.concatenate([far[:half], near_y[half:side - 8], near_y[cut:half]], 0), "groups", 1)
+        last_y = flipped(jnp.concatenate([far[:half], near_x[side - 8:]], 0), "orient", 1)
         corner = flipped(near_x[half:], "orient", 3)
-        last_y = flipped(far[:half], "orient", 1)
-        early = maps([template, beside], [near, near_x], (((0, 0), (1, 0)), ((0, half), (1, half))), 16)
+        block = lambda array, start=0, rows=half: ((array, start, start + rows),)
+        early = maps([template, beside], [near, near_x], ((block(0), block(1)), (block(0, half), block(1, half))), 16)
         last_x, last_y, corner, early = lax.optimization_barrier((last_x, last_y, corner, early))
         late = maps(
             [],
             [near_y, last_x, last_y, far, corner],
             (
-                ((0, 0), (3, half)),
-                ((0, half), (1, half)),
-                ((3, 0), (1, 0)),
-                ((2, 0), (4, 0)),
+                (block(0), block(3, half, cut) + block(1, side - 8, cut)),
+                (block(0, half), block(1, half, most) + block(2, half, 8)),
+                (block(3), block(1)),
+                (block(2), block(4)),
             ),
         )
         calls = [early, late]

time: 35.4 us -> 35.1 us (level)
  waiting for transfers between devices: 13.8 us -> 12.6 us
  starting transfers between devices: 15 us -> 15.5 us
    ppermute x11, waiting for transfers between devices: 13.8 us -> 12.6 us  [flipped(): lax.ppermute(x, axis, [(i, i ^ bits) for i in range(lax.axis_size(axis))])]
    ppermute x11, starting transfers between devices: 15 us -> 15.5 us  [flipped(): lax.ppermute(x, axis, [(i, i ^ bits) for i in range(lax.axis_size(axis))])]
    squeeze x2 -> x1, local copies, waits for them, and re-layouts: 0.98 us -> 0.97 us  [shards(): lax.dynamic_index_in_dim(whole, n, 0, keepdims=False)]
  transfers between devices with their start and end apart: 11 -> 11, of which waited for: 8 -> 5; matrix products, arithmetic and copies ran while one was open for 0% -> 0% of each run, Pallas kernels for 10% -> 10%
where the time goes in v9:
time: 35.1 us; the launch traced here: 34.6 us
  starting transfers between devices  15.5 us (44%)
  waiting for transfers between devices  12.6 us (36%)
  Pallas kernels  4.56 us (13%)
  local copies, waits for them, and re-layouts  1.08 us (3%)
  between operations  0.75 us (2%)
    ppermute x11, starting transfers between devices, flipped(): lax.ppermute(x, axis, [(i, i ^ bits) for i in range(lax.axis_size(axis))])  15.5 us
    ppermute x11, waiting for transfers between devices, flipped(): lax.ppermute(x, axis, [(i, i ^ bits) for i in range(lax.axis_size(axis))])  12.6 us
    pallas_call x2, Pallas kernels, maps(): pl.pallas_call(functools.partial(maps_kernel, len(wholes), places), in_sp...  2.64 us
    pallas_call x1, Pallas kernels, shards(): pl.pallas_call(functools.partial(stats_kernel, len(keeps), 2 * side * sid...  1.18 us
    squeeze x1, local copies, waits for them, and re-layouts, shards(): lax.dynamic_index_in_dim(whole, n, 0, keepdims=False)  0.97 us
    pallas_call x1, Pallas kernels, shards(): pl.pallas_call(prepare_kernel, in_specs=[hbm] * 3, out_specs=[vmem] * 3,...  0.75 us
  transfers between devices with their start and end apart: 11, of which 5 were waited for; matrix products, arithmetic and copies ran while one was open for 0% of the time, Pallas kernels for 10%

profile of v9, /device:TPU:0, one launch (start us, length us, event | category | flops | bytes accessed | tf_op | source)
XLA Modules:
  0.0 34.6 jit_solution(16440287783820468164)
XLA Ops:
  0.6 0.0 copy-start
  0.6 1.0 %dynamic-slice_bitcast_fusion = f32[128,256]{1,0:T(8,128)S(1)} fusion(f32[1,2,128,256]{3,2,1,0:T(8,128)} %param.6, s32[]{:T(128)S(6)} %select_n.7), kind=kLoop, calls=%fused_computation.3 | loop fusion | bytes 262148 | tf_op jit(solution)/shard_map/jit(dynamic_index_in_dim)/squeeze | solution.py:175
  1.6 0.0 copy-done
  1.6 3.0 %collective-permute-start.2 = (f32[2,128,256]{2,1,0:T(8,128)S(1)}, f32[2,128,256]{2,1,0:T(8,128)S(1)}, u32[]{:S(2)}, u32[]{:S(2)}) collective-permute-start(f32[2,128,256]{2,1,0:T(8,128)S(1)} %bitcast.6), channel_id=1, source_target_pairs={{0,2},{2,0},{4,6},{6,4},{8,10},{10,8},{12,14},{14,12},{1,3},{3,1},... | collective-permute-start | bytes 786440 | tf_op jit(solution)/shard_map/ppermute | solution.py:137
  4.7 2.6 %collective-permute-start.1 = (f32[128,256]{1,0:T(8,128)S(1)}, f32[128,256]{1,0:T(8,128)S(1)}, u32[]{:S(2)}, u32[]{:S(2)}) collective-permute-start(f32[128,256]{1,0:T(8,128)S(1)} %dynamic-slice_bitcast_fusion), channel_id=1, source_target_pairs={{0,8},{2,10},{4,12},{6,14},{8,0},{10,2},{12,4},{14,6},{1,9},{3,11}... | collective-permute-start | bytes 393224 | tf_op jit(solution)/shard_map/ppermute | solution.py:137
  7.3 1.6 %collective-permute-start = (f32[128,256]{1,0:T(8,128)S(1)}, f32[128,256]{1,0:T(8,128)S(1)}, u32[]{:S(2)}, u32[]{:S(2)}) collective-permute-start(f32[128,256]{1,0:T(8,128)S(1)} %dynamic-slice_bitcast_fusion), channel_id=1, source_target_pairs={{0,4},{2,6},{4,0},{6,2},{8,12},{10,14},{12,8},{14,10},{1,5},{3,7},... | collective-permute-start | bytes 393224 | tf_op jit(solution)/shard_map/ppermute | solution.py:137
  8.8 0.0 copy-start.1
  8.8 4.6 %collective-permute-done.1 = f32[128,256]{1,0:T(8,128)S(1)} collective-permute-done((f32[128,256]{1,0:T(8,128)S(1)}, f32[128,256]{1,0:T(8,128)S(1)}, u32[]{:S(2)}, u32[]{:S(2)}) %collective-permute-start.1) | collective-permute-done | bytes 131104 | tf_op jit(solution)/shard_map/ppermute | solution.py:137
  13.4 0.2 collective-permute-done
  13.6 0.0 collective-permute-done.2.refs_1_
  13.7 0.0 copy-start.2
  13.7 0.0 copy-start.3
  13.7 0.5 %collective-permute-start.5 = (f32[256,256]{1,0:T(8,128)S(1)}, f32[256,256]{1,0:T(8,128)S(1)}, u32[]{:S(2)}, u32[]{:S(2)}) collective-permute-start(f32[256,256]{1,0:T(8,128)S(1)} %constant_dynamic-update-slice_fusion.refs_2_), channel_id=1, source_target_pairs={{0,2},{2,0},{4,6},{6,4},{8,10},{10,8},{12,14},{14,12},{1,3},{3,1},... | collective-permute-start | bytes 786440 | tf_op jit(solution)/shard_map/ppermute | solution.py:137
  14.2 1.5 %collective-permute-start.4 = (f32[256,256]{1,0:T(8,128)S(1)}, f32[256,256]{1,0:T(8,128)S(1)}, u32[]{:S(2)}, u32[]{:S(2)}) collective-permute-start(f32[256,256]{1,0:T(8,128)S(1)} %constant_dynamic-update-slice_fusion.refs_2_), channel_id=1, source_target_pairs={{0,16},{16,0},{1,17},{17,1},{2,18},{18,2},{3,19},{19,3},{4,20},{20... | collective-permute-start | bytes 786440 | tf_op jit(solution)/shard_map/ppermute | solution.py:137
  15.8 1.4 %collective-permute-start.3 = (f32[192,256]{1,0:T(8,128)S(1)}, f32[192,256]{1,0:T(8,128)S(1)}, u32[]{:S(2)}, u32[]{:S(2)}) collective-permute-start(f32[192,256]{1,0:T(8,128)S(1)} %pad_maximum_fusion.1), channel_id=1, source_target_pairs={{0,4},{2,6},{4,0},{6,2},{8,12},{10,14},{12,8},{14,10},{1,5},{3,7},... | collective-permute-start | bytes 589832 | tf_op jit(solution)/shard_map/ppermute | solution.py:137
  17.2 0.0 copy-done.1
  17.2 0.0 copy-done.2
  17.2 0.0 copy-done.3
  17.2 0.7 %prepare.1 = (f32[4,128,256]{2,1,0:T(8,128)S(1)}, bf16[2,256,256]{2,1,0:T(8,128)(2,1)S(1)}, bf16[2,256,256]{2,1,0:T(8,128)(2,1)S(1)}) custom-call(f32[2,128,256]{2,1,0:T(8,128)S(1)} %bitcast.8, f32[256,256]{1,0:T(8,128)S(1)} %copy-done.3, f32[2,256,256]{2,1,0:T(8,128)S(1)} %copy-done.1), custom_call_target="tpu_custom_call" | custom-call | tf_op jit(solution)/shard_map/prepare/pallas_call | solution.py:150
  18.0 3.5 %collective-permute-done.3.refs_3_ = f32[192,256]{1,0:T(8,128)S(1)} collective-permute-done((f32[192,256]{1,0:T(8,128)S(1)}, f32[192,256]{1,0:T(8,128)S(1)}, u32[]{:S(2)}, u32[]{:S(2)}) %collective-permute-start.3) | collective-permute-done | bytes 196640 | tf_op jit(solution)/shard_map/ppermute | solution.py:137
  21.5 0.0 collective-permute-done.5.refs_0_
  21.5 0.0 collective-permute-done.4.refs_3_
  21.6 0.7 %collective-permute-start.6 = (f32[312,256]{1,0:T(8,128)S(1)}, f32[312,256]{1,0:T(8,128)S(1)}, u32[]{:S(2)}, u32[]{:S(2)}) collective-permute-start(f32[312,256]{1,0:T(8,128)S(1)} %pad_maximum_fusion), channel_id=1, source_target_pairs={{0,16},{16,0},{1,17},{17,1},{2,18},{18,2},{3,19},{19,3},{4,20},{20... | collective-permute-start | bytes 958472 | tf_op jit(solution)/shard_map/ppermute | solution.py:137
  22.3 1.6 %collective-permute-start.7 = (f32[136,256]{1,0:T(8,128)S(1)}, f32[136,256]{1,0:T(8,128)S(1)}, u32[]{:S(2)}, u32[]{:S(2)}) collective-permute-start(f32[136,256]{1,0:T(8,128)S(1)} %pad_maximum_fusion.2), channel_id=1, source_target_pairs={{0,2},{2,0},{4,6},{6,4},{8,10},{10,8},{12,14},{14,12},{1,3},{3,1},... | collective-permute-start | bytes 417800 | tf_op jit(solution)/shard_map/ppermute | solution.py:137
  23.9 1.9 %collective-permute-start.8 = (f32[128,256]{1,0:T(8,128)S(1)}, f32[128,256]{1,0:T(8,128)S(1)}, u32[]{:S(2)}, u32[]{:S(2)}) collective-permute-start(f32[128,256]{1,0:T(8,128)S(1)} %slice.28), channel_id=1, source_target_pairs={{0,6},{2,4},{4,2},{6,0},{8,14},{10,12},{12,10},{14,8},{1,7},{3,5},... | collective-permute-start | bytes 393224 | tf_op jit(solution)/shard_map/ppermute | solution.py:137
  25.8 1.3 %maps.2 = (f32[4,144,256]{2,1,0:T(8,128)S(1)}, f32[4,144,256]{2,1,0:T(8,128)S(1)}) custom-call(f32[4,128,256]{2,1,0:T(8,128)S(1)} %get-tuple-element.31.coef_ref, bf16[2,256,256]{2,1,0:T(8,128)(2,1)S(1)} %get-tuple-element.32.rt_ref, bf16[2,256,256]{2,1,0:T(8,128)(2,1)S(1)} %get-tuple-element.33.col_ref, f32[2,128,256]{2,1,0:T(8,128)S(1)} %bitcast.7, ...), custom_call_target="tpu_custom_call" | custom-call | tf_op jit(solution)/shard_map/maps/pallas_call | solution.py:163
  27.2 2.7 %collective-permute-done.8.refs_4_ = f32[128,256]{1,0:T(8,128)S(1)} collective-permute-done((f32[128,256]{1,0:T(8,128)S(1)}, f32[128,256]{1,0:T(8,128)S(1)}, u32[]{:S(2)}, u32[]{:S(2)}) %collective-permute-start.8) | collective-permute-done | bytes 131104 | tf_op jit(solution)/shard_map/ppermute | solution.py:137
  29.9 0.0 collective-permute-done.7.refs_2_
  29.9 0.0 collective-permute-done.6.refs_1_
  29.9 0.0 copy-start.4
  29.9 0.1 collective-permute-start.9
  30.0 1.3 %maps.3 = (f32[4,136,256]{2,1,0:T(8,128)S(1)}, f32[4,136,256]{2,1,0:T(8,128)S(1)}) custom-call(f32[4,128,256]{2,1,0:T(8,128)S(1)} %get-tuple-element.31.coef_ref, bf16[2,256,256]{2,1,0:T(8,128)(2,1)S(1)} %get-tuple-element.32.rt_ref, bf16[2,256,256]{2,1,0:T(8,128)(2,1)S(1)} %get-tuple-element.33.col_ref, f32[256,256]{1,0:T(8,128)S(1)} %collective-permute-done.5.refs_0_, ...), custom_call_target="tpu_custom_call" | custom-call | tf_op jit(solution)/shard_map/maps/pallas_call | solution.py:163
  31.3 0.6 %collective-permute-start.10 = (f32[4,136,256]{2,1,0:T(8,128)S(1)}, f32[4,136,256]{2,1,0:T(8,128)S(1)}, u32[]{:S(2)}, u32[]{:S(2)}) collective-permute-start(f32[4,136,256]{2,1,0:T(8,128)S(1)} %get-tuple-element.42), channel_id=1, source_target_pairs={{0,1},{1,0},{2,3},{3,2},{4,5},{5,4},{6,7},{7,6},{8,9},{9,8},{10,11... | collective-permute-start | bytes 1671176 | tf_op jit(solution)/shard_map/ppermute | solution.py:137
  31.8 1.6 %collective-permute-done.10.refs_3_ = f32[4,136,256]{2,1,0:T(8,128)S(1)} collective-permute-done((f32[4,136,256]{2,1,0:T(8,128)S(1)}, f32[4,136,256]{2,1,0:T(8,128)S(1)}, u32[]{:S(2)}, u32[]{:S(2)}) %collective-permute-start.10) | collective-permute-done | bytes 557088 | tf_op jit(solution)/shard_map/ppermute | solution.py:137
  33.4 0.0 collective-permute-done.9.refs_2_
  33.4 0.0 copy-done.4
  33.4 1.2 %statistics.1 = (f32[1,128,256]{2,1,0:T(8,128)}, f32[1,128,256]{2,1,0:T(8,128)}, f32[1,128,256]{2,1,0:T(8,128)}) custom-call(f32[4,144,256]{2,1,0:T(8,128)S(1)} %get-tuple-element.36.refs_0_, f32[4,136,256]{2,1,0:T(8,128)S(1)} %get-tuple-element.40.refs_1_, f32[4,144,256]{2,1,0:T(8,128)S(1)} %collective-permute-done.9.refs_2_, ...), custom_call_target="tpu_custom_call" | custom-call | tf_op jit(solution)/shard_map/statistics/pallas_call | solution.py:207
  (11 shorter events, 0.1 us)
Async XLA Ops:
  0.6 1.0 %copy-start = (f32[1,2,128,256]{3,2,1,0:T(8,128)S(1)}, f32[1,2,128,256]{3,2,1,0:T(8,128)}, u32[]{:S(2)}) copy-start(f32[1,2,128,256]{3,2,1,0:T(8,128)} %param.6) | copy-start | bytes 786436
  1.6 12.0 %collective-permute-start.2 = (f32[2,128,256]{2,1,0:T(8,128)S(1)}, f32[2,128,256]{2,1,0:T(8,128)S(1)}, u32[]{:S(2)}, u32[]{:S(2)}) collective-permute-start(f32[2,128,256]{2,1,0:T(8,128)S(1)} %bitcast.6), channel_id=1, source_target_pairs={{0,2},{2,0},{4,6},{6,4},{8,10},{10,8},{12,14},{14,12},{1,3},{3,1},... | collective-permute-start | bytes 786440 | tf_op jit(solution)/shard_map/ppermute | solution.py:137
  4.7 8.8 %collective-permute-start.1 = (f32[128,256]{1,0:T(8,128)S(1)}, f32[128,256]{1,0:T(8,128)S(1)}, u32[]{:S(2)}, u32[]{:S(2)}) collective-permute-start(f32[128,256]{1,0:T(8,128)S(1)} %dynamic-slice_bitcast_fusion), channel_id=1, source_target_pairs={{0,8},{2,10},{4,12},{6,14},{8,0},{10,2},{12,4},{14,6},{1,9},{3,11}... | collective-permute-start | bytes 393224 | tf_op jit(solution)/shard_map/ppermute | solution.py:137
  7.3 6.4 %collective-permute-start = (f32[128,256]{1,0:T(8,128)S(1)}, f32[128,256]{1,0:T(8,128)S(1)}, u32[]{:S(2)}, u32[]{:S(2)}) collective-permute-start(f32[128,256]{1,0:T(8,128)S(1)} %dynamic-slice_bitcast_fusion), channel_id=1, source_target_pairs={{0,4},{2,6},{4,0},{6,2},{8,12},{10,14},{12,8},{14,10},{1,5},{3,7},... | collective-permute-start | bytes 393224 | tf_op jit(solution)/shard_map/ppermute | solution.py:137
  8.8 8.4 %copy-start.1 = (f32[2,256,256]{2,1,0:T(8,128)S(1)}, f32[2,256,256]{2,1,0:T(8,128)}, u32[]{:S(2)}) copy-start(f32[2,256,256]{2,1,0:T(8,128)} %constant.23.clone.table_hbm) | copy-start | bytes 1572868
  13.7 3.6 %copy-start.2 = (f32[1,2,128,256]{3,2,1,0:T(8,128)S(1)}, f32[1,2,128,256]{3,2,1,0:T(8,128)}, u32[]{:S(2)}) copy-start(f32[1,2,128,256]{3,2,1,0:T(8,128)} %param.5) | copy-start | bytes 786436
  13.7 3.5 %copy-start.3 = (f32[256,256]{1,0:T(8,128)S(1)}, f32[256,256]{1,0:T(8,128)}, u32[]{:S(2)}) copy-start(f32[256,256]{1,0:T(8,128)} %w_hbm.1) | copy-start | bytes 786436
  13.7 7.8 %collective-permute-start.5 = (f32[256,256]{1,0:T(8,128)S(1)}, f32[256,256]{1,0:T(8,128)S(1)}, u32[]{:S(2)}, u32[]{:S(2)}) collective-permute-start(f32[256,256]{1,0:T(8,128)S(1)} %constant_dynamic-update-slice_fusion.refs_2_), channel_id=1, source_target_pairs={{0,2},{2,0},{4,6},{6,4},{8,10},{10,8},{12,14},{14,12},{1,3},{3,1},... | collective-permute-start | bytes 786440 | tf_op jit(solution)/shard_map/ppermute | solution.py:137
  14.2 7.3 %collective-permute-start.4 = (f32[256,256]{1,0:T(8,128)S(1)}, f32[256,256]{1,0:T(8,128)S(1)}, u32[]{:S(2)}, u32[]{:S(2)}) collective-permute-start(f32[256,256]{1,0:T(8,128)S(1)} %constant_dynamic-update-slice_fusion.refs_2_), channel_id=1, source_target_pairs={{0,16},{16,0},{1,17},{17,1},{2,18},{18,2},{3,19},{19,3},{4,20},{20... | collective-permute-start | bytes 786440 | tf_op jit(solution)/shard_map/ppermute | solution.py:137
  15.8 5.7 %collective-permute-start.3 = (f32[192,256]{1,0:T(8,128)S(1)}, f32[192,256]{1,0:T(8,128)S(1)}, u32[]{:S(2)}, u32[]{:S(2)}) collective-permute-start(f32[192,256]{1,0:T(8,128)S(1)} %pad_maximum_fusion.1), channel_id=1, source_target_pairs={{0,4},{2,6},{4,0},{6,2},{8,12},{10,14},{12,8},{14,10},{1,5},{3,7},... | collective-permute-start | bytes 589832 | tf_op jit(solution)/shard_map/ppermute | solution.py:137
  21.6 8.3 %collective-permute-start.6 = (f32[312,256]{1,0:T(8,128)S(1)}, f32[312,256]{1,0:T(8,128)S(1)}, u32[]{:S(2)}, u32[]{:S(2)}) collective-permute-start(f32[312,256]{1,0:T(8,128)S(1)} %pad_maximum_fusion), channel_id=1, source_target_pairs={{0,16},{16,0},{1,17},{17,1},{2,18},{18,2},{3,19},{19,3},{4,20},{20... | collective-permute-start | bytes 958472 | tf_op jit(solution)/shard_map/ppermute | solution.py:137
  22.3 7.5 %collective-permute-start.7 = (f32[136,256]{1,0:T(8,128)S(1)}, f32[136,256]{1,0:T(8,128)S(1)}, u32[]{:S(2)}, u32[]{:S(2)}) collective-permute-start(f32[136,256]{1,0:T(8,128)S(1)} %pad_maximum_fusion.2), channel_id=1, source_target_pairs={{0,2},{2,0},{4,6},{6,4},{8,10},{10,8},{12,14},{14,12},{1,3},{3,1},... | collective-permute-start | bytes 417800 | tf_op jit(solution)/shard_map/ppermute | solution.py:137
  23.9 5.9 %collective-permute-start.8 = (f32[128,256]{1,0:T(8,128)S(1)}, f32[128,256]{1,0:T(8,128)S(1)}, u32[]{:S(2)}, u32[]{:S(2)}) collective-permute-start(f32[128,256]{1,0:T(8,128)S(1)} %slice.28), channel_id=1, source_target_pairs={{0,6},{2,4},{4,2},{6,0},{8,14},{10,12},{12,10},{14,8},{1,7},{3,5},... | collective-permute-start | bytes 393224 | tf_op jit(solution)/shard_map/ppermute | solution.py:137
  29.9 3.6 %copy-start.4 = (f32[128,128]{1,0:T(8,128)S(1)}, f32[128,128]{1,0:T(8,128)}, u32[]{:S(2)}) copy-start(f32[128,128]{1,0:T(8,128)} %constant.24.clone.refs_4_) | copy-start | bytes 196612
  29.9 3.5 %collective-permute-start.9 = (f32[4,144,256]{2,1,0:T(8,128)S(1)}, f32[4,144,256]{2,1,0:T(8,128)S(1)}, u32[]{:S(2)}, u32[]{:S(2)}) collective-permute-start(f32[4,144,256]{2,1,0:T(8,128)S(1)} %get-tuple-element.41), channel_id=1, source_target_pairs={{0,1},{1,0},{2,3},{3,2},{4,5},{5,4},{6,7},{7,6},{8,9},{9,8},{10,11... | collective-permute-start | bytes 1769480 | tf_op jit(solution)/shard_map/ppermute | solution.py:137
  31.3 2.1 %collective-permute-start.10 = (f32[4,136,256]{2,1,0:T(8,128)S(1)}, f32[4,136,256]{2,1,0:T(8,128)S(1)}, u32[]{:S(2)}, u32[]{:S(2)}) collective-permute-start(f32[4,136,256]{2,1,0:T(8,128)S(1)} %get-tuple-element.42), channel_id=1, source_target_pairs={{0,1},{1,0},{2,3},{3,2},{4,5},{5,4},{6,7},{7,6},{8,9},{9,8},{10,11... | collective-permute-start | bytes 1671176 | tf_op jit(solution)/shard_map/ppermute | solution.py:137

commit v10 on v9

--- a/solution.py
+++ b/solution.py
@@ -171,28 +171,31 @@
 
     if lax.axis_size("groups") == 2 and orients == 8:
         plane = lax.axis_index("groups")
-        cut, most = half // 2, half - 8
+        most = half - 8
         pick = lambda whole, n: lax.dynamic_index_in_dim(whole, n, 0, keepdims=False)
         part = pick(template, plane)
         near1, near2 = (flipped(part, "orient", 2 * k) for k in (1, 2))
         beside = flipped(lax.optimization_barrier((template, part))[0], "orient", 1)
         near1, near2, beside = lax.optimization_barrier((near1, near2, beside))
         near = jnp.concatenate([near1, near2], 0)
-        far = flipped(jnp.concatenate([near2, pick(beside, 1 - plane)[:cut]], 0), "orient", 2)
+        far = flipped(jnp.concatenate([near2, pick(beside, 1 - plane)], 0), "orient", 2)
         near_x = flipped(near, "groups", 1)
         near_y = flipped(near, "orient", 1)
         far, near_x, near_y, coef = lax.optimization_barrier((far, near_x, near_y, coef))
-        last_x = flipped(jnp.concatenate([far[:half], near_y[half:side - 8], near_y[cut:half]], 0), "groups", 1)
+        last_x = flipped(jnp.concatenate([far[:half], near_y[half:side - 8]], 0), "groups", 1)
         last_y = flipped(jnp.concatenate([far[:half], near_x[side - 8:]], 0), "orient", 1)
         corner = flipped(near_x[half:], "orient", 3)
         block = lambda array, start=0, rows=half: ((array, start, start + rows),)
-        early = maps([template, beside], [near, near_x], ((block(0), block(1)), (block(0, half), block(1, half))), 16)
+        early = maps(
+            [template, beside],
+            [near, near_x, near_y, far],
+            ((block(0), block(1)), (block(0, half), block(1, half)), (block(2), block(3, half))),
+        )
         last_x, last_y, corner, early = lax.optimization_barrier((last_x, last_y, corner, early))
         late = maps(
             [],
             [near_y, last_x, last_y, far, corner],
             (
-                (block(0), block(3, half, cut) + block(1, side - 8, cut)),
                 (block(0, half), block(1, half, most) + block(2, half, 8)),
                 (block(3), block(1)),
                 (block(2), block(4)),

time: 35.1 us -> 35 us (level)
  waiting for transfers between devices: 12.6 us -> 13.2 us
    ppermute x11, waiting for transfers between devices: 12.6 us -> 13.2 us  [flipped(): lax.ppermute(x, axis, [(i, i ^ bits) for i in range(lax.axis_size(axis))])]
    squeeze x1 -> x2, local copies, waits for them, and re-layouts: 0.97 us -> 0.98 us  [shards(): lax.dynamic_index_in_dim(whole, n, 0, keepdims=False)]
  transfers between devices with their start and end apart: 11 -> 11, of which waited for: 5 -> 7; matrix products, arithmetic and copies ran while one was open for 0% -> 0% of each run, Pallas kernels for 10% -> 10%
where the time goes in v10:
time: 35 us; the launch traced here: 34.8 us
  starting transfers between devices  15.2 us (43%)
  waiting for transfers between devices  13.2 us (38%)
  Pallas kernels  4.6 us (13%)
  local copies, waits for them, and re-layouts  1.08 us (3%)
  between operations  0.76 us (2%)
    ppermute x11, starting transfers between devices, flipped(): lax.ppermute(x, axis, [(i, i ^ bits) for i in range(lax.axis_size(axis))])  15.2 us
    ppermute x11, waiting for transfers between devices, flipped(): lax.ppermute(x, axis, [(i, i ^ bits) for i in range(lax.axis_size(axis))])  13.2 us
    pallas_call x2, Pallas kernels, maps(): pl.pallas_call(functools.partial(maps_kernel, len(wholes), places), in_sp...  2.65 us
    pallas_call x1, Pallas kernels, shards(): pl.pallas_call(functools.partial(stats_kernel, len(keeps), 2 * side * sid...  1.2 us
    squeeze x2, local copies, waits for them, and re-layouts, shards(): lax.dynamic_index_in_dim(whole, n, 0, keepdims=False)  0.98 us
    pallas_call x1, Pallas kernels, shards(): pl.pallas_call(prepare_kernel, in_specs=[hbm] * 3, out_specs=[vmem] * 3,...  0.75 us
  transfers between devices with their start and end apart: 11, of which 7 were waited for; matrix products, arithmetic and copies ran while one was open for 0% of the time, Pallas kernels for 10%

profile of v10, /device:TPU:0, one launch (start us, length us, event | category | flops | bytes accessed | tf_op | source)
XLA Modules:
  0.0 34.8 jit_solution(2750889261233307276)
XLA Ops:
  0.6 0.0 copy-start
  0.6 1.0 %dynamic-slice_bitcast_fusion.1 = f32[128,256]{1,0:T(8,128)S(1)} fusion(f32[1,2,128,256]{3,2,1,0:T(8,128)} %param.6, s32[]{:T(128)S(6)} %select_n.7), kind=kLoop, calls=%fused_computation.4 | loop fusion | bytes 262148 | tf_op jit(solution)/shard_map/jit(dynamic_index_in_dim)/squeeze | solution.py:175
  1.6 0.0 copy-done
  1.6 3.0 %collective-permute-start.2 = (f32[2,128,256]{2,1,0:T(8,128)S(1)}, f32[2,128,256]{2,1,0:T(8,128)S(1)}, u32[]{:S(2)}, u32[]{:S(2)}) collective-permute-start(f32[2,128,256]{2,1,0:T(8,128)S(1)} %bitcast.6), channel_id=1, source_target_pairs={{0,2},{2,0},{4,6},{6,4},{8,10},{10,8},{12,14},{14,12},{1,3},{3,1},... | collective-permute-start | bytes 786440 | tf_op jit(solution)/shard_map/ppermute | solution.py:137
  4.7 2.6 %collective-permute-start.1 = (f32[128,256]{1,0:T(8,128)S(1)}, f32[128,256]{1,0:T(8,128)S(1)}, u32[]{:S(2)}, u32[]{:S(2)}) collective-permute-start(f32[128,256]{1,0:T(8,128)S(1)} %dynamic-slice_bitcast_fusion.1), channel_id=1, source_target_pairs={{0,8},{2,10},{4,12},{6,14},{8,0},{10,2},{12,4},{14,6},{1,9},{3,11}... | collective-permute-start | bytes 393224 | tf_op jit(solution)/shard_map/ppermute | solution.py:137
  7.3 1.6 %collective-permute-start = (f32[128,256]{1,0:T(8,128)S(1)}, f32[128,256]{1,0:T(8,128)S(1)}, u32[]{:S(2)}, u32[]{:S(2)}) collective-permute-start(f32[128,256]{1,0:T(8,128)S(1)} %dynamic-slice_bitcast_fusion.1), channel_id=1, source_target_pairs={{0,4},{2,6},{4,0},{6,2},{8,12},{10,14},{12,8},{14,10},{1,5},{3,7},... | collective-permute-start | bytes 393224 | tf_op jit(solution)/shard_map/ppermute | solution.py:137
  8.8 4.6 %collective-permute-done.1 = f32[128,256]{1,0:T(8,128)S(1)} collective-permute-done((f32[128,256]{1,0:T(8,128)S(1)}, f32[128,256]{1,0:T(8,128)S(1)}, u32[]{:S(2)}, u32[]{:S(2)}) %collective-permute-start.1) | collective-permute-done | bytes 131104 | tf_op jit(solution)/shard_map/ppermute | solution.py:137
  13.4 0.2 collective-permute-done
  13.6 0.0 collective-permute-done.2.refs_1_
  13.7 0.0 copy-start.1
  13.7 0.5 %collective-permute-start.5 = (f32[256,256]{1,0:T(8,128)S(1)}, f32[256,256]{1,0:T(8,128)S(1)}, u32[]{:S(2)}, u32[]{:S(2)}) collective-permute-start(f32[256,256]{1,0:T(8,128)S(1)} %constant_dynamic-update-slice_fusion.refs_2_), channel_id=1, source_target_pairs={{0,2},{2,0},{4,6},{6,4},{8,10},{10,8},{12,14},{14,12},{1,3},{3,1},... | collective-permute-start | bytes 786440 | tf_op jit(solution)/shard_map/ppermute | solution.py:137
  14.2 1.5 %collective-permute-start.4 = (f32[256,256]{1,0:T(8,128)S(1)}, f32[256,256]{1,0:T(8,128)S(1)}, u32[]{:S(2)}, u32[]{:S(2)}) collective-permute-start(f32[256,256]{1,0:T(8,128)S(1)} %constant_dynamic-update-slice_fusion.refs_2_), channel_id=1, source_target_pairs={{0,16},{16,0},{1,17},{17,1},{2,18},{18,2},{3,19},{19,3},{4,20},{20... | collective-permute-start | bytes 786440 | tf_op jit(solution)/shard_map/ppermute | solution.py:137
  15.8 0.0 copy-start.2
  15.8 0.0 copy-start.3
  15.8 1.4 %collective-permute-start.3 = (f32[256,256]{1,0:T(8,128)S(1)}, f32[256,256]{1,0:T(8,128)S(1)}, u32[]{:S(2)}, u32[]{:S(2)}) collective-permute-start(f32[256,256]{1,0:T(8,128)S(1)} %pad_maximum_fusion), channel_id=1, source_target_pairs={{0,4},{2,6},{4,0},{6,2},{8,12},{10,14},{12,8},{14,10},{1,5},{3,7},... | collective-permute-start | bytes 786440 | tf_op jit(solution)/shard_map/ppermute | solution.py:137
  17.3 0.0 copy-done.1
  17.3 0.0 copy-done.2
  17.3 0.0 copy-done.3
  17.3 0.7 %prepare.1 = (f32[4,128,256]{2,1,0:T(8,128)S(1)}, bf16[2,256,256]{2,1,0:T(8,128)(2,1)S(1)}, bf16[2,256,256]{2,1,0:T(8,128)(2,1)S(1)}) custom-call(f32[2,128,256]{2,1,0:T(8,128)S(1)} %bitcast.8, f32[256,256]{1,0:T(8,128)S(1)} %copy-done.3, f32[2,256,256]{2,1,0:T(8,128)S(1)} %copy-done.1), custom_call_target="tpu_custom_call" | custom-call | tf_op jit(solution)/shard_map/prepare/pallas_call | solution.py:150
  18.0 2.1 %collective-permute-done.5.refs_4_.refs_0_ = f32[256,256]{1,0:T(8,128)S(1)} collective-permute-done((f32[256,256]{1,0:T(8,128)S(1)}, f32[256,256]{1,0:T(8,128)S(1)}, u32[]{:S(2)}, u32[]{:S(2)}) %collective-permute-start.5) | collective-permute-done | bytes 262176 | tf_op jit(solution)/shard_map/ppermute | solution.py:137
  20.1 0.5 %collective-permute-done.4.refs_3_ = f32[256,256]{1,0:T(8,128)S(1)} collective-permute-done((f32[256,256]{1,0:T(8,128)S(1)}, f32[256,256]{1,0:T(8,128)S(1)}, u32[]{:S(2)}, u32[]{:S(2)}) %collective-permute-start.4) | collective-permute-done | bytes 262176 | tf_op jit(solution)/shard_map/ppermute | solution.py:137
  20.6 1.7 %collective-permute-done.3.refs_5_.refs_3_ = f32[256,256]{1,0:T(8,128)S(1)} collective-permute-done((f32[256,256]{1,0:T(8,128)S(1)}, f32[256,256]{1,0:T(8,128)S(1)}, u32[]{:S(2)}, u32[]{:S(2)}) %collective-permute-start.3) | collective-permute-done | bytes 262176 | tf_op jit(solution)/shard_map/ppermute | solution.py:137
  22.3 0.5 %collective-permute-start.6 = (f32[248,256]{1,0:T(8,128)S(1)}, f32[248,256]{1,0:T(8,128)S(1)}, u32[]{:S(2)}, u32[]{:S(2)}) collective-permute-start(f32[248,256]{1,0:T(8,128)S(1)} %pad_maximum_fusion.1), channel_id=1, source_target_pairs={{0,16},{16,0},{1,17},{17,1},{2,18},{18,2},{3,19},{19,3},{4,20},{20... | collective-permute-start | bytes 761864 | tf_op jit(solution)/shard_map/ppermute | solution.py:137
  22.9 1.6 %collective-permute-start.7 = (f32[136,256]{1,0:T(8,128)S(1)}, f32[136,256]{1,0:T(8,128)S(1)}, u32[]{:S(2)}, u32[]{:S(2)}) collective-permute-start(f32[136,256]{1,0:T(8,128)S(1)} %pad_maximum_fusion.2), channel_id=1, source_target_pairs={{0,2},{2,0},{4,6},{6,4},{8,10},{10,8},{12,14},{14,12},{1,3},{3,1},... | collective-permute-start | bytes 417800 | tf_op jit(solution)/shard_map/ppermute | solution.py:137
  24.5 1.7 %collective-permute-start.8 = (f32[128,256]{1,0:T(8,128)S(1)}, f32[128,256]{1,0:T(8,128)S(1)}, u32[]{:S(2)}, u32[]{:S(2)}) collective-permute-start(f32[128,256]{1,0:T(8,128)S(1)} %slice.16), channel_id=1, source_target_pairs={{0,6},{2,4},{4,2},{6,0},{8,14},{10,12},{12,10},{14,8},{1,7},{3,5},... | collective-permute-start | bytes 393224 | tf_op jit(solution)/shard_map/ppermute | solution.py:137
  26.2 1.5 %maps.2 = (f32[5,136,256]{2,1,0:T(8,128)S(1)}, f32[5,136,256]{2,1,0:T(8,128)S(1)}) custom-call(f32[4,128,256]{2,1,0:T(8,128)S(1)} %get-tuple-element.31.coef_ref, bf16[2,256,256]{2,1,0:T(8,128)(2,1)S(1)} %get-tuple-element.32.rt_ref, bf16[2,256,256]{2,1,0:T(8,128)(2,1)S(1)} %get-tuple-element.33.col_ref, f32[2,128,256]{2,1,0:T(8,128)S(1)} %bitcast.7, ...), custom_call_target="tpu_custom_call" | custom-call | tf_op jit(solution)/shard_map/maps/pallas_call | solution.py:163
  27.7 2.7 %collective-permute-done.8.refs_4_ = f32[128,256]{1,0:T(8,128)S(1)} collective-permute-done((f32[128,256]{1,0:T(8,128)S(1)}, f32[128,256]{1,0:T(8,128)S(1)}, u32[]{:S(2)}, u32[]{:S(2)}) %collective-permute-start.8) | collective-permute-done | bytes 131104 | tf_op jit(solution)/shard_map/ppermute | solution.py:137
  30.5 0.0 collective-permute-done.7.refs_2_
  30.5 0.0 collective-permute-done.6.refs_1_
  30.5 0.0 copy-start.4
  30.5 0.1 collective-permute-start.9
  30.6 1.1 %maps.3 = (f32[3,136,256]{2,1,0:T(8,128)S(1)}, f32[3,136,256]{2,1,0:T(8,128)S(1)}) custom-call(f32[4,128,256]{2,1,0:T(8,128)S(1)} %get-tuple-element.31.coef_ref, bf16[2,256,256]{2,1,0:T(8,128)(2,1)S(1)} %get-tuple-element.32.rt_ref, bf16[2,256,256]{2,1,0:T(8,128)(2,1)S(1)} %get-tuple-element.33.col_ref, ...), custom_call_target="tpu_custom_call" | custom-call | tf_op jit(solution)/shard_map/maps/pallas_call | solution.py:163
  31.7 0.6 %collective-permute-start.10 = (f32[3,136,256]{2,1,0:T(8,128)S(1)}, f32[3,136,256]{2,1,0:T(8,128)S(1)}, u32[]{:S(2)}, u32[]{:S(2)}) collective-permute-start(f32[3,136,256]{2,1,0:T(8,128)S(1)} %get-tuple-element.42), channel_id=1, source_target_pairs={{0,1},{1,0},{2,3},{3,2},{4,5},{5,4},{6,7},{7,6},{8,9},{9,8},{10,11... | collective-permute-start | bytes 1253384 | tf_op jit(solution)/shard_map/ppermute | solution.py:137
  32.2 1.4 %collective-permute-done.10.refs_3_ = f32[3,136,256]{2,1,0:T(8,128)S(1)} collective-permute-done((f32[3,136,256]{2,1,0:T(8,128)S(1)}, f32[3,136,256]{2,1,0:T(8,128)S(1)}, u32[]{:S(2)}, u32[]{:S(2)}) %collective-permute-start.10) | collective-permute-done | bytes 417824 | tf_op jit(solution)/shard_map/ppermute | solution.py:137
  33.6 0.0 collective-permute-done.9.refs_2_
  33.6 0.0 copy-done.4
  33.6 1.2 %statistics.1 = (f32[1,128,256]{2,1,0:T(8,128)}, f32[1,128,256]{2,1,0:T(8,128)}, f32[1,128,256]{2,1,0:T(8,128)}) custom-call(f32[5,136,256]{2,1,0:T(8,128)S(1)} %get-tuple-element.36.refs_0_, f32[3,136,256]{2,1,0:T(8,128)S(1)} %get-tuple-element.40.refs_1_, f32[5,136,256]{2,1,0:T(8,128)S(1)} %collective-permute-done.9.refs_2_, ...), custom_call_target="tpu_custom_call" | custom-call | tf_op jit(solution)/shard_map/statistics/pallas_call | solution.py:210
  (10 shorter events, 0.1 us)
Async XLA Ops:
  0.6 1.0 %copy-start = (f32[1,2,128,256]{3,2,1,0:T(8,128)S(1)}, f32[1,2,128,256]{3,2,1,0:T(8,128)}, u32[]{:S(2)}) copy-start(f32[1,2,128,256]{3,2,1,0:T(8,128)} %param.6) | copy-start | bytes 786436
  1.6 12.0 %collective-permute-start.2 = (f32[2,128,256]{2,1,0:T(8,128)S(1)}, f32[2,128,256]{2,1,0:T(8,128)S(1)}, u32[]{:S(2)}, u32[]{:S(2)}) collective-permute-start(f32[2,128,256]{2,1,0:T(8,128)S(1)} %bitcast.6), channel_id=1, source_target_pairs={{0,2},{2,0},{4,6},{6,4},{8,10},{10,8},{12,14},{14,12},{1,3},{3,1},... | collective-permute-start | bytes 786440 | tf_op jit(solution)/shard_map/ppermute | solution.py:137
  4.7 8.8 %collective-permute-start.1 = (f32[128,256]{1,0:T(8,128)S(1)}, f32[128,256]{1,0:T(8,128)S(1)}, u32[]{:S(2)}, u32[]{:S(2)}) collective-permute-start(f32[128,256]{1,0:T(8,128)S(1)} %dynamic-slice_bitcast_fusion.1), channel_id=1, source_target_pairs={{0,8},{2,10},{4,12},{6,14},{8,0},{10,2},{12,4},{14,6},{1,9},{3,11}... | collective-permute-start | bytes 393224 | tf_op jit(solution)/shard_map/ppermute | solution.py:137
  7.3 6.4 %collective-permute-start = (f32[128,256]{1,0:T(8,128)S(1)}, f32[128,256]{1,0:T(8,128)S(1)}, u32[]{:S(2)}, u32[]{:S(2)}) collective-permute-start(f32[128,256]{1,0:T(8,128)S(1)} %dynamic-slice_bitcast_fusion.1), channel_id=1, source_target_pairs={{0,4},{2,6},{4,0},{6,2},{8,12},{10,14},{12,8},{14,10},{1,5},{3,7},... | collective-permute-start | bytes 393224 | tf_op jit(solution)/shard_map/ppermute | solution.py:137
  13.7 3.6 %copy-start.1 = (f32[2,256,256]{2,1,0:T(8,128)S(1)}, f32[2,256,256]{2,1,0:T(8,128)}, u32[]{:S(2)}) copy-start(f32[2,256,256]{2,1,0:T(8,128)} %constant.23.clone.table_hbm) | copy-start | bytes 1572868
  13.7 6.4 %collective-permute-start.5 = (f32[256,256]{1,0:T(8,128)S(1)}, f32[256,256]{1,0:T(8,128)S(1)}, u32[]{:S(2)}, u32[]{:S(2)}) collective-permute-start(f32[256,256]{1,0:T(8,128)S(1)} %constant_dynamic-update-slice_fusion.refs_2_), channel_id=1, source_target_pairs={{0,2},{2,0},{4,6},{6,4},{8,10},{10,8},{12,14},{14,12},{1,3},{3,1},... | collective-permute-start | bytes 786440 | tf_op jit(solution)/shard_map/ppermute | solution.py:137
  14.2 6.4 %collective-permute-start.4 = (f32[256,256]{1,0:T(8,128)S(1)}, f32[256,256]{1,0:T(8,128)S(1)}, u32[]{:S(2)}, u32[]{:S(2)}) collective-permute-start(f32[256,256]{1,0:T(8,128)S(1)} %constant_dynamic-update-slice_fusion.refs_2_), channel_id=1, source_target_pairs={{0,16},{16,0},{1,17},{17,1},{2,18},{18,2},{3,19},{19,3},{4,20},{20... | collective-permute-start | bytes 786440 | tf_op jit(solution)/shard_map/ppermute | solution.py:137
  15.8 1.5 %copy-start.2 = (f32[1,2,128,256]{3,2,1,0:T(8,128)S(1)}, f32[1,2,128,256]{3,2,1,0:T(8,128)}, u32[]{:S(2)}) copy-start(f32[1,2,128,256]{3,2,1,0:T(8,128)} %param.5) | copy-start | bytes 786436
  15.8 1.5 %copy-start.3 = (f32[256,256]{1,0:T(8,128)S(1)}, f32[256,256]{1,0:T(8,128)}, u32[]{:S(2)}) copy-start(f32[256,256]{1,0:T(8,128)} %w_hbm.1) | copy-start | bytes 786436
  15.8 6.4 %collective-permute-start.3 = (f32[256,256]{1,0:T(8,128)S(1)}, f32[256,256]{1,0:T(8,128)S(1)}, u32[]{:S(2)}, u32[]{:S(2)}) collective-permute-start(f32[256,256]{1,0:T(8,128)S(1)} %pad_maximum_fusion), channel_id=1, source_target_pairs={{0,4},{2,6},{4,0},{6,2},{8,12},{10,14},{12,8},{14,10},{1,5},{3,7},... | collective-permute-start | bytes 786440 | tf_op jit(solution)/shard_map/ppermute | solution.py:137
  22.3 8.2 %collective-permute-start.6 = (f32[248,256]{1,0:T(8,128)S(1)}, f32[248,256]{1,0:T(8,128)S(1)}, u32[]{:S(2)}, u32[]{:S(2)}) collective-permute-start(f32[248,256]{1,0:T(8,128)S(1)} %pad_maximum_fusion.1), channel_id=1, source_target_pairs={{0,16},{16,0},{1,17},{17,1},{2,18},{18,2},{3,19},{19,3},{4,20},{20... | collective-permute-start | bytes 761864 | tf_op jit(solution)/shard_map/ppermute | solution.py:137
  22.9 7.6 %collective-permute-start.7 = (f32[136,256]{1,0:T(8,128)S(1)}, f32[136,256]{1,0:T(8,128)S(1)}, u32[]{:S(2)}, u32[]{:S(2)}) collective-permute-start(f32[136,256]{1,0:T(8,128)S(1)} %pad_maximum_fusion.2), channel_id=1, source_target_pairs={{0,2},{2,0},{4,6},{6,4},{8,10},{10,8},{12,14},{14,12},{1,3},{3,1},... | collective-permute-start | bytes 417800 | tf_op jit(solution)/shard_map/ppermute | solution.py:137
  24.5 5.9 %collective-permute-start.8 = (f32[128,256]{1,0:T(8,128)S(1)}, f32[128,256]{1,0:T(8,128)S(1)}, u32[]{:S(2)}, u32[]{:S(2)}) collective-permute-start(f32[128,256]{1,0:T(8,128)S(1)} %slice.16), channel_id=1, source_target_pairs={{0,6},{2,4},{4,2},{6,0},{8,14},{10,12},{12,10},{14,8},{1,7},{3,5},... | collective-permute-start | bytes 393224 | tf_op jit(solution)/shard_map/ppermute | solution.py:137
  30.5 3.2 %copy-start.4 = (f32[128,128]{1,0:T(8,128)S(1)}, f32[128,128]{1,0:T(8,128)}, u32[]{:S(2)}) copy-start(f32[128,128]{1,0:T(8,128)} %constant.24.clone.refs_4_) | copy-start | bytes 196612
  30.5 3.1 %collective-permute-start.9 = (f32[5,136,256]{2,1,0:T(8,128)S(1)}, f32[5,136,256]{2,1,0:T(8,128)S(1)}, u32[]{:S(2)}, u32[]{:S(2)}) collective-permute-start(f32[5,136,256]{2,1,0:T(8,128)S(1)} %get-tuple-element.41), channel_id=1, source_target_pairs={{0,1},{1,0},{2,3},{3,2},{4,5},{5,4},{6,7},{7,6},{8,9},{9,8},{10,11... | collective-permute-start | bytes 2088968 | tf_op jit(solution)/shard_map/ppermute | solution.py:137
  31.7 1.9 %collective-permute-start.10 = (f32[3,136,256]{2,1,0:T(8,128)S(1)}, f32[3,136,256]{2,1,0:T(8,128)S(1)}, u32[]{:S(2)}, u32[]{:S(2)}) collective-permute-start(f32[3,136,256]{2,1,0:T(8,128)S(1)} %get-tuple-element.42), channel_id=1, source_target_pairs={{0,1},{1,0},{2,3},{3,2},{4,5},{5,4},{6,7},{7,6},{8,9},{9,8},{10,11... | collective-permute-start | bytes 1253384 | tf_op jit(solution)/shard_map/ppermute | solution.py:137

commit v11 on v10

--- a/solution.py
+++ b/solution.py
@@ -137,6 +137,17 @@
     return lax.ppermute(x, axis, [(i, i ^ bits) for i in range(lax.axis_size(axis))])
 
 
+def crossed(x, even, odd):
+    groups, orients, cores = (lax.axis_size(axis) for axis in ("groups", "orient", "tile"))
+    pairs = []
+    for g in range(groups):
+        for o in range(orients):
+            for c in range(cores):
+                group_bits, orient_bits = odd if c else even
+                pairs.append(((g * orients + o) * cores + c, ((g ^ group_bits) * orients + (o ^ orient_bits)) * cores + c))
+    return lax.ppermute(x, ("groups", "orient", "tile"), pairs)
+
+
 def shards(spectra, templates, weights):
     half, side = spectra.shape[2:]
     orients = lax.axis_size("orient")
@@ -171,7 +182,7 @@
 
     if lax.axis_size("groups") == 2 and orients == 8:
         plane = lax.axis_index("groups")
-        most = half - 8
+        few = 24
         pick = lambda whole, n: lax.dynamic_index_in_dim(whole, n, 0, keepdims=False)
         part = pick(template, plane)
         near1, near2 = (flipped(part, "orient", 2 * k) for k in (1, 2))
@@ -182,9 +193,10 @@
         near_x = flipped(near, "groups", 1)
         near_y = flipped(near, "orient", 1)
         far, near_x, near_y, coef = lax.optimization_barrier((far, near_x, near_y, coef))
-        last_x = flipped(jnp.concatenate([far[:half], near_y[half:side - 8]], 0), "groups", 1)
-        last_y = flipped(jnp.concatenate([far[:half], near_x[side - 8:]], 0), "orient", 1)
-        corner = flipped(near_x[half:], "orient", 3)
+        last_y = flipped(jnp.concatenate([far[:half], near_x[half + few:]], 0), "orient", 1)
+        last_x = flipped(jnp.concatenate([far[:half], near_y[half:half + few]], 0), "groups", 1)
+        second = jnp.where(lax.axis_index("tile") == 0, near_x[half:], near_y[half:])
+        corner = crossed(second, (0, 3), (1, 2))
         block = lambda array, start=0, rows=half: ((array, start, start + rows),)
         early = maps(
             [template, beside],
@@ -196,7 +208,7 @@
             [],
             [near_y, last_x, last_y, far, corner],
             (
-                (block(0, half), block(1, half, most) + block(2, half, 8)),
+                (block(0, half), block(1, half, few) + block(2, half, half - few)),
                 (block(3), block(1)),
                 (block(2), block(4)),
             ),

time: 35 us -> 34.9 us (level)
    ppermute x11 -> x10, waiting for transfers between devices: 13.2 us -> 10.4 us  [flipped(): lax.ppermute(x, axis, [(i, i ^ bits) for i in range(lax.axis_size(axis))])]
    ppermute x0 -> x1, waiting for transfers between devices: none -> 2.72 us  [crossed(): return lax.ppermute(x, ('groups', 'orient', 'tile'), pairs)]
    ppermute x11 -> x10, starting transfers between devices: 15.2 us -> 13.4 us  [flipped(): lax.ppermute(x, axis, [(i, i ^ bits) for i in range(lax.axis_size(axis))])]
    ppermute x0 -> x1, starting transfers between devices: none -> 1.67 us  [crossed(): return lax.ppermute(x, ('groups', 'orient', 'tile'), pairs)]
where the time goes in v11:
time: 34.9 us; the launch traced here: 34.8 us
  starting transfers between devices  15.1 us (43%)
  waiting for transfers between devices  13.2 us (38%)
  Pallas kernels  4.6 us (13%)
  local copies, waits for them, and re-layouts  1.07 us (3%)
  between operations  0.77 us (2%)
    ppermute x10, starting transfers between devices, flipped(): lax.ppermute(x, axis, [(i, i ^ bits) for i in range(lax.axis_size(axis))])  13.4 us
    ppermute x10, waiting for transfers between devices, flipped(): lax.ppermute(x, axis, [(i, i ^ bits) for i in range(lax.axis_size(axis))])  10.4 us
    ppermute x1, waiting for transfers between devices, crossed(): return lax.ppermute(x, ('groups', 'orient', 'tile'), pairs)  2.72 us
    pallas_call x2, Pallas kernels, maps(): pl.pallas_call(functools.partial(maps_kernel, len(wholes), places), in_sp...  2.65 us
    ppermute x1, starting transfers between devices, crossed(): return lax.ppermute(x, ('groups', 'orient', 'tile'), pairs)  1.67 us
    pallas_call x1, Pallas kernels, shards(): pl.pallas_call(functools.partial(stats_kernel, len(keeps), 2 * side * sid...  1.2 us
    squeeze x2, local copies, waits for them, and re-layouts, shards(): lax.dynamic_index_in_dim(whole, n, 0, keepdims=False)  0.98 us
    pallas_call x1, Pallas kernels, shards(): pl.pallas_call(prepare_kernel, in_specs=[hbm] * 3, out_specs=[vmem] * 3,...  0.75 us
  transfers between devices with their start and end apart: 11, of which 7 were waited for; matrix products, arithmetic and copies ran while one was open for 0% of the time, Pallas kernels for 10%

profile of v11, /device:TPU:0, one launch (start us, length us, event | category | flops | bytes accessed | tf_op | source)
XLA Modules:
  0.0 34.8 jit_solution(12493424527806778810)
XLA Ops:
  0.6 0.0 copy-start
  0.6 1.0 %dynamic-slice_bitcast_fusion.1 = f32[128,256]{1,0:T(8,128)S(1)} fusion(f32[1,2,128,256]{3,2,1,0:T(8,128)} %param.6, s32[]{:T(128)S(6)} %select_n.15), kind=kLoop, calls=%fused_computation.5 | loop fusion | bytes 262148 | tf_op jit(solution)/shard_map/jit(dynamic_index_in_dim)/squeeze | solution.py:186
  1.6 0.0 copy-done
  1.6 3.0 %collective-permute-start.2 = (f32[2,128,256]{2,1,0:T(8,128)S(1)}, f32[2,128,256]{2,1,0:T(8,128)S(1)}, u32[]{:S(2)}, u32[]{:S(2)}) collective-permute-start(f32[2,128,256]{2,1,0:T(8,128)S(1)} %bitcast.6), channel_id=1, source_target_pairs={{0,2},{2,0},{4,6},{6,4},{8,10},{10,8},{12,14},{14,12},{1,3},{3,1},... | collective-permute-start | bytes 786440 | tf_op jit(solution)/shard_map/ppermute | solution.py:137
  4.7 2.6 %collective-permute-start.1 = (f32[128,256]{1,0:T(8,128)S(1)}, f32[128,256]{1,0:T(8,128)S(1)}, u32[]{:S(2)}, u32[]{:S(2)}) collective-permute-start(f32[128,256]{1,0:T(8,128)S(1)} %dynamic-slice_bitcast_fusion.1), channel_id=1, source_target_pairs={{0,8},{2,10},{4,12},{6,14},{8,0},{10,2},{12,4},{14,6},{1,9},{3,11}... | collective-permute-start | bytes 393224 | tf_op jit(solution)/shard_map/ppermute | solution.py:137
  7.3 1.6 %collective-permute-start = (f32[128,256]{1,0:T(8,128)S(1)}, f32[128,256]{1,0:T(8,128)S(1)}, u32[]{:S(2)}, u32[]{:S(2)}) collective-permute-start(f32[128,256]{1,0:T(8,128)S(1)} %dynamic-slice_bitcast_fusion.1), channel_id=1, source_target_pairs={{0,4},{2,6},{4,0},{6,2},{8,12},{10,14},{12,8},{14,10},{1,5},{3,7},... | collective-permute-start | bytes 393224 | tf_op jit(solution)/shard_map/ppermute | solution.py:137
  8.8 4.6 %collective-permute-done.1 = f32[128,256]{1,0:T(8,128)S(1)} collective-permute-done((f32[128,256]{1,0:T(8,128)S(1)}, f32[128,256]{1,0:T(8,128)S(1)}, u32[]{:S(2)}, u32[]{:S(2)}) %collective-permute-start.1) | collective-permute-done | bytes 131104 | tf_op jit(solution)/shard_map/ppermute | solution.py:137
  13.4 0.2 collective-permute-done
  13.6 0.0 collective-permute-done.2.refs_1_
  13.7 0.0 copy-start.1
  13.7 0.5 %collective-permute-start.5 = (f32[256,256]{1,0:T(8,128)S(1)}, f32[256,256]{1,0:T(8,128)S(1)}, u32[]{:S(2)}, u32[]{:S(2)}) collective-permute-start(f32[256,256]{1,0:T(8,128)S(1)} %constant_dynamic-update-slice_fusion.refs_2_), channel_id=1, source_target_pairs={{0,2},{2,0},{4,6},{6,4},{8,10},{10,8},{12,14},{14,12},{1,3},{3,1},... | collective-permute-start | bytes 786440 | tf_op jit(solution)/shard_map/ppermute | solution.py:137
  14.2 1.5 %collective-permute-start.4 = (f32[256,256]{1,0:T(8,128)S(1)}, f32[256,256]{1,0:T(8,128)S(1)}, u32[]{:S(2)}, u32[]{:S(2)}) collective-permute-start(f32[256,256]{1,0:T(8,128)S(1)} %constant_dynamic-update-slice_fusion.refs_2_), channel_id=1, source_target_pairs={{0,16},{16,0},{1,17},{17,1},{2,18},{18,2},{3,19},{19,3},{4,20},{20... | collective-permute-start | bytes 786440 | tf_op jit(solution)/shard_map/ppermute | solution.py:137
  15.8 0.0 copy-start.2
  15.8 0.0 copy-start.3
  15.8 1.4 %collective-permute-start.3 = (f32[256,256]{1,0:T(8,128)S(1)}, f32[256,256]{1,0:T(8,128)S(1)}, u32[]{:S(2)}, u32[]{:S(2)}) collective-permute-start(f32[256,256]{1,0:T(8,128)S(1)} %pad_maximum_fusion), channel_id=1, source_target_pairs={{0,4},{2,6},{4,0},{6,2},{8,12},{10,14},{12,8},{14,10},{1,5},{3,7},... | collective-permute-start | bytes 786440 | tf_op jit(solution)/shard_map/ppermute | solution.py:137
  17.3 0.0 copy-done.1
  17.3 0.0 copy-done.2
  17.3 0.0 copy-done.3
  17.3 0.7 %prepare.1 = (f32[4,128,256]{2,1,0:T(8,128)S(1)}, bf16[2,256,256]{2,1,0:T(8,128)(2,1)S(1)}, bf16[2,256,256]{2,1,0:T(8,128)(2,1)S(1)}) custom-call(f32[2,128,256]{2,1,0:T(8,128)S(1)} %bitcast.8, f32[256,256]{1,0:T(8,128)S(1)} %copy-done.3, f32[2,256,256]{2,1,0:T(8,128)S(1)} %copy-done.1), custom_call_target="tpu_custom_call" | custom-call | tf_op jit(solution)/shard_map/prepare/pallas_call | solution.py:161
  18.0 2.1 %collective-permute-done.5.refs_4_.refs_0_ = f32[256,256]{1,0:T(8,128)S(1)} collective-permute-done((f32[256,256]{1,0:T(8,128)S(1)}, f32[256,256]{1,0:T(8,128)S(1)}, u32[]{:S(2)}, u32[]{:S(2)}) %collective-permute-start.5) | collective-permute-done | bytes 262176 | tf_op jit(solution)/shard_map/ppermute | solution.py:137
  20.1 0.5 %collective-permute-done.4.refs_3_ = f32[256,256]{1,0:T(8,128)S(1)} collective-permute-done((f32[256,256]{1,0:T(8,128)S(1)}, f32[256,256]{1,0:T(8,128)S(1)}, u32[]{:S(2)}, u32[]{:S(2)}) %collective-permute-start.4) | collective-permute-done | bytes 262176 | tf_op jit(solution)/shard_map/ppermute | solution.py:137
  20.6 1.7 %collective-permute-done.3.refs_5_.refs_3_ = f32[256,256]{1,0:T(8,128)S(1)} collective-permute-done((f32[256,256]{1,0:T(8,128)S(1)}, f32[256,256]{1,0:T(8,128)S(1)}, u32[]{:S(2)}, u32[]{:S(2)}) %collective-permute-start.3) | collective-permute-done | bytes 262176 | tf_op jit(solution)/shard_map/ppermute | solution.py:137
  22.3 0.5 %collective-permute-start.6 = (f32[152,256]{1,0:T(8,128)S(1)}, f32[152,256]{1,0:T(8,128)S(1)}, u32[]{:S(2)}, u32[]{:S(2)}) collective-permute-start(f32[152,256]{1,0:T(8,128)S(1)} %pad_maximum_fusion.2), channel_id=1, source_target_pairs={{0,16},{16,0},{1,17},{17,1},{2,18},{18,2},{3,19},{19,3},{4,20},{20... | collective-permute-start | bytes 466952 | tf_op jit(solution)/shard_map/ppermute | solution.py:137
  22.9 1.6 %collective-permute-start.7 = (f32[232,256]{1,0:T(8,128)S(1)}, f32[232,256]{1,0:T(8,128)S(1)}, u32[]{:S(2)}, u32[]{:S(2)}) collective-permute-start(f32[232,256]{1,0:T(8,128)S(1)} %pad_maximum_fusion.1), channel_id=1, source_target_pairs={{0,2},{2,0},{4,6},{6,4},{8,10},{10,8},{12,14},{14,12},{1,3},{3,1},... | collective-permute-start | bytes 712712 | tf_op jit(solution)/shard_map/ppermute | solution.py:137
  24.5 1.7 %collective-permute-start.8 = (f32[128,256]{1,0:T(8,128)S(1)}, f32[128,256]{1,0:T(8,128)S(1)}, u32[]{:S(2)}, u32[]{:S(2)}) collective-permute-start(f32[128,256]{1,0:T(8,128)S(1)} %slice_select_fusion), channel_id=1, source_target_pairs={{0,6},{1,21},{2,4},{3,23},{4,2},{5,17},{6,0},{7,19},{8,14},{9,29},... | collective-permute-start | bytes 393224 | tf_op jit(solution)/shard_map/ppermute | solution.py:148
  26.1 1.5 %maps.2 = (f32[5,136,256]{2,1,0:T(8,128)S(1)}, f32[5,136,256]{2,1,0:T(8,128)S(1)}) custom-call(f32[4,128,256]{2,1,0:T(8,128)S(1)} %get-tuple-element.31.coef_ref, bf16[2,256,256]{2,1,0:T(8,128)(2,1)S(1)} %get-tuple-element.32.rt_ref, bf16[2,256,256]{2,1,0:T(8,128)(2,1)S(1)} %get-tuple-element.33.col_ref, f32[2,128,256]{2,1,0:T(8,128)S(1)} %bitcast.7, ...), custom_call_target="tpu_custom_call" | custom-call | tf_op jit(solution)/shard_map/maps/pallas_call | solution.py:174
  27.7 2.7 %collective-permute-done.8.refs_4_ = f32[128,256]{1,0:T(8,128)S(1)} collective-permute-done((f32[128,256]{1,0:T(8,128)S(1)}, f32[128,256]{1,0:T(8,128)S(1)}, u32[]{:S(2)}, u32[]{:S(2)}) %collective-permute-start.8) | collective-permute-done | bytes 131104 | tf_op jit(solution)/shard_map/ppermute | solution.py:148
  30.4 0.0 collective-permute-done.6.refs_1_
  30.4 0.0 collective-permute-done.7.refs_2_
  30.4 0.0 copy-start.4
  30.4 0.1 collective-permute-start.9
  30.5 1.1 %maps.3 = (f32[3,136,256]{2,1,0:T(8,128)S(1)}, f32[3,136,256]{2,1,0:T(8,128)S(1)}) custom-call(f32[4,128,256]{2,1,0:T(8,128)S(1)} %get-tuple-element.31.coef_ref, bf16[2,256,256]{2,1,0:T(8,128)(2,1)S(1)} %get-tuple-element.32.rt_ref, bf16[2,256,256]{2,1,0:T(8,128)(2,1)S(1)} %get-tuple-element.33.col_ref, ...), custom_call_target="tpu_custom_call" | custom-call | tf_op jit(solution)/shard_map/maps/pallas_call | solution.py:174
  31.6 0.6 %collective-permute-start.10 = (f32[3,136,256]{2,1,0:T(8,128)S(1)}, f32[3,136,256]{2,1,0:T(8,128)S(1)}, u32[]{:S(2)}, u32[]{:S(2)}) collective-permute-start(f32[3,136,256]{2,1,0:T(8,128)S(1)} %get-tuple-element.42), channel_id=1, source_target_pairs={{0,1},{1,0},{2,3},{3,2},{4,5},{5,4},{6,7},{7,6},{8,9},{9,8},{10,11... | collective-permute-start | bytes 1253384 | tf_op jit(solution)/shard_map/ppermute | solution.py:137
  32.2 1.4 %collective-permute-done.10.refs_3_ = f32[3,136,256]{2,1,0:T(8,128)S(1)} collective-permute-done((f32[3,136,256]{2,1,0:T(8,128)S(1)}, f32[3,136,256]{2,1,0:T(8,128)S(1)}, u32[]{:S(2)}, u32[]{:S(2)}) %collective-permute-start.10) | collective-permute-done | bytes 417824 | tf_op jit(solution)/shard_map/ppermute | solution.py:137
  33.6 0.0 collective-permute-done.9.refs_2_
  33.6 0.0 copy-done.4
  33.6 1.2 %statistics.1 = (f32[1,128,256]{2,1,0:T(8,128)}, f32[1,128,256]{2,1,0:T(8,128)}, f32[1,128,256]{2,1,0:T(8,128)}) custom-call(f32[5,136,256]{2,1,0:T(8,128)S(1)} %get-tuple-element.36.refs_0_, f32[3,136,256]{2,1,0:T(8,128)S(1)} %get-tuple-element.40.refs_1_, f32[5,136,256]{2,1,0:T(8,128)S(1)} %collective-permute-done.9.refs_2_, ...), custom_call_target="tpu_custom_call" | custom-call | tf_op jit(solution)/shard_map/statistics/pallas_call | solution.py:222
  (10 shorter events, 0.1 us)
Async XLA Ops:
  0.6 1.0 %copy-start = (f32[1,2,128,256]{3,2,1,0:T(8,128)S(1)}, f32[1,2,128,256]{3,2,1,0:T(8,128)}, u32[]{:S(2)}) copy-start(f32[1,2,128,256]{3,2,1,0:T(8,128)} %param.6) | copy-start | bytes 786436
  1.6 12.0 %collective-permute-start.2 = (f32[2,128,256]{2,1,0:T(8,128)S(1)}, f32[2,128,256]{2,1,0:T(8,128)S(1)}, u32[]{:S(2)}, u32[]{:S(2)}) collective-permute-start(f32[2,128,256]{2,1,0:T(8,128)S(1)} %bitcast.6), channel_id=1, source_target_pairs={{0,2},{2,0},{4,6},{6,4},{8,10},{10,8},{12,14},{14,12},{1,3},{3,1},... | collective-permute-start | bytes 786440 | tf_op jit(solution)/shard_map/ppermute | solution.py:137
  4.7 8.8 %collective-permute-start.1 = (f32[128,256]{1,0:T(8,128)S(1)}, f32[128,256]{1,0:T(8,128)S(1)}, u32[]{:S(2)}, u32[]{:S(2)}) collective-permute-start(f32[128,256]{1,0:T(8,128)S(1)} %dynamic-slice_bitcast_fusion.1), channel_id=1, source_target_pairs={{0,8},{2,10},{4,12},{6,14},{8,0},{10,2},{12,4},{14,6},{1,9},{3,11}... | collective-permute-start | bytes 393224 | tf_op jit(solution)/shard_map/ppermute | solution.py:137
  7.3 6.4 %collective-permute-start = (f32[128,256]{1,0:T(8,128)S(1)}, f32[128,256]{1,0:T(8,128)S(1)}, u32[]{:S(2)}, u32[]{:S(2)}) collective-permute-start(f32[128,256]{1,0:T(8,128)S(1)} %dynamic-slice_bitcast_fusion.1), channel_id=1, source_target_pairs={{0,4},{2,6},{4,0},{6,2},{8,12},{10,14},{12,8},{14,10},{1,5},{3,7},... | collective-permute-start | bytes 393224 | tf_op jit(solution)/shard_map/ppermute | solution.py:137
  13.7 3.6 %copy-start.1 = (f32[2,256,256]{2,1,0:T(8,128)S(1)}, f32[2,256,256]{2,1,0:T(8,128)}, u32[]{:S(2)}) copy-start(f32[2,256,256]{2,1,0:T(8,128)} %constant.26.clone.table_hbm) | copy-start | bytes 1572868
  13.7 6.4 %collective-permute-start.5 = (f32[256,256]{1,0:T(8,128)S(1)}, f32[256,256]{1,0:T(8,128)S(1)}, u32[]{:S(2)}, u32[]{:S(2)}) collective-permute-start(f32[256,256]{1,0:T(8,128)S(1)} %constant_dynamic-update-slice_fusion.refs_2_), channel_id=1, source_target_pairs={{0,2},{2,0},{4,6},{6,4},{8,10},{10,8},{12,14},{14,12},{1,3},{3,1},... | collective-permute-start | bytes 786440 | tf_op jit(solution)/shard_map/ppermute | solution.py:137
  14.2 6.4 %collective-permute-start.4 = (f32[256,256]{1,0:T(8,128)S(1)}, f32[256,256]{1,0:T(8,128)S(1)}, u32[]{:S(2)}, u32[]{:S(2)}) collective-permute-start(f32[256,256]{1,0:T(8,128)S(1)} %constant_dynamic-update-slice_fusion.refs_2_), channel_id=1, source_target_pairs={{0,16},{16,0},{1,17},{17,1},{2,18},{18,2},{3,19},{19,3},{4,20},{20... | collective-permute-start | bytes 786440 | tf_op jit(solution)/shard_map/ppermute | solution.py:137
  15.8 1.5 %copy-start.2 = (f32[1,2,128,256]{3,2,1,0:T(8,128)S(1)}, f32[1,2,128,256]{3,2,1,0:T(8,128)}, u32[]{:S(2)}) copy-start(f32[1,2,128,256]{3,2,1,0:T(8,128)} %param.5) | copy-start | bytes 786436
  15.8 1.5 %copy-start.3 = (f32[256,256]{1,0:T(8,128)S(1)}, f32[256,256]{1,0:T(8,128)}, u32[]{:S(2)}) copy-start(f32[256,256]{1,0:T(8,128)} %w_hbm.1) | copy-start | bytes 786436
  15.8 6.4 %collective-permute-start.3 = (f32[256,256]{1,0:T(8,128)S(1)}, f32[256,256]{1,0:T(8,128)S(1)}, u32[]{:S(2)}, u32[]{:S(2)}) collective-permute-start(f32[256,256]{1,0:T(8,128)S(1)} %pad_maximum_fusion), channel_id=1, source_target_pairs={{0,4},{2,6},{4,0},{6,2},{8,12},{10,14},{12,8},{14,10},{1,5},{3,7},... | collective-permute-start | bytes 786440 | tf_op jit(solution)/shard_map/ppermute | solution.py:137
  22.3 8.1 %collective-permute-start.6 = (f32[152,256]{1,0:T(8,128)S(1)}, f32[152,256]{1,0:T(8,128)S(1)}, u32[]{:S(2)}, u32[]{:S(2)}) collective-permute-start(f32[152,256]{1,0:T(8,128)S(1)} %pad_maximum_fusion.2), channel_id=1, source_target_pairs={{0,16},{16,0},{1,17},{17,1},{2,18},{18,2},{3,19},{19,3},{4,20},{20... | collective-permute-start | bytes 466952 | tf_op jit(solution)/shard_map/ppermute | solution.py:137
  22.9 7.5 %collective-permute-start.7 = (f32[232,256]{1,0:T(8,128)S(1)}, f32[232,256]{1,0:T(8,128)S(1)}, u32[]{:S(2)}, u32[]{:S(2)}) collective-permute-start(f32[232,256]{1,0:T(8,128)S(1)} %pad_maximum_fusion.1), channel_id=1, source_target_pairs={{0,2},{2,0},{4,6},{6,4},{8,10},{10,8},{12,14},{14,12},{1,3},{3,1},... | collective-permute-start | bytes 712712 | tf_op jit(solution)/shard_map/ppermute | solution.py:137
  24.5 5.9 %collective-permute-start.8 = (f32[128,256]{1,0:T(8,128)S(1)}, f32[128,256]{1,0:T(8,128)S(1)}, u32[]{:S(2)}, u32[]{:S(2)}) collective-permute-start(f32[128,256]{1,0:T(8,128)S(1)} %slice_select_fusion), channel_id=1, source_target_pairs={{0,6},{1,21},{2,4},{3,23},{4,2},{5,17},{6,0},{7,19},{8,14},{9,29},... | collective-permute-start | bytes 393224 | tf_op jit(solution)/shard_map/ppermute | solution.py:148
  30.4 3.2 %copy-start.4 = (f32[128,128]{1,0:T(8,128)S(1)}, f32[128,128]{1,0:T(8,128)}, u32[]{:S(2)}) copy-start(f32[128,128]{1,0:T(8,128)} %constant.27.clone.refs_4_) | copy-start | bytes 196612
  30.4 3.1 %collective-permute-start.9 = (f32[5,136,256]{2,1,0:T(8,128)S(1)}, f32[5,136,256]{2,1,0:T(8,128)S(1)}, u32[]{:S(2)}, u32[]{:S(2)}) collective-permute-start(f32[5,136,256]{2,1,0:T(8,128)S(1)} %get-tuple-element.41), channel_id=1, source_target_pairs={{0,1},{1,0},{2,3},{3,2},{4,5},{5,4},{6,7},{7,6},{8,9},{9,8},{10,11... | collective-permute-start | bytes 2088968 | tf_op jit(solution)/shard_map/ppermute | solution.py:137
  31.6 1.9 %collective-permute-start.10 = (f32[3,136,256]{2,1,0:T(8,128)S(1)}, f32[3,136,256]{2,1,0:T(8,128)S(1)}, u32[]{:S(2)}, u32[]{:S(2)}) collective-permute-start(f32[3,136,256]{2,1,0:T(8,128)S(1)} %get-tuple-element.42), channel_id=1, source_target_pairs={{0,1},{1,0},{2,3},{3,2},{4,5},{5,4},{6,7},{7,6},{8,9},{9,8},{10,11... | collective-permute-start | bytes 1253384 | tf_op jit(solution)/shard_map/ppermute | solution.py:137

commit v12 on v11

--- a/solution.py
+++ b/solution.py
@@ -182,7 +182,7 @@
 
     if lax.axis_size("groups") == 2 and orients == 8:
         plane = lax.axis_index("groups")
-        few = 24
+        few = 104
         pick = lambda whole, n: lax.dynamic_index_in_dim(whole, n, 0, keepdims=False)
         part = pick(template, plane)
         near1, near2 = (flipped(part, "orient", 2 * k) for k in (1, 2))

time: 34.9 us -> 36.7 us (1.052)
  the two profiles are of different devices: /device:TPU:0 before, /device:TPU:17 now
where the time goes in v12:
time: 36.7 us; the launch traced here: 36.6 us
  waiting for transfers between devices  15.7 us (43%)
  starting transfers between devices  13.3 us (36%)
  Pallas kernels  4.79 us (13%)
  local copies, waits for them, and re-layouts  1.94 us (5%)
  between operations  0.76 us (2%)
    ppermute x10, waiting for transfers between devices, flipped(): lax.ppermute(x, axis, [(i, i ^ bits) for i in range(lax.axis_size(axis))])  14.7 us
    ppermute x10, starting transfers between devices, flipped(): lax.ppermute(x, axis, [(i, i ^ bits) for i in range(lax.axis_size(axis))])  11.1 us
    pallas_call x2, Pallas kernels, maps(): pl.pallas_call(functools.partial(maps_kernel, len(wholes), places), in_sp...  2.85 us
    ppermute x1, starting transfers between devices, crossed(): return lax.ppermute(x, ('groups', 'orient', 'tile'), pairs)  2.14 us
    pallas_call x1, Pallas kernels, shards(): pl.pallas_call(functools.partial(stats_kernel, len(keeps), 2 * side * sid...  1.2 us
    ppermute x1, waiting for transfers between devices, crossed(): return lax.ppermute(x, ('groups', 'orient', 'tile'), pairs)  1.05 us
    squeeze x2, local copies, waits for them, and re-layouts, shards(): lax.dynamic_index_in_dim(whole, n, 0, keepdims=False)  0.98 us
    slice x2, local copies, waits for them, and re-layouts, shards(): near_y[half:half + few]  0.87 us
  transfers between devices with their start and end apart: 11, of which 8 were waited for; matrix products, arithmetic and copies ran while one was open for 0% of the time, Pallas kernels for 10%

profile of v12, /device:TPU:17, one launch (start us, length us, event | category | flops | bytes accessed | tf_op | source)
XLA Modules:
  0.0 36.6 jit_solution(11601321900108964113)
XLA Ops:
  0.6 0.0 copy-start.2
  0.6 1.0 %dynamic-slice_bitcast_fusion.1 = f32[128,256]{1,0:T(8,128)S(1)} fusion(f32[1,2,128,256]{3,2,1,0:T(8,128)} %param.6, s32[]{:T(128)S(6)} %select_n.15), kind=kLoop, calls=%fused_computation.5 | loop fusion | bytes 262148 | tf_op jit(solution)/shard_map/jit(dynamic_index_in_dim)/squeeze | solution.py:186
  1.6 0.0 copy-done.2
  1.6 1.3 %collective-permute-start.2 = (f32[2,128,256]{2,1,0:T(8,128)S(1)}, f32[2,128,256]{2,1,0:T(8,128)S(1)}, u32[]{:S(2)}, u32[]{:S(2)}) collective-permute-start(f32[2,128,256]{2,1,0:T(8,128)S(1)} %bitcast.6), channel_id=1, source_target_pairs={{0,2},{2,0},{4,6},{6,4},{8,10},{10,8},{12,14},{14,12},{1,3},{3,1},... | collective-permute-start | bytes 786440 | tf_op jit(solution)/shard_map/ppermute | solution.py:137
  2.9 0.1 collective-permute-start.1
  3.0 1.3 %collective-permute-start = (f32[128,256]{1,0:T(8,128)S(1)}, f32[128,256]{1,0:T(8,128)S(1)}, u32[]{:S(2)}, u32[]{:S(2)}) collective-permute-start(f32[128,256]{1,0:T(8,128)S(1)} %dynamic-slice_bitcast_fusion.1), channel_id=1, source_target_pairs={{0,4},{2,6},{4,0},{6,2},{8,12},{10,14},{12,8},{14,10},{1,5},{3,7},... | collective-permute-start | bytes 393224 | tf_op jit(solution)/shard_map/ppermute | solution.py:137
  4.3 3.5 %collective-permute-done.1 = f32[128,256]{1,0:T(8,128)S(1)} collective-permute-done((f32[128,256]{1,0:T(8,128)S(1)}, f32[128,256]{1,0:T(8,128)S(1)}, u32[]{:S(2)}, u32[]{:S(2)}) %collective-permute-start.1) | collective-permute-done | bytes 131104 | tf_op jit(solution)/shard_map/ppermute | solution.py:137
  7.8 2.0 %collective-permute-done = f32[128,256]{1,0:T(8,128)S(1)} collective-permute-done((f32[128,256]{1,0:T(8,128)S(1)}, f32[128,256]{1,0:T(8,128)S(1)}, u32[]{:S(2)}, u32[]{:S(2)}) %collective-permute-start) | collective-permute-done | bytes 131104 | tf_op jit(solution)/shard_map/ppermute | solution.py:137
  9.8 0.0 collective-permute-done.2.refs_1_
  9.8 0.0 copy-start.3
  9.8 0.4 %collective-permute-start.5 = (f32[256,256]{1,0:T(8,128)S(1)}, f32[256,256]{1,0:T(8,128)S(1)}, u32[]{:S(2)}, u32[]{:S(2)}) collective-permute-start(f32[256,256]{1,0:T(8,128)S(1)} %constant_dynamic-update-slice_fusion.refs_2_), channel_id=1, source_target_pairs={{0,2},{2,0},{4,6},{6,4},{8,10},{10,8},{12,14},{14,12},{1,3},{3,1},... | collective-permute-start | bytes 786440 | tf_op jit(solution)/shard_map/ppermute | solution.py:137
  10.2 1.2 %collective-permute-start.4 = (f32[256,256]{1,0:T(8,128)S(1)}, f32[256,256]{1,0:T(8,128)S(1)}, u32[]{:S(2)}, u32[]{:S(2)}) collective-permute-start(f32[256,256]{1,0:T(8,128)S(1)} %constant_dynamic-update-slice_fusion.refs_2_), channel_id=1, source_target_pairs={{0,16},{16,0},{1,17},{17,1},{2,18},{18,2},{3,19},{19,3},{4,20},{20... | collective-permute-start | bytes 786440 | tf_op jit(solution)/shard_map/ppermute | solution.py:137
  11.4 0.0 copy-start.4
  11.5 0.0 copy-start.5
  11.5 3.4 %collective-permute-start.3 = (f32[256,256]{1,0:T(8,128)S(1)}, f32[256,256]{1,0:T(8,128)S(1)}, u32[]{:S(2)}, u32[]{:S(2)}) collective-permute-start(f32[256,256]{1,0:T(8,128)S(1)} %pad_maximum_fusion), channel_id=1, source_target_pairs={{0,4},{2,6},{4,0},{6,2},{8,12},{10,14},{12,8},{14,10},{1,5},{3,7},... | collective-permute-start | bytes 786440 | tf_op jit(solution)/shard_map/ppermute | solution.py:137
  14.9 0.0 copy-done.3
  14.9 0.0 copy-done.4
  14.9 0.0 copy-done.5
  14.9 0.7 %prepare.1 = (f32[4,128,256]{2,1,0:T(8,128)S(1)}, bf16[2,256,256]{2,1,0:T(8,128)(2,1)S(1)}, bf16[2,256,256]{2,1,0:T(8,128)(2,1)S(1)}) custom-call(f32[2,128,256]{2,1,0:T(8,128)S(1)} %bitcast.8, f32[256,256]{1,0:T(8,128)S(1)} %copy-done.5, f32[2,256,256]{2,1,0:T(8,128)S(1)} %copy-done.3), custom_call_target="tpu_custom_call" | custom-call | tf_op jit(solution)/shard_map/prepare/pallas_call | solution.py:161
  15.7 0.2 collective-permute-done.5.refs_4_.refs_0_
  15.9 0.0 copy-start
  15.9 0.2 collective-permute-done.4.refs_3_
  16.0 4.5 %collective-permute-done.3.refs_5_.refs_3_ = f32[256,256]{1,0:T(8,128)S(1)} collective-permute-done((f32[256,256]{1,0:T(8,128)S(1)}, f32[256,256]{1,0:T(8,128)S(1)}, u32[]{:S(2)}, u32[]{:S(2)}) %collective-permute-start.3) | collective-permute-done | bytes 262176 | tf_op jit(solution)/shard_map/ppermute | solution.py:137
  20.5 0.0 copy-done
  20.6 0.0 slice-start
  20.6 0.9 %slice-done = f32[104,256]{1,0:T(8,128)S(1)} async-done(((f32[256,256]{1,0:T(8,128)}), f32[104,256]{1,0:T(8,128)S(1)}, s32[]{:S(2)}) %slice-start) | async-done | bytes 106520 | tf_op jit(solution)/shard_map/slice | solution.py:197
  21.4 0.0 copy-start.1
  21.5 1.3 %collective-permute-start.7 = (f32[152,256]{1,0:T(8,128)S(1)}, f32[152,256]{1,0:T(8,128)S(1)}, u32[]{:S(2)}, u32[]{:S(2)}) collective-permute-start(f32[152,256]{1,0:T(8,128)S(1)} %pad_maximum_fusion.2), channel_id=1, source_target_pairs={{0,2},{2,0},{4,6},{6,4},{8,10},{10,8},{12,14},{14,12},{1,3},{3,1},... | collective-permute-start | bytes 466952 | tf_op jit(solution)/shard_map/ppermute | solution.py:137
  22.8 0.3 collective-permute-start.6
  23.0 0.0 copy-done.1
  23.1 2.1 %collective-permute-start.8 = (f32[128,256]{1,0:T(8,128)S(1)}, f32[128,256]{1,0:T(8,128)S(1)}, u32[]{:S(2)}, u32[]{:S(2)}) collective-permute-start(f32[128,256]{1,0:T(8,128)S(1)} %slice_select_fusion), channel_id=1, source_target_pairs={{0,6},{1,21},{2,4},{3,23},{4,2},{5,17},{6,0},{7,19},{8,14},{9,29},... | collective-permute-start | bytes 393224 | tf_op jit(solution)/shard_map/ppermute | solution.py:148
  25.2 1.7 %maps.2 = (f32[5,136,256]{2,1,0:T(8,128)S(1)}, f32[5,136,256]{2,1,0:T(8,128)S(1)}) custom-call(f32[4,128,256]{2,1,0:T(8,128)S(1)} %get-tuple-element.31.coef_ref, bf16[2,256,256]{2,1,0:T(8,128)(2,1)S(1)} %get-tuple-element.32.rt_ref, bf16[2,256,256]{2,1,0:T(8,128)(2,1)S(1)} %get-tuple-element.33.col_ref, f32[2,128,256]{2,1,0:T(8,128)S(1)} %bitcast.7, ...), custom_call_target="tpu_custom_call" | custom-call | tf_op jit(solution)/shard_map/maps/pallas_call | solution.py:174
  26.9 1.1 %collective-permute-done.8.refs_4_ = f32[128,256]{1,0:T(8,128)S(1)} collective-permute-done((f32[128,256]{1,0:T(8,128)S(1)}, f32[128,256]{1,0:T(8,128)S(1)}, u32[]{:S(2)}, u32[]{:S(2)}) %collective-permute-start.8) | collective-permute-done | bytes 131104 | tf_op jit(solution)/shard_map/ppermute | solution.py:148
  27.9 0.0 collective-permute-done.7.refs_2_
  27.9 2.6 %collective-permute-done.6.refs_1_ = f32[232,256]{1,0:T(8,128)S(1)} collective-permute-done((f32[232,256]{1,0:T(8,128)S(1)}, f32[232,256]{1,0:T(8,128)S(1)}, u32[]{:S(2)}, u32[]{:S(2)}) %collective-permute-start.6) | collective-permute-done | bytes 237600 | tf_op jit(solution)/shard_map/ppermute | solution.py:137
  30.6 0.0 copy-start.6
  30.6 1.8 %collective-permute-start.9 = (f32[5,136,256]{2,1,0:T(8,128)S(1)}, f32[5,136,256]{2,1,0:T(8,128)S(1)}, u32[]{:S(2)}, u32[]{:S(2)}) collective-permute-start(f32[5,136,256]{2,1,0:T(8,128)S(1)} %get-tuple-element.41), channel_id=1, source_target_pairs={{0,1},{1,0},{2,3},{3,2},{4,5},{5,4},{6,7},{7,6},{8,9},{9,8},{10,11... | collective-permute-start | bytes 2088968 | tf_op jit(solution)/shard_map/ppermute | solution.py:137
  32.4 1.2 %maps.3 = (f32[3,136,256]{2,1,0:T(8,128)S(1)}, f32[3,136,256]{2,1,0:T(8,128)S(1)}) custom-call(f32[4,128,256]{2,1,0:T(8,128)S(1)} %get-tuple-element.31.coef_ref, bf16[2,256,256]{2,1,0:T(8,128)(2,1)S(1)} %get-tuple-element.32.rt_ref, bf16[2,256,256]{2,1,0:T(8,128)(2,1)S(1)} %get-tuple-element.33.col_ref, f32[256,256]{1,0:T(8,128)S(1)} %copy-done.1, ...), custom_call_target="tpu_custom_call" | custom-call | tf_op jit(solution)/shard_map/maps/pallas_call | solution.py:174
  33.5 0.1 collective-permute-start.10
  33.6 1.7 %collective-permute-done.10.refs_3_ = f32[3,136,256]{2,1,0:T(8,128)S(1)} collective-permute-done((f32[3,136,256]{2,1,0:T(8,128)S(1)}, f32[3,136,256]{2,1,0:T(8,128)S(1)}, u32[]{:S(2)}, u32[]{:S(2)}) %collective-permute-start.10) | collective-permute-done | bytes 417824 | tf_op jit(solution)/shard_map/ppermute | solution.py:137
  35.4 0.0 collective-permute-done.9.refs_2_
  35.4 0.0 copy-done.6
  35.4 1.2 %statistics.1 = (f32[1,128,256]{2,1,0:T(8,128)}, f32[1,128,256]{2,1,0:T(8,128)}, f32[1,128,256]{2,1,0:T(8,128)}) custom-call(f32[5,136,256]{2,1,0:T(8,128)S(1)} %get-tuple-element.36.refs_0_, f32[3,136,256]{2,1,0:T(8,128)S(1)} %get-tuple-element.40.refs_1_, f32[5,136,256]{2,1,0:T(8,128)S(1)} %collective-permute-done.9.refs_2_, ...), custom_call_target="tpu_custom_call" | custom-call | tf_op jit(solution)/shard_map/statistics/pallas_call | solution.py:222
  (9 shorter events, 0.1 us)
Async XLA Ops:
  0.6 1.0 %copy-start.2 = (f32[1,2,128,256]{3,2,1,0:T(8,128)S(1)}, f32[1,2,128,256]{3,2,1,0:T(8,128)}, u32[]{:S(2)}) copy-start(f32[1,2,128,256]{3,2,1,0:T(8,128)} %param.6) | copy-start | bytes 786436
  1.6 8.1 %collective-permute-start.2 = (f32[2,128,256]{2,1,0:T(8,128)S(1)}, f32[2,128,256]{2,1,0:T(8,128)S(1)}, u32[]{:S(2)}, u32[]{:S(2)}) collective-permute-start(f32[2,128,256]{2,1,0:T(8,128)S(1)} %bitcast.6), channel_id=1, source_target_pairs={{0,2},{2,0},{4,6},{6,4},{8,10},{10,8},{12,14},{14,12},{1,3},{3,1},... | collective-permute-start | bytes 786440 | tf_op jit(solution)/shard_map/ppermute | solution.py:137
  2.9 4.8 %collective-permute-start.1 = (f32[128,256]{1,0:T(8,128)S(1)}, f32[128,256]{1,0:T(8,128)S(1)}, u32[]{:S(2)}, u32[]{:S(2)}) collective-permute-start(f32[128,256]{1,0:T(8,128)S(1)} %dynamic-slice_bitcast_fusion.1), channel_id=1, source_target_pairs={{0,8},{2,10},{4,12},{6,14},{8,0},{10,2},{12,4},{14,6},{1,9},{3,11}... | collective-permute-start | bytes 393224 | tf_op jit(solution)/shard_map/ppermute | solution.py:137
  3.0 6.8 %collective-permute-start = (f32[128,256]{1,0:T(8,128)S(1)}, f32[128,256]{1,0:T(8,128)S(1)}, u32[]{:S(2)}, u32[]{:S(2)}) collective-permute-start(f32[128,256]{1,0:T(8,128)S(1)} %dynamic-slice_bitcast_fusion.1), channel_id=1, source_target_pairs={{0,4},{2,6},{4,0},{6,2},{8,12},{10,14},{12,8},{14,10},{1,5},{3,7},... | collective-permute-start | bytes 393224 | tf_op jit(solution)/shard_map/ppermute | solution.py:137
  9.8 5.1 %copy-start.3 = (f32[2,256,256]{2,1,0:T(8,128)S(1)}, f32[2,256,256]{2,1,0:T(8,128)}, u32[]{:S(2)}) copy-start(f32[2,256,256]{2,1,0:T(8,128)} %constant.26.clone.table_hbm) | copy-start | bytes 1572868
  9.8 6.0 %collective-permute-start.5 = (f32[256,256]{1,0:T(8,128)S(1)}, f32[256,256]{1,0:T(8,128)S(1)}, u32[]{:S(2)}, u32[]{:S(2)}) collective-permute-start(f32[256,256]{1,0:T(8,128)S(1)} %constant_dynamic-update-slice_fusion.refs_2_), channel_id=1, source_target_pairs={{0,2},{2,0},{4,6},{6,4},{8,10},{10,8},{12,14},{14,12},{1,3},{3,1},... | collective-permute-start | bytes 786440 | tf_op jit(solution)/shard_map/ppermute | solution.py:137
  10.2 5.8 %collective-permute-start.4 = (f32[256,256]{1,0:T(8,128)S(1)}, f32[256,256]{1,0:T(8,128)S(1)}, u32[]{:S(2)}, u32[]{:S(2)}) collective-permute-start(f32[256,256]{1,0:T(8,128)S(1)} %constant_dynamic-update-slice_fusion.refs_2_), channel_id=1, source_target_pairs={{0,16},{16,0},{1,17},{17,1},{2,18},{18,2},{3,19},{19,3},{4,20},{20... | collective-permute-start | bytes 786440 | tf_op jit(solution)/shard_map/ppermute | solution.py:137
  11.4 3.5 %copy-start.4 = (f32[1,2,128,256]{3,2,1,0:T(8,128)S(1)}, f32[1,2,128,256]{3,2,1,0:T(8,128)}, u32[]{:S(2)}) copy-start(f32[1,2,128,256]{3,2,1,0:T(8,128)} %param.5) | copy-start | bytes 786436
  11.5 3.5 %copy-start.5 = (f32[256,256]{1,0:T(8,128)S(1)}, f32[256,256]{1,0:T(8,128)}, u32[]{:S(2)}) copy-start(f32[256,256]{1,0:T(8,128)} %w_hbm.1) | copy-start | bytes 786436
  11.5 9.0 %collective-permute-start.3 = (f32[256,256]{1,0:T(8,128)S(1)}, f32[256,256]{1,0:T(8,128)S(1)}, u32[]{:S(2)}, u32[]{:S(2)}) collective-permute-start(f32[256,256]{1,0:T(8,128)S(1)} %pad_maximum_fusion), channel_id=1, source_target_pairs={{0,4},{2,6},{4,0},{6,2},{8,12},{10,14},{12,8},{14,10},{1,5},{3,7},... | collective-permute-start | bytes 786440 | tf_op jit(solution)/shard_map/ppermute | solution.py:137
  15.9 4.7 %copy-start = (f32[256,256]{1,0:T(8,128)}, f32[256,256]{1,0:T(8,128)S(1)}, u32[]{:S(2)}) copy-start(f32[256,256]{1,0:T(8,128)S(1)} %collective-permute-done.5.refs_4_.refs_0_) | copy-start | bytes 786436
  20.6 0.9 %slice-start = ((f32[256,256]{1,0:T(8,128)}), f32[104,256]{1,0:T(8,128)S(1)}, s32[]{:S(2)}) async-start(f32[256,256]{1,0:T(8,128)} %copy-done), calls=%async_computation | async-start | bytes 212992 | tf_op jit(solution)/shard_map/slice | solution.py:197
  21.4 1.6 %copy-start.1 = (f32[256,256]{1,0:T(8,128)S(1)}, f32[256,256]{1,0:T(8,128)}, u32[]{:S(2)}) copy-start(f32[256,256]{1,0:T(8,128)} %copy-done) | copy-start | bytes 786436
  21.5 6.5 %collective-permute-start.7 = (f32[152,256]{1,0:T(8,128)S(1)}, f32[152,256]{1,0:T(8,128)S(1)}, u32[]{:S(2)}, u32[]{:S(2)}) collective-permute-start(f32[152,256]{1,0:T(8,128)S(1)} %pad_maximum_fusion.2), channel_id=1, source_target_pairs={{0,2},{2,0},{4,6},{6,4},{8,10},{10,8},{12,14},{14,12},{1,3},{3,1},... | collective-permute-start | bytes 466952 | tf_op jit(solution)/shard_map/ppermute | solution.py:137
  22.8 7.8 %collective-permute-start.6 = (f32[232,256]{1,0:T(8,128)S(1)}, f32[232,256]{1,0:T(8,128)S(1)}, u32[]{:S(2)}, u32[]{:S(2)}) collective-permute-start(f32[232,256]{1,0:T(8,128)S(1)} %pad_maximum_fusion.1), channel_id=1, source_target_pairs={{0,16},{16,0},{1,17},{17,1},{2,18},{18,2},{3,19},{19,3},{4,20},{20... | collective-permute-start | bytes 712712 | tf_op jit(solution)/shard_map/ppermute | solution.py:137
  23.1 4.9 %collective-permute-start.8 = (f32[128,256]{1,0:T(8,128)S(1)}, f32[128,256]{1,0:T(8,128)S(1)}, u32[]{:S(2)}, u32[]{:S(2)}) collective-permute-start(f32[128,256]{1,0:T(8,128)S(1)} %slice_select_fusion), channel_id=1, source_target_pairs={{0,6},{1,21},{2,4},{3,23},{4,2},{5,17},{6,0},{7,19},{8,14},{9,29},... | collective-permute-start | bytes 393224 | tf_op jit(solution)/shard_map/ppermute | solution.py:148
  30.6 4.8 %copy-start.6 = (f32[128,128]{1,0:T(8,128)S(1)}, f32[128,128]{1,0:T(8,128)}, u32[]{:S(2)}) copy-start(f32[128,128]{1,0:T(8,128)} %constant.27.clone.refs_4_) | copy-start | bytes 196612
  30.6 4.8 %collective-permute-start.9 = (f32[5,136,256]{2,1,0:T(8,128)S(1)}, f32[5,136,256]{2,1,0:T(8,128)S(1)}, u32[]{:S(2)}, u32[]{:S(2)}) collective-permute-start(f32[5,136,256]{2,1,0:T(8,128)S(1)} %get-tuple-element.41), channel_id=1, source_target_pairs={{0,1},{1,0},{2,3},{3,2},{4,5},{5,4},{6,7},{7,6},{8,9},{9,8},{10,11... | collective-permute-start | bytes 2088968 | tf_op jit(solution)/shard_map/ppermute | solution.py:137
  33.5 1.8 %collective-permute-start.10 = (f32[3,136,256]{2,1,0:T(8,128)S(1)}, f32[3,136,256]{2,1,0:T(8,128)S(1)}, u32[]{:S(2)}, u32[]{:S(2)}) collective-permute-start(f32[3,136,256]{2,1,0:T(8,128)S(1)} %get-tuple-element.42), channel_id=1, source_target_pairs={{0,1},{1,0},{2,3},{3,2},{4,5},{5,4},{6,7},{7,6},{8,9},{9,8},{10,11... | collective-permute-start | bytes 1253384 | tf_op jit(solution)/shard_map/ppermute | solution.py:137

commit v13 on v12

--- a/solution.py
+++ b/solution.py
@@ -112,12 +112,16 @@
     mid = side // 2
     pairs = [(keep, recv, n) for keep, recv in zip(keeps, recvs) for n in range(keep.shape[0])]
     count = len(pairs)
-    for block in range(half // 8):
-        rows = pl.ds(block * 8, 8)
+    scales = []
+    for keep, recv, n in pairs:
+        power = (keep[n, half:half + 8] + recv[n, half:half + 8]) * (1.0 / entries)
+        scales.append(lax.rsqrt(power + 1e-6) * (1.0 / side))
+
+    def block(i, carry):
+        start = pl.multiple_of(i * 8, 8)
+        rows = pl.ds(start, 8)
         best = total = squares = None
-        for keep, recv, n in pairs:
-            power = (keep[n, half:half + 8] + recv[n, half:half + 8]) * (1.0 / entries)
-            scale = lax.rsqrt(power + 1e-6) * (1.0 / side)
+        for (keep, recv, n), scale in zip(pairs, scales):
             c = (keep[n, rows] + recv[n, rows]) * scale
             if best is None:
                 best, total, squares = c, c, c * c
@@ -127,7 +131,10 @@
         squares = squares * (1.0 / count)
         for n, (ref, value) in enumerate(((peak_ref, best), (mean_ref, total), (square_ref, squares))):
             ref[0, rows, :mid] = value[:, :mid]
-            flip_ref[pl.ds(n * half + block * 8, 8)] = value[:, mid:]
+            flip_ref[pl.ds(pl.multiple_of(n * half + start, 8), 8)] = value[:, mid:]
+        return carry
+
+    lax.fori_loop(0, half // 8, block, 0, unroll=2)
     right = jnp.dot(flip_ref[...], fold_ref[...], precision=lax.Precision.HIGHEST, preferred_element_type=jnp.float32)
     for n, ref in enumerate((peak_ref, mean_ref, square_ref)):
         ref[0, :, mid:] = right[n * half:(n + 1) * half]
@@ -182,7 +189,7 @@
 
     if lax.axis_size("groups") == 2 and orients == 8:
         plane = lax.axis_index("groups")
-        few = 104
+        few = 56
         pick = lambda whole, n: lax.dynamic_index_in_dim(whole, n, 0, keepdims=False)
         part = pick(template, plane)
         near1, near2 = (flipped(part, "orient", 2 * k) for k in (1, 2))

time: 36.7 us -> 35 us (0.954)
  the two profiles are of different devices: /device:TPU:17 before, /device:TPU:0 now
where the time goes in v13:
time: 35 us; the launch traced here: 34.9 us
  starting transfers between devices  15.1 us (43%)
  waiting for transfers between devices  13.2 us (38%)
  Pallas kernels  4.72 us (13%)
  local copies, waits for them, and re-layouts  1.07 us (3%)
  between operations  0.77 us (2%)
    ppermute x10, starting transfers between devices, flipped(): lax.ppermute(x, axis, [(i, i ^ bits) for i in range(lax.axis_size(axis))])  13.4 us
    ppermute x10, waiting for transfers between devices, flipped(): lax.ppermute(x, axis, [(i, i ^ bits) for i in range(lax.axis_size(axis))])  10.4 us
    ppermute x1, waiting for transfers between devices, crossed(): return lax.ppermute(x, ('groups', 'orient', 'tile'), pairs)  2.72 us
    pallas_call x2, Pallas kernels, maps(): pl.pallas_call(functools.partial(maps_kernel, len(wholes), places), in_sp...  2.66 us
    ppermute x1, starting transfers between devices, crossed(): return lax.ppermute(x, ('groups', 'orient', 'tile'), pairs)  1.67 us
    pallas_call x1, Pallas kernels, shards(): pl.pallas_call(functools.partial(stats_kernel, len(keeps), 2 * side * sid...  1.31 us
    squeeze x2, local copies, waits for them, and re-layouts, shards(): lax.dynamic_index_in_dim(whole, n, 0, keepdims=False)  0.98 us
    pallas_call x1, Pallas kernels, shards(): pl.pallas_call(prepare_kernel, in_specs=[hbm] * 3, out_specs=[vmem] * 3,...  0.75 us
  transfers between devices with their start and end apart: 11, of which 7 were waited for; matrix products, arithmetic and copies ran while one was open for 0% of the time, Pallas kernels for 10%

profile of v13, /device:TPU:0, one launch (start us, length us, event | category | flops | bytes accessed | tf_op | source)
XLA Modules:
  0.0 34.9 jit_solution(11427164399719970490)
XLA Ops:
  0.6 0.0 copy-start
  0.6 1.0 %dynamic-slice_bitcast_fusion.1 = f32[128,256]{1,0:T(8,128)S(1)} fusion(f32[1,2,128,256]{3,2,1,0:T(8,128)} %param.6, s32[]{:T(128)S(6)} %select_n.15), kind=kLoop, calls=%fused_computation.5 | loop fusion | bytes 262148 | tf_op jit(solution)/shard_map/jit(dynamic_index_in_dim)/squeeze | solution.py:193
  1.6 0.0 copy-done
  1.6 3.0 %collective-permute-start.2 = (f32[2,128,256]{2,1,0:T(8,128)S(1)}, f32[2,128,256]{2,1,0:T(8,128)S(1)}, u32[]{:S(2)}, u32[]{:S(2)}) collective-permute-start(f32[2,128,256]{2,1,0:T(8,128)S(1)} %bitcast.6), channel_id=1, source_target_pairs={{0,2},{2,0},{4,6},{6,4},{8,10},{10,8},{12,14},{14,12},{1,3},{3,1},... | collective-permute-start | bytes 786440 | tf_op jit(solution)/shard_map/ppermute | solution.py:144
  4.7 2.6 %collective-permute-start.1 = (f32[128,256]{1,0:T(8,128)S(1)}, f32[128,256]{1,0:T(8,128)S(1)}, u32[]{:S(2)}, u32[]{:S(2)}) collective-permute-start(f32[128,256]{1,0:T(8,128)S(1)} %dynamic-slice_bitcast_fusion.1), channel_id=1, source_target_pairs={{0,8},{2,10},{4,12},{6,14},{8,0},{10,2},{12,4},{14,6},{1,9},{3,11}... | collective-permute-start | bytes 393224 | tf_op jit(solution)/shard_map/ppermute | solution.py:144
  7.3 1.6 %collective-permute-start = (f32[128,256]{1,0:T(8,128)S(1)}, f32[128,256]{1,0:T(8,128)S(1)}, u32[]{:S(2)}, u32[]{:S(2)}) collective-permute-start(f32[128,256]{1,0:T(8,128)S(1)} %dynamic-slice_bitcast_fusion.1), channel_id=1, source_target_pairs={{0,4},{2,6},{4,0},{6,2},{8,12},{10,14},{12,8},{14,10},{1,5},{3,7},... | collective-permute-start | bytes 393224 | tf_op jit(solution)/shard_map/ppermute | solution.py:144
  8.8 4.6 %collective-permute-done.1 = f32[128,256]{1,0:T(8,128)S(1)} collective-permute-done((f32[128,256]{1,0:T(8,128)S(1)}, f32[128,256]{1,0:T(8,128)S(1)}, u32[]{:S(2)}, u32[]{:S(2)}) %collective-permute-start.1) | collective-permute-done | bytes 131104 | tf_op jit(solution)/shard_map/ppermute | solution.py:144
  13.4 0.2 collective-permute-done
  13.6 0.0 collective-permute-done.2.refs_1_
  13.7 0.0 copy-start.1
  13.7 0.5 %collective-permute-start.5 = (f32[256,256]{1,0:T(8,128)S(1)}, f32[256,256]{1,0:T(8,128)S(1)}, u32[]{:S(2)}, u32[]{:S(2)}) collective-permute-start(f32[256,256]{1,0:T(8,128)S(1)} %constant_dynamic-update-slice_fusion.refs_2_), channel_id=1, source_target_pairs={{0,2},{2,0},{4,6},{6,4},{8,10},{10,8},{12,14},{14,12},{1,3},{3,1},... | collective-permute-start | bytes 786440 | tf_op jit(solution)/shard_map/ppermute | solution.py:144
  14.2 1.5 %collective-permute-start.4 = (f32[256,256]{1,0:T(8,128)S(1)}, f32[256,256]{1,0:T(8,128)S(1)}, u32[]{:S(2)}, u32[]{:S(2)}) collective-permute-start(f32[256,256]{1,0:T(8,128)S(1)} %constant_dynamic-update-slice_fusion.refs_2_), channel_id=1, source_target_pairs={{0,16},{16,0},{1,17},{17,1},{2,18},{18,2},{3,19},{19,3},{4,20},{20... | collective-permute-start | bytes 786440 | tf_op jit(solution)/shard_map/ppermute | solution.py:144
  15.8 0.0 copy-start.2
  15.8 0.0 copy-start.3
  15.8 1.4 %collective-permute-start.3 = (f32[256,256]{1,0:T(8,128)S(1)}, f32[256,256]{1,0:T(8,128)S(1)}, u32[]{:S(2)}, u32[]{:S(2)}) collective-permute-start(f32[256,256]{1,0:T(8,128)S(1)} %pad_maximum_fusion), channel_id=1, source_target_pairs={{0,4},{2,6},{4,0},{6,2},{8,12},{10,14},{12,8},{14,10},{1,5},{3,7},... | collective-permute-start | bytes 786440 | tf_op jit(solution)/shard_map/ppermute | solution.py:144
  17.3 0.0 copy-done.1
  17.3 0.0 copy-done.2
  17.3 0.0 copy-done.3
  17.3 0.7 %prepare.1 = (f32[4,128,256]{2,1,0:T(8,128)S(1)}, bf16[2,256,256]{2,1,0:T(8,128)(2,1)S(1)}, bf16[2,256,256]{2,1,0:T(8,128)(2,1)S(1)}) custom-call(f32[2,128,256]{2,1,0:T(8,128)S(1)} %bitcast.8, f32[256,256]{1,0:T(8,128)S(1)} %copy-done.3, f32[2,256,256]{2,1,0:T(8,128)S(1)} %copy-done.1), custom_call_target="tpu_custom_call" | custom-call | tf_op jit(solution)/shard_map/prepare/pallas_call | solution.py:168
  18.0 2.1 %collective-permute-done.5.refs_4_.refs_0_ = f32[256,256]{1,0:T(8,128)S(1)} collective-permute-done((f32[256,256]{1,0:T(8,128)S(1)}, f32[256,256]{1,0:T(8,128)S(1)}, u32[]{:S(2)}, u32[]{:S(2)}) %collective-permute-start.5) | collective-permute-done | bytes 262176 | tf_op jit(solution)/shard_map/ppermute | solution.py:144
  20.1 0.5 %collective-permute-done.4.refs_3_ = f32[256,256]{1,0:T(8,128)S(1)} collective-permute-done((f32[256,256]{1,0:T(8,128)S(1)}, f32[256,256]{1,0:T(8,128)S(1)}, u32[]{:S(2)}, u32[]{:S(2)}) %collective-permute-start.4) | collective-permute-done | bytes 262176 | tf_op jit(solution)/shard_map/ppermute | solution.py:144
  20.6 1.7 %collective-permute-done.3.refs_5_.refs_3_ = f32[256,256]{1,0:T(8,128)S(1)} collective-permute-done((f32[256,256]{1,0:T(8,128)S(1)}, f32[256,256]{1,0:T(8,128)S(1)}, u32[]{:S(2)}, u32[]{:S(2)}) %collective-permute-start.3) | collective-permute-done | bytes 262176 | tf_op jit(solution)/shard_map/ppermute | solution.py:144
  22.3 0.5 %collective-permute-start.6 = (f32[184,256]{1,0:T(8,128)S(1)}, f32[184,256]{1,0:T(8,128)S(1)}, u32[]{:S(2)}, u32[]{:S(2)}) collective-permute-start(f32[184,256]{1,0:T(8,128)S(1)} %pad_maximum_fusion.2), channel_id=1, source_target_pairs={{0,16},{16,0},{1,17},{17,1},{2,18},{18,2},{3,19},{19,3},{4,20},{20... | collective-permute-start | bytes 565256 | tf_op jit(solution)/shard_map/ppermute | solution.py:144
  22.9 1.6 %collective-permute-start.7 = (f32[200,256]{1,0:T(8,128)S(1)}, f32[200,256]{1,0:T(8,128)S(1)}, u32[]{:S(2)}, u32[]{:S(2)}) collective-permute-start(f32[200,256]{1,0:T(8,128)S(1)} %pad_maximum_fusion.1), channel_id=1, source_target_pairs={{0,2},{2,0},{4,6},{6,4},{8,10},{10,8},{12,14},{14,12},{1,3},{3,1},... | collective-permute-start | bytes 614408 | tf_op jit(solution)/shard_map/ppermute | solution.py:144
  24.5 1.7 %collective-permute-start.8 = (f32[128,256]{1,0:T(8,128)S(1)}, f32[128,256]{1,0:T(8,128)S(1)}, u32[]{:S(2)}, u32[]{:S(2)}) collective-permute-start(f32[128,256]{1,0:T(8,128)S(1)} %slice_select_fusion), channel_id=1, source_target_pairs={{0,6},{1,21},{2,4},{3,23},{4,2},{5,17},{6,0},{7,19},{8,14},{9,29},... | collective-permute-start | bytes 393224 | tf_op jit(solution)/shard_map/ppermute | solution.py:155
  26.1 1.5 %maps.2 = (f32[5,136,256]{2,1,0:T(8,128)S(1)}, f32[5,136,256]{2,1,0:T(8,128)S(1)}) custom-call(f32[4,128,256]{2,1,0:T(8,128)S(1)} %get-tuple-element.31.coef_ref, bf16[2,256,256]{2,1,0:T(8,128)(2,1)S(1)} %get-tuple-element.32.rt_ref, bf16[2,256,256]{2,1,0:T(8,128)(2,1)S(1)} %get-tuple-element.33.col_ref, f32[2,128,256]{2,1,0:T(8,128)S(1)} %bitcast.7, ...), custom_call_target="tpu_custom_call" | custom-call | tf_op jit(solution)/shard_map/maps/pallas_call | solution.py:181
  27.7 2.7 %collective-permute-done.8.refs_4_ = f32[128,256]{1,0:T(8,128)S(1)} collective-permute-done((f32[128,256]{1,0:T(8,128)S(1)}, f32[128,256]{1,0:T(8,128)S(1)}, u32[]{:S(2)}, u32[]{:S(2)}) %collective-permute-start.8) | collective-permute-done | bytes 131104 | tf_op jit(solution)/shard_map/ppermute | solution.py:155
  30.4 0.0 collective-permute-done.6.refs_1_
  30.4 0.0 collective-permute-done.7.refs_2_
  30.4 0.0 copy-start.4
  30.4 0.1 collective-permute-start.9
  30.5 1.1 %maps.3 = (f32[3,136,256]{2,1,0:T(8,128)S(1)}, f32[3,136,256]{2,1,0:T(8,128)S(1)}) custom-call(f32[4,128,256]{2,1,0:T(8,128)S(1)} %get-tuple-element.31.coef_ref, bf16[2,256,256]{2,1,0:T(8,128)(2,1)S(1)} %get-tuple-element.32.rt_ref, bf16[2,256,256]{2,1,0:T(8,128)(2,1)S(1)} %get-tuple-element.33.col_ref, ...), custom_call_target="tpu_custom_call" | custom-call | tf_op jit(solution)/shard_map/maps/pallas_call | solution.py:181
  31.6 0.6 %collective-permute-start.10 = (f32[3,136,256]{2,1,0:T(8,128)S(1)}, f32[3,136,256]{2,1,0:T(8,128)S(1)}, u32[]{:S(2)}, u32[]{:S(2)}) collective-permute-start(f32[3,136,256]{2,1,0:T(8,128)S(1)} %get-tuple-element.42), channel_id=1, source_target_pairs={{0,1},{1,0},{2,3},{3,2},{4,5},{5,4},{6,7},{7,6},{8,9},{9,8},{10,11... | collective-permute-start | bytes 1253384 | tf_op jit(solution)/shard_map/ppermute | solution.py:144
  32.2 1.4 %collective-permute-done.10.refs_3_ = f32[3,136,256]{2,1,0:T(8,128)S(1)} collective-permute-done((f32[3,136,256]{2,1,0:T(8,128)S(1)}, f32[3,136,256]{2,1,0:T(8,128)S(1)}, u32[]{:S(2)}, u32[]{:S(2)}) %collective-permute-start.10) | collective-permute-done | bytes 417824 | tf_op jit(solution)/shard_map/ppermute | solution.py:144
  33.6 0.0 collective-permute-done.9.refs_2_
  33.6 0.0 copy-done.4
  33.6 1.3 %statistics.1 = (f32[1,128,256]{2,1,0:T(8,128)}, f32[1,128,256]{2,1,0:T(8,128)}, f32[1,128,256]{2,1,0:T(8,128)}) custom-call(f32[5,136,256]{2,1,0:T(8,128)S(1)} %get-tuple-element.36.refs_0_, f32[3,136,256]{2,1,0:T(8,128)S(1)} %get-tuple-element.40.refs_1_, f32[5,136,256]{2,1,0:T(8,128)S(1)} %collective-permute-done.9.refs_2_, ...), custom_call_target="tpu_custom_call" | custom-call | tf_op jit(solution)/shard_map/statistics/pallas_call | solution.py:229
  (10 shorter events, 0.1 us)
Async XLA Ops:
  0.6 1.0 %copy-start = (f32[1,2,128,256]{3,2,1,0:T(8,128)S(1)}, f32[1,2,128,256]{3,2,1,0:T(8,128)}, u32[]{:S(2)}) copy-start(f32[1,2,128,256]{3,2,1,0:T(8,128)} %param.6) | copy-start | bytes 786436
  1.6 12.0 %collective-permute-start.2 = (f32[2,128,256]{2,1,0:T(8,128)S(1)}, f32[2,128,256]{2,1,0:T(8,128)S(1)}, u32[]{:S(2)}, u32[]{:S(2)}) collective-permute-start(f32[2,128,256]{2,1,0:T(8,128)S(1)} %bitcast.6), channel_id=1, source_target_pairs={{0,2},{2,0},{4,6},{6,4},{8,10},{10,8},{12,14},{14,12},{1,3},{3,1},... | collective-permute-start | bytes 786440 | tf_op jit(solution)/shard_map/ppermute | solution.py:144
  4.7 8.8 %collective-permute-start.1 = (f32[128,256]{1,0:T(8,128)S(1)}, f32[128,256]{1,0:T(8,128)S(1)}, u32[]{:S(2)}, u32[]{:S(2)}) collective-permute-start(f32[128,256]{1,0:T(8,128)S(1)} %dynamic-slice_bitcast_fusion.1), channel_id=1, source_target_pairs={{0,8},{2,10},{4,12},{6,14},{8,0},{10,2},{12,4},{14,6},{1,9},{3,11}... | collective-permute-start | bytes 393224 | tf_op jit(solution)/shard_map/ppermute | solution.py:144
  7.3 6.4 %collective-permute-start = (f32[128,256]{1,0:T(8,128)S(1)}, f32[128,256]{1,0:T(8,128)S(1)}, u32[]{:S(2)}, u32[]{:S(2)}) collective-permute-start(f32[128,256]{1,0:T(8,128)S(1)} %dynamic-slice_bitcast_fusion.1), channel_id=1, source_target_pairs={{0,4},{2,6},{4,0},{6,2},{8,12},{10,14},{12,8},{14,10},{1,5},{3,7},... | collective-permute-start | bytes 393224 | tf_op jit(solution)/shard_map/ppermute | solution.py:144
  13.7 3.6 %copy-start.1 = (f32[2,256,256]{2,1,0:T(8,128)S(1)}, f32[2,256,256]{2,1,0:T(8,128)}, u32[]{:S(2)}) copy-start(f32[2,256,256]{2,1,0:T(8,128)} %constant.26.clone.table_hbm) | copy-start | bytes 1572868
  13.7 6.4 %collective-permute-start.5 = (f32[256,256]{1,0:T(8,128)S(1)}, f32[256,256]{1,0:T(8,128)S(1)}, u32[]{:S(2)}, u32[]{:S(2)}) collective-permute-start(f32[256,256]{1,0:T(8,128)S(1)} %constant_dynamic-update-slice_fusion.refs_2_), channel_id=1, source_target_pairs={{0,2},{2,0},{4,6},{6,4},{8,10},{10,8},{12,14},{14,12},{1,3},{3,1},... | collective-permute-start | bytes 786440 | tf_op jit(solution)/shard_map/ppermute | solution.py:144
  14.2 6.4 %collective-permute-start.4 = (f32[256,256]{1,0:T(8,128)S(1)}, f32[256,256]{1,0:T(8,128)S(1)}, u32[]{:S(2)}, u32[]{:S(2)}) collective-permute-start(f32[256,256]{1,0:T(8,128)S(1)} %constant_dynamic-update-slice_fusion.refs_2_), channel_id=1, source_target_pairs={{0,16},{16,0},{1,17},{17,1},{2,18},{18,2},{3,19},{19,3},{4,20},{20... | collective-permute-start | bytes 786440 | tf_op jit(solution)/shard_map/ppermute | solution.py:144
  15.8 1.5 %copy-start.2 = (f32[1,2,128,256]{3,2,1,0:T(8,128)S(1)}, f32[1,2,128,256]{3,2,1,0:T(8,128)}, u32[]{:S(2)}) copy-start(f32[1,2,128,256]{3,2,1,0:T(8,128)} %param.5) | copy-start | bytes 786436
  15.8 1.5 %copy-start.3 = (f32[256,256]{1,0:T(8,128)S(1)}, f32[256,256]{1,0:T(8,128)}, u32[]{:S(2)}) copy-start(f32[256,256]{1,0:T(8,128)} %w_hbm.1) | copy-start | bytes 786436
  15.8 6.4 %collective-permute-start.3 = (f32[256,256]{1,0:T(8,128)S(1)}, f32[256,256]{1,0:T(8,128)S(1)}, u32[]{:S(2)}, u32[]{:S(2)}) collective-permute-start(f32[256,256]{1,0:T(8,128)S(1)} %pad_maximum_fusion), channel_id=1, source_target_pairs={{0,4},{2,6},{4,0},{6,2},{8,12},{10,14},{12,8},{14,10},{1,5},{3,7},... | collective-permute-start | bytes 786440 | tf_op jit(solution)/shard_map/ppermute | solution.py:144
  22.3 8.1 %collective-permute-start.6 = (f32[184,256]{1,0:T(8,128)S(1)}, f32[184,256]{1,0:T(8,128)S(1)}, u32[]{:S(2)}, u32[]{:S(2)}) collective-permute-start(f32[184,256]{1,0:T(8,128)S(1)} %pad_maximum_fusion.2), channel_id=1, source_target_pairs={{0,16},{16,0},{1,17},{17,1},{2,18},{18,2},{3,19},{19,3},{4,20},{20... | collective-permute-start | bytes 565256 | tf_op jit(solution)/shard_map/ppermute | solution.py:144
  22.9 7.5 %collective-permute-start.7 = (f32[200,256]{1,0:T(8,128)S(1)}, f32[200,256]{1,0:T(8,128)S(1)}, u32[]{:S(2)}, u32[]{:S(2)}) collective-permute-start(f32[200,256]{1,0:T(8,128)S(1)} %pad_maximum_fusion.1), channel_id=1, source_target_pairs={{0,2},{2,0},{4,6},{6,4},{8,10},{10,8},{12,14},{14,12},{1,3},{3,1},... | collective-permute-start | bytes 614408 | tf_op jit(solution)/shard_map/ppermute | solution.py:144
  24.5 5.9 %collective-permute-start.8 = (f32[128,256]{1,0:T(8,128)S(1)}, f32[128,256]{1,0:T(8,128)S(1)}, u32[]{:S(2)}, u32[]{:S(2)}) collective-permute-start(f32[128,256]{1,0:T(8,128)S(1)} %slice_select_fusion), channel_id=1, source_target_pairs={{0,6},{1,21},{2,4},{3,23},{4,2},{5,17},{6,0},{7,19},{8,14},{9,29},... | collective-permute-start | bytes 393224 | tf_op jit(solution)/shard_map/ppermute | solution.py:155
  30.4 3.2 %copy-start.4 = (f32[128,128]{1,0:T(8,128)S(1)}, f32[128,128]{1,0:T(8,128)}, u32[]{:S(2)}) copy-start(f32[128,128]{1,0:T(8,128)} %constant.27.clone.refs_4_) | copy-start | bytes 196612
  30.4 3.1 %collective-permute-start.9 = (f32[5,136,256]{2,1,0:T(8,128)S(1)}, f32[5,136,256]{2,1,0:T(8,128)S(1)}, u32[]{:S(2)}, u32[]{:S(2)}) collective-permute-start(f32[5,136,256]{2,1,0:T(8,128)S(1)} %get-tuple-element.41), channel_id=1, source_target_pairs={{0,1},{1,0},{2,3},{3,2},{4,5},{5,4},{6,7},{7,6},{8,9},{9,8},{10,11... | collective-permute-start | bytes 2088968 | tf_op jit(solution)/shard_map/ppermute | solution.py:144
  31.6 1.9 %collective-permute-start.10 = (f32[3,136,256]{2,1,0:T(8,128)S(1)}, f32[3,136,256]{2,1,0:T(8,128)S(1)}, u32[]{:S(2)}, u32[]{:S(2)}) collective-permute-start(f32[3,136,256]{2,1,0:T(8,128)S(1)} %get-tuple-element.42), channel_id=1, source_target_pairs={{0,1},{1,0},{2,3},{3,2},{4,5},{5,4},{6,7},{7,6},{8,9},{9,8},{10,11... | collective-permute-start | bytes 1253384 | tf_op jit(solution)/shard_map/ppermute | solution.py:144

commit v14 on v12

--- a/solution.py
+++ b/solution.py
@@ -182,7 +182,7 @@
 
     if lax.axis_size("groups") == 2 and orients == 8:
         plane = lax.axis_index("groups")
-        few = 104
+        few = 72
         pick = lambda whole, n: lax.dynamic_index_in_dim(whole, n, 0, keepdims=False)
         part = pick(template, plane)
         near1, near2 = (flipped(part, "orient", 2 * k) for k in (1, 2))
@@ -195,8 +195,7 @@
         far, near_x, near_y, coef = lax.optimization_barrier((far, near_x, near_y, coef))
         last_y = flipped(jnp.concatenate([far[:half], near_x[half + few:]], 0), "orient", 1)
         last_x = flipped(jnp.concatenate([far[:half], near_y[half:half + few]], 0), "groups", 1)
-        second = jnp.where(lax.axis_index("tile") == 0, near_x[half:], near_y[half:])
-        corner = crossed(second, (0, 3), (1, 2))
+        corner = crossed(near_y[half:], (1, 2), (1, 2))
         block = lambda array, start=0, rows=half: ((array, start, start + rows),)
         early = maps(
             [template, beside],

time: 36.7 us -> 35.3 us (0.962)
  the two profiles are of different devices: /device:TPU:17 before, /device:TPU:0 now
where the time goes in v14:
time: 35.3 us; the launch traced here: 34.8 us
  starting transfers between devices  16.2 us (46%)
  waiting for transfers between devices  12.2 us (35%)
  Pallas kernels  4.6 us (13%)
  local copies, waits for them, and re-layouts  1.08 us (3%)
  between operations  0.76 us (2%)
    ppermute x10, starting transfers between devices, flipped(): lax.ppermute(x, axis, [(i, i ^ bits) for i in range(lax.axis_size(axis))])  13.5 us
    ppermute x10, waiting for transfers between devices, flipped(): lax.ppermute(x, axis, [(i, i ^ bits) for i in range(lax.axis_size(axis))])  10.4 us
    pallas_call x2, Pallas kernels, maps(): pl.pallas_call(functools.partial(maps_kernel, len(wholes), places), in_sp...  2.65 us
    ppermute x1, starting transfers between devices, crossed(): return lax.ppermute(x, ('groups', 'orient', 'tile'), pairs)  2.65 us
    ppermute x1, waiting for transfers between devices, crossed(): return lax.ppermute(x, ('groups', 'orient', 'tile'), pairs)  1.74 us
    pallas_call x1, Pallas kernels, shards(): pl.pallas_call(functools.partial(stats_kernel, len(keeps), 2 * side * sid...  1.2 us
    squeeze x2, local copies, waits for them, and re-layouts, shards(): lax.dynamic_index_in_dim(whole, n, 0, keepdims=False)  0.98 us
    pallas_call x1, Pallas kernels, shards(): pl.pallas_call(prepare_kernel, in_specs=[hbm] * 3, out_specs=[vmem] * 3,...  0.75 us
  transfers between devices with their start and end apart: 11, of which 7 were waited for; matrix products, arithmetic and copies ran while one was open for 0% of the time, Pallas kernels for 10%

profile of v14, /device:TPU:0, one launch (start us, length us, event | category | flops | bytes accessed | tf_op | source)
XLA Modules:
  0.0 34.8 jit_solution(5173228632131142416)
XLA Ops:
  0.6 0.0 copy-start
  0.6 1.0 %dynamic-slice_bitcast_fusion.1 = f32[128,256]{1,0:T(8,128)S(1)} fusion(f32[1,2,128,256]{3,2,1,0:T(8,128)} %param.6, s32[]{:T(128)S(6)} %select_n.7), kind=kLoop, calls=%fused_computation.4 | loop fusion | bytes 262148 | tf_op jit(solution)/shard_map/jit(dynamic_index_in_dim)/squeeze | solution.py:186
  1.6 0.0 copy-done
  1.6 3.0 %collective-permute-start.2 = (f32[2,128,256]{2,1,0:T(8,128)S(1)}, f32[2,128,256]{2,1,0:T(8,128)S(1)}, u32[]{:S(2)}, u32[]{:S(2)}) collective-permute-start(f32[2,128,256]{2,1,0:T(8,128)S(1)} %bitcast.6), channel_id=1, source_target_pairs={{0,2},{2,0},{4,6},{6,4},{8,10},{10,8},{12,14},{14,12},{1,3},{3,1},... | collective-permute-start | bytes 786440 | tf_op jit(solution)/shard_map/ppermute | solution.py:137
  4.7 2.6 %collective-permute-start.1 = (f32[128,256]{1,0:T(8,128)S(1)}, f32[128,256]{1,0:T(8,128)S(1)}, u32[]{:S(2)}, u32[]{:S(2)}) collective-permute-start(f32[128,256]{1,0:T(8,128)S(1)} %dynamic-slice_bitcast_fusion.1), channel_id=1, source_target_pairs={{0,8},{2,10},{4,12},{6,14},{8,0},{10,2},{12,4},{14,6},{1,9},{3,11}... | collective-permute-start | bytes 393224 | tf_op jit(solution)/shard_map/ppermute | solution.py:137
  7.3 1.6 %collective-permute-start = (f32[128,256]{1,0:T(8,128)S(1)}, f32[128,256]{1,0:T(8,128)S(1)}, u32[]{:S(2)}, u32[]{:S(2)}) collective-permute-start(f32[128,256]{1,0:T(8,128)S(1)} %dynamic-slice_bitcast_fusion.1), channel_id=1, source_target_pairs={{0,4},{2,6},{4,0},{6,2},{8,12},{10,14},{12,8},{14,10},{1,5},{3,7},... | collective-permute-start | bytes 393224 | tf_op jit(solution)/shard_map/ppermute | solution.py:137
  8.8 4.6 %collective-permute-done.1 = f32[128,256]{1,0:T(8,128)S(1)} collective-permute-done((f32[128,256]{1,0:T(8,128)S(1)}, f32[128,256]{1,0:T(8,128)S(1)}, u32[]{:S(2)}, u32[]{:S(2)}) %collective-permute-start.1) | collective-permute-done | bytes 131104 | tf_op jit(solution)/shard_map/ppermute | solution.py:137
  13.4 0.2 collective-permute-done
  13.6 0.0 collective-permute-done.2.refs_1_
  13.7 0.0 copy-start.1
  13.7 0.5 %collective-permute-start.5 = (f32[256,256]{1,0:T(8,128)S(1)}, f32[256,256]{1,0:T(8,128)S(1)}, u32[]{:S(2)}, u32[]{:S(2)}) collective-permute-start(f32[256,256]{1,0:T(8,128)S(1)} %constant_dynamic-update-slice_fusion.refs_2_), channel_id=1, source_target_pairs={{0,2},{2,0},{4,6},{6,4},{8,10},{10,8},{12,14},{14,12},{1,3},{3,1},... | collective-permute-start | bytes 786440 | tf_op jit(solution)/shard_map/ppermute | solution.py:137
  14.2 1.5 %collective-permute-start.4 = (f32[256,256]{1,0:T(8,128)S(1)}, f32[256,256]{1,0:T(8,128)S(1)}, u32[]{:S(2)}, u32[]{:S(2)}) collective-permute-start(f32[256,256]{1,0:T(8,128)S(1)} %constant_dynamic-update-slice_fusion.refs_2_), channel_id=1, source_target_pairs={{0,16},{16,0},{1,17},{17,1},{2,18},{18,2},{3,19},{19,3},{4,20},{20... | collective-permute-start | bytes 786440 | tf_op jit(solution)/shard_map/ppermute | solution.py:137
  15.8 0.0 copy-start.2
  15.8 0.0 copy-start.3
  15.8 1.4 %collective-permute-start.3 = (f32[256,256]{1,0:T(8,128)S(1)}, f32[256,256]{1,0:T(8,128)S(1)}, u32[]{:S(2)}, u32[]{:S(2)}) collective-permute-start(f32[256,256]{1,0:T(8,128)S(1)} %pad_maximum_fusion), channel_id=1, source_target_pairs={{0,4},{2,6},{4,0},{6,2},{8,12},{10,14},{12,8},{14,10},{1,5},{3,7},... | collective-permute-start | bytes 786440 | tf_op jit(solution)/shard_map/ppermute | solution.py:137
  17.3 0.0 copy-done.1
  17.3 0.0 copy-done.2
  17.3 0.0 copy-done.3
  17.3 0.7 %prepare.1 = (f32[4,128,256]{2,1,0:T(8,128)S(1)}, bf16[2,256,256]{2,1,0:T(8,128)(2,1)S(1)}, bf16[2,256,256]{2,1,0:T(8,128)(2,1)S(1)}) custom-call(f32[2,128,256]{2,1,0:T(8,128)S(1)} %bitcast.8, f32[256,256]{1,0:T(8,128)S(1)} %copy-done.3, f32[2,256,256]{2,1,0:T(8,128)S(1)} %copy-done.1), custom_call_target="tpu_custom_call" | custom-call | tf_op jit(solution)/shard_map/prepare/pallas_call | solution.py:161
  18.0 2.1 %collective-permute-done.5.refs_4_.refs_0_ = f32[256,256]{1,0:T(8,128)S(1)} collective-permute-done((f32[256,256]{1,0:T(8,128)S(1)}, f32[256,256]{1,0:T(8,128)S(1)}, u32[]{:S(2)}, u32[]{:S(2)}) %collective-permute-start.5) | collective-permute-done | bytes 262176 | tf_op jit(solution)/shard_map/ppermute | solution.py:137
  20.1 0.5 %collective-permute-done.4.refs_3_ = f32[256,256]{1,0:T(8,128)S(1)} collective-permute-done((f32[256,256]{1,0:T(8,128)S(1)}, f32[256,256]{1,0:T(8,128)S(1)}, u32[]{:S(2)}, u32[]{:S(2)}) %collective-permute-start.4) | collective-permute-done | bytes 262176 | tf_op jit(solution)/shard_map/ppermute | solution.py:137
  20.6 1.7 %collective-permute-done.3.refs_5_.refs_3_ = f32[256,256]{1,0:T(8,128)S(1)} collective-permute-done((f32[256,256]{1,0:T(8,128)S(1)}, f32[256,256]{1,0:T(8,128)S(1)}, u32[]{:S(2)}, u32[]{:S(2)}) %collective-permute-start.3) | collective-permute-done | bytes 262176 | tf_op jit(solution)/shard_map/ppermute | solution.py:137
  22.3 0.5 %collective-permute-start.6 = (f32[200,256]{1,0:T(8,128)S(1)}, f32[200,256]{1,0:T(8,128)S(1)}, u32[]{:S(2)}, u32[]{:S(2)}) collective-permute-start(f32[200,256]{1,0:T(8,128)S(1)} %pad_maximum_fusion.1), channel_id=1, source_target_pairs={{0,16},{16,0},{1,17},{17,1},{2,18},{18,2},{3,19},{19,3},{4,20},{20... | collective-permute-start | bytes 614408 | tf_op jit(solution)/shard_map/ppermute | solution.py:137
  22.9 1.6 %collective-permute-start.7 = (f32[184,256]{1,0:T(8,128)S(1)}, f32[184,256]{1,0:T(8,128)S(1)}, u32[]{:S(2)}, u32[]{:S(2)}) collective-permute-start(f32[184,256]{1,0:T(8,128)S(1)} %pad_maximum_fusion.2), channel_id=1, source_target_pairs={{0,2},{2,0},{4,6},{6,4},{8,10},{10,8},{12,14},{14,12},{1,3},{3,1},... | collective-permute-start | bytes 565256 | tf_op jit(solution)/shard_map/ppermute | solution.py:137
  24.5 2.7 %collective-permute-start.8 = (f32[128,256]{1,0:T(8,128)S(1)}, f32[128,256]{1,0:T(8,128)S(1)}, u32[]{:S(2)}, u32[]{:S(2)}) collective-permute-start(f32[128,256]{1,0:T(8,128)S(1)} %slice.16), channel_id=1, source_target_pairs={{0,20},{1,21},{2,22},{3,23},{4,16},{5,17},{6,18},{7,19},{8,28},{9,... | collective-permute-start | bytes 393224 | tf_op jit(solution)/shard_map/ppermute | solution.py:148
  27.2 1.5 %maps.2 = (f32[5,136,256]{2,1,0:T(8,128)S(1)}, f32[5,136,256]{2,1,0:T(8,128)S(1)}) custom-call(f32[4,128,256]{2,1,0:T(8,128)S(1)} %get-tuple-element.31.coef_ref, bf16[2,256,256]{2,1,0:T(8,128)(2,1)S(1)} %get-tuple-element.32.rt_ref, bf16[2,256,256]{2,1,0:T(8,128)(2,1)S(1)} %get-tuple-element.33.col_ref, f32[2,128,256]{2,1,0:T(8,128)S(1)} %bitcast.7, ...), custom_call_target="tpu_custom_call" | custom-call | tf_op jit(solution)/shard_map/maps/pallas_call | solution.py:174
  28.7 1.7 %collective-permute-done.8.refs_4_ = f32[128,256]{1,0:T(8,128)S(1)} collective-permute-done((f32[128,256]{1,0:T(8,128)S(1)}, f32[128,256]{1,0:T(8,128)S(1)}, u32[]{:S(2)}, u32[]{:S(2)}) %collective-permute-start.8) | collective-permute-done | bytes 131104 | tf_op jit(solution)/shard_map/ppermute | solution.py:148
  30.5 0.0 collective-permute-done.7.refs_2_
  30.5 0.0 collective-permute-done.6.refs_1_
  30.5 0.0 copy-start.4
  30.5 0.1 collective-permute-start.9
  30.6 1.1 %maps.3 = (f32[3,136,256]{2,1,0:T(8,128)S(1)}, f32[3,136,256]{2,1,0:T(8,128)S(1)}) custom-call(f32[4,128,256]{2,1,0:T(8,128)S(1)} %get-tuple-element.31.coef_ref, bf16[2,256,256]{2,1,0:T(8,128)(2,1)S(1)} %get-tuple-element.32.rt_ref, bf16[2,256,256]{2,1,0:T(8,128)(2,1)S(1)} %get-tuple-element.33.col_ref, ...), custom_call_target="tpu_custom_call" | custom-call | tf_op jit(solution)/shard_map/maps/pallas_call | solution.py:174
  31.7 0.6 %collective-permute-start.10 = (f32[3,136,256]{2,1,0:T(8,128)S(1)}, f32[3,136,256]{2,1,0:T(8,128)S(1)}, u32[]{:S(2)}, u32[]{:S(2)}) collective-permute-start(f32[3,136,256]{2,1,0:T(8,128)S(1)} %get-tuple-element.42), channel_id=1, source_target_pairs={{0,1},{1,0},{2,3},{3,2},{4,5},{5,4},{6,7},{7,6},{8,9},{9,8},{10,11... | collective-permute-start | bytes 1253384 | tf_op jit(solution)/shard_map/ppermute | solution.py:137
  32.2 1.4 %collective-permute-done.10.refs_3_ = f32[3,136,256]{2,1,0:T(8,128)S(1)} collective-permute-done((f32[3,136,256]{2,1,0:T(8,128)S(1)}, f32[3,136,256]{2,1,0:T(8,128)S(1)}, u32[]{:S(2)}, u32[]{:S(2)}) %collective-permute-start.10) | collective-permute-done | bytes 417824 | tf_op jit(solution)/shard_map/ppermute | solution.py:137
  33.6 0.0 collective-permute-done.9.refs_2_
  33.6 0.0 copy-done.4
  33.6 1.2 %statistics.1 = (f32[1,128,256]{2,1,0:T(8,128)}, f32[1,128,256]{2,1,0:T(8,128)}, f32[1,128,256]{2,1,0:T(8,128)}) custom-call(f32[5,136,256]{2,1,0:T(8,128)S(1)} %get-tuple-element.36.refs_0_, f32[3,136,256]{2,1,0:T(8,128)S(1)} %get-tuple-element.40.refs_1_, f32[5,136,256]{2,1,0:T(8,128)S(1)} %collective-permute-done.9.refs_2_, ...), custom_call_target="tpu_custom_call" | custom-call | tf_op jit(solution)/shard_map/statistics/pallas_call | solution.py:221
  (10 shorter events, 0.1 us)
Async XLA Ops:
  0.6 1.0 %copy-start = (f32[1,2,128,256]{3,2,1,0:T(8,128)S(1)}, f32[1,2,128,256]{3,2,1,0:T(8,128)}, u32[]{:S(2)}) copy-start(f32[1,2,128,256]{3,2,1,0:T(8,128)} %param.6) | copy-start | bytes 786436
  1.6 12.0 %collective-permute-start.2 = (f32[2,128,256]{2,1,0:T(8,128)S(1)}, f32[2,128,256]{2,1,0:T(8,128)S(1)}, u32[]{:S(2)}, u32[]{:S(2)}) collective-permute-start(f32[2,128,256]{2,1,0:T(8,128)S(1)} %bitcast.6), channel_id=1, source_target_pairs={{0,2},{2,0},{4,6},{6,4},{8,10},{10,8},{12,14},{14,12},{1,3},{3,1},... | collective-permute-start | bytes 786440 | tf_op jit(solution)/shard_map/ppermute | solution.py:137
  4.7 8.8 %collective-permute-start.1 = (f32[128,256]{1,0:T(8,128)S(1)}, f32[128,256]{1,0:T(8,128)S(1)}, u32[]{:S(2)}, u32[]{:S(2)}) collective-permute-start(f32[128,256]{1,0:T(8,128)S(1)} %dynamic-slice_bitcast_fusion.1), channel_id=1, source_target_pairs={{0,8},{2,10},{4,12},{6,14},{8,0},{10,2},{12,4},{14,6},{1,9},{3,11}... | collective-permute-start | bytes 393224 | tf_op jit(solution)/shard_map/ppermute | solution.py:137
  7.3 6.4 %collective-permute-start = (f32[128,256]{1,0:T(8,128)S(1)}, f32[128,256]{1,0:T(8,128)S(1)}, u32[]{:S(2)}, u32[]{:S(2)}) collective-permute-start(f32[128,256]{1,0:T(8,128)S(1)} %dynamic-slice_bitcast_fusion.1), channel_id=1, source_target_pairs={{0,4},{2,6},{4,0},{6,2},{8,12},{10,14},{12,8},{14,10},{1,5},{3,7},... | collective-permute-start | bytes 393224 | tf_op jit(solution)/shard_map/ppermute | solution.py:137
  13.7 3.6 %copy-start.1 = (f32[2,256,256]{2,1,0:T(8,128)S(1)}, f32[2,256,256]{2,1,0:T(8,128)}, u32[]{:S(2)}) copy-start(f32[2,256,256]{2,1,0:T(8,128)} %constant.23.clone.table_hbm) | copy-start | bytes 1572868
  13.7 6.4 %collective-permute-start.5 = (f32[256,256]{1,0:T(8,128)S(1)}, f32[256,256]{1,0:T(8,128)S(1)}, u32[]{:S(2)}, u32[]{:S(2)}) collective-permute-start(f32[256,256]{1,0:T(8,128)S(1)} %constant_dynamic-update-slice_fusion.refs_2_), channel_id=1, source_target_pairs={{0,2},{2,0},{4,6},{6,4},{8,10},{10,8},{12,14},{14,12},{1,3},{3,1},... | collective-permute-start | bytes 786440 | tf_op jit(solution)/shard_map/ppermute | solution.py:137
  14.2 6.4 %collective-permute-start.4 = (f32[256,256]{1,0:T(8,128)S(1)}, f32[256,256]{1,0:T(8,128)S(1)}, u32[]{:S(2)}, u32[]{:S(2)}) collective-permute-start(f32[256,256]{1,0:T(8,128)S(1)} %constant_dynamic-update-slice_fusion.refs_2_), channel_id=1, source_target_pairs={{0,16},{16,0},{1,17},{17,1},{2,18},{18,2},{3,19},{19,3},{4,20},{20... | collective-permute-start | bytes 786440 | tf_op jit(solution)/shard_map/ppermute | solution.py:137
  15.8 1.5 %copy-start.2 = (f32[1,2,128,256]{3,2,1,0:T(8,128)S(1)}, f32[1,2,128,256]{3,2,1,0:T(8,128)}, u32[]{:S(2)}) copy-start(f32[1,2,128,256]{3,2,1,0:T(8,128)} %param.5) | copy-start | bytes 786436
  15.8 1.5 %copy-start.3 = (f32[256,256]{1,0:T(8,128)S(1)}, f32[256,256]{1,0:T(8,128)}, u32[]{:S(2)}) copy-start(f32[256,256]{1,0:T(8,128)} %w_hbm.1) | copy-start | bytes 786436
  15.8 6.4 %collective-permute-start.3 = (f32[256,256]{1,0:T(8,128)S(1)}, f32[256,256]{1,0:T(8,128)S(1)}, u32[]{:S(2)}, u32[]{:S(2)}) collective-permute-start(f32[256,256]{1,0:T(8,128)S(1)} %pad_maximum_fusion), channel_id=1, source_target_pairs={{0,4},{2,6},{4,0},{6,2},{8,12},{10,14},{12,8},{14,10},{1,5},{3,7},... | collective-permute-start | bytes 786440 | tf_op jit(solution)/shard_map/ppermute | solution.py:137
  22.3 8.2 %collective-permute-start.6 = (f32[200,256]{1,0:T(8,128)S(1)}, f32[200,256]{1,0:T(8,128)S(1)}, u32[]{:S(2)}, u32[]{:S(2)}) collective-permute-start(f32[200,256]{1,0:T(8,128)S(1)} %pad_maximum_fusion.1), channel_id=1, source_target_pairs={{0,16},{16,0},{1,17},{17,1},{2,18},{18,2},{3,19},{19,3},{4,20},{20... | collective-permute-start | bytes 614408 | tf_op jit(solution)/shard_map/ppermute | solution.py:137
  22.9 7.6 %collective-permute-start.7 = (f32[184,256]{1,0:T(8,128)S(1)}, f32[184,256]{1,0:T(8,128)S(1)}, u32[]{:S(2)}, u32[]{:S(2)}) collective-permute-start(f32[184,256]{1,0:T(8,128)S(1)} %pad_maximum_fusion.2), channel_id=1, source_target_pairs={{0,2},{2,0},{4,6},{6,4},{8,10},{10,8},{12,14},{14,12},{1,3},{3,1},... | collective-permute-start | bytes 565256 | tf_op jit(solution)/shard_map/ppermute | solution.py:137
  24.5 5.9 %collective-permute-start.8 = (f32[128,256]{1,0:T(8,128)S(1)}, f32[128,256]{1,0:T(8,128)S(1)}, u32[]{:S(2)}, u32[]{:S(2)}) collective-permute-start(f32[128,256]{1,0:T(8,128)S(1)} %slice.16), channel_id=1, source_target_pairs={{0,20},{1,21},{2,22},{3,23},{4,16},{5,17},{6,18},{7,19},{8,28},{9,... | collective-permute-start | bytes 393224 | tf_op jit(solution)/shard_map/ppermute | solution.py:148
  30.5 3.2 %copy-start.4 = (f32[128,128]{1,0:T(8,128)S(1)}, f32[128,128]{1,0:T(8,128)}, u32[]{:S(2)}) copy-start(f32[128,128]{1,0:T(8,128)} %constant.24.clone.refs_4_) | copy-start | bytes 196612
  30.5 3.1 %collective-permute-start.9 = (f32[5,136,256]{2,1,0:T(8,128)S(1)}, f32[5,136,256]{2,1,0:T(8,128)S(1)}, u32[]{:S(2)}, u32[]{:S(2)}) collective-permute-start(f32[5,136,256]{2,1,0:T(8,128)S(1)} %get-tuple-element.41), channel_id=1, source_target_pairs={{0,1},{1,0},{2,3},{3,2},{4,5},{5,4},{6,7},{7,6},{8,9},{9,8},{10,11... | collective-permute-start | bytes 2088968 | tf_op jit(solution)/shard_map/ppermute | solution.py:137
  31.7 1.9 %collective-permute-start.10 = (f32[3,136,256]{2,1,0:T(8,128)S(1)}, f32[3,136,256]{2,1,0:T(8,128)S(1)}, u32[]{:S(2)}, u32[]{:S(2)}) collective-permute-start(f32[3,136,256]{2,1,0:T(8,128)S(1)} %get-tuple-element.42), channel_id=1, source_target_pairs={{0,1},{1,0},{2,3},{3,2},{4,5},{5,4},{6,7},{7,6},{8,9},{9,8},{10,11... | collective-permute-start | bytes 1253384 | tf_op jit(solution)/shard_map/ppermute | solution.py:137

commit v15 on v10

--- a/solution.py
+++ b/solution.py
@@ -79,7 +79,7 @@
     z = jnp.concatenate([coef_ref[0] * a + coef_ref[1] * b, coef_ref[3] * a - coef_ref[2] * b], 0)
     zh, zl = parts(z)
     ch, cl = col_ref[0], col_ref[1]
-    m = dot(zh, ch) + (dot(zl, ch) + dot(zh, cl))
+    m = dot(jnp.concatenate([zh, zl, zh], 1), jnp.concatenate([ch, ch, cl], 0))
     mcr, mci = m[:half, :mid], m[half:, :mid]
     msr, msi = m[:half, mid:], m[half:, mid:]
     first = lax.broadcasted_iota(jnp.int32, (half, mid), 1) == 0
@@ -87,7 +87,7 @@
     imag = jnp.concatenate([mci + jnp.where(first, 0.0, msr), jnp.where(first, msi, mci - msr)], 1)
     ah, al = parts(jnp.concatenate([real, imag], 0))
     rh, rl = rt_ref[0], rt_ref[1]
-    p = dot(rh, ah) + (dot(rh, al) + dot(rl, ah))
+    p = dot(jnp.concatenate([rh, rh, rl], 1), jnp.concatenate([ah, al, ah], 0))
     keep_ref[n, :half] = p[:half]
     keep_ref[n, half:] = power
     send_ref[n, :half] = p[half:]

time: 35 us -> 35 us (level)
  no operation moved by 1% of the time
where the time goes in v15:
time: 35 us; the launch traced here: 34.8 us
  starting transfers between devices  15.2 us (43%)
  waiting for transfers between devices  13.2 us (38%)
  Pallas kernels  4.6 us (13%)
  local copies, waits for them, and re-layouts  1.08 us (3%)
  between operations  0.76 us (2%)
    ppermute x11, starting transfers between devices, flipped(): lax.ppermute(x, axis, [(i, i ^ bits) for i in range(lax.axis_size(axis))])  15.2 us
    ppermute x11, waiting for transfers between devices, flipped(): lax.ppermute(x, axis, [(i, i ^ bits) for i in range(lax.axis_size(axis))])  13.2 us
    pallas_call x2, Pallas kernels, maps(): pl.pallas_call(functools.partial(maps_kernel, len(wholes), places), in_sp...  2.65 us
    pallas_call x1, Pallas kernels, shards(): pl.pallas_call(functools.partial(stats_kernel, len(keeps), 2 * side * sid...  1.2 us
    squeeze x2, local copies, waits for them, and re-layouts, shards(): lax.dynamic_index_in_dim(whole, n, 0, keepdims=False)  0.98 us
    pallas_call x1, Pallas kernels, shards(): pl.pallas_call(prepare_kernel, in_specs=[hbm] * 3, out_specs=[vmem] * 3,...  0.75 us
  transfers between devices with their start and end apart: 11, of which 7 were waited for; matrix products, arithmetic and copies ran while one was open for 0% of the time, Pallas kernels for 10%

profile of v15, /device:TPU:0, one launch (start us, length us, event | category | flops | bytes accessed | tf_op | source)
XLA Modules:
  0.0 34.8 jit_solution(3671134389215657664)
XLA Ops:
  0.6 0.0 copy-start
  0.6 1.0 %dynamic-slice_bitcast_fusion.1 = f32[128,256]{1,0:T(8,128)S(1)} fusion(f32[1,2,128,256]{3,2,1,0:T(8,128)} %param.6, s32[]{:T(128)S(6)} %select_n.7), kind=kLoop, calls=%fused_computation.4 | loop fusion | bytes 262148 | tf_op jit(solution)/shard_map/jit(dynamic_index_in_dim)/squeeze | solution.py:175
  1.6 0.0 copy-done
  1.6 3.0 %collective-permute-start.2 = (f32[2,128,256]{2,1,0:T(8,128)S(1)}, f32[2,128,256]{2,1,0:T(8,128)S(1)}, u32[]{:S(2)}, u32[]{:S(2)}) collective-permute-start(f32[2,128,256]{2,1,0:T(8,128)S(1)} %bitcast.6), channel_id=1, source_target_pairs={{0,2},{2,0},{4,6},{6,4},{8,10},{10,8},{12,14},{14,12},{1,3},{3,1},... | collective-permute-start | bytes 786440 | tf_op jit(solution)/shard_map/ppermute | solution.py:137
  4.7 2.6 %collective-permute-start.1 = (f32[128,256]{1,0:T(8,128)S(1)}, f32[128,256]{1,0:T(8,128)S(1)}, u32[]{:S(2)}, u32[]{:S(2)}) collective-permute-start(f32[128,256]{1,0:T(8,128)S(1)} %dynamic-slice_bitcast_fusion.1), channel_id=1, source_target_pairs={{0,8},{2,10},{4,12},{6,14},{8,0},{10,2},{12,4},{14,6},{1,9},{3,11}... | collective-permute-start | bytes 393224 | tf_op jit(solution)/shard_map/ppermute | solution.py:137
  7.3 1.6 %collective-permute-start = (f32[128,256]{1,0:T(8,128)S(1)}, f32[128,256]{1,0:T(8,128)S(1)}, u32[]{:S(2)}, u32[]{:S(2)}) collective-permute-start(f32[128,256]{1,0:T(8,128)S(1)} %dynamic-slice_bitcast_fusion.1), channel_id=1, source_target_pairs={{0,4},{2,6},{4,0},{6,2},{8,12},{10,14},{12,8},{14,10},{1,5},{3,7},... | collective-permute-start | bytes 393224 | tf_op jit(solution)/shard_map/ppermute | solution.py:137
  8.8 4.6 %collective-permute-done.1 = f32[128,256]{1,0:T(8,128)S(1)} collective-permute-done((f32[128,256]{1,0:T(8,128)S(1)}, f32[128,256]{1,0:T(8,128)S(1)}, u32[]{:S(2)}, u32[]{:S(2)}) %collective-permute-start.1) | collective-permute-done | bytes 131104 | tf_op jit(solution)/shard_map/ppermute | solution.py:137
  13.4 0.2 collective-permute-done
  13.6 0.0 collective-permute-done.2.refs_1_
  13.7 0.0 copy-start.1
  13.7 0.5 %collective-permute-start.5 = (f32[256,256]{1,0:T(8,128)S(1)}, f32[256,256]{1,0:T(8,128)S(1)}, u32[]{:S(2)}, u32[]{:S(2)}) collective-permute-start(f32[256,256]{1,0:T(8,128)S(1)} %constant_dynamic-update-slice_fusion.refs_2_), channel_id=1, source_target_pairs={{0,2},{2,0},{4,6},{6,4},{8,10},{10,8},{12,14},{14,12},{1,3},{3,1},... | collective-permute-start | bytes 786440 | tf_op jit(solution)/shard_map/ppermute | solution.py:137
  14.2 1.5 %collective-permute-start.4 = (f32[256,256]{1,0:T(8,128)S(1)}, f32[256,256]{1,0:T(8,128)S(1)}, u32[]{:S(2)}, u32[]{:S(2)}) collective-permute-start(f32[256,256]{1,0:T(8,128)S(1)} %constant_dynamic-update-slice_fusion.refs_2_), channel_id=1, source_target_pairs={{0,16},{16,0},{1,17},{17,1},{2,18},{18,2},{3,19},{19,3},{4,20},{20... | collective-permute-start | bytes 786440 | tf_op jit(solution)/shard_map/ppermute | solution.py:137
  15.8 0.0 copy-start.2
  15.8 0.0 copy-start.3
  15.8 1.4 %collective-permute-start.3 = (f32[256,256]{1,0:T(8,128)S(1)}, f32[256,256]{1,0:T(8,128)S(1)}, u32[]{:S(2)}, u32[]{:S(2)}) collective-permute-start(f32[256,256]{1,0:T(8,128)S(1)} %pad_maximum_fusion), channel_id=1, source_target_pairs={{0,4},{2,6},{4,0},{6,2},{8,12},{10,14},{12,8},{14,10},{1,5},{3,7},... | collective-permute-start | bytes 786440 | tf_op jit(solution)/shard_map/ppermute | solution.py:137
  17.3 0.0 copy-done.1
  17.3 0.0 copy-done.2
  17.3 0.0 copy-done.3
  17.3 0.7 %prepare.1 = (f32[4,128,256]{2,1,0:T(8,128)S(1)}, bf16[2,256,256]{2,1,0:T(8,128)(2,1)S(1)}, bf16[2,256,256]{2,1,0:T(8,128)(2,1)S(1)}) custom-call(f32[2,128,256]{2,1,0:T(8,128)S(1)} %bitcast.8, f32[256,256]{1,0:T(8,128)S(1)} %copy-done.3, f32[2,256,256]{2,1,0:T(8,128)S(1)} %copy-done.1), custom_call_target="tpu_custom_call" | custom-call | tf_op jit(solution)/shard_map/prepare/pallas_call | solution.py:150
  18.0 2.1 %collective-permute-done.5.refs_4_.refs_0_ = f32[256,256]{1,0:T(8,128)S(1)} collective-permute-done((f32[256,256]{1,0:T(8,128)S(1)}, f32[256,256]{1,0:T(8,128)S(1)}, u32[]{:S(2)}, u32[]{:S(2)}) %collective-permute-start.5) | collective-permute-done | bytes 262176 | tf_op jit(solution)/shard_map/ppermute | solution.py:137
  20.1 0.5 %collective-permute-done.4.refs_3_ = f32[256,256]{1,0:T(8,128)S(1)} collective-permute-done((f32[256,256]{1,0:T(8,128)S(1)}, f32[256,256]{1,0:T(8,128)S(1)}, u32[]{:S(2)}, u32[]{:S(2)}) %collective-permute-start.4) | collective-permute-done | bytes 262176 | tf_op jit(solution)/shard_map/ppermute | solution.py:137
  20.6 1.7 %collective-permute-done.3.refs_5_.refs_3_ = f32[256,256]{1,0:T(8,128)S(1)} collective-permute-done((f32[256,256]{1,0:T(8,128)S(1)}, f32[256,256]{1,0:T(8,128)S(1)}, u32[]{:S(2)}, u32[]{:S(2)}) %collective-permute-start.3) | collective-permute-done | bytes 262176 | tf_op jit(solution)/shard_map/ppermute | solution.py:137
  22.3 0.5 %collective-permute-start.6 = (f32[248,256]{1,0:T(8,128)S(1)}, f32[248,256]{1,0:T(8,128)S(1)}, u32[]{:S(2)}, u32[]{:S(2)}) collective-permute-start(f32[248,256]{1,0:T(8,128)S(1)} %pad_maximum_fusion.1), channel_id=1, source_target_pairs={{0,16},{16,0},{1,17},{17,1},{2,18},{18,2},{3,19},{19,3},{4,20},{20... | collective-permute-start | bytes 761864 | tf_op jit(solution)/shard_map/ppermute | solution.py:137
  22.9 1.6 %collective-permute-start.7 = (f32[136,256]{1,0:T(8,128)S(1)}, f32[136,256]{1,0:T(8,128)S(1)}, u32[]{:S(2)}, u32[]{:S(2)}) collective-permute-start(f32[136,256]{1,0:T(8,128)S(1)} %pad_maximum_fusion.2), channel_id=1, source_target_pairs={{0,2},{2,0},{4,6},{6,4},{8,10},{10,8},{12,14},{14,12},{1,3},{3,1},... | collective-permute-start | bytes 417800 | tf_op jit(solution)/shard_map/ppermute | solution.py:137
  24.5 1.7 %collective-permute-start.8 = (f32[128,256]{1,0:T(8,128)S(1)}, f32[128,256]{1,0:T(8,128)S(1)}, u32[]{:S(2)}, u32[]{:S(2)}) collective-permute-start(f32[128,256]{1,0:T(8,128)S(1)} %slice.16), channel_id=1, source_target_pairs={{0,6},{2,4},{4,2},{6,0},{8,14},{10,12},{12,10},{14,8},{1,7},{3,5},... | collective-permute-start | bytes 393224 | tf_op jit(solution)/shard_map/ppermute | solution.py:137
  26.2 1.5 %maps.2 = (f32[5,136,256]{2,1,0:T(8,128)S(1)}, f32[5,136,256]{2,1,0:T(8,128)S(1)}) custom-call(f32[4,128,256]{2,1,0:T(8,128)S(1)} %get-tuple-element.31.coef_ref, bf16[2,256,256]{2,1,0:T(8,128)(2,1)S(1)} %get-tuple-element.32.rt_ref, bf16[2,256,256]{2,1,0:T(8,128)(2,1)S(1)} %get-tuple-element.33.col_ref, f32[2,128,256]{2,1,0:T(8,128)S(1)} %bitcast.7, ...), custom_call_target="tpu_custom_call" | custom-call | tf_op jit(solution)/shard_map/maps/pallas_call | solution.py:163
  27.7 2.7 %collective-permute-done.8.refs_4_ = f32[128,256]{1,0:T(8,128)S(1)} collective-permute-done((f32[128,256]{1,0:T(8,128)S(1)}, f32[128,256]{1,0:T(8,128)S(1)}, u32[]{:S(2)}, u32[]{:S(2)}) %collective-permute-start.8) | collective-permute-done | bytes 131104 | tf_op jit(solution)/shard_map/ppermute | solution.py:137
  30.5 0.0 collective-permute-done.7.refs_2_
  30.5 0.0 collective-permute-done.6.refs_1_
  30.5 0.0 copy-start.4
  30.5 0.1 collective-permute-start.9
  30.6 1.1 %maps.3 = (f32[3,136,256]{2,1,0:T(8,128)S(1)}, f32[3,136,256]{2,1,0:T(8,128)S(1)}) custom-call(f32[4,128,256]{2,1,0:T(8,128)S(1)} %get-tuple-element.31.coef_ref, bf16[2,256,256]{2,1,0:T(8,128)(2,1)S(1)} %get-tuple-element.32.rt_ref, bf16[2,256,256]{2,1,0:T(8,128)(2,1)S(1)} %get-tuple-element.33.col_ref, ...), custom_call_target="tpu_custom_call" | custom-call | tf_op jit(solution)/shard_map/maps/pallas_call | solution.py:163
  31.7 0.6 %collective-permute-start.10 = (f32[3,136,256]{2,1,0:T(8,128)S(1)}, f32[3,136,256]{2,1,0:T(8,128)S(1)}, u32[]{:S(2)}, u32[]{:S(2)}) collective-permute-start(f32[3,136,256]{2,1,0:T(8,128)S(1)} %get-tuple-element.42), channel_id=1, source_target_pairs={{0,1},{1,0},{2,3},{3,2},{4,5},{5,4},{6,7},{7,6},{8,9},{9,8},{10,11... | collective-permute-start | bytes 1253384 | tf_op jit(solution)/shard_map/ppermute | solution.py:137
  32.2 1.4 %collective-permute-done.10.refs_3_ = f32[3,136,256]{2,1,0:T(8,128)S(1)} collective-permute-done((f32[3,136,256]{2,1,0:T(8,128)S(1)}, f32[3,136,256]{2,1,0:T(8,128)S(1)}, u32[]{:S(2)}, u32[]{:S(2)}) %collective-permute-start.10) | collective-permute-done | bytes 417824 | tf_op jit(solution)/shard_map/ppermute | solution.py:137
  33.6 0.0 collective-permute-done.9.refs_2_
  33.6 0.0 copy-done.4
  33.6 1.2 %statistics.1 = (f32[1,128,256]{2,1,0:T(8,128)}, f32[1,128,256]{2,1,0:T(8,128)}, f32[1,128,256]{2,1,0:T(8,128)}) custom-call(f32[5,136,256]{2,1,0:T(8,128)S(1)} %get-tuple-element.36.refs_0_, f32[3,136,256]{2,1,0:T(8,128)S(1)} %get-tuple-element.40.refs_1_, f32[5,136,256]{2,1,0:T(8,128)S(1)} %collective-permute-done.9.refs_2_, ...), custom_call_target="tpu_custom_call" | custom-call | tf_op jit(solution)/shard_map/statistics/pallas_call | solution.py:210
  (10 shorter events, 0.1 us)
Async XLA Ops:
  0.6 1.0 %copy-start = (f32[1,2,128,256]{3,2,1,0:T(8,128)S(1)}, f32[1,2,128,256]{3,2,1,0:T(8,128)}, u32[]{:S(2)}) copy-start(f32[1,2,128,256]{3,2,1,0:T(8,128)} %param.6) | copy-start | bytes 786436
  1.6 12.0 %collective-permute-start.2 = (f32[2,128,256]{2,1,0:T(8,128)S(1)}, f32[2,128,256]{2,1,0:T(8,128)S(1)}, u32[]{:S(2)}, u32[]{:S(2)}) collective-permute-start(f32[2,128,256]{2,1,0:T(8,128)S(1)} %bitcast.6), channel_id=1, source_target_pairs={{0,2},{2,0},{4,6},{6,4},{8,10},{10,8},{12,14},{14,12},{1,3},{3,1},... | collective-permute-start | bytes 786440 | tf_op jit(solution)/shard_map/ppermute | solution.py:137
  4.7 8.8 %collective-permute-start.1 = (f32[128,256]{1,0:T(8,128)S(1)}, f32[128,256]{1,0:T(8,128)S(1)}, u32[]{:S(2)}, u32[]{:S(2)}) collective-permute-start(f32[128,256]{1,0:T(8,128)S(1)} %dynamic-slice_bitcast_fusion.1), channel_id=1, source_target_pairs={{0,8},{2,10},{4,12},{6,14},{8,0},{10,2},{12,4},{14,6},{1,9},{3,11}... | collective-permute-start | bytes 393224 | tf_op jit(solution)/shard_map/ppermute | solution.py:137
  7.3 6.4 %collective-permute-start = (f32[128,256]{1,0:T(8,128)S(1)}, f32[128,256]{1,0:T(8,128)S(1)}, u32[]{:S(2)}, u32[]{:S(2)}) collective-permute-start(f32[128,256]{1,0:T(8,128)S(1)} %dynamic-slice_bitcast_fusion.1), channel_id=1, source_target_pairs={{0,4},{2,6},{4,0},{6,2},{8,12},{10,14},{12,8},{14,10},{1,5},{3,7},... | collective-permute-start | bytes 393224 | tf_op jit(solution)/shard_map/ppermute | solution.py:137
  13.7 3.6 %copy-start.1 = (f32[2,256,256]{2,1,0:T(8,128)S(1)}, f32[2,256,256]{2,1,0:T(8,128)}, u32[]{:S(2)}) copy-start(f32[2,256,256]{2,1,0:T(8,128)} %constant.23.clone.table_hbm) | copy-start | bytes 1572868
  13.7 6.4 %collective-permute-start.5 = (f32[256,256]{1,0:T(8,128)S(1)}, f32[256,256]{1,0:T(8,128)S(1)}, u32[]{:S(2)}, u32[]{:S(2)}) collective-permute-start(f32[256,256]{1,0:T(8,128)S(1)} %constant_dynamic-update-slice_fusion.refs_2_), channel_id=1, source_target_pairs={{0,2},{2,0},{4,6},{6,4},{8,10},{10,8},{12,14},{14,12},{1,3},{3,1},... | collective-permute-start | bytes 786440 | tf_op jit(solution)/shard_map/ppermute | solution.py:137
  14.2 6.4 %collective-permute-start.4 = (f32[256,256]{1,0:T(8,128)S(1)}, f32[256,256]{1,0:T(8,128)S(1)}, u32[]{:S(2)}, u32[]{:S(2)}) collective-permute-start(f32[256,256]{1,0:T(8,128)S(1)} %constant_dynamic-update-slice_fusion.refs_2_), channel_id=1, source_target_pairs={{0,16},{16,0},{1,17},{17,1},{2,18},{18,2},{3,19},{19,3},{4,20},{20... | collective-permute-start | bytes 786440 | tf_op jit(solution)/shard_map/ppermute | solution.py:137
  15.8 1.5 %copy-start.2 = (f32[1,2,128,256]{3,2,1,0:T(8,128)S(1)}, f32[1,2,128,256]{3,2,1,0:T(8,128)}, u32[]{:S(2)}) copy-start(f32[1,2,128,256]{3,2,1,0:T(8,128)} %param.5) | copy-start | bytes 786436
  15.8 1.5 %copy-start.3 = (f32[256,256]{1,0:T(8,128)S(1)}, f32[256,256]{1,0:T(8,128)}, u32[]{:S(2)}) copy-start(f32[256,256]{1,0:T(8,128)} %w_hbm.1) | copy-start | bytes 786436
  15.8 6.4 %collective-permute-start.3 = (f32[256,256]{1,0:T(8,128)S(1)}, f32[256,256]{1,0:T(8,128)S(1)}, u32[]{:S(2)}, u32[]{:S(2)}) collective-permute-start(f32[256,256]{1,0:T(8,128)S(1)} %pad_maximum_fusion), channel_id=1, source_target_pairs={{0,4},{2,6},{4,0},{6,2},{8,12},{10,14},{12,8},{14,10},{1,5},{3,7},... | collective-permute-start | bytes 786440 | tf_op jit(solution)/shard_map/ppermute | solution.py:137
  22.3 8.2 %collective-permute-start.6 = (f32[248,256]{1,0:T(8,128)S(1)}, f32[248,256]{1,0:T(8,128)S(1)}, u32[]{:S(2)}, u32[]{:S(2)}) collective-permute-start(f32[248,256]{1,0:T(8,128)S(1)} %pad_maximum_fusion.1), channel_id=1, source_target_pairs={{0,16},{16,0},{1,17},{17,1},{2,18},{18,2},{3,19},{19,3},{4,20},{20... | collective-permute-start | bytes 761864 | tf_op jit(solution)/shard_map/ppermute | solution.py:137
  22.9 7.6 %collective-permute-start.7 = (f32[136,256]{1,0:T(8,128)S(1)}, f32[136,256]{1,0:T(8,128)S(1)}, u32[]{:S(2)}, u32[]{:S(2)}) collective-permute-start(f32[136,256]{1,0:T(8,128)S(1)} %pad_maximum_fusion.2), channel_id=1, source_target_pairs={{0,2},{2,0},{4,6},{6,4},{8,10},{10,8},{12,14},{14,12},{1,3},{3,1},... | collective-permute-start | bytes 417800 | tf_op jit(solution)/shard_map/ppermute | solution.py:137
  24.5 5.9 %collective-permute-start.8 = (f32[128,256]{1,0:T(8,128)S(1)}, f32[128,256]{1,0:T(8,128)S(1)}, u32[]{:S(2)}, u32[]{:S(2)}) collective-permute-start(f32[128,256]{1,0:T(8,128)S(1)} %slice.16), channel_id=1, source_target_pairs={{0,6},{2,4},{4,2},{6,0},{8,14},{10,12},{12,10},{14,8},{1,7},{3,5},... | collective-permute-start | bytes 393224 | tf_op jit(solution)/shard_map/ppermute | solution.py:137
  30.5 3.1 %copy-start.4 = (f32[128,128]{1,0:T(8,128)S(1)}, f32[128,128]{1,0:T(8,128)}, u32[]{:S(2)}) copy-start(f32[128,128]{1,0:T(8,128)} %constant.24.clone.refs_4_) | copy-start | bytes 196612
  30.5 3.1 %collective-permute-start.9 = (f32[5,136,256]{2,1,0:T(8,128)S(1)}, f32[5,136,256]{2,1,0:T(8,128)S(1)}, u32[]{:S(2)}, u32[]{:S(2)}) collective-permute-start(f32[5,136,256]{2,1,0:T(8,128)S(1)} %get-tuple-element.41), channel_id=1, source_target_pairs={{0,1},{1,0},{2,3},{3,2},{4,5},{5,4},{6,7},{7,6},{8,9},{9,8},{10,11... | collective-permute-start | bytes 2088968 | tf_op jit(solution)/shard_map/ppermute | solution.py:137
  31.7 1.9 %collective-permute-start.10 = (f32[3,136,256]{2,1,0:T(8,128)S(1)}, f32[3,136,256]{2,1,0:T(8,128)S(1)}, u32[]{:S(2)}, u32[]{:S(2)}) collective-permute-start(f32[3,136,256]{2,1,0:T(8,128)S(1)} %get-tuple-element.42), channel_id=1, source_target_pairs={{0,1},{1,0},{2,3},{3,2},{4,5},{5,4},{6,7},{7,6},{8,9},{9,8},{10,11... | collective-permute-start | bytes 1253384 | tf_op jit(solution)/shard_map/ppermute | solution.py:137

commit v16 on v10

--- a/solution.py
+++ b/solution.py
@@ -112,12 +112,14 @@
     mid = side // 2
     pairs = [(keep, recv, n) for keep, recv in zip(keeps, recvs) for n in range(keep.shape[0])]
     count = len(pairs)
+    scales = []
+    for keep, recv, n in pairs:
+        power = (keep[n, half:half + 8] + recv[n, half:half + 8]) * (1.0 / entries)
+        scales.append(lax.rsqrt(power + 1e-6) * (1.0 / side))
     for block in range(half // 8):
         rows = pl.ds(block * 8, 8)
         best = total = squares = None
-        for keep, recv, n in pairs:
-            power = (keep[n, half:half + 8] + recv[n, half:half + 8]) * (1.0 / entries)
-            scale = lax.rsqrt(power + 1e-6) * (1.0 / side)
+        for (keep, recv, n), scale in zip(pairs, scales):
             c = (keep[n, rows] + recv[n, rows]) * scale
             if best is None:
                 best, total, squares = c, c, c * c

time: 35 us -> 34.9 us (level)
  no operation moved by 1% of the time
where the time goes in v16:
time: 34.9 us; the launch traced here: 34.8 us
  starting transfers between devices  15.2 us (44%)
  waiting for transfers between devices  13.2 us (38%)
  Pallas kernels  4.56 us (13%)
  local copies, waits for them, and re-layouts  1.08 us (3%)
  between operations  0.76 us (2%)
    ppermute x11, starting transfers between devices, flipped(): lax.ppermute(x, axis, [(i, i ^ bits) for i in range(lax.axis_size(axis))])  15.2 us
    ppermute x11, waiting for transfers between devices, flipped(): lax.ppermute(x, axis, [(i, i ^ bits) for i in range(lax.axis_size(axis))])  13.2 us
    pallas_call x2, Pallas kernels, maps(): pl.pallas_call(functools.partial(maps_kernel, len(wholes), places), in_sp...  2.65 us
    pallas_call x1, Pallas kernels, shards(): pl.pallas_call(functools.partial(stats_kernel, len(keeps), 2 * side * sid...  1.16 us
    squeeze x2, local copies, waits for them, and re-layouts, shards(): lax.dynamic_index_in_dim(whole, n, 0, keepdims=False)  0.98 us
    pallas_call x1, Pallas kernels, shards(): pl.pallas_call(prepare_kernel, in_specs=[hbm] * 3, out_specs=[vmem] * 3,...  0.75 us
  transfers between devices with their start and end apart: 11, of which 7 were waited for; matrix products, arithmetic and copies ran while one was open for 0% of the time, Pallas kernels for 10%

profile of v16, /device:TPU:0, one launch (start us, length us, event | category | flops | bytes accessed | tf_op | source)
XLA Modules:
  0.0 34.8 jit_solution(1402120353872653344)
XLA Ops:
  0.6 0.0 copy-start
  0.6 1.0 %dynamic-slice_bitcast_fusion.1 = f32[128,256]{1,0:T(8,128)S(1)} fusion(f32[1,2,128,256]{3,2,1,0:T(8,128)} %param.6, s32[]{:T(128)S(6)} %select_n.7), kind=kLoop, calls=%fused_computation.4 | loop fusion | bytes 262148 | tf_op jit(solution)/shard_map/jit(dynamic_index_in_dim)/squeeze | solution.py:177
  1.6 0.0 copy-done
  1.6 3.0 %collective-permute-start.2 = (f32[2,128,256]{2,1,0:T(8,128)S(1)}, f32[2,128,256]{2,1,0:T(8,128)S(1)}, u32[]{:S(2)}, u32[]{:S(2)}) collective-permute-start(f32[2,128,256]{2,1,0:T(8,128)S(1)} %bitcast.6), channel_id=1, source_target_pairs={{0,2},{2,0},{4,6},{6,4},{8,10},{10,8},{12,14},{14,12},{1,3},{3,1},... | collective-permute-start | bytes 786440 | tf_op jit(solution)/shard_map/ppermute | solution.py:139
  4.7 2.6 %collective-permute-start.1 = (f32[128,256]{1,0:T(8,128)S(1)}, f32[128,256]{1,0:T(8,128)S(1)}, u32[]{:S(2)}, u32[]{:S(2)}) collective-permute-start(f32[128,256]{1,0:T(8,128)S(1)} %dynamic-slice_bitcast_fusion.1), channel_id=1, source_target_pairs={{0,8},{2,10},{4,12},{6,14},{8,0},{10,2},{12,4},{14,6},{1,9},{3,11}... | collective-permute-start | bytes 393224 | tf_op jit(solution)/shard_map/ppermute | solution.py:139
  7.3 1.6 %collective-permute-start = (f32[128,256]{1,0:T(8,128)S(1)}, f32[128,256]{1,0:T(8,128)S(1)}, u32[]{:S(2)}, u32[]{:S(2)}) collective-permute-start(f32[128,256]{1,0:T(8,128)S(1)} %dynamic-slice_bitcast_fusion.1), channel_id=1, source_target_pairs={{0,4},{2,6},{4,0},{6,2},{8,12},{10,14},{12,8},{14,10},{1,5},{3,7},... | collective-permute-start | bytes 393224 | tf_op jit(solution)/shard_map/ppermute | solution.py:139
  8.8 4.6 %collective-permute-done.1 = f32[128,256]{1,0:T(8,128)S(1)} collective-permute-done((f32[128,256]{1,0:T(8,128)S(1)}, f32[128,256]{1,0:T(8,128)S(1)}, u32[]{:S(2)}, u32[]{:S(2)}) %collective-permute-start.1) | collective-permute-done | bytes 131104 | tf_op jit(solution)/shard_map/ppermute | solution.py:139
  13.4 0.2 collective-permute-done
  13.6 0.0 collective-permute-done.2.refs_1_
  13.7 0.0 copy-start.1
  13.7 0.5 %collective-permute-start.5 = (f32[256,256]{1,0:T(8,128)S(1)}, f32[256,256]{1,0:T(8,128)S(1)}, u32[]{:S(2)}, u32[]{:S(2)}) collective-permute-start(f32[256,256]{1,0:T(8,128)S(1)} %constant_dynamic-update-slice_fusion.refs_2_), channel_id=1, source_target_pairs={{0,2},{2,0},{4,6},{6,4},{8,10},{10,8},{12,14},{14,12},{1,3},{3,1},... | collective-permute-start | bytes 786440 | tf_op jit(solution)/shard_map/ppermute | solution.py:139
  14.2 1.5 %collective-permute-start.4 = (f32[256,256]{1,0:T(8,128)S(1)}, f32[256,256]{1,0:T(8,128)S(1)}, u32[]{:S(2)}, u32[]{:S(2)}) collective-permute-start(f32[256,256]{1,0:T(8,128)S(1)} %constant_dynamic-update-slice_fusion.refs_2_), channel_id=1, source_target_pairs={{0,16},{16,0},{1,17},{17,1},{2,18},{18,2},{3,19},{19,3},{4,20},{20... | collective-permute-start | bytes 786440 | tf_op jit(solution)/shard_map/ppermute | solution.py:139
  15.8 0.0 copy-start.2
  15.8 0.0 copy-start.3
  15.8 1.4 %collective-permute-start.3 = (f32[256,256]{1,0:T(8,128)S(1)}, f32[256,256]{1,0:T(8,128)S(1)}, u32[]{:S(2)}, u32[]{:S(2)}) collective-permute-start(f32[256,256]{1,0:T(8,128)S(1)} %pad_maximum_fusion), channel_id=1, source_target_pairs={{0,4},{2,6},{4,0},{6,2},{8,12},{10,14},{12,8},{14,10},{1,5},{3,7},... | collective-permute-start | bytes 786440 | tf_op jit(solution)/shard_map/ppermute | solution.py:139
  17.3 0.0 copy-done.1
  17.3 0.0 copy-done.2
  17.3 0.0 copy-done.3
  17.3 0.7 %prepare.1 = (f32[4,128,256]{2,1,0:T(8,128)S(1)}, bf16[2,256,256]{2,1,0:T(8,128)(2,1)S(1)}, bf16[2,256,256]{2,1,0:T(8,128)(2,1)S(1)}) custom-call(f32[2,128,256]{2,1,0:T(8,128)S(1)} %bitcast.8, f32[256,256]{1,0:T(8,128)S(1)} %copy-done.3, f32[2,256,256]{2,1,0:T(8,128)S(1)} %copy-done.1), custom_call_target="tpu_custom_call" | custom-call | tf_op jit(solution)/shard_map/prepare/pallas_call | solution.py:152
  18.0 2.1 %collective-permute-done.5.refs_4_.refs_0_ = f32[256,256]{1,0:T(8,128)S(1)} collective-permute-done((f32[256,256]{1,0:T(8,128)S(1)}, f32[256,256]{1,0:T(8,128)S(1)}, u32[]{:S(2)}, u32[]{:S(2)}) %collective-permute-start.5) | collective-permute-done | bytes 262176 | tf_op jit(solution)/shard_map/ppermute | solution.py:139
  20.1 0.5 %collective-permute-done.4.refs_3_ = f32[256,256]{1,0:T(8,128)S(1)} collective-permute-done((f32[256,256]{1,0:T(8,128)S(1)}, f32[256,256]{1,0:T(8,128)S(1)}, u32[]{:S(2)}, u32[]{:S(2)}) %collective-permute-start.4) | collective-permute-done | bytes 262176 | tf_op jit(solution)/shard_map/ppermute | solution.py:139
  20.6 1.7 %collective-permute-done.3.refs_5_.refs_3_ = f32[256,256]{1,0:T(8,128)S(1)} collective-permute-done((f32[256,256]{1,0:T(8,128)S(1)}, f32[256,256]{1,0:T(8,128)S(1)}, u32[]{:S(2)}, u32[]{:S(2)}) %collective-permute-start.3) | collective-permute-done | bytes 262176 | tf_op jit(solution)/shard_map/ppermute | solution.py:139
  22.3 0.5 %collective-permute-start.6 = (f32[248,256]{1,0:T(8,128)S(1)}, f32[248,256]{1,0:T(8,128)S(1)}, u32[]{:S(2)}, u32[]{:S(2)}) collective-permute-start(f32[248,256]{1,0:T(8,128)S(1)} %pad_maximum_fusion.1), channel_id=1, source_target_pairs={{0,16},{16,0},{1,17},{17,1},{2,18},{18,2},{3,19},{19,3},{4,20},{20... | collective-permute-start | bytes 761864 | tf_op jit(solution)/shard_map/ppermute | solution.py:139
  22.9 1.6 %collective-permute-start.7 = (f32[136,256]{1,0:T(8,128)S(1)}, f32[136,256]{1,0:T(8,128)S(1)}, u32[]{:S(2)}, u32[]{:S(2)}) collective-permute-start(f32[136,256]{1,0:T(8,128)S(1)} %pad_maximum_fusion.2), channel_id=1, source_target_pairs={{0,2},{2,0},{4,6},{6,4},{8,10},{10,8},{12,14},{14,12},{1,3},{3,1},... | collective-permute-start | bytes 417800 | tf_op jit(solution)/shard_map/ppermute | solution.py:139
  24.5 1.7 %collective-permute-start.8 = (f32[128,256]{1,0:T(8,128)S(1)}, f32[128,256]{1,0:T(8,128)S(1)}, u32[]{:S(2)}, u32[]{:S(2)}) collective-permute-start(f32[128,256]{1,0:T(8,128)S(1)} %slice.16), channel_id=1, source_target_pairs={{0,6},{2,4},{4,2},{6,0},{8,14},{10,12},{12,10},{14,8},{1,7},{3,5},... | collective-permute-start | bytes 393224 | tf_op jit(solution)/shard_map/ppermute | solution.py:139
  26.2 1.5 %maps.2 = (f32[5,136,256]{2,1,0:T(8,128)S(1)}, f32[5,136,256]{2,1,0:T(8,128)S(1)}) custom-call(f32[4,128,256]{2,1,0:T(8,128)S(1)} %get-tuple-element.31.coef_ref, bf16[2,256,256]{2,1,0:T(8,128)(2,1)S(1)} %get-tuple-element.32.rt_ref, bf16[2,256,256]{2,1,0:T(8,128)(2,1)S(1)} %get-tuple-element.33.col_ref, f32[2,128,256]{2,1,0:T(8,128)S(1)} %bitcast.7, ...), custom_call_target="tpu_custom_call" | custom-call | tf_op jit(solution)/shard_map/maps/pallas_call | solution.py:165
  27.7 2.7 %collective-permute-done.8.refs_4_ = f32[128,256]{1,0:T(8,128)S(1)} collective-permute-done((f32[128,256]{1,0:T(8,128)S(1)}, f32[128,256]{1,0:T(8,128)S(1)}, u32[]{:S(2)}, u32[]{:S(2)}) %collective-permute-start.8) | collective-permute-done | bytes 131104 | tf_op jit(solution)/shard_map/ppermute | solution.py:139
  30.5 0.0 collective-permute-done.7.refs_2_
  30.5 0.0 collective-permute-done.6.refs_1_
  30.5 0.0 copy-start.4
  30.5 0.1 collective-permute-start.9
  30.6 1.1 %maps.3 = (f32[3,136,256]{2,1,0:T(8,128)S(1)}, f32[3,136,256]{2,1,0:T(8,128)S(1)}) custom-call(f32[4,128,256]{2,1,0:T(8,128)S(1)} %get-tuple-element.31.coef_ref, bf16[2,256,256]{2,1,0:T(8,128)(2,1)S(1)} %get-tuple-element.32.rt_ref, bf16[2,256,256]{2,1,0:T(8,128)(2,1)S(1)} %get-tuple-element.33.col_ref, ...), custom_call_target="tpu_custom_call" | custom-call | tf_op jit(solution)/shard_map/maps/pallas_call | solution.py:165
  31.7 0.6 %collective-permute-start.10 = (f32[3,136,256]{2,1,0:T(8,128)S(1)}, f32[3,136,256]{2,1,0:T(8,128)S(1)}, u32[]{:S(2)}, u32[]{:S(2)}) collective-permute-start(f32[3,136,256]{2,1,0:T(8,128)S(1)} %get-tuple-element.42), channel_id=1, source_target_pairs={{0,1},{1,0},{2,3},{3,2},{4,5},{5,4},{6,7},{7,6},{8,9},{9,8},{10,11... | collective-permute-start | bytes 1253384 | tf_op jit(solution)/shard_map/ppermute | solution.py:139
  32.2 1.4 %collective-permute-done.10.refs_3_ = f32[3,136,256]{2,1,0:T(8,128)S(1)} collective-permute-done((f32[3,136,256]{2,1,0:T(8,128)S(1)}, f32[3,136,256]{2,1,0:T(8,128)S(1)}, u32[]{:S(2)}, u32[]{:S(2)}) %collective-permute-start.10) | collective-permute-done | bytes 417824 | tf_op jit(solution)/shard_map/ppermute | solution.py:139
  33.6 0.0 collective-permute-done.9.refs_2_
  33.6 0.0 copy-done.4
  33.6 1.2 %statistics.1 = (f32[1,128,256]{2,1,0:T(8,128)}, f32[1,128,256]{2,1,0:T(8,128)}, f32[1,128,256]{2,1,0:T(8,128)}) custom-call(f32[5,136,256]{2,1,0:T(8,128)S(1)} %get-tuple-element.36.refs_0_, f32[3,136,256]{2,1,0:T(8,128)S(1)} %get-tuple-element.40.refs_1_, f32[5,136,256]{2,1,0:T(8,128)S(1)} %collective-permute-done.9.refs_2_, ...), custom_call_target="tpu_custom_call" | custom-call | tf_op jit(solution)/shard_map/statistics/pallas_call | solution.py:212
  (10 shorter events, 0.1 us)
Async XLA Ops:
  0.6 1.0 %copy-start = (f32[1,2,128,256]{3,2,1,0:T(8,128)S(1)}, f32[1,2,128,256]{3,2,1,0:T(8,128)}, u32[]{:S(2)}) copy-start(f32[1,2,128,256]{3,2,1,0:T(8,128)} %param.6) | copy-start | bytes 786436
  1.6 12.0 %collective-permute-start.2 = (f32[2,128,256]{2,1,0:T(8,128)S(1)}, f32[2,128,256]{2,1,0:T(8,128)S(1)}, u32[]{:S(2)}, u32[]{:S(2)}) collective-permute-start(f32[2,128,256]{2,1,0:T(8,128)S(1)} %bitcast.6), channel_id=1, source_target_pairs={{0,2},{2,0},{4,6},{6,4},{8,10},{10,8},{12,14},{14,12},{1,3},{3,1},... | collective-permute-start | bytes 786440 | tf_op jit(solution)/shard_map/ppermute | solution.py:139
  4.7 8.8 %collective-permute-start.1 = (f32[128,256]{1,0:T(8,128)S(1)}, f32[128,256]{1,0:T(8,128)S(1)}, u32[]{:S(2)}, u32[]{:S(2)}) collective-permute-start(f32[128,256]{1,0:T(8,128)S(1)} %dynamic-slice_bitcast_fusion.1), channel_id=1, source_target_pairs={{0,8},{2,10},{4,12},{6,14},{8,0},{10,2},{12,4},{14,6},{1,9},{3,11}... | collective-permute-start | bytes 393224 | tf_op jit(solution)/shard_map/ppermute | solution.py:139
  7.3 6.4 %collective-permute-start = (f32[128,256]{1,0:T(8,128)S(1)}, f32[128,256]{1,0:T(8,128)S(1)}, u32[]{:S(2)}, u32[]{:S(2)}) collective-permute-start(f32[128,256]{1,0:T(8,128)S(1)} %dynamic-slice_bitcast_fusion.1), channel_id=1, source_target_pairs={{0,4},{2,6},{4,0},{6,2},{8,12},{10,14},{12,8},{14,10},{1,5},{3,7},... | collective-permute-start | bytes 393224 | tf_op jit(solution)/shard_map/ppermute | solution.py:139
  13.7 3.6 %copy-start.1 = (f32[2,256,256]{2,1,0:T(8,128)S(1)}, f32[2,256,256]{2,1,0:T(8,128)}, u32[]{:S(2)}) copy-start(f32[2,256,256]{2,1,0:T(8,128)} %constant.23.clone.table_hbm) | copy-start | bytes 1572868
  13.7 6.4 %collective-permute-start.5 = (f32[256,256]{1,0:T(8,128)S(1)}, f32[256,256]{1,0:T(8,128)S(1)}, u32[]{:S(2)}, u32[]{:S(2)}) collective-permute-start(f32[256,256]{1,0:T(8,128)S(1)} %constant_dynamic-update-slice_fusion.refs_2_), channel_id=1, source_target_pairs={{0,2},{2,0},{4,6},{6,4},{8,10},{10,8},{12,14},{14,12},{1,3},{3,1},... | collective-permute-start | bytes 786440 | tf_op jit(solution)/shard_map/ppermute | solution.py:139
  14.2 6.4 %collective-permute-start.4 = (f32[256,256]{1,0:T(8,128)S(1)}, f32[256,256]{1,0:T(8,128)S(1)}, u32[]{:S(2)}, u32[]{:S(2)}) collective-permute-start(f32[256,256]{1,0:T(8,128)S(1)} %constant_dynamic-update-slice_fusion.refs_2_), channel_id=1, source_target_pairs={{0,16},{16,0},{1,17},{17,1},{2,18},{18,2},{3,19},{19,3},{4,20},{20... | collective-permute-start | bytes 786440 | tf_op jit(solution)/shard_map/ppermute | solution.py:139
  15.8 1.5 %copy-start.2 = (f32[1,2,128,256]{3,2,1,0:T(8,128)S(1)}, f32[1,2,128,256]{3,2,1,0:T(8,128)}, u32[]{:S(2)}) copy-start(f32[1,2,128,256]{3,2,1,0:T(8,128)} %param.5) | copy-start | bytes 786436
  15.8 1.5 %copy-start.3 = (f32[256,256]{1,0:T(8,128)S(1)}, f32[256,256]{1,0:T(8,128)}, u32[]{:S(2)}) copy-start(f32[256,256]{1,0:T(8,128)} %w_hbm.1) | copy-start | bytes 786436
  15.8 6.4 %collective-permute-start.3 = (f32[256,256]{1,0:T(8,128)S(1)}, f32[256,256]{1,0:T(8,128)S(1)}, u32[]{:S(2)}, u32[]{:S(2)}) collective-permute-start(f32[256,256]{1,0:T(8,128)S(1)} %pad_maximum_fusion), channel_id=1, source_target_pairs={{0,4},{2,6},{4,0},{6,2},{8,12},{10,14},{12,8},{14,10},{1,5},{3,7},... | collective-permute-start | bytes 786440 | tf_op jit(solution)/shard_map/ppermute | solution.py:139
  22.3 8.2 %collective-permute-start.6 = (f32[248,256]{1,0:T(8,128)S(1)}, f32[248,256]{1,0:T(8,128)S(1)}, u32[]{:S(2)}, u32[]{:S(2)}) collective-permute-start(f32[248,256]{1,0:T(8,128)S(1)} %pad_maximum_fusion.1), channel_id=1, source_target_pairs={{0,16},{16,0},{1,17},{17,1},{2,18},{18,2},{3,19},{19,3},{4,20},{20... | collective-permute-start | bytes 761864 | tf_op jit(solution)/shard_map/ppermute | solution.py:139
  22.9 7.6 %collective-permute-start.7 = (f32[136,256]{1,0:T(8,128)S(1)}, f32[136,256]{1,0:T(8,128)S(1)}, u32[]{:S(2)}, u32[]{:S(2)}) collective-permute-start(f32[136,256]{1,0:T(8,128)S(1)} %pad_maximum_fusion.2), channel_id=1, source_target_pairs={{0,2},{2,0},{4,6},{6,4},{8,10},{10,8},{12,14},{14,12},{1,3},{3,1},... | collective-permute-start | bytes 417800 | tf_op jit(solution)/shard_map/ppermute | solution.py:139
  24.5 5.9 %collective-permute-start.8 = (f32[128,256]{1,0:T(8,128)S(1)}, f32[128,256]{1,0:T(8,128)S(1)}, u32[]{:S(2)}, u32[]{:S(2)}) collective-permute-start(f32[128,256]{1,0:T(8,128)S(1)} %slice.16), channel_id=1, source_target_pairs={{0,6},{2,4},{4,2},{6,0},{8,14},{10,12},{12,10},{14,8},{1,7},{3,5},... | collective-permute-start | bytes 393224 | tf_op jit(solution)/shard_map/ppermute | solution.py:139
  30.5 3.2 %copy-start.4 = (f32[128,128]{1,0:T(8,128)S(1)}, f32[128,128]{1,0:T(8,128)}, u32[]{:S(2)}) copy-start(f32[128,128]{1,0:T(8,128)} %constant.24.clone.refs_4_) | copy-start | bytes 196612
  30.5 3.1 %collective-permute-start.9 = (f32[5,136,256]{2,1,0:T(8,128)S(1)}, f32[5,136,256]{2,1,0:T(8,128)S(1)}, u32[]{:S(2)}, u32[]{:S(2)}) collective-permute-start(f32[5,136,256]{2,1,0:T(8,128)S(1)} %get-tuple-element.41), channel_id=1, source_target_pairs={{0,1},{1,0},{2,3},{3,2},{4,5},{5,4},{6,7},{7,6},{8,9},{9,8},{10,11... | collective-permute-start | bytes 2088968 | tf_op jit(solution)/shard_map/ppermute | solution.py:139
  31.7 1.9 %collective-permute-start.10 = (f32[3,136,256]{2,1,0:T(8,128)S(1)}, f32[3,136,256]{2,1,0:T(8,128)S(1)}, u32[]{:S(2)}, u32[]{:S(2)}) collective-permute-start(f32[3,136,256]{2,1,0:T(8,128)S(1)} %get-tuple-element.42), channel_id=1, source_target_pairs={{0,1},{1,0},{2,3},{3,2},{4,5},{5,4},{6,7},{7,6},{8,9},{9,8},{10,11... | collective-permute-start | bytes 1253384 | tf_op jit(solution)/shard_map/ppermute | solution.py:139
